TPU v7x, 32 devices: a whole 2x2x4 slice. The times are simulated.
32 devices in a mesh: clip: 4 (over z), frame: 8 (over y, x, core).
Axes of the slice: x: 2, y: 2, z: 4, core: 2. Of those that a mesh axis runs over, the one named last changes fastest.
Arguments:
- tokens: bfloat16 [4, 8, 196, 1024], P('clip', 'frame'), may hold values from -6 to 6
- counts: int32 [4], P('clip'), may hold values from 1 to 8, 16 in all
- norm_gain: float32 [1024], replicated, may hold values from 0.1 to 1.9
- input_weights: bfloat16 [1024, 3072], P('frame', 'clip'), may hold values from -5 to 5
- output_weights: bfloat16 [1024, 1024], P('frame', 'clip'), may hold values from -0.1875 to 0.1875
- cotangent: bfloat16 [4, 8, 196, 1024], P('clip', 'frame'), may hold values from -6 to 6
Outputs:
- result: bfloat16 [4, 8, 196, 1024], P('clip', 'frame')
- grad_tokens: bfloat16 [4, 8, 196, 1024], P('clip', 'frame')
Inputs may be any that keep to these rules, and one draw needn't show every extreme that they name: The 4 counts sum to 16.
All inputs are finite; a program needn't handle non-finite values. No bound on the sum of `counts` on one device may be relied on, other than what follows from the above.
Results may differ from a plain program's by a relative error of at most 0.006.
Values may be sent and summed in bfloat16 or wider, within the bound.
No kernel may reach another device: no remote copies, remote signals or barrier semaphores. Data moves between devices by JAX's collectives and lax.ppermute only.
A program may use at most 64 MiB of HBM per device.

v0:
```python
import jax
import jax.numpy as jnp
from jax import lax
from jax.sharding import PartitionSpec as P

DH = 64


EPSILON = 1e-06
NEGATIVE = -1e30


def layer_norm(wide_precision_rows, norm_gain):
    average = jnp.mean(wide_precision_rows, axis=-1, keepdims=True)
    centred = wide_precision_rows - average
    variance = jnp.mean(centred * centred, axis=-1, keepdims=True)
    return centred * lax.rsqrt(variance + EPSILON) * norm_gain


def to_items(source):
    slot_count, patches, embedding_width = source.shape
    pair_count = embedding_width // (2 * DH)
    shaped = source.reshape(slot_count, 4, patches // 4, pair_count, 2 * DH)
    return shaped.transpose(0, 1, 3, 2, 4).reshape(slot_count, 4 * pair_count, patches // 4, 2 * DH)


def from_items(source):
    slot_count, item_count, quarter, pair_width = source.shape
    pair_count = item_count // 4
    shaped = source.reshape(slot_count, 4, pair_count, quarter, pair_width)
    return shaped.transpose(0, 1, 3, 2, 4).reshape(slot_count, 4 * quarter, pair_count * pair_width)


def split_heads(source):
    return source.reshape(source.shape[:3] + (2, DH))


def attention_probs(query_heads, key_heads, length):
    frames_total = query_heads.shape[0]
    scores = jnp.einsum(
        "tiphd,uiphd->iphtu", query_heads, key_heads, preferred_element_type=jnp.float32
    ) * DH ** (-0.5)
    live_keys = jnp.arange(frames_total) < length
    scores = jnp.where(live_keys, scores, NEGATIVE)
    highest = jnp.max(scores, axis=-1, keepdims=True)
    expanded = jnp.exp(scores - highest)
    return expanded / jnp.sum(expanded, axis=-1, keepdims=True)


def product(source, weights, pattern, out_width):
    flat_rows = source.reshape(-1, source.shape[-1])
    joined = jnp.einsum(pattern, flat_rows, weights, preferred_element_type=jnp.float32)
    return joined.reshape(source.shape[0], source.shape[1], out_width)


def per_device(tokens, counts, norm_gain, input_weights, output_weights, cotangent):
    columns_input, columns_output = (
        lax.all_gather(input_weights, "clip", axis=1, tiled=True),
        lax.all_gather(output_weights, "clip", axis=1, tiled=True),
    )
    whole_input, whole_output = (
        lax.all_gather(columns_input, "frame", axis=0, tiled=True),
        lax.all_gather(columns_output, "frame", axis=0, tiled=True),
    )
    slot_count = tokens.shape[1]
    embedding_width = tokens.shape[3]
    length = counts[0]
    position = lax.axis_index("frame") * slot_count + jnp.arange(slot_count)
    occupied_frame_slots = position < length
    frame_presence_mask = occupied_frame_slots.astype(jnp.float32)[:, None, None]
    wide_precision_rows = tokens[0].astype(jnp.float32)
    normed = layer_norm(wide_precision_rows, norm_gain).astype(jnp.bfloat16)
    projected = product(normed, whole_input, "pk,kn->pn", 3 * embedding_width).astype(jnp.bfloat16)
    query_items, key_items, value_items = (
        lax.all_to_all(
            to_items(projected[..., :embedding_width]),
            "frame",
            split_axis=1,
            concat_axis=0,
            tiled=True,
        ),
        lax.all_to_all(
            to_items(projected[..., embedding_width : 2 * embedding_width]),
            "frame",
            split_axis=1,
            concat_axis=0,
            tiled=True,
        ),
        lax.all_to_all(
            to_items(projected[..., 2 * embedding_width :]),
            "frame",
            split_axis=1,
            concat_axis=0,
            tiled=True,
        ),
    )
    query_heads = split_heads(query_items)
    key_heads = split_heads(key_items)
    value_heads = split_heads(value_items)
    probabilities = attention_probs(query_heads, key_heads, length)
    probs_low = probabilities.astype(jnp.bfloat16)
    attended = jnp.einsum(
        "iphtu,uiphd->tiphd", probs_low, value_heads, preferred_element_type=jnp.float32
    ).astype(jnp.bfloat16)
    item_shape = query_items.shape
    returned = lax.all_to_all(
        attended.reshape(item_shape), "frame", split_axis=0, concat_axis=1, tiled=True
    )
    attended_rows = from_items(returned)
    temporal_mixed_rows = product(attended_rows, whole_output, "pk,kn->pn", embedding_width)
    result = (wide_precision_rows + frame_presence_mask * temporal_mixed_rows).astype(jnp.bfloat16)
    wide_precision_cotangent = cotangent[0].astype(jnp.float32)
    output_gradient = (wide_precision_cotangent * frame_presence_mask).astype(jnp.bfloat16)
    grad_attended = product(output_gradient, whole_output, "pk,nk->pn", embedding_width).astype(
        jnp.bfloat16
    )
    grad_items = lax.all_to_all(
        to_items(grad_attended), "frame", split_axis=1, concat_axis=0, tiled=True
    )
    grad_heads = split_heads(grad_items)
    grad_probs = jnp.einsum(
        "tiphd,uiphd->iphtu", grad_heads, value_heads, preferred_element_type=jnp.float32
    )
    row_delta = jnp.einsum(
        "tiphd,tiphd->ipht", grad_heads, attended, preferred_element_type=jnp.float32
    )
    grad_scores = (probabilities * (grad_probs - row_delta[..., None])).astype(jnp.bfloat16)
    score_scale = DH ** (-0.5)
    grad_query = (
        jnp.einsum("iphtu,uiphd->tiphd", grad_scores, key_heads, preferred_element_type=jnp.float32)
        * score_scale
    ).astype(jnp.bfloat16)
    grad_keys = (
        jnp.einsum(
            "iphtu,tiphd->uiphd", grad_scores, query_heads, preferred_element_type=jnp.float32
        )
        * score_scale
    ).astype(jnp.bfloat16)
    grad_values = jnp.einsum(
        "iphtu,tiphd->uiphd", probs_low, grad_heads, preferred_element_type=jnp.float32
    ).astype(jnp.bfloat16)
    returned_grads = (
        lax.all_to_all(
            grad_query.reshape(item_shape), "frame", split_axis=0, concat_axis=1, tiled=True
        ),
        lax.all_to_all(
            grad_keys.reshape(item_shape), "frame", split_axis=0, concat_axis=1, tiled=True
        ),
        lax.all_to_all(
            grad_values.reshape(item_shape), "frame", split_axis=0, concat_axis=1, tiled=True
        ),
    )
    grad_projected = jnp.concatenate(
        [from_items(returned_piece) for returned_piece in returned_grads], axis=-1
    )
    grad_normed = product(grad_projected, whole_input, "pk,nk->pn", embedding_width)
    pullback = jax.vjp(lambda source: layer_norm(source, norm_gain), wide_precision_rows)[1]
    grad_rows = pullback(grad_normed)[0]
    grad_tokens = (wide_precision_cotangent + grad_rows).astype(jnp.bfloat16)
    return (result[None], grad_tokens[None])


def solution(mesh):
    in_specs = (
        P("clip", "frame", None, None),
        P("clip"),
        P(),
        P("frame", "clip"),
        P("frame", "clip"),
        P("clip", "frame", None, None),
    )
    out_specs = (P("clip", "frame", None, None), P("clip", "frame", None, None))
    return jax.shard_map(
        per_device, mesh=mesh, in_specs=in_specs, out_specs=out_specs, check_vma=False
    )
```

profile of v0, /device:TPU:0, one launch (start us, length us, event | category | flops | bytes accessed | tf_op | source)
XLA Modules:
  0.0 221.2 jit_solution(17323085621104630823)
XLA Ops:
  7.2 17.6 %all_gather.14 = bf16[128,1024]{1,0:T(8,128)(2,1)} all-gather(bf16[128,256]{1,0:T(8,128)(2,1)} %param.10), channel_id=1, replica_groups=mesh['clip'=4,'frame'=8] {'clip'}, dimensions={1}, use_global_device_ids=true | all-gather | bytes 327680 | tf_op jit(solution)/shard_map/all_gather | solution.py:59
  24.9 18.6 %all_gather.12 = bf16[128,3072]{1,0:T(8,128)(2,1)} all-gather(bf16[128,768]{1,0:T(8,128)(2,1)} %param.9), channel_id=1, replica_groups=mesh['clip'=4,'frame'=8] {'clip'}, dimensions={1}, use_global_device_ids=true | all-gather | bytes 983040 | tf_op jit(solution)/shard_map/all_gather | solution.py:58
  44.2 0.1 convert_reduce_fusion
  44.3 0.3 fusion.24
  44.6 8.4 %all-gather.5.cloned.1.call-done = bf16[1024,1024]{1,0:T(8,128)(2,1)} async-done(((bf16[128,1024]{1,0:T(8,128)(2,1)}), bf16[1024,1024]{1,0:T(8,128)(2,1)}) %all-gather.5.cloned.1.call-update) | async-done | bytes 2097168 | tf_op jit(solution)/shard_map/all_gather | solution.py:63
  53.0 2.4 %convolution_convert_fusion.3 = bf16[196,1024]{1,0:T(8,128)(2,1)S(1)} fusion(bf16[1024,1024]{1,0:T(8,128)(2,1)} %all-gather.5.cloned.1.call-done, bf16[1,1,196,1024]{3,2,1,0:T(8,128)(2,1)S(1)} %copy-done.6, f32[]{:T(128)} %bitcast.4), kind=kOutput, calls=%fused_computation.20 | convolution fusion | flops 411844608 | bytes 2899972 | tf_op jit(solution)/shard_map/pk,nk->pn/dot_general | solution.py:52
  55.5 0.1 copy.198
  55.6 0.9 copy.118
  56.5 3.5 %all-to-all-start.4 = ((bf16[1,32,49,128]{3,2,0,1:T(8,128)(2,1)}), bf16[1,32,49,128]{3,2,0,1:T(8,128)(2,1)S(1)}, u32[]{:S(2)}, u32[]{:S(2)}) async-start(bf16[1,32,49,128]{3,2,0,1:T(8,128)(2,1)} %copy.118), calls=%async_computation.4 | async-start | bytes 917504 | tf_op jit(solution)/shard_map/all_to_all | solution.py:117
  60.0 42.9 %all-gather.3.cloned.1.call-done = bf16[1024,3072]{1,0:T(8,128)(2,1)} async-done(((bf16[128,3072]{1,0:T(8,128)(2,1)}), bf16[1024,3072]{1,0:T(8,128)(2,1)}) %all-gather.3.cloned.1.call-update) | async-done | bytes 6291472 | tf_op jit(solution)/shard_map/all_gather | solution.py:62
  102.9 4.3 %fusion.1 = bf16[1,196,3072]{2,1,0:T(8,128)(2,1)S(1)} fusion(bf16[1024,3072]{1,0:T(8,128)(2,1)} %all-gather.3.cloned.1.call-done, bf16[1,1,196,1024]{3,2,1,0:T(8,128)(2,1)S(1)} %copy-done, f32[1024]{0:T(1024)S(1)} %copy-done.8, f32[196]{0:T(256)S(1)} %fusion.42, f32[196]{0:T(256)S(1)} %broadcast_multiply_fusion), kind=kOutput, calls=%fused_computation.2 | convolution fusion | flops 1234731008 | bytes 7902752 | tf_op jit(solution)/shard_map/pk,kn->pn/dot_general | solution.py:52
  107.2 0.1 fusion.51
  107.5 0.1 copy.199
  107.5 1.0 copy.107
  108.5 3.5 %all-to-all-start.2 = ((bf16[1,32,49,128]{3,2,0,1:T(8,128)(2,1)}), bf16[1,32,49,128]{3,2,0,1:T(8,128)(2,1)S(1)}, u32[]{:S(2)}, u32[]{:S(2)}) async-start(bf16[1,32,49,128]{3,2,0,1:T(8,128)(2,1)} %copy.107), calls=%async_computation.2 | async-start | bytes 917504 | tf_op jit(solution)/shard_map/all_to_all | solution.py:82
  112.1 0.1 copy.200
  112.2 1.0 copy.104
  113.1 7.8 %all-to-all-done.2 = bf16[1,32,49,128]{3,2,0,1:T(8,128)(2,1)S(1)} async-done(((bf16[1,32,49,128]{3,2,0,1:T(8,128)(2,1)}), bf16[1,32,49,128]{3,2,0,1:T(8,128)(2,1)S(1)}, u32[]{:S(2)}, u32[]{:S(2)}) %all-to-all-start.2) | async-done | bytes 401440 | tf_op jit(solution)/shard_map/all_to_all | solution.py:82
  121.0 3.5 %all-to-all-start.1 = ((bf16[1,32,49,128]{3,2,0,1:T(8,128)(2,1)}), bf16[1,32,49,128]{3,2,0,1:T(8,128)(2,1)S(1)}, u32[]{:S(2)}, u32[]{:S(2)}) async-start(bf16[1,32,49,128]{3,2,0,1:T(8,128)(2,1)} %copy.104), calls=%async_computation.1 | async-start | bytes 917504 | tf_op jit(solution)/shard_map/all_to_all | solution.py:75
  124.5 0.3 reshape.285
  125.0 0.1 copy.201
  125.1 1.0 copy.101
  126.0 7.4 %all-to-all-done.1 = bf16[1,32,49,128]{3,2,0,1:T(8,128)(2,1)S(1)} async-done(((bf16[1,32,49,128]{3,2,0,1:T(8,128)(2,1)}), bf16[1,32,49,128]{3,2,0,1:T(8,128)(2,1)S(1)}, u32[]{:S(2)}, u32[]{:S(2)}) %all-to-all-start.1) | async-done | bytes 401440 | tf_op jit(solution)/shard_map/all_to_all | solution.py:75
  133.4 4.3 %all-to-all-start = ((bf16[1,32,49,128]{3,2,0,1:T(8,128)(2,1)}), bf16[1,32,49,128]{3,2,0,1:T(8,128)(2,1)}, u32[]{:S(2)}, u32[]{:S(2)}) async-start(bf16[1,32,49,128]{3,2,0,1:T(8,128)(2,1)} %copy.101), calls=%async_computation | async-start | bytes 917504 | tf_op jit(solution)/shard_map/all_to_all | solution.py:89
  137.7 1.8 bitcast_convert_fusion
  139.5 0.3 reshape.307
  139.9 0.3 reshape.308
  140.2 2.6 %exponential_reduce_fusion = (f32[4,49,2,8]{3,2,1,0:T(2,128)S(1)}, f32[4,49,2,8,8]{3,4,2,1,0:T(8,128)}) fusion(pred[8]{0:T(512)(128)(4,1)S(1)} %iota_compare_fusion, bf16[8,4,49,2,64]{4,3,2,1,0:T(2,128)(2,1)S(1)} %reshape.308, bf16[8,4,49,2,64]{4,3,2,1,0:T(2,128)(2,1)S(1)} %reshape.307), kind=kOutput, calls=%fused_computation.10 | convolution fusion | flops 3311623 | bytes 915720 | tf_op jit(solution)/shard_map/sub | solution.py:46
  142.8 3.8 %all-to-all-done = bf16[1,32,49,128]{3,2,0,1:T(8,128)(2,1)} async-done(((bf16[1,32,49,128]{3,2,0,1:T(8,128)(2,1)}), bf16[1,32,49,128]{3,2,0,1:T(8,128)(2,1)}, u32[]{:S(2)}, u32[]{:S(2)}) %all-to-all-start) | async-done | bytes 401440 | tf_op jit(solution)/shard_map/all_to_all | solution.py:89
  146.6 2.8 %reshape.306 = bf16[8,4,49,2,64]{4,3,2,1,0:T(2,128)(2,1)} reshape(bf16[1,32,49,128]{3,2,0,1:T(8,128)(2,1)} %all-to-all-done) | data formatting | bytes 802816 | tf_op jit(solution)/shard_map/reshape | solution.py:35
  149.4 4.0 %multiply_reduce_fusion = (f32[4,49,2,8]{3,2,1,0:T(2,128)}, bf16[4,49,2,64,8]{3,4,2,1,0:T(8,128)(2,1)S(1)}) fusion(f32[4,49,2,8,64]{4,2,0,3,1:T(2,128)} %bitcast_convert_fusion, f32[4,49,2,8]{3,2,1,0:T(2,128)S(1)} %get-tuple-element.5, f32[4,49,2,8,8]{3,4,2,1,0:T(8,128)} %get-tuple-element.6, bf16[8,4,49,2,64]{4,3,2,1,0:T(2,128)(2,1)} %reshape.306), kind=kOutput, calls=%fused_computation.4 | convolution fusion | flops 4061120 | bytes 1731072 | tf_op jit(solution)/shard_map/iphtu,uiphd->tiphd/dot_general | solution.py:102
  153.4 1.5 copy.148
  154.9 2.9 %reshape.302 = bf16[8,4,49,128]{3,1,2,0:T(4,128)(2,1)} reshape(bf16[8,4,49,2,64]{4,3,1,2,0:T(2,128)(2,1)} %copy.148) | data formatting | bytes 802816 | tf_op jit(solution)/shard_map/reshape | solution.py:107
  157.9 3.5 %all-to-all-start.3 = ((bf16[8,4,49,128]{3,1,2,0:T(4,128)(2,1)}), bf16[8,4,49,128]{3,1,2,0:T(4,128)(2,1)S(1)}, u32[]{:S(2)}, u32[]{:S(2)}) async-start(bf16[8,4,49,128]{3,1,2,0:T(4,128)(2,1)} %reshape.302), calls=%async_computation.3 | async-start | bytes 802816 | tf_op jit(solution)/shard_map/all_to_all | solution.py:106
  161.3 2.5 %multiply_convert_fusion.2 = bf16[4,49,2,8,8]{3,4,2,1,0:T(8,128)(2,1)S(1)} fusion(f32[4,49,2,8]{3,2,1,0:T(2,128)} %get-tuple-element.7, bf16[8,4,49,2,64]{4,3,2,1,0:T(2,128)(2,1)} %reshape.306, bf16[8,4,49,2,64]{4,3,1,0,2:T(2,128)(2,1)S(1)} %reshape.285, f32[4,49,2,8]{3,2,1,0:T(2,128)} %copy-done.9, f32[4,49,2,8,8]{3,4,2,1,0:T(8,128)} %get-tuple-element.6), kind=kOutput, calls=%fused_computation.7 | convolution fusion | flops 3311616 | bytes 978432 | tf_op jit(solution)/shard_map/tiphd,uiphd->iphtu/dot_general | solution.py:121
  163.8 0.6 fusion.6
  164.4 0.3 copy-done.1
  164.7 1.5 copy.150
  166.2 3.0 %reshape.304 = bf16[8,4,49,128]{3,1,2,0:T(4,128)(2,1)} reshape(bf16[8,4,49,2,64]{4,3,1,2,0:T(2,128)(2,1)} %copy.150) | data formatting | bytes 802816 | tf_op jit(solution)/shard_map/reshape | solution.py:147
  169.3 0.4 all-to-all-done.3
  169.7 4.1 %all-to-all-start.6 = ((bf16[8,4,49,128]{3,1,2,0:T(4,128)(2,1)}), bf16[8,4,49,128]{3,1,2,0:T(4,128)(2,1)}, u32[]{:S(2)}, u32[]{:S(2)}) async-start(bf16[8,4,49,128]{3,1,2,0:T(4,128)(2,1)} %reshape.304), calls=%async_computation.6 | async-start | bytes 802816 | tf_op jit(solution)/shard_map/all_to_all | solution.py:146
  173.8 0.7 fusion.5
  174.5 0.6 copy.149
  175.1 1.1 reshape.303
  176.2 6.0 %all-to-all-done.6 = bf16[8,4,49,128]{3,1,2,0:T(4,128)(2,1)} async-done(((bf16[8,4,49,128]{3,1,2,0:T(4,128)(2,1)}), bf16[8,4,49,128]{3,1,2,0:T(4,128)(2,1)}, u32[]{:S(2)}, u32[]{:S(2)}) %all-to-all-start.6) | async-done | bytes 401440 | tf_op jit(solution)/shard_map/all_to_all | solution.py:146
  182.2 3.7 %all-to-all-start.5 = ((bf16[8,4,49,128]{3,1,2,0:T(4,128)(2,1)}), bf16[8,4,49,128]{3,1,2,0:T(4,128)(2,1)S(1)}, u32[]{:S(2)}, u32[]{:S(2)}) async-start(bf16[8,4,49,128]{3,1,2,0:T(4,128)(2,1)} %reshape.303), calls=%async_computation.5 | async-start | bytes 802816 | tf_op jit(solution)/shard_map/all_to_all | solution.py:143
  185.9 2.0 fusion.4
  187.9 0.6 copy.151
  188.6 1.1 reshape.305
  189.7 4.4 %all-to-all-done.5 = bf16[8,4,49,128]{3,1,2,0:T(4,128)(2,1)S(1)} async-done(((bf16[8,4,49,128]{3,1,2,0:T(4,128)(2,1)}), bf16[8,4,49,128]{3,1,2,0:T(4,128)(2,1)S(1)}, u32[]{:S(2)}, u32[]{:S(2)}) %all-to-all-start.5) | async-done | bytes 401440 | tf_op jit(solution)/shard_map/all_to_all | solution.py:143
  194.1 3.5 %all-to-all-start.7 = ((bf16[8,4,49,128]{3,1,2,0:T(4,128)(2,1)}), bf16[8,4,49,128]{3,1,2,0:T(4,128)(2,1)S(1)}, u32[]{:S(2)}, u32[]{:S(2)}) async-start(bf16[8,4,49,128]{3,1,2,0:T(4,128)(2,1)} %reshape.305), calls=%async_computation.7 | async-start | bytes 802816 | tf_op jit(solution)/shard_map/all_to_all | solution.py:149
  197.5 0.1 copy.115
  197.9 1.1 copy.132
  199.1 0.2 reshape.291
  199.3 0.1 copy.127
  199.5 0.2 reshape.288
  199.7 6.2 %all-to-all-done.7 = bf16[8,4,49,128]{3,1,2,0:T(4,128)(2,1)S(1)} async-done(((bf16[8,4,49,128]{3,1,2,0:T(4,128)(2,1)}), bf16[8,4,49,128]{3,1,2,0:T(4,128)(2,1)S(1)}, u32[]{:S(2)}, u32[]{:S(2)}) %all-to-all-start.7) | async-done | bytes 401440 | tf_op jit(solution)/shard_map/all_to_all | solution.py:149
  205.9 0.1 copy.137
  206.1 0.2 reshape.294
  206.3 5.1 %fusion.21 = (f32[196]{0:T(256)S(1)}, f32[196,1024]{1,0:T(8,128)S(1)}) fusion(bf16[1,1,196,1024]{3,2,1,0:T(8,128)(2,1)S(1)} %copy-done, f32[196]{0:T(256)S(1)} %broadcast_multiply_fusion, f32[1024]{0:T(1024)S(1)} %copy-done.8, bf16[1024,3072]{1,0:T(8,128)(2,1)} %all-gather.3.cloned.1.call-done, bf16[1,196,1024]{2,1,0:T(8,128)(2,1)S(1)} %reshape.294, ...), kind=kOutput, calls=%fused_computation.41 | convolution fusion | flops 1237741312 | bytes 8705568 | tf_op jit(solution)/shard_map/pk,nk->pn/dot_general | solution.py:52
  211.4 0.4 fusion.48
  211.8 1.1 fusion.35
  212.9 0.1 copy-done.3
  213.0 1.4 fusion.12
  (45 shorter events, 1.0 us)
Async XLA Ops:
  7.2 37.0 %copy-start = (bf16[1,1,196,1024]{3,2,1,0:T(8,128)(2,1)S(1)}, bf16[1,1,196,1024]{3,2,1,0:T(8,128)(2,1)}, u32[]{:S(2)}) copy-start(bf16[1,1,196,1024]{3,2,1,0:T(8,128)(2,1)} %param.6) | copy-start | bytes 1204228
  7.2 45.8 %copy-start.6 = (bf16[1,1,196,1024]{3,2,1,0:T(8,128)(2,1)S(1)}, bf16[1,1,196,1024]{3,2,1,0:T(8,128)(2,1)}, u32[]{:S(2)}) copy-start(bf16[1,1,196,1024]{3,2,1,0:T(8,128)(2,1)} %param.11) | copy-start | bytes 1204228
  7.2 45.8 %all-gather.5.cloned.1.call-start = ((), (), s32[]{:S(2)}) async-start(), calls=%async_computation.9 | async-start | bytes 2359296 | tf_op jit(solution)/shard_map/all_gather | solution.py:63
  24.9 78.0 %all-gather.3.cloned.1.call-start = ((), (), s32[]{:S(2)}) async-start(), calls=%async_computation.8 | async-start | bytes 7077888 | tf_op jit(solution)/shard_map/all_gather | solution.py:62
  55.5 47.4 %copy-start.8 = (f32[1024]{0:T(1024)S(1)}, f32[1024]{0:T(1024)}, u32[]{:S(2)}) copy-start(f32[1024]{0:T(1024)} %param.8) | copy-start | bytes 12292
  56.5 52.0 %all-to-all-start.4 = ((bf16[1,32,49,128]{3,2,0,1:T(8,128)(2,1)}), bf16[1,32,49,128]{3,2,0,1:T(8,128)(2,1)S(1)}, u32[]{:S(2)}, u32[]{:S(2)}) async-start(bf16[1,32,49,128]{3,2,0,1:T(8,128)(2,1)} %copy.118), calls=%async_computation.4 | async-start | bytes 917504 | tf_op jit(solution)/shard_map/all_to_all | solution.py:117
  108.5 12.5 %all-to-all-start.2 = ((bf16[1,32,49,128]{3,2,0,1:T(8,128)(2,1)}), bf16[1,32,49,128]{3,2,0,1:T(8,128)(2,1)S(1)}, u32[]{:S(2)}, u32[]{:S(2)}) async-start(bf16[1,32,49,128]{3,2,0,1:T(8,128)(2,1)} %copy.107), calls=%async_computation.2 | async-start | bytes 917504 | tf_op jit(solution)/shard_map/all_to_all | solution.py:82
  121.0 12.5 %all-to-all-start.1 = ((bf16[1,32,49,128]{3,2,0,1:T(8,128)(2,1)}), bf16[1,32,49,128]{3,2,0,1:T(8,128)(2,1)S(1)}, u32[]{:S(2)}, u32[]{:S(2)}) async-start(bf16[1,32,49,128]{3,2,0,1:T(8,128)(2,1)} %copy.104), calls=%async_computation.1 | async-start | bytes 917504 | tf_op jit(solution)/shard_map/all_to_all | solution.py:75
  133.4 13.2 %all-to-all-start = ((bf16[1,32,49,128]{3,2,0,1:T(8,128)(2,1)}), bf16[1,32,49,128]{3,2,0,1:T(8,128)(2,1)}, u32[]{:S(2)}, u32[]{:S(2)}) async-start(bf16[1,32,49,128]{3,2,0,1:T(8,128)(2,1)} %copy.101), calls=%async_computation | async-start | bytes 917504 | tf_op jit(solution)/shard_map/all_to_all | solution.py:89
  142.8 10.6 %copy-start.9 = (f32[4,49,2,8]{3,2,1,0:T(2,128)}, f32[4,49,2,8]{3,2,1,0:T(2,128)S(1)}, u32[]{:S(2)}) copy-start(f32[4,49,2,8]{3,2,1,0:T(2,128)S(1)} %get-tuple-element.5) | copy-start | bytes 37636
  157.9 11.8 %all-to-all-start.3 = ((bf16[8,4,49,128]{3,1,2,0:T(4,128)(2,1)}), bf16[8,4,49,128]{3,1,2,0:T(4,128)(2,1)S(1)}, u32[]{:S(2)}, u32[]{:S(2)}) async-start(bf16[8,4,49,128]{3,1,2,0:T(4,128)(2,1)} %reshape.302), calls=%async_computation.3 | async-start | bytes 802816 | tf_op jit(solution)/shard_map/all_to_all | solution.py:106
  163.8 0.9 copy-start.1
  166.2 7.6 %copy-start.2 = (bf16[4,49,2,8,8]{3,4,2,1,0:T(8,128)(2,1)S(1)}, bf16[4,49,2,8,8]{3,4,2,1,0:T(8,128)(2,1)}, u32[]{:S(2)}) copy-start(bf16[4,49,2,8,8]{3,4,2,1,0:T(8,128)(2,1)} %copy-done.1) | copy-start | bytes 150532
  169.7 4.1 %copy-start.4 = (bf16[8,4,49,128]{3,1,2,0:T(4,128)(2,1)}, bf16[8,4,49,128]{3,1,2,0:T(4,128)(2,1)S(1)}, u32[]{:S(2)}) copy-start(bf16[8,4,49,128]{3,1,2,0:T(4,128)(2,1)S(1)} %all-to-all-done.3) | copy-start | bytes 1204228
  169.7 12.5 %all-to-all-start.6 = ((bf16[8,4,49,128]{3,1,2,0:T(4,128)(2,1)}), bf16[8,4,49,128]{3,1,2,0:T(4,128)(2,1)}, u32[]{:S(2)}, u32[]{:S(2)}) async-start(bf16[8,4,49,128]{3,1,2,0:T(4,128)(2,1)} %reshape.304), calls=%async_computation.6 | async-start | bytes 802816 | tf_op jit(solution)/shard_map/all_to_all | solution.py:146
  174.5 11.4 %copy-start.10 = (f32[4,49,2,8]{3,2,1,0:T(2,128)S(1)}, f32[4,49,2,8]{3,2,1,0:T(2,128)}, u32[]{:S(2)}) copy-start(f32[4,49,2,8]{3,2,1,0:T(2,128)} %copy-done.9) | copy-start | bytes 37636
  182.2 11.8 %all-to-all-start.5 = ((bf16[8,4,49,128]{3,1,2,0:T(4,128)(2,1)}), bf16[8,4,49,128]{3,1,2,0:T(4,128)(2,1)S(1)}, u32[]{:S(2)}, u32[]{:S(2)}) async-start(bf16[8,4,49,128]{3,1,2,0:T(4,128)(2,1)} %reshape.303), calls=%async_computation.5 | async-start | bytes 802816 | tf_op jit(solution)/shard_map/all_to_all | solution.py:143
  187.9 9.6 %copy-start.5 = (bf16[8,4,49,128]{3,1,2,0:T(4,128)(2,1)S(1)}, bf16[8,4,49,128]{3,1,2,0:T(4,128)(2,1)}, u32[]{:S(2)}) copy-start(bf16[8,4,49,128]{3,1,2,0:T(4,128)(2,1)} %copy-done.4) | copy-start | bytes 1204228
  194.1 11.8 %all-to-all-start.7 = ((bf16[8,4,49,128]{3,1,2,0:T(4,128)(2,1)}), bf16[8,4,49,128]{3,1,2,0:T(4,128)(2,1)S(1)}, u32[]{:S(2)}, u32[]{:S(2)}) async-start(bf16[8,4,49,128]{3,1,2,0:T(4,128)(2,1)} %reshape.305), calls=%async_computation.7 | async-start | bytes 802816 | tf_op jit(solution)/shard_map/all_to_all | solution.py:149
  206.3 5.5 %copy-start.7 = (bf16[1,1,196,1024]{3,2,1,0:T(8,128)(2,1)S(1)}, bf16[1,1,196,1024]{3,2,1,0:T(8,128)(2,1)}, u32[]{:S(2)}) copy-start(bf16[1,1,196,1024]{3,2,1,0:T(8,128)(2,1)} %param.11) | copy-start | bytes 1204228
  211.4 1.6 copy-start.3
Sparse Core Ops, SparseCore 0:
  25.0 27.9 all-gather.4
  54.8 48.0 all-gather.2
where the time goes:
time: 222 us; the launch traced here: 221 us
  waiting for transfers between devices  87.3 us (39%)
  blocking collectives  36.2 us (16%)
  starting transfers between devices  29.5 us (13%)
  matrix products  25.4 us (11%)
  local copies, waits for them, and re-layouts  24 us (11%)
  between operations  15.2 us (7%)
  other arithmetic  3.67 us (2%)
    all_gather x1, waiting for transfers between devices, per_device(): lax.all_gather(columns_input, 'frame', axis=0, tiled=True)  42.9 us
    all_gather x1, blocking collectives, per_device(): lax.all_gather(input_weights, 'clip', axis=1, tiled=True)  18.6 us
    all_gather x1, blocking collectives, per_device(): lax.all_gather(output_weights, 'clip', axis=1, tiled=True)  17.6 us
    dot_general x4, matrix products, product(): jnp.einsum(pattern, flat_rows, weights, preferred_element_type=jnp.float32)  13.2 us
    all_gather x1, waiting for transfers between devices, per_device(): lax.all_gather(columns_output, 'frame', axis=0, tiled=True)  8.39 us
    all_to_all x1, waiting for transfers between devices, per_device(): lax.all_to_all(to_items(projected[..., embedding_width:2 * embedding_widt...  7.82 us
    all_to_all x1, waiting for transfers between devices, per_device(): lax.all_to_all(to_items(projected[..., :embedding_width]), 'frame', split...  7.4 us
    all_to_all x1, waiting for transfers between devices, per_device(): lax.all_to_all(grad_values.reshape(item_shape), 'frame', split_axis=0, co...  6.16 us
  transfers between devices with their start and end apart: 10, of which 9 were waited for; matrix products, arithmetic and copies ran while one was open for 15% of the time, Pallas kernels for 0%

commit v1 on v0

v1 whole, which is shorter than its diff:
```python
import functools

import jax
import jax.numpy as jnp
from jax import lax
from jax.experimental import pallas as pl
from jax.experimental.pallas import tpu as pltpu
from jax.sharding import PartitionSpec as P

DH = 64
PAIR = 2 * DH
SUB = 16
EPSILON = 1e-06
NEGATIVE = -1e30
NN = (((1,), (0,)), ((), ()))
NT = (((1,), (1,)), ((), ()))
TN = (((0,), (0,)), ((), ()))


def dot(a, b, dims):
    return lax.dot_general(a, b, dims, preferred_element_type=jnp.float32)


def attention_pair(q, k, v, ga, mask, low_lanes):
    zero = jnp.zeros_like(q)

    def apart(block):
        return jnp.concatenate(
            [jnp.where(low_lanes, block, zero), jnp.where(low_lanes, zero, block)], axis=0
        )

    rows = q.shape[0]
    q_two, k_two, v_two, ga_two = apart(q), apart(k), apart(v), apart(ga)
    scores = dot(q_two, k, NT) * DH ** (-0.5)
    grad_probs = dot(ga_two, v, NT)
    scores = jnp.where(mask, scores, NEGATIVE)
    highest = jnp.max(scores, axis=-1, keepdims=True)
    expanded = jnp.exp(scores - highest)
    probs = expanded * (1.0 / jnp.sum(expanded, axis=-1, keepdims=True))
    probs_low = probs.astype(jnp.bfloat16)
    beside = jnp.concatenate([probs_low[:rows], probs_low[rows:]], axis=1)
    attended = dot(beside, v_two, NN).astype(jnp.bfloat16)
    grad_values = dot(probs_low, ga_two, TN).astype(jnp.bfloat16)
    both = attended.astype(jnp.float32)
    delta = jnp.sum(
        ga_two.astype(jnp.float32) * jnp.concatenate([both, both], axis=0), axis=-1, keepdims=True
    )
    grad_scores = (probs * (grad_probs - delta)).astype(jnp.bfloat16)
    beside = jnp.concatenate([grad_scores[:rows], grad_scores[rows:]], axis=1)
    grad_query = (dot(beside, k_two, NN) * DH ** (-0.5)).astype(jnp.bfloat16)
    grad_keys = (dot(grad_scores, q_two, TN) * DH ** (-0.5)).astype(jnp.bfloat16)
    return attended, grad_query, grad_keys, grad_values


def block_kernel(
    pieces, frames, patches, width,
    counts_ref, gain_ref, tokens_ref, cot_ref, *rest,
):
    weight_refs = rest[: len(rest) - 11]
    result_ref, grad_ref, w_in, w_out, normed, proj, ga, att, gproj, stats, sems = rest[-11:]
    groups = patches // SUB
    rows = frames * SUB
    total = groups * rows
    count = counts_ref[0]

    copies = []
    for which, (target, found) in enumerate(zip((w_in, w_out), pieces)):
        mine = []
        for ref, index, lanes, row, column in found:
            source = weight_refs[ref].at[index] if index is not None else weight_refs[ref]
            depth = source.shape[0]
            mine.append(
                pltpu.make_async_copy(
                    source.at[:, pl.ds(*lanes)],
                    target.at[pl.ds(row, depth), pl.ds(column, lanes[1])],
                    sems.at[which],
                )
            )
        copies.append(mine)
    for mine in copies:
        for copy in mine:
            copy.start()

    live = (lax.broadcasted_iota(jnp.int32, (rows, 1), 0) // SUB < count).astype(jnp.float32)
    gain = gain_ref[...]

    def load(ref, group):
        start = pl.multiple_of(group * SUB, SUB)
        return ref[:, pl.ds(start, SUB), :].reshape(rows, width)

    def store(ref, group, value):
        start = pl.multiple_of(group * SUB, SUB)
        ref[:, pl.ds(start, SUB), :] = value.reshape(frames, SUB, width)

    for group in range(groups):
        here = pl.ds(group * rows, rows)
        wide = load(tokens_ref, group).astype(jnp.float32)
        average = jnp.mean(wide, axis=-1, keepdims=True)
        centred = wide - average
        variance = jnp.mean(centred * centred, axis=-1, keepdims=True)
        scale = lax.rsqrt(variance + EPSILON)
        normed[here, :] = (centred * scale * gain).astype(jnp.bfloat16)
        stats[here, 0:1] = average
        stats[here, 1:2] = scale

    for copy in copies[0]:
        copy.wait()

    step = 512

    @pl.loop(0, 3 * width // step)
    def _(j):
        columns = pl.ds(pl.multiple_of(j * step, step), step)
        proj[:, columns] = dot(normed[...], w_in[:, columns], NN).astype(jnp.bfloat16)

    for copy in copies[1]:
        copy.wait()

    for group in range(groups):
        here = pl.ds(group * rows, rows)
        normed[here, :] = (load(cot_ref, group).astype(jnp.float32) * live).astype(jnp.bfloat16)

    @pl.loop(0, width // step)
    def _(j):
        columns = pl.ds(pl.multiple_of(j * step, step), step)
        ga[:, columns] = dot(normed[...], w_out[columns, :], NT).astype(jnp.bfloat16)

    row = lax.broadcasted_iota(jnp.int32, (2 * rows, rows), 0)
    key = lax.broadcasted_iota(jnp.int32, (2 * rows, rows), 1)
    mask = (row % SUB == key % SUB) & (key // SUB < count)
    low_lanes = lax.broadcasted_iota(jnp.int32, (rows, PAIR), 1) < DH
    unroll = 4 if rows <= 128 else 1

    for group in range(groups):
        here = pl.ds(group * rows, rows)

        @pl.loop(0, width // (PAIR * unroll))
        def _(step_index):
            for inner in range(unroll):
                pair = step_index * unroll + inner

                def lanes(part):
                    return pl.ds(pl.multiple_of(part * width + pair * PAIR, PAIR), PAIR)

                attended, grad_query, grad_keys, grad_values = attention_pair(
                    proj[here, lanes(0)],
                    proj[here, lanes(1)],
                    proj[here, lanes(2)],
                    ga[here, lanes(0)],
                    mask,
                    low_lanes,
                )
                att[here, lanes(0)] = attended
                gproj[here, lanes(0)] = grad_query
                gproj[here, lanes(1)] = grad_keys
                gproj[here, lanes(2)] = grad_values

    for group in range(groups):
        here = pl.ds(group * rows, rows)
        mixed = dot(att[here, :], w_out[...], NN)
        store(
            result_ref,
            group,
            (load(tokens_ref, group).astype(jnp.float32) + live * mixed).astype(jnp.bfloat16),
        )

    for group in range(groups):
        here = pl.ds(group * rows, rows)
        grad = dot(gproj[here, :], w_in[...], NT) * gain
        scale = stats[here, 1:2]
        hat = (load(tokens_ref, group).astype(jnp.float32) - stats[here, 0:1]) * scale
        grad_rows = scale * (
            grad
            - jnp.mean(grad, axis=-1, keepdims=True)
            - hat * jnp.mean(grad * hat, axis=-1, keepdims=True)
        )
        store(
            grad_ref,
            group,
            (load(cot_ref, group).astype(jnp.float32) + grad_rows).astype(jnp.bfloat16),
        )


def run_block(counts, gain, tokens, cot, weights, pieces):
    frames, patches, width = tokens.shape
    total = frames * patches
    vmem = pl.BlockSpec(memory_space=pltpu.VMEM)
    anywhere = pl.BlockSpec(memory_space=pl.ANY)
    out = jax.ShapeDtypeStruct(tokens.shape, jnp.bfloat16)
    return pl.pallas_call(
        functools.partial(block_kernel, pieces, frames, patches, width),
        out_shape=(out, out),
        in_specs=[pl.BlockSpec(memory_space=pltpu.SMEM), vmem, vmem, vmem]
        + [anywhere] * len(weights),
        out_specs=(vmem, vmem),
        scratch_shapes=[
            pltpu.VMEM((width, 3 * width), jnp.bfloat16),
            pltpu.VMEM((width, width), jnp.bfloat16),
            pltpu.VMEM((total, width), jnp.bfloat16),
            pltpu.VMEM((total, 3 * width), jnp.bfloat16),
            pltpu.VMEM((total, width), jnp.bfloat16),
            pltpu.VMEM((total, width), jnp.bfloat16),
            pltpu.VMEM((total, 3 * width), jnp.bfloat16),
            pltpu.VMEM((total, 128), jnp.float32),
            pltpu.SemaphoreType.DMA((2,)),
        ],
        compiler_params=pltpu.CompilerParams(vmem_limit_bytes=48 * 1024 * 1024),
        cost_estimate=pl.CostEstimate(
            flops=16 * total * width * width,
            bytes_accessed=8 * width * width + 8 * total * width,
            transcendentals=total * 2048,
        ),
        name="block",
    )(counts, gain, tokens, cot, *weights)


def gather_weights(input_weights, output_weights, clips, devices):
    depth, in_columns = input_weights.shape
    out_columns = output_weights.shape[1]
    if in_columns % 128 == 0 and out_columns % 128 == 0 and depth % 16 == 0:
        joined = jnp.concatenate([input_weights, output_weights], axis=1)
        whole = lax.all_gather(joined, ("clip", "frame"), axis=0)
        whole = whole.reshape(clips * devices, depth, in_columns + out_columns)
        pieces = ([], [])
        for c in range(clips):
            for f in range(devices):
                index = c * devices + f
                pieces[0].append((0, index, (0, in_columns), f * depth, c * in_columns))
                pieces[1].append((0, index, (in_columns, out_columns), f * depth, c * out_columns))
        return [whole], pieces
    both = []
    for weights in (input_weights, output_weights):
        columns = lax.all_gather(weights, "clip", axis=1, tiled=True)
        both.append(lax.all_gather(columns, "frame", axis=0, tiled=True))
    pieces = tuple([(i, None, (0, w.shape[1]), 0, 0)] for i, w in enumerate(both))
    return both, pieces


def per_device(clips, devices, tokens, counts, norm_gain, input_weights, output_weights, cotangent):
    _, slots, patches, width = tokens.shape
    weights, pieces = gather_weights(input_weights, output_weights, clips, devices)
    share = -(-patches // devices)
    share = -(-share // SUB) * SUB
    extra = devices * share - patches
    both = jnp.concatenate([tokens, cotangent], axis=0)
    both = jnp.pad(both, ((0, 0), (0, 0), (0, extra), (0, 0)))
    both = both.reshape(2, slots, devices, share, width)
    both = lax.all_to_all(both, "frame", split_axis=2, concat_axis=1, tiled=True)
    both = both.reshape(2, devices * slots, share, width)
    outs = run_block(counts, norm_gain.reshape(1, width), both[0], both[1], weights, pieces)
    back = jnp.stack(outs).reshape(2, devices * slots, 1, share, width)
    back = lax.all_to_all(back, "frame", split_axis=1, concat_axis=2, tiled=True)
    back = back.reshape(2, slots, devices * share, width)[:, :, :patches]
    return back[0][None], back[1][None]


def solution(mesh):
    in_specs = (
        P("clip", "frame", None, None),
        P("clip"),
        P(),
        P("frame", "clip"),
        P("frame", "clip"),
        P("clip", "frame", None, None),
    )
    out_specs = (P("clip", "frame", None, None), P("clip", "frame", None, None))
    body = functools.partial(per_device, mesh.shape["clip"], mesh.shape["frame"])
    return jax.shard_map(body, mesh=mesh, in_specs=in_specs, out_specs=out_specs, check_vma=False)
```

time: 222 us -> 144 us (0.65)
  matrix products: 25.4 us -> 0 us
  starting transfers between devices: 29.5 us -> 5.34 us
  local copies, waits for them, and re-layouts: 24 us -> 2.37 us
  Pallas kernels: 0 us -> 21.6 us
  blocking collectives: 36.2 us -> 17.9 us
  waiting for transfers between devices: 87.3 us -> 78.5 us
    all_gather x2 -> x0, blocking collectives: 36.2 us -> none  [the longest x1 18.6 us: per_device(): lax.all_gather(input_weights, 'clip', axis=1, tiled=True)]
    all_to_all x8 -> x1, starting transfers between devices: 29.4 us -> 5.3 us  [per_device(): lax.all_to_all(both, 'frame', split_axis=2, concat_axis=1, tiled=True)]
    dot_general x9 -> x0, matrix products: 22.8 us -> none  [the longest x4 13.2 us: product(): jnp.einsum(pattern, flat_rows, weights, preferred_element_type=jnp.float32)]
    pallas_call x0 -> x1, Pallas kernels: none -> 21.6 us  [run_block(): pl.pallas_call(functools.partial(block_kernel, pieces, frames, patches, w...]
    reshape x23 -> x2, local copies, waits for them, and re-layouts: 21 us -> 1.25 us  [the longest x1 1.17 us: per_device(): both = both.reshape(2, slots, devices, share, width)]
    all_to_all x8 -> x1, waiting for transfers between devices: 35.9 us -> 16.6 us  [per_device(): lax.all_to_all(both, 'frame', split_axis=2, concat_axis=1, tiled=True)]
    all_to_all x0 -> x1, blocking collectives: none -> 17.9 us  [per_device(): lax.all_to_all(back, 'frame', split_axis=1, concat_axis=2, tiled=True)]
    all_gather x2 -> x1, waiting for transfers between devices: 51.3 us -> 61.9 us  [gather_weights(): whole = lax.all_gather(joined, ('clip', 'frame'), axis=0)]
  transfers between devices with their start and end apart: 10 -> 2, of which waited for: 9 -> 2; matrix products, arithmetic and copies ran while one was open for 15% -> 2% of each run, Pallas kernels for 0% -> 0%
where the time goes in v1:
time: 144 us; the launch traced here: 143 us
  waiting for transfers between devices  78.5 us (55%)
  Pallas kernels  21.6 us (15%)
  blocking collectives  17.9 us (12%)
  between operations  14.7 us (10%)
  starting transfers between devices  5.34 us (4%)
  other arithmetic  3.04 us (2%)
  local copies, waits for them, and re-layouts  2.37 us (2%)
    all_gather x1, waiting for transfers between devices, gather_weights(): whole = lax.all_gather(joined, ('clip', 'frame'), axis=0)  61.9 us
    pallas_call x1, Pallas kernels, run_block(): pl.pallas_call(functools.partial(block_kernel, pieces, frames, patches, w...  21.6 us
    all_to_all x1, blocking collectives, per_device(): lax.all_to_all(back, 'frame', split_axis=1, concat_axis=2, tiled=True)  17.9 us
    all_to_all x1, waiting for transfers between devices, per_device(): lax.all_to_all(both, 'frame', split_axis=2, concat_axis=1, tiled=True)  16.6 us
    all_to_all x1, starting transfers between devices, per_device(): lax.all_to_all(both, 'frame', split_axis=2, concat_axis=1, tiled=True)  5.3 us
  transfers between devices with their start and end apart: 2, of which 2 were waited for; matrix products, arithmetic and copies ran while one was open for 2% of the time, Pallas kernels for 0%

profile of v1, /device:TPU:0, one launch (start us, length us, event | category | flops | bytes accessed | tf_op | source)
XLA Modules:
  0.0 143.5 jit_solution(3242999713346892898)
XLA Ops:
  7.2 0.0 all-gather.3.cloned.1.call-start
  7.2 1.7 %pad_maximum_fusion = bf16[128,1024]{1,0:T(8,128)(2,1)} fusion(bf16[128,256]{1,0:T(8,128)(2,1)} %param.10, bf16[128,768]{1,0:T(8,128)(2,1)} %param.9), kind=kLoop, calls=%fused_computation.9 | loop fusion | flops 524288 | bytes 524288 | tf_op jit(solution)/shard_map/concatenate | solution.py:221
  8.9 0.0 all-gather.3.cloned.1.call-update
  8.9 1.2 fusion.2
  10.2 1.2 copy.15
  11.4 0.0 copy-start
  11.4 5.3 %all-to-all-start = ((bf16[2,1,8,32,1024]{4,3,1,0,2:T(8,128)(2,1)}), bf16[2,1,8,32,1024]{4,3,1,0,2:T(8,128)(2,1)S(1)}, u32[]{:S(2)}, u32[]{:S(2)}) async-start(bf16[2,1,8,32,1024]{4,3,1,0,2:T(8,128)(2,1)} %copy.15), calls=%async_computation | async-start | bytes 2097152 | tf_op jit(solution)/shard_map/all_to_all | solution.py:248
  17.3 16.6 %all-to-all-done = bf16[2,1,8,32,1024]{4,3,1,0,2:T(8,128)(2,1)S(1)} async-done(((bf16[2,1,8,32,1024]{4,3,1,0,2:T(8,128)(2,1)}), bf16[2,1,8,32,1024]{4,3,1,0,2:T(8,128)(2,1)S(1)}, u32[]{:S(2)}, u32[]{:S(2)}) %all-to-all-start) | async-done | bytes 1048608 | tf_op jit(solution)/shard_map/all_to_all | solution.py:248
  34.0 0.1 slice_bitcast_fusion
  34.0 61.9 %all-gather.3.cloned.1.call-done = bf16[4096,1024]{1,0:T(8,128)(2,1)} async-done(((bf16[128,1024]{1,0:T(8,128)(2,1)}), bf16[4096,1024]{1,0:T(8,128)(2,1)}) %all-gather.3.cloned.1.call-update) | async-done | bytes 8388624 | tf_op jit(solution)/shard_map/all_gather | solution.py:222
  95.9 0.0 copy-done
  95.9 21.6 %block.1 = (bf16[8,32,1024]{2,1,0:T(8,128)(2,1)S(1)}, bf16[8,32,1024]{2,1,0:T(8,128)(2,1)S(1)}) custom-call(s32[1]{0:T(128)S(6)} %copy.24.counts_ref, f32[1,1024]{1,0:T(1,128)S(1)} %bitcast.24, bf16[8,32,1024]{2,1,0:T(8,128)(2,1)S(1)} %get-tuple-element.11.tokens_ref, bf16[8,32,1024]{2,1,0:T(8,128)(2,1)S(1)} %get-tuple-element.10.cot_ref, ...), custom_call_target="tpu_custom_call" | custom-call | flops 4294967296 | bytes 10485760 | tf_op jit(solution)/shard_map/block/pallas_call | solution.py:190
  117.5 0.1 maximum_bitcast_fusion
  117.6 0.1 copy.18
  117.7 17.9 %all_to_all.8 = bf16[2,8,1,32,1024]{4,3,0,2,1:T(8,128)(2,1)S(1)} all-to-all(bf16[2,8,1,32,1024]{4,3,0,2,1:T(8,128)(2,1)S(1)} %copy.18), channel_id=1, replica_groups=mesh['clip'=4,'frame'=8] {'frame'}, dimensions={1} | all-to-all | bytes 2097152 | tf_op jit(solution)/shard_map/all_to_all | solution.py:252
  135.6 0.1 copy.19
  135.7 0.9 slice_bitcast_fusion.2
Async XLA Ops:
  7.2 88.7 %all-gather.3.cloned.1.call-start = ((), (), s32[]{:S(2)}) async-start(), calls=%async_computation.2 | async-start | bytes 8650752 | tf_op jit(solution)/shard_map/all_gather | solution.py:222
  11.4 84.6 %copy-start = (f32[1024]{0:T(1024)S(1)}, f32[1024]{0:T(1024)}, u32[]{:S(2)}) copy-start(f32[1024]{0:T(1024)} %param.8) | copy-start | bytes 12292
  11.4 22.6 %all-to-all-start = ((bf16[2,1,8,32,1024]{4,3,1,0,2:T(8,128)(2,1)}), bf16[2,1,8,32,1024]{4,3,1,0,2:T(8,128)(2,1)S(1)}, u32[]{:S(2)}, u32[]{:S(2)}) async-start(bf16[2,1,8,32,1024]{4,3,1,0,2:T(8,128)(2,1)} %copy.15), calls=%async_computation | async-start | bytes 2097152 | tf_op jit(solution)/shard_map/all_to_all | solution.py:248
Sparse Core Ops, SparseCore 0:
  11.4 84.4 all-gather.2

commit v2 on v1

--- a/solution.py
+++ b/solution.py
@@ -64,7 +64,7 @@
     count = counts_ref[0]
 
     copies = []
-    for which, (target, found) in enumerate(zip((w_in, w_out), pieces)):
+    for which, (target, found) in enumerate(zip((w_in, w_out), pieces())):
         mine = []
         for ref, index, lanes, row, column in found:
             source = weight_refs[ref].at[index] if index is not None else weight_refs[ref]
@@ -72,7 +72,10 @@
             mine.append(
                 pltpu.make_async_copy(
                     source.at[:, pl.ds(*lanes)],
-                    target.at[pl.ds(row, depth), pl.ds(column, lanes[1])],
+                    target.at[
+                        pl.ds(pl.multiple_of(row, 16), depth),
+                        pl.ds(pl.multiple_of(column, 128), lanes[1]),
+                    ],
                     sems.at[which],
                 )
             )
@@ -214,26 +217,55 @@
     )(counts, gain, tokens, cot, *weights)
 
 
+def swap(array, distance, devices):
+    return lax.ppermute(array, "frame", [(f, f ^ distance) for f in range(devices)])
+
+
 def gather_weights(input_weights, output_weights, clips, devices):
     depth, in_columns = input_weights.shape
     out_columns = output_weights.shape[1]
-    if in_columns % 128 == 0 and out_columns % 128 == 0 and depth % 16 == 0:
+    if devices == 8 and in_columns % 128 == 0 and out_columns % 128 == 0 and depth % 32 == 0:
         joined = jnp.concatenate([input_weights, output_weights], axis=1)
-        whole = lax.all_gather(joined, ("clip", "frame"), axis=0)
-        whole = whole.reshape(clips * devices, depth, in_columns + out_columns)
-        pieces = ([], [])
-        for c in range(clips):
-            for f in range(devices):
-                index = c * devices + f
-                pieces[0].append((0, index, (0, in_columns), f * depth, c * in_columns))
-                pieces[1].append((0, index, (in_columns, out_columns), f * depth, c * out_columns))
-        return [whole], pieces
+        half = depth // 2
+        found = []
+        for offset in range(clips):
+            own = joined
+            if offset > 0:
+                own = lax.ppermute(
+                    joined, "clip", [(c, (c + offset) % clips) for c in range(clips)]
+                )
+            by_x, by_y = swap(own, 2, devices), swap(own, 4, devices)
+            top = swap(by_y[:half], 2, devices)
+            bottom = swap(by_x[half:], 4, devices)
+            for array, distance, row in (
+                (own, 0, 0),
+                (by_x, 2, 0),
+                (by_y, 4, 0),
+                (top, 6, 0),
+                (bottom, 6, half),
+            ):
+                found.append((array, offset, distance, row))
+                found.append((swap(array, 1, devices), offset, distance ^ 1, row))
+        arrays = [entry[0] for entry in found]
+        places = [entry[1:] for entry in found]
+
+        def pieces():
+            clip, frame = lax.axis_index("clip"), lax.axis_index("frame")
+            both = ([], [])
+            for ref, (offset, distance, row) in enumerate(places):
+                column = lax.rem(clip + (clips - offset), clips)
+                start = (frame ^ distance) * depth + row
+                both[0].append((ref, None, (0, in_columns), start, column * in_columns))
+                both[1].append((ref, None, (in_columns, out_columns), start, column * out_columns))
+            return both
+
+        return arrays, pieces
     both = []
     for weights in (input_weights, output_weights):
         columns = lax.all_gather(weights, "clip", axis=1, tiled=True)
         both.append(lax.all_gather(columns, "frame", axis=0, tiled=True))
     pieces = tuple([(i, None, (0, w.shape[1]), 0, 0)] for i, w in enumerate(both))
-    return both, pieces
+    return both, lambda: pieces
 
 
 def per_device(clips, devices, tokens, counts, norm_gain, input_weights, output_weights, cotangent):

time: 144 us -> 133 us (0.924); the launches traced: 143 us -> 130 us
  waiting for transfers between devices: 78.5 us -> 35.6 us
  starting transfers between devices: 5.34 us -> 38.7 us
  between operations: 14.7 us -> 1.69 us
  local copies, waits for them, and re-layouts: 2.37 us -> 11.2 us
  other arithmetic: 3.04 us -> 1.42 us
  Pallas kernels: 21.6 us -> 23.1 us
    all_gather x1 -> x0, waiting for transfers between devices: 61.9 us -> none  [gather_weights(): whole = lax.all_gather(joined, ('clip', 'frame'), axis=0)]
    ppermute x0 -> x39, waiting for transfers between devices: none -> 35.6 us  [the longest x36 23.5 us: swap(): lax.ppermute(array, 'frame', [(f, f ^ distance) for f in range(devices)])]
    ppermute x0 -> x39, starting transfers between devices: none -> 34.5 us  [the longest x36 26.5 us: swap(): lax.ppermute(array, 'frame', [(f, f ^ distance) for f in range(devices)])]
    all_to_all x1, waiting for transfers between devices: 16.6 us -> 0.01 us  [per_device(): lax.all_to_all(both, 'frame', split_axis=2, concat_axis=1, tiled=True)]
    unnamed x3 -> x50, local copies, waits for them, and re-layouts: 0.94 us -> 5.66 us
    squeeze x1, local copies, waits for them, and re-layouts: 0.09 us -> 2.38 us  [per_device(): both[1]]
    concatenate x1 -> x0, other arithmetic: 1.7 us -> none  [gather_weights(): joined = jnp.concatenate([input_weights, output_weights], axis=1)]
    pallas_call x1, Pallas kernels: 21.6 us -> 23.1 us  [run_block(): pl.pallas_call(functools.partial(block_kernel, pieces, frames, patches, w...]
  transfers between devices with their start and end apart: 2 -> 40, of which waited for: 2 -> 11; matrix products, arithmetic and copies ran while one was open for 2% -> 4% of each run, Pallas kernels for 0% -> 0%
where the time goes in v2:
time: 133 us; the launch traced here: 130 us
  starting transfers between devices  38.7 us (29%)
  waiting for transfers between devices  35.6 us (27%)
  Pallas kernels  23.1 us (17%)
  blocking collectives  18.9 us (14%)
  local copies, waits for them, and re-layouts  11.2 us (8%)
  between operations  1.69 us (1%)
  other arithmetic  1.42 us (1%)
    ppermute x36, starting transfers between devices, swap(): lax.ppermute(array, 'frame', [(f, f ^ distance) for f in range(devices)])  26.5 us
    ppermute x36, waiting for transfers between devices, swap(): lax.ppermute(array, 'frame', [(f, f ^ distance) for f in range(devices)])  23.5 us
    pallas_call x1, Pallas kernels, run_block(): pl.pallas_call(functools.partial(block_kernel, pieces, frames, patches, w...  23.1 us
    all_to_all x1, blocking collectives, per_device(): lax.all_to_all(back, 'frame', split_axis=1, concat_axis=2, tiled=True)  18.9 us
    ppermute x3, waiting for transfers between devices, gather_weights(): lax.ppermute(joined, 'clip', [(c, (c + offset) % clips) for c in range(cl...  12.1 us
    ppermute x3, starting transfers between devices, gather_weights(): lax.ppermute(joined, 'clip', [(c, (c + offset) % clips) for c in range(cl...  8.02 us
    unnamed x50, local copies, waits for them, and re-layouts  5.66 us
    all_to_all x1, starting transfers between devices, per_device(): lax.all_to_all(both, 'frame', split_axis=2, concat_axis=1, tiled=True)  4.24 us
  transfers between devices with their start and end apart: 40, of which 11 were waited for; matrix products, arithmetic and copies ran while one was open for 4% of the time, Pallas kernels for 0%

profile of v2, /device:TPU:0, one launch (start us, length us, event | category | flops | bytes accessed | tf_op | source)
XLA Modules:
  0.0 130.5 jit_solution(6165827258472425619)
XLA Ops:
  0.6 1.0 constant_dynamic-update-slice_fusion.1
  1.7 0.8 constant_dynamic-update-slice_fusion.rest_0_
  2.5 2.9 %collective-permute-start.1 = (bf16[128,1024]{1,0:T(8,128)(2,1)S(1)}, bf16[128,1024]{1,0:T(8,128)(2,1)S(1)}, u32[]{:S(2)}, u32[]{:S(2)}) collective-permute-start(bf16[128,1024]{1,0:T(8,128)(2,1)S(1)} %constant_dynamic-update-slice_fusion.rest_0_), channel_id=1, source_target_pairs={{0,2},{1,3},{2,0},{3,1},{4,6},{5,7},{6,4},{7,5},{8,10},{9,11},{10,... | collective-permute-start | bytes 786440 | tf_op jit(solution)/shard_map/ppermute | solution.py:221
  5.5 1.5 %collective-permute-start.3 = (bf16[128,1024]{1,0:T(8,128)(2,1)S(1)}, bf16[128,1024]{1,0:T(8,128)(2,1)S(1)}, u32[]{:S(2)}, u32[]{:S(2)}) collective-permute-start(bf16[128,1024]{1,0:T(8,128)(2,1)S(1)} %constant_dynamic-update-slice_fusion.rest_0_), channel_id=1, source_target_pairs={{0,4},{1,5},{2,6},{3,7},{4,0},{5,1},{6,2},{7,3},{8,12},{9,13},{10,... | collective-permute-start | bytes 786440 | tf_op jit(solution)/shard_map/ppermute | solution.py:221
  7.0 1.6 %collective-permute-start.9 = (bf16[128,1024]{1,0:T(8,128)(2,1)S(1)}, bf16[128,1024]{1,0:T(8,128)(2,1)S(1)}, u32[]{:S(2)}, u32[]{:S(2)}) collective-permute-start(bf16[128,1024]{1,0:T(8,128)(2,1)S(1)} %constant_dynamic-update-slice_fusion.rest_0_), channel_id=1, source_target_pairs={{0,8},{8,16},{16,24},{24,0},{1,9},{9,17},{17,25},{25,1},{2,10},{10... | collective-permute-start | bytes 786440 | tf_op jit(solution)/shard_map/ppermute | solution.py:234
  8.6 2.6 %collective-permute-start.19 = (bf16[128,1024]{1,0:T(8,128)(2,1)S(1)}, bf16[128,1024]{1,0:T(8,128)(2,1)S(1)}, u32[]{:S(2)}, u32[]{:S(2)}) collective-permute-start(bf16[128,1024]{1,0:T(8,128)(2,1)S(1)} %constant_dynamic-update-slice_fusion.rest_0_), channel_id=1, source_target_pairs={{0,16},{8,24},{16,0},{24,8},{1,17},{9,25},{17,1},{25,9},{2,18},{10... | collective-permute-start | bytes 786440 | tf_op jit(solution)/shard_map/ppermute | solution.py:234
  11.1 0.6 collective-permute-done.1.rest_2_
  11.8 3.9 %collective-permute-start.29 = (bf16[128,1024]{1,0:T(8,128)(2,1)S(1)}, bf16[128,1024]{1,0:T(8,128)(2,1)}, u32[]{:S(2)}, u32[]{:S(2)}) collective-permute-start(bf16[128,1024]{1,0:T(8,128)(2,1)S(1)} %constant_dynamic-update-slice_fusion.rest_0_), channel_id=1, source_target_pairs={{0,24},{8,0},{16,8},{24,16},{1,25},{9,1},{17,9},{25,17},{2,26},{10... | collective-permute-start | bytes 786440 | tf_op jit(solution)/shard_map/ppermute | solution.py:234
  15.6 0.0 collective-permute-done.rest_1_
  15.6 0.6 collective-permute-start.4
  16.2 1.8 %collective-permute-done.9.rest_10_ = bf16[128,1024]{1,0:T(8,128)(2,1)S(1)} collective-permute-done((bf16[128,1024]{1,0:T(8,128)(2,1)S(1)}, bf16[128,1024]{1,0:T(8,128)(2,1)S(1)}, u32[]{:S(2)}, u32[]{:S(2)}) %collective-permute-start.9) | collective-permute-done | bytes 262176 | tf_op jit(solution)/shard_map/ppermute | solution.py:234
  18.0 0.5 collective-permute-start.5
  18.6 10.3 %collective-permute-done.19.rest_20_ = bf16[128,1024]{1,0:T(8,128)(2,1)S(1)} collective-permute-done((bf16[128,1024]{1,0:T(8,128)(2,1)S(1)}, bf16[128,1024]{1,0:T(8,128)(2,1)S(1)}, u32[]{:S(2)}, u32[]{:S(2)}) %collective-permute-start.19) | collective-permute-done | bytes 262176 | tf_op jit(solution)/shard_map/ppermute | solution.py:234
  28.9 0.5 collective-permute-start.7
  29.4 0.5 collective-permute-start.10
  29.9 4.4 %collective-permute-done.7.rest_8_ = bf16[64,1024]{1,0:T(8,128)(2,1)S(1)} collective-permute-done((bf16[64,1024]{1,0:T(8,128)(2,1)S(1)}, bf16[64,1024]{1,0:T(8,128)(2,1)S(1)}, u32[]{:S(2)}, u32[]{:S(2)}) %collective-permute-start.7) | collective-permute-done | bytes 131104 | tf_op jit(solution)/shard_map/ppermute | solution.py:221
  34.3 0.5 collective-permute-start.11
  34.8 0.5 collective-permute-start.13
  35.3 1.5 %collective-permute-start.23 = (bf16[128,1024]{1,0:T(8,128)(2,1)S(1)}, bf16[128,1024]{1,0:T(8,128)(2,1)}, u32[]{:S(2)}, u32[]{:S(2)}) collective-permute-start(bf16[128,1024]{1,0:T(8,128)(2,1)S(1)} %collective-permute-done.19.rest_20_), channel_id=1, source_target_pairs={{0,4},{1,5},{2,6},{3,7},{4,0},{5,1},{6,2},{7,3},{8,12},{9,13},{10,... | collective-permute-start | bytes 786440 | tf_op jit(solution)/shard_map/ppermute | solution.py:221
  36.9 0.1 fusion.2
  37.0 1.1 copy.15
  38.1 4.2 %all-to-all-start = ((bf16[2,1,8,32,1024]{4,3,1,0,2:T(8,128)(2,1)}), bf16[2,1,8,32,1024]{4,3,1,0,2:T(8,128)(2,1)}, u32[]{:S(2)}, u32[]{:S(2)}) async-start(bf16[2,1,8,32,1024]{4,3,1,0,2:T(8,128)(2,1)} %copy.15), calls=%async_computation | async-start | bytes 2097152 | tf_op jit(solution)/shard_map/all_to_all | solution.py:280
  42.4 0.6 copy-done.8
  43.0 0.4 collective-permute-start.20
  43.5 1.6 %collective-permute-start.21 = (bf16[128,1024]{1,0:T(8,128)(2,1)S(1)}, bf16[128,1024]{1,0:T(8,128)(2,1)S(1)}, u32[]{:S(2)}, u32[]{:S(2)}) collective-permute-start(bf16[128,1024]{1,0:T(8,128)(2,1)S(1)} %collective-permute-done.19.rest_20_), channel_id=1, source_target_pairs={{0,2},{1,3},{2,0},{3,1},{4,6},{5,7},{6,4},{7,5},{8,10},{9,11},{10,... | collective-permute-start | bytes 786440 | tf_op jit(solution)/shard_map/ppermute | solution.py:221
  45.1 0.4 collective-permute-start.31
  45.5 1.6 %collective-permute-start.33 = (bf16[128,1024]{1,0:T(8,128)(2,1)}, bf16[128,1024]{1,0:T(8,128)(2,1)S(1)}, u32[]{:S(2)}, u32[]{:S(2)}) collective-permute-start(bf16[128,1024]{1,0:T(8,128)(2,1)} %collective-permute-done.29.rest_30_), channel_id=1, source_target_pairs={{0,4},{1,5},{2,6},{3,7},{4,0},{5,1},{6,2},{7,3},{8,12},{9,13},{10,... | collective-permute-start | bytes 786440 | tf_op jit(solution)/shard_map/ppermute | solution.py:221
  47.1 4.9 %collective-permute-done.23.rest_24_ = bf16[128,1024]{1,0:T(8,128)(2,1)} collective-permute-done((bf16[128,1024]{1,0:T(8,128)(2,1)S(1)}, bf16[128,1024]{1,0:T(8,128)(2,1)}, u32[]{:S(2)}, u32[]{:S(2)}) %collective-permute-start.23) | collective-permute-done | bytes 262176 | tf_op jit(solution)/shard_map/ppermute | solution.py:221
  52.1 0.9 slice.60
  53.0 4.7 %collective-permute-start.15 = (bf16[64,1024]{1,0:T(8,128)(2,1)S(1)}, bf16[64,1024]{1,0:T(8,128)(2,1)S(1)}, u32[]{:S(2)}, u32[]{:S(2)}) collective-permute-start(bf16[64,1024]{1,0:T(8,128)(2,1)S(1)} %slice.58), channel_id=1, source_target_pairs={{0,2},{1,3},{2,0},{3,1},{4,6},{5,7},{6,4},{7,5},{8,10},{9,11},{10,... | collective-permute-start | bytes 393224 | tf_op jit(solution)/shard_map/ppermute | solution.py:221
  57.7 5.2 %collective-permute-done.21.rest_22_ = bf16[128,1024]{1,0:T(8,128)(2,1)S(1)} collective-permute-done((bf16[128,1024]{1,0:T(8,128)(2,1)S(1)}, bf16[128,1024]{1,0:T(8,128)(2,1)S(1)}, u32[]{:S(2)}, u32[]{:S(2)}) %collective-permute-start.21) | collective-permute-done | bytes 262176 | tf_op jit(solution)/shard_map/ppermute | solution.py:221
  62.9 1.5 %collective-permute-start.17 = (bf16[64,1024]{1,0:T(8,128)(2,1)S(1)}, bf16[64,1024]{1,0:T(8,128)(2,1)}, u32[]{:S(2)}, u32[]{:S(2)}) collective-permute-start(bf16[64,1024]{1,0:T(8,128)(2,1)S(1)} %slice.59), channel_id=1, source_target_pairs={{0,4},{1,5},{2,6},{3,7},{4,0},{5,1},{6,2},{7,3},{8,12},{9,13},{10,... | collective-permute-start | bytes 393224 | tf_op jit(solution)/shard_map/ppermute | solution.py:221
  64.4 4.1 %collective-permute-done.31.rest_32_ = bf16[128,1024]{1,0:T(8,128)(2,1)S(1)} collective-permute-done((bf16[128,1024]{1,0:T(8,128)(2,1)}, bf16[128,1024]{1,0:T(8,128)(2,1)S(1)}, u32[]{:S(2)}, u32[]{:S(2)}) %collective-permute-start.31) | collective-permute-done | bytes 262176 | tf_op jit(solution)/shard_map/ppermute | solution.py:221
  68.5 0.2 collective-permute-start.25
  68.8 2.0 %collective-permute-start.27 = (bf16[64,1024]{1,0:T(8,128)(2,1)S(1)}, bf16[64,1024]{1,0:T(8,128)(2,1)}, u32[]{:S(2)}, u32[]{:S(2)}) collective-permute-start(bf16[64,1024]{1,0:T(8,128)(2,1)S(1)} %slice.61), channel_id=1, source_target_pairs={{0,4},{1,5},{2,6},{3,7},{4,0},{5,1},{6,2},{7,3},{8,12},{9,13},{10,... | collective-permute-start | bytes 393224 | tf_op jit(solution)/shard_map/ppermute | solution.py:221
  70.8 0.1 collective-permute-done.15.rest_16_
  70.8 1.4 %collective-permute-start.35 = (bf16[64,1024]{1,0:T(8,128)(2,1)S(1)}, bf16[64,1024]{1,0:T(8,128)(2,1)}, u32[]{:S(2)}, u32[]{:S(2)}) collective-permute-start(bf16[64,1024]{1,0:T(8,128)(2,1)S(1)} %slice.62), channel_id=1, source_target_pairs={{0,2},{1,3},{2,0},{3,1},{4,6},{5,7},{6,4},{7,5},{8,10},{9,11},{10,... | collective-permute-start | bytes 393224 | tf_op jit(solution)/shard_map/ppermute | solution.py:221
  72.3 0.6 collective-permute-start.37
  72.9 2.1 %collective-permute-done.25.rest_26_ = bf16[64,1024]{1,0:T(8,128)(2,1)} collective-permute-done((bf16[64,1024]{1,0:T(8,128)(2,1)S(1)}, bf16[64,1024]{1,0:T(8,128)(2,1)}, u32[]{:S(2)}, u32[]{:S(2)}) %collective-permute-start.25) | collective-permute-done | bytes 131104 | tf_op jit(solution)/shard_map/ppermute | solution.py:221
  75.0 0.5 collective-permute-start.22
  75.5 1.8 %collective-permute-done.35.rest_36_ = bf16[64,1024]{1,0:T(8,128)(2,1)} collective-permute-done((bf16[64,1024]{1,0:T(8,128)(2,1)S(1)}, bf16[64,1024]{1,0:T(8,128)(2,1)}, u32[]{:S(2)}, u32[]{:S(2)}) %collective-permute-start.35) | collective-permute-done | bytes 131104 | tf_op jit(solution)/shard_map/ppermute | solution.py:221
  77.4 0.2 collective-permute-done.37.rest_38_
  77.5 0.4 collective-permute-start.32
  77.9 0.7 copy-done
  78.6 0.2 collective-permute-start.34
  78.7 0.7 copy-done.2
  79.4 0.4 collective-permute-start.16
  79.8 0.7 copy-done.10
  81.1 0.0 copy-start.14
  81.1 0.2 collective-permute-start.18
  81.4 0.4 collective-permute-start.26
  81.7 0.2 collective-permute-start.28
  81.9 0.4 collective-permute-start.36
  82.3 0.1 copy-done.22
  82.4 0.1 copy-done.23
  82.6 0.6 copy-done.12
  83.2 0.4 collective-permute-start.38
  83.6 2.4 %slice_bitcast_fusion = (bf16[8,32,1024]{2,1,0:T(8,128)(2,1)}, bf16[8,32,1024]{2,1,0:T(8,128)(2,1)}) fusion(bf16[2,1,8,32,1024]{4,3,1,0,2:T(8,128)(2,1)} %all-to-all-done), kind=kLoop, calls=%fused_computation.5 | loop fusion | bytes 2097152 | tf_op jit(solution)/shard_map/squeeze | solution.py:282
  86.1 23.1 %block.1 = (bf16[8,32,1024]{2,1,0:T(8,128)(2,1)}, bf16[8,32,1024]{2,1,0:T(8,128)(2,1)}) custom-call(s32[1]{0:T(128)S(6)} %copy.25.counts_ref, f32[1,1024]{1,0:T(1,128)S(1)} %bitcast.21, bf16[8,32,1024]{2,1,0:T(8,128)(2,1)} %get-tuple-element.11.tokens_ref, bf16[8,32,1024]{2,1,0:T(8,128)(2,1)} %get-tuple-element.10.cot_ref, ...), custom_call_target="tpu_custom_call" | custom-call | flops 4294967296 | bytes 10485760 | tf_op jit(solution)/shard_map/block/pallas_call | solution.py:193
  109.2 1.3 maximum_bitcast_fusion
  110.5 0.1 copy.18
  110.6 18.9 %all_to_all.8 = bf16[2,8,1,32,1024]{4,3,0,2,1:T(8,128)(2,1)S(1)} all-to-all(bf16[2,8,1,32,1024]{4,3,0,2,1:T(8,128)(2,1)S(1)} %copy.18), channel_id=1, replica_groups=mesh['clip'=4,'frame'=8] {'frame'}, dimensions={1} | all-to-all | bytes 2097152 | tf_op jit(solution)/shard_map/all_to_all | solution.py:284
  129.5 0.1 copy.19
  129.5 0.9 slice_bitcast_fusion.2
  (83 shorter events, 0.2 us)
Async XLA Ops:
  0.6 36.2 %copy-start.15 = (bf16[1,1,196,1024]{3,2,1,0:T(8,128)(2,1)S(1)}, bf16[1,1,196,1024]{3,2,1,0:T(8,128)(2,1)}, u32[]{:S(2)}) copy-start(bf16[1,1,196,1024]{3,2,1,0:T(8,128)(2,1)} %param.11) | copy-start | bytes 1204228
  0.6 36.2 %copy-start.16 = (bf16[1,1,196,1024]{3,2,1,0:T(8,128)(2,1)S(1)}, bf16[1,1,196,1024]{3,2,1,0:T(8,128)(2,1)}, u32[]{:S(2)}) copy-start(bf16[1,1,196,1024]{3,2,1,0:T(8,128)(2,1)} %param.6) | copy-start | bytes 1204228
  2.5 9.2 %collective-permute-start.1 = (bf16[128,1024]{1,0:T(8,128)(2,1)S(1)}, bf16[128,1024]{1,0:T(8,128)(2,1)S(1)}, u32[]{:S(2)}, u32[]{:S(2)}) collective-permute-start(bf16[128,1024]{1,0:T(8,128)(2,1)S(1)} %constant_dynamic-update-slice_fusion.rest_0_), channel_id=1, source_target_pairs={{0,2},{1,3},{2,0},{3,1},{4,6},{5,7},{6,4},{7,5},{8,10},{9,11},{10,... | collective-permute-start | bytes 786440 | tf_op jit(solution)/shard_map/ppermute | solution.py:221
  5.5 10.2 %collective-permute-start.3 = (bf16[128,1024]{1,0:T(8,128)(2,1)S(1)}, bf16[128,1024]{1,0:T(8,128)(2,1)S(1)}, u32[]{:S(2)}, u32[]{:S(2)}) collective-permute-start(bf16[128,1024]{1,0:T(8,128)(2,1)S(1)} %constant_dynamic-update-slice_fusion.rest_0_), channel_id=1, source_target_pairs={{0,4},{1,5},{2,6},{3,7},{4,0},{5,1},{6,2},{7,3},{8,12},{9,13},{10,... | collective-permute-start | bytes 786440 | tf_op jit(solution)/shard_map/ppermute | solution.py:221
  7.0 8.7 %collective-permute-start = (bf16[128,1024]{1,0:T(8,128)(2,1)S(1)}, bf16[128,1024]{1,0:T(8,128)(2,1)S(1)}, u32[]{:S(2)}, u32[]{:S(2)}) collective-permute-start(bf16[128,1024]{1,0:T(8,128)(2,1)S(1)} %constant_dynamic-update-slice_fusion.rest_0_), channel_id=1, source_target_pairs={{0,1},{1,0},{2,3},{3,2},{4,5},{5,4},{6,7},{7,6},{8,9},{9,8},{10,11... | collective-permute-start | bytes 786440 | tf_op jit(solution)/shard_map/ppermute | solution.py:221
  7.0 11.0 %collective-permute-start.9 = (bf16[128,1024]{1,0:T(8,128)(2,1)S(1)}, bf16[128,1024]{1,0:T(8,128)(2,1)S(1)}, u32[]{:S(2)}, u32[]{:S(2)}) collective-permute-start(bf16[128,1024]{1,0:T(8,128)(2,1)S(1)} %constant_dynamic-update-slice_fusion.rest_0_), channel_id=1, source_target_pairs={{0,8},{8,16},{16,24},{24,0},{1,9},{9,17},{17,25},{25,1},{2,10},{10... | collective-permute-start | bytes 786440 | tf_op jit(solution)/shard_map/ppermute | solution.py:234
  8.6 20.3 %collective-permute-start.19 = (bf16[128,1024]{1,0:T(8,128)(2,1)S(1)}, bf16[128,1024]{1,0:T(8,128)(2,1)S(1)}, u32[]{:S(2)}, u32[]{:S(2)}) collective-permute-start(bf16[128,1024]{1,0:T(8,128)(2,1)S(1)} %constant_dynamic-update-slice_fusion.rest_0_), channel_id=1, source_target_pairs={{0,16},{8,24},{16,0},{24,8},{1,17},{9,25},{17,1},{25,9},{2,18},{10... | collective-permute-start | bytes 786440 | tf_op jit(solution)/shard_map/ppermute | solution.py:234
  11.8 17.7 %collective-permute-start.29 = (bf16[128,1024]{1,0:T(8,128)(2,1)S(1)}, bf16[128,1024]{1,0:T(8,128)(2,1)}, u32[]{:S(2)}, u32[]{:S(2)}) collective-permute-start(bf16[128,1024]{1,0:T(8,128)(2,1)S(1)} %constant_dynamic-update-slice_fusion.rest_0_), channel_id=1, source_target_pairs={{0,24},{8,0},{16,8},{24,16},{1,25},{9,1},{17,9},{25,17},{2,26},{10... | collective-permute-start | bytes 786440 | tf_op jit(solution)/shard_map/ppermute | solution.py:234
  15.6 19.2 %collective-permute-start.2 = (bf16[128,1024]{1,0:T(8,128)(2,1)S(1)}, bf16[128,1024]{1,0:T(8,128)(2,1)S(1)}, u32[]{:S(2)}, u32[]{:S(2)}) collective-permute-start(bf16[128,1024]{1,0:T(8,128)(2,1)S(1)} %collective-permute-done.1.rest_2_), channel_id=1, source_target_pairs={{0,1},{1,0},{2,3},{3,2},{4,5},{5,4},{6,7},{7,6},{8,9},{9,8},{10,11... | collective-permute-start | bytes 786440 | tf_op jit(solution)/shard_map/ppermute | solution.py:221
  15.6 19.7 %collective-permute-start.4 = (bf16[128,1024]{1,0:T(8,128)(2,1)S(1)}, bf16[128,1024]{1,0:T(8,128)(2,1)S(1)}, u32[]{:S(2)}, u32[]{:S(2)}) collective-permute-start(bf16[128,1024]{1,0:T(8,128)(2,1)S(1)} %collective-permute-done.3.rest_4_), channel_id=1, source_target_pairs={{0,1},{1,0},{2,3},{3,2},{4,5},{5,4},{6,7},{7,6},{8,9},{9,8},{10,11... | collective-permute-start | bytes 786440 | tf_op jit(solution)/shard_map/ppermute | solution.py:221
  18.0 11.4 %collective-permute-start.5 = (bf16[64,1024]{1,0:T(8,128)(2,1)S(1)}, bf16[64,1024]{1,0:T(8,128)(2,1)S(1)}, u32[]{:S(2)}, u32[]{:S(2)}) collective-permute-start(bf16[64,1024]{1,0:T(8,128)(2,1)S(1)} %slice.56), channel_id=1, source_target_pairs={{0,2},{1,3},{2,0},{3,1},{4,6},{5,7},{6,4},{7,5},{8,10},{9,11},{10,... | collective-permute-start | bytes 393224 | tf_op jit(solution)/shard_map/ppermute | solution.py:221
  28.9 5.4 %collective-permute-start.7 = (bf16[64,1024]{1,0:T(8,128)(2,1)S(1)}, bf16[64,1024]{1,0:T(8,128)(2,1)S(1)}, u32[]{:S(2)}, u32[]{:S(2)}) collective-permute-start(bf16[64,1024]{1,0:T(8,128)(2,1)S(1)} %slice.57), channel_id=1, source_target_pairs={{0,4},{1,5},{2,6},{3,7},{4,0},{5,1},{6,2},{7,3},{8,12},{9,13},{10,... | collective-permute-start | bytes 393224 | tf_op jit(solution)/shard_map/ppermute | solution.py:221
  29.4 7.4 %collective-permute-start.6 = (bf16[64,1024]{1,0:T(8,128)(2,1)S(1)}, bf16[64,1024]{1,0:T(8,128)(2,1)S(1)}, u32[]{:S(2)}, u32[]{:S(2)}) collective-permute-start(bf16[64,1024]{1,0:T(8,128)(2,1)S(1)} %collective-permute-done.5.rest_6_), channel_id=1, source_target_pairs={{0,1},{1,0},{2,3},{3,2},{4,5},{5,4},{6,7},{7,6},{8,9},{9,8},{10,11... | collective-permute-start | bytes 393224 | tf_op jit(solution)/shard_map/ppermute | solution.py:221
  29.4 14.0 %collective-permute-start.10 = (bf16[128,1024]{1,0:T(8,128)(2,1)S(1)}, bf16[128,1024]{1,0:T(8,128)(2,1)S(1)}, u32[]{:S(2)}, u32[]{:S(2)}) collective-permute-start(bf16[128,1024]{1,0:T(8,128)(2,1)S(1)} %collective-permute-done.9.rest_10_), channel_id=1, source_target_pairs={{0,1},{1,0},{2,3},{3,2},{4,5},{5,4},{6,7},{7,6},{8,9},{9,8},{10,11... | collective-permute-start | bytes 786440 | tf_op jit(solution)/shard_map/ppermute | solution.py:221
  34.3 3.8 %copy-start.4 = (bf16[64,1024]{1,0:T(8,128)(2,1)}, bf16[64,1024]{1,0:T(8,128)(2,1)S(1)}, u32[]{:S(2)}) copy-start(bf16[64,1024]{1,0:T(8,128)(2,1)S(1)} %collective-permute-done.7.rest_8_) | copy-start | bytes 393220
  34.3 10.8 %collective-permute-start.11 = (bf16[128,1024]{1,0:T(8,128)(2,1)S(1)}, bf16[128,1024]{1,0:T(8,128)(2,1)S(1)}, u32[]{:S(2)}, u32[]{:S(2)}) collective-permute-start(bf16[128,1024]{1,0:T(8,128)(2,1)S(1)} %collective-permute-done.9.rest_10_), channel_id=1, source_target_pairs={{0,2},{1,3},{2,0},{3,1},{4,6},{5,7},{6,4},{7,5},{8,10},{9,11},{10,... | collective-permute-start | bytes 786440 | tf_op jit(solution)/shard_map/ppermute | solution.py:221
  34.8 10.7 %collective-permute-start.13 = (bf16[128,1024]{1,0:T(8,128)(2,1)S(1)}, bf16[128,1024]{1,0:T(8,128)(2,1)S(1)}, u32[]{:S(2)}, u32[]{:S(2)}) collective-permute-start(bf16[128,1024]{1,0:T(8,128)(2,1)S(1)} %collective-permute-done.9.rest_10_), channel_id=1, source_target_pairs={{0,4},{1,5},{2,6},{3,7},{4,0},{5,1},{6,2},{7,3},{8,12},{9,13},{10,... | collective-permute-start | bytes 786440 | tf_op jit(solution)/shard_map/ppermute | solution.py:221
  35.3 16.7 %collective-permute-start.23 = (bf16[128,1024]{1,0:T(8,128)(2,1)S(1)}, bf16[128,1024]{1,0:T(8,128)(2,1)}, u32[]{:S(2)}, u32[]{:S(2)}) collective-permute-start(bf16[128,1024]{1,0:T(8,128)(2,1)S(1)} %collective-permute-done.19.rest_20_), channel_id=1, source_target_pairs={{0,4},{1,5},{2,6},{3,7},{4,0},{5,1},{6,2},{7,3},{8,12},{9,13},{10,... | collective-permute-start | bytes 786440 | tf_op jit(solution)/shard_map/ppermute | solution.py:221
  36.9 1.3 copy-start.6
  36.9 5.5 %collective-permute-start.8 = (bf16[64,1024]{1,0:T(8,128)(2,1)S(1)}, bf16[64,1024]{1,0:T(8,128)(2,1)S(1)}, u32[]{:S(2)}, u32[]{:S(2)}) collective-permute-start(bf16[64,1024]{1,0:T(8,128)(2,1)S(1)} %collective-permute-done.7.rest_8_), channel_id=1, source_target_pairs={{0,1},{1,0},{2,3},{3,2},{4,5},{5,4},{6,7},{7,6},{8,9},{9,8},{10,11... | collective-permute-start | bytes 393224 | tf_op jit(solution)/shard_map/ppermute | solution.py:221
  38.1 45.5 %all-to-all-start = ((bf16[2,1,8,32,1024]{4,3,1,0,2:T(8,128)(2,1)}), bf16[2,1,8,32,1024]{4,3,1,0,2:T(8,128)(2,1)}, u32[]{:S(2)}, u32[]{:S(2)}) async-start(bf16[2,1,8,32,1024]{4,3,1,0,2:T(8,128)(2,1)} %copy.15), calls=%async_computation | async-start | bytes 2097152 | tf_op jit(solution)/shard_map/all_to_all | solution.py:280
  42.4 0.6 copy-start.8
  43.0 10.0 %collective-permute-start.20 = (bf16[128,1024]{1,0:T(8,128)(2,1)S(1)}, bf16[128,1024]{1,0:T(8,128)(2,1)S(1)}, u32[]{:S(2)}, u32[]{:S(2)}) collective-permute-start(bf16[128,1024]{1,0:T(8,128)(2,1)S(1)} %collective-permute-done.19.rest_20_), channel_id=1, source_target_pairs={{0,1},{1,0},{2,3},{3,2},{4,5},{5,4},{6,7},{7,6},{8,9},{9,8},{10,11... | collective-permute-start | bytes 786440 | tf_op jit(solution)/shard_map/ppermute | solution.py:221
  43.5 19.4 %collective-permute-start.21 = (bf16[128,1024]{1,0:T(8,128)(2,1)S(1)}, bf16[128,1024]{1,0:T(8,128)(2,1)S(1)}, u32[]{:S(2)}, u32[]{:S(2)}) collective-permute-start(bf16[128,1024]{1,0:T(8,128)(2,1)S(1)} %collective-permute-done.19.rest_20_), channel_id=1, source_target_pairs={{0,2},{1,3},{2,0},{3,1},{4,6},{5,7},{6,4},{7,5},{8,10},{9,11},{10,... | collective-permute-start | bytes 786440 | tf_op jit(solution)/shard_map/ppermute | solution.py:221
  45.1 23.4 %collective-permute-start.31 = (bf16[128,1024]{1,0:T(8,128)(2,1)}, bf16[128,1024]{1,0:T(8,128)(2,1)S(1)}, u32[]{:S(2)}, u32[]{:S(2)}) collective-permute-start(bf16[128,1024]{1,0:T(8,128)(2,1)} %collective-permute-done.29.rest_30_), channel_id=1, source_target_pairs={{0,2},{1,3},{2,0},{3,1},{4,6},{5,7},{6,4},{7,5},{8,10},{9,11},{10,... | collective-permute-start | bytes 786440 | tf_op jit(solution)/shard_map/ppermute | solution.py:221
  45.5 23.0 %collective-permute-start.33 = (bf16[128,1024]{1,0:T(8,128)(2,1)}, bf16[128,1024]{1,0:T(8,128)(2,1)S(1)}, u32[]{:S(2)}, u32[]{:S(2)}) collective-permute-start(bf16[128,1024]{1,0:T(8,128)(2,1)} %collective-permute-done.29.rest_30_), channel_id=1, source_target_pairs={{0,4},{1,5},{2,6},{3,7},{4,0},{5,1},{6,2},{7,3},{8,12},{9,13},{10,... | collective-permute-start | bytes 786440 | tf_op jit(solution)/shard_map/ppermute | solution.py:221
  52.1 16.7 %collective-permute-start.30 = (bf16[128,1024]{1,0:T(8,128)(2,1)}, bf16[128,1024]{1,0:T(8,128)(2,1)S(1)}, u32[]{:S(2)}, u32[]{:S(2)}) collective-permute-start(bf16[128,1024]{1,0:T(8,128)(2,1)} %collective-permute-done.29.rest_30_), channel_id=1, source_target_pairs={{0,1},{1,0},{2,3},{3,2},{4,5},{5,4},{6,7},{7,6},{8,9},{9,8},{10,11... | collective-permute-start | bytes 786440 | tf_op jit(solution)/shard_map/ppermute | solution.py:221
  53.0 17.8 %collective-permute-start.15 = (bf16[64,1024]{1,0:T(8,128)(2,1)S(1)}, bf16[64,1024]{1,0:T(8,128)(2,1)S(1)}, u32[]{:S(2)}, u32[]{:S(2)}) collective-permute-start(bf16[64,1024]{1,0:T(8,128)(2,1)S(1)} %slice.58), channel_id=1, source_target_pairs={{0,2},{1,3},{2,0},{3,1},{4,6},{5,7},{6,4},{7,5},{8,10},{9,11},{10,... | collective-permute-start | bytes 393224 | tf_op jit(solution)/shard_map/ppermute | solution.py:221
  62.9 9.4 %collective-permute-start.17 = (bf16[64,1024]{1,0:T(8,128)(2,1)S(1)}, bf16[64,1024]{1,0:T(8,128)(2,1)}, u32[]{:S(2)}, u32[]{:S(2)}) collective-permute-start(bf16[64,1024]{1,0:T(8,128)(2,1)S(1)} %slice.59), channel_id=1, source_target_pairs={{0,4},{1,5},{2,6},{3,7},{4,0},{5,1},{6,2},{7,3},{8,12},{9,13},{10,... | collective-permute-start | bytes 393224 | tf_op jit(solution)/shard_map/ppermute | solution.py:221
  68.5 13.7 %copy-start.17 = (bf16[128,1024]{1,0:T(8,128)(2,1)}, bf16[128,1024]{1,0:T(8,128)(2,1)S(1)}, u32[]{:S(2)}) copy-start(bf16[128,1024]{1,0:T(8,128)(2,1)S(1)} %collective-permute-done.31.rest_32_) | copy-start | bytes 786436
  68.5 9.4 %collective-permute-start.12 = (bf16[128,1024]{1,0:T(8,128)(2,1)S(1)}, bf16[128,1024]{1,0:T(8,128)(2,1)S(1)}, u32[]{:S(2)}, u32[]{:S(2)}) collective-permute-start(bf16[128,1024]{1,0:T(8,128)(2,1)S(1)} %collective-permute-done.11.rest_12_), channel_id=1, source_target_pairs={{0,1},{1,0},{2,3},{3,2},{4,5},{5,4},{6,7},{7,6},{8,9},{9,8},{10,11... | collective-permute-start | bytes 786440 | tf_op jit(solution)/shard_map/ppermute | solution.py:221
  68.5 13.7 %copy-start.18 = (bf16[128,1024]{1,0:T(8,128)(2,1)}, bf16[128,1024]{1,0:T(8,128)(2,1)S(1)}, u32[]{:S(2)}) copy-start(bf16[128,1024]{1,0:T(8,128)(2,1)S(1)} %collective-permute-done.33.rest_34_) | copy-start | bytes 786436
  68.5 6.5 %collective-permute-start.25 = (bf16[64,1024]{1,0:T(8,128)(2,1)S(1)}, bf16[64,1024]{1,0:T(8,128)(2,1)}, u32[]{:S(2)}, u32[]{:S(2)}) collective-permute-start(bf16[64,1024]{1,0:T(8,128)(2,1)S(1)} %slice.60), channel_id=1, source_target_pairs={{0,2},{1,3},{2,0},{3,1},{4,6},{5,7},{6,4},{7,5},{8,10},{9,11},{10,... | collective-permute-start | bytes 393224 | tf_op jit(solution)/shard_map/ppermute | solution.py:221
  68.8 13.5 %copy-start.19 = (bf16[128,1024]{1,0:T(8,128)(2,1)}, bf16[128,1024]{1,0:T(8,128)(2,1)S(1)}, u32[]{:S(2)}) copy-start(bf16[128,1024]{1,0:T(8,128)(2,1)S(1)} %collective-permute-done.30.rest_31_) | copy-start | bytes 786436
  68.8 6.2 %collective-permute-start.27 = (bf16[64,1024]{1,0:T(8,128)(2,1)S(1)}, bf16[64,1024]{1,0:T(8,128)(2,1)}, u32[]{:S(2)}, u32[]{:S(2)}) collective-permute-start(bf16[64,1024]{1,0:T(8,128)(2,1)S(1)} %slice.61), channel_id=1, source_target_pairs={{0,4},{1,5},{2,6},{3,7},{4,0},{5,1},{6,2},{7,3},{8,12},{9,13},{10,... | collective-permute-start | bytes 393224 | tf_op jit(solution)/shard_map/ppermute | solution.py:221
  70.8 6.5 %collective-permute-start.35 = (bf16[64,1024]{1,0:T(8,128)(2,1)S(1)}, bf16[64,1024]{1,0:T(8,128)(2,1)}, u32[]{:S(2)}, u32[]{:S(2)}) collective-permute-start(bf16[64,1024]{1,0:T(8,128)(2,1)S(1)} %slice.62), channel_id=1, source_target_pairs={{0,2},{1,3},{2,0},{3,1},{4,6},{5,7},{6,4},{7,5},{8,10},{9,11},{10,... | collective-permute-start | bytes 393224 | tf_op jit(solution)/shard_map/ppermute | solution.py:221
  72.3 5.3 %collective-permute-start.37 = (bf16[64,1024]{1,0:T(8,128)(2,1)S(1)}, bf16[64,1024]{1,0:T(8,128)(2,1)}, u32[]{:S(2)}, u32[]{:S(2)}) collective-permute-start(bf16[64,1024]{1,0:T(8,128)(2,1)S(1)} %slice.63), channel_id=1, source_target_pairs={{0,4},{1,5},{2,6},{3,7},{4,0},{5,1},{6,2},{7,3},{8,12},{9,13},{10,... | collective-permute-start | bytes 393224 | tf_op jit(solution)/shard_map/ppermute | solution.py:221
  75.0 3.7 %collective-permute-start.14 = (bf16[128,1024]{1,0:T(8,128)(2,1)S(1)}, bf16[128,1024]{1,0:T(8,128)(2,1)S(1)}, u32[]{:S(2)}, u32[]{:S(2)}) collective-permute-start(bf16[128,1024]{1,0:T(8,128)(2,1)S(1)} %collective-permute-done.13.rest_14_), channel_id=1, source_target_pairs={{0,1},{1,0},{2,3},{3,2},{4,5},{5,4},{6,7},{7,6},{8,9},{9,8},{10,11... | collective-permute-start | bytes 786440 | tf_op jit(solution)/shard_map/ppermute | solution.py:221
  75.0 6.1 %collective-permute-start.22 = (bf16[128,1024]{1,0:T(8,128)(2,1)S(1)}, bf16[128,1024]{1,0:T(8,128)(2,1)S(1)}, u32[]{:S(2)}, u32[]{:S(2)}) collective-permute-start(bf16[128,1024]{1,0:T(8,128)(2,1)S(1)} %collective-permute-done.21.rest_22_), channel_id=1, source_target_pairs={{0,1},{1,0},{2,3},{3,2},{4,5},{5,4},{6,7},{7,6},{8,9},{9,8},{10,11... | collective-permute-start | bytes 786440 | tf_op jit(solution)/shard_map/ppermute | solution.py:221
  77.4 4.0 %collective-permute-start.24 = (bf16[128,1024]{1,0:T(8,128)(2,1)}, bf16[128,1024]{1,0:T(8,128)(2,1)S(1)}, u32[]{:S(2)}, u32[]{:S(2)}) collective-permute-start(bf16[128,1024]{1,0:T(8,128)(2,1)} %collective-permute-done.23.rest_24_), channel_id=1, source_target_pairs={{0,1},{1,0},{2,3},{3,2},{4,5},{5,4},{6,7},{7,6},{8,9},{9,8},{10,11... | collective-permute-start | bytes 786440 | tf_op jit(solution)/shard_map/ppermute | solution.py:221
  77.5 4.2 %collective-permute-start.32 = (bf16[128,1024]{1,0:T(8,128)(2,1)S(1)}, bf16[128,1024]{1,0:T(8,128)(2,1)S(1)}, u32[]{:S(2)}, u32[]{:S(2)}) collective-permute-start(bf16[128,1024]{1,0:T(8,128)(2,1)S(1)} %collective-permute-done.31.rest_32_), channel_id=1, source_target_pairs={{0,1},{1,0},{2,3},{3,2},{4,5},{5,4},{6,7},{7,6},{8,9},{9,8},{10,11... | collective-permute-start | bytes 786440 | tf_op jit(solution)/shard_map/ppermute | solution.py:221
  77.9 0.7 copy-start
  78.6 3.3 %collective-permute-start.34 = (bf16[128,1024]{1,0:T(8,128)(2,1)S(1)}, bf16[128,1024]{1,0:T(8,128)(2,1)S(1)}, u32[]{:S(2)}, u32[]{:S(2)}) collective-permute-start(bf16[128,1024]{1,0:T(8,128)(2,1)S(1)} %collective-permute-done.33.rest_34_), channel_id=1, source_target_pairs={{0,1},{1,0},{2,3},{3,2},{4,5},{5,4},{6,7},{7,6},{8,9},{9,8},{10,11... | collective-permute-start | bytes 786440 | tf_op jit(solution)/shard_map/ppermute | solution.py:221
  78.7 0.7 copy-start.2
  79.4 2.8 %collective-permute-start.16 = (bf16[64,1024]{1,0:T(8,128)(2,1)S(1)}, bf16[64,1024]{1,0:T(8,128)(2,1)S(1)}, u32[]{:S(2)}, u32[]{:S(2)}) collective-permute-start(bf16[64,1024]{1,0:T(8,128)(2,1)S(1)} %collective-permute-done.15.rest_16_), channel_id=1, source_target_pairs={{0,1},{1,0},{2,3},{3,2},{4,5},{5,4},{6,7},{7,6},{8,9},{9,8},{10,11... | collective-permute-start | bytes 393224 | tf_op jit(solution)/shard_map/ppermute | solution.py:221
  79.8 0.7 copy-start.10
  81.1 4.9 %copy-start.14 = (f32[1024]{0:T(1024)S(1)}, f32[1024]{0:T(1024)}, u32[]{:S(2)}) copy-start(f32[1024]{0:T(1024)} %param.8) | copy-start | bytes 12292
  81.1 1.1 copy-start.20
  81.1 4.9 %collective-permute-start.18 = (bf16[64,1024]{1,0:T(8,128)(2,1)}, bf16[64,1024]{1,0:T(8,128)(2,1)}, u32[]{:S(2)}, u32[]{:S(2)}) collective-permute-start(bf16[64,1024]{1,0:T(8,128)(2,1)} %collective-permute-done.17.rest_18_), channel_id=1, source_target_pairs={{0,1},{1,0},{2,3},{3,2},{4,5},{5,4},{6,7},{7,6},{8,9},{9,8},{10,11... | collective-permute-start | bytes 393224 | tf_op jit(solution)/shard_map/ppermute | solution.py:221
  81.4 0.9 copy-start.21
  81.4 4.7 %collective-permute-start.26 = (bf16[64,1024]{1,0:T(8,128)(2,1)}, bf16[64,1024]{1,0:T(8,128)(2,1)}, u32[]{:S(2)}, u32[]{:S(2)}) collective-permute-start(bf16[64,1024]{1,0:T(8,128)(2,1)} %collective-permute-done.25.rest_26_), channel_id=1, source_target_pairs={{0,1},{1,0},{2,3},{3,2},{4,5},{5,4},{6,7},{7,6},{8,9},{9,8},{10,11... | collective-permute-start | bytes 393224 | tf_op jit(solution)/shard_map/ppermute | solution.py:221
  81.7 0.7 copy-start.22
  81.7 4.3 %collective-permute-start.28 = (bf16[64,1024]{1,0:T(8,128)(2,1)}, bf16[64,1024]{1,0:T(8,128)(2,1)}, u32[]{:S(2)}, u32[]{:S(2)}) collective-permute-start(bf16[64,1024]{1,0:T(8,128)(2,1)} %collective-permute-done.27.rest_28_), channel_id=1, source_target_pairs={{0,1},{1,0},{2,3},{3,2},{4,5},{5,4},{6,7},{7,6},{8,9},{9,8},{10,11... | collective-permute-start | bytes 393224 | tf_op jit(solution)/shard_map/ppermute | solution.py:221
  81.9 0.7 copy-start.23
  81.9 4.1 %collective-permute-start.36 = (bf16[64,1024]{1,0:T(8,128)(2,1)}, bf16[64,1024]{1,0:T(8,128)(2,1)}, u32[]{:S(2)}, u32[]{:S(2)}) collective-permute-start(bf16[64,1024]{1,0:T(8,128)(2,1)} %collective-permute-done.35.rest_36_), channel_id=1, source_target_pairs={{0,1},{1,0},{2,3},{3,2},{4,5},{5,4},{6,7},{7,6},{8,9},{9,8},{10,11... | collective-permute-start | bytes 393224 | tf_op jit(solution)/shard_map/ppermute | solution.py:221
  82.6 0.6 copy-start.12
  83.2 2.8 %collective-permute-start.38 = (bf16[64,1024]{1,0:T(8,128)(2,1)}, bf16[64,1024]{1,0:T(8,128)(2,1)}, u32[]{:S(2)}, u32[]{:S(2)}) collective-permute-start(bf16[64,1024]{1,0:T(8,128)(2,1)} %collective-permute-done.37.rest_38_), channel_id=1, source_target_pairs={{0,1},{1,0},{2,3},{3,2},{4,5},{5,4},{6,7},{7,6},{8,9},{9,8},{10,11... | collective-permute-start | bytes 393224 | tf_op jit(solution)/shard_map/ppermute | solution.py:221
  83.6 2.5 %copy-start.1 = (bf16[128,1024]{1,0:T(8,128)(2,1)S(1)}, bf16[128,1024]{1,0:T(8,128)(2,1)}, u32[]{:S(2)}) copy-start(bf16[128,1024]{1,0:T(8,128)(2,1)} %copy-done) | copy-start | bytes 786436
  83.6 2.5 %copy-start.3 = (bf16[128,1024]{1,0:T(8,128)(2,1)S(1)}, bf16[128,1024]{1,0:T(8,128)(2,1)}, u32[]{:S(2)}) copy-start(bf16[128,1024]{1,0:T(8,128)(2,1)} %copy-done.2) | copy-start | bytes 786436
  83.6 2.5 %copy-start.5 = (bf16[64,1024]{1,0:T(8,128)(2,1)S(1)}, bf16[64,1024]{1,0:T(8,128)(2,1)}, u32[]{:S(2)}) copy-start(bf16[64,1024]{1,0:T(8,128)(2,1)} %copy-done.4) | copy-start | bytes 393220
  83.6 2.5 %copy-start.7 = (bf16[64,1024]{1,0:T(8,128)(2,1)S(1)}, bf16[64,1024]{1,0:T(8,128)(2,1)}, u32[]{:S(2)}) copy-start(bf16[64,1024]{1,0:T(8,128)(2,1)} %copy-done.6) | copy-start | bytes 393220
  83.6 2.5 %copy-start.9 = (bf16[64,1024]{1,0:T(8,128)(2,1)S(1)}, bf16[64,1024]{1,0:T(8,128)(2,1)}, u32[]{:S(2)}) copy-start(bf16[64,1024]{1,0:T(8,128)(2,1)} %copy-done.8) | copy-start | bytes 393220
  83.6 2.5 %copy-start.11 = (bf16[64,1024]{1,0:T(8,128)(2,1)S(1)}, bf16[64,1024]{1,0:T(8,128)(2,1)}, u32[]{:S(2)}) copy-start(bf16[64,1024]{1,0:T(8,128)(2,1)} %copy-done.10) | copy-start | bytes 393220
  83.6 2.5 %copy-start.13 = (bf16[64,1024]{1,0:T(8,128)(2,1)S(1)}, bf16[64,1024]{1,0:T(8,128)(2,1)}, u32[]{:S(2)}) copy-start(bf16[64,1024]{1,0:T(8,128)(2,1)} %copy-done.12) | copy-start | bytes 393220

commit v3 on v1

v3 whole, which is shorter than its diff:
```python
import functools

import jax
import jax.numpy as jnp
from jax import lax
from jax.experimental import pallas as pl
from jax.experimental.pallas import tpu as pltpu
from jax.sharding import PartitionSpec as P

DH = 64
PAIR = 2 * DH
SUB = 16
EPSILON = 1e-06
NEGATIVE = -1e30
NN = (((1,), (0,)), ((), ()))
NT = (((1,), (1,)), ((), ()))
TN = (((0,), (0,)), ((), ()))


def dot(a, b, dims):
    return lax.dot_general(a, b, dims, preferred_element_type=jnp.float32)


def attention_pair(q, k, v, ga, mask, low_lanes):
    zero = jnp.zeros_like(q)

    def apart(block):
        return jnp.concatenate(
            [jnp.where(low_lanes, block, zero), jnp.where(low_lanes, zero, block)], axis=0
        )

    def stacked(block):
        return jnp.concatenate([block[:, :rows], block[:, rows:]], axis=0)

    rows = q.shape[0]
    q_two, k_two, v_two, ga_two = apart(q), apart(k), apart(v), apart(ga)
    scores = dot(k, q_two, NT) * DH ** (-0.5)
    grad_probs = dot(v, ga_two, NT)
    scores = jnp.where(mask, scores, NEGATIVE)
    highest = jnp.max(scores, axis=0, keepdims=True)
    expanded = jnp.exp(scores - highest)
    probs = expanded * (1.0 / jnp.sum(expanded, axis=0, keepdims=True))
    probs_low = probs.astype(jnp.bfloat16)
    weighted = probs * grad_probs
    delta = jnp.sum(weighted, axis=0, keepdims=True)
    grad_scores = (weighted - probs * delta).astype(jnp.bfloat16)
    attended = dot(stacked(probs_low), v_two, TN).astype(jnp.bfloat16)
    grad_values = dot(probs_low, ga_two, NN).astype(jnp.bfloat16)
    grad_query = (dot(stacked(grad_scores), k_two, TN) * DH ** (-0.5)).astype(jnp.bfloat16)
    grad_keys = (dot(grad_scores, q_two, NN) * DH ** (-0.5)).astype(jnp.bfloat16)
    return attended, grad_query, grad_keys, grad_values


def block_kernel(
    pieces, frames, patches, width,
    counts_ref, gain_ref, both_ref, *rest,
):
    weight_refs = rest[: len(rest) - 10]
    out_ref, w_in, w_out, normed, proj, ga, att, gproj, stats, sems = rest[-10:]
    groups = patches // SUB
    rows = frames * SUB
    total = groups * rows
    count = counts_ref[0]

    copies = []
    for which, (target, found) in enumerate(zip((w_in, w_out), pieces())):
        mine = []
        for ref, first, depth, lanes, row, column in found:
            source = weight_refs[ref].at[pl.ds(first, depth)]
            mine.append(
                pltpu.make_async_copy(
                    source.at[:, pl.ds(*lanes)],
                    target.at[
                        pl.ds(pl.multiple_of(row, 16), depth),
                        pl.ds(pl.multiple_of(column, 128), lanes[1]),
                    ],
                    sems.at[which],
                )
            )
        copies.append(mine)
    for mine in copies:
        for copy in mine:
            copy.start()

    live = (lax.broadcasted_iota(jnp.int32, (rows, 1), 0) // SUB < count).astype(jnp.float32)
    gain = gain_ref[...]

    def load(which, group):
        return both_ref[:, which, group * SUB : (group + 1) * SUB, :].reshape(rows, width)

    def store(which, group, value):
        out_ref[:, which, group * SUB : (group + 1) * SUB, :] = value.reshape(frames, SUB, width)

    for group in range(groups):
        here = pl.ds(group * rows, rows)
        wide = load(0, group).astype(jnp.float32)
        average = jnp.mean(wide, axis=-1, keepdims=True)
        centred = wide - average
        variance = jnp.mean(centred * centred, axis=-1, keepdims=True)
        scale = lax.rsqrt(variance + EPSILON)
        normed[here, :] = (centred * scale * gain).astype(jnp.bfloat16)
        stats[here, 0:1] = average
        stats[here, 1:2] = scale

    for copy in copies[0]:
        copy.wait()

    step = 512

    @pl.loop(0, 3 * width // step)
    def _(j):
        columns = pl.ds(pl.multiple_of(j * step, step), step)
        proj[:, columns] = dot(normed[...], w_in[:, columns], NN).astype(jnp.bfloat16)

    for copy in copies[1]:
        copy.wait()

    for group in range(groups):
        here = pl.ds(group * rows, rows)
        normed[here, :] = (load(1, group).astype(jnp.float32) * live).astype(jnp.bfloat16)

    @pl.loop(0, width // step)
    def _(j):
        columns = pl.ds(pl.multiple_of(j * step, step), step)
        ga[:, columns] = dot(normed[...], w_out[columns, :], NT).astype(jnp.bfloat16)

    key = lax.broadcasted_iota(jnp.int32, (rows, 2 * rows), 0)
    query = lax.broadcasted_iota(jnp.int32, (rows, 2 * rows), 1)
    mask = (query % SUB == key % SUB) & (key // SUB < count)
    low_lanes = lax.broadcasted_iota(jnp.int32, (rows, PAIR), 1) < DH
    unroll = 4 if rows <= 128 else 1

    for group in range(groups):
        here = pl.ds(group * rows, rows)

        @pl.loop(0, width // (PAIR * unroll))
        def _(step_index):
            for inner in range(unroll):
                pair = step_index * unroll + inner

                def lanes(part):
                    return pl.ds(pl.multiple_of(part * width + pair * PAIR, PAIR), PAIR)

                attended, grad_query, grad_keys, grad_values = attention_pair(
                    proj[here, lanes(0)],
                    proj[here, lanes(1)],
                    proj[here, lanes(2)],
                    ga[here, lanes(0)],
                    mask,
                    low_lanes,
                )
                att[here, lanes(0)] = attended
                gproj[here, lanes(0)] = grad_query
                gproj[here, lanes(1)] = grad_keys
                gproj[here, lanes(2)] = grad_values

    for group in range(groups):
        here = pl.ds(group * rows, rows)
        mixed = dot(att[here, :], w_out[...], NN)
        store(
            0,
            group,
            (load(0, group).astype(jnp.float32) + live * mixed).astype(jnp.bfloat16),
        )

    for group in range(groups):
        here = pl.ds(group * rows, rows)
        grad = dot(gproj[here, :], w_in[...], NT) * gain
        scale = stats[here, 1:2]
        hat = (load(0, group).astype(jnp.float32) - stats[here, 0:1]) * scale
        grad_rows = scale * (
            grad
            - jnp.mean(grad, axis=-1, keepdims=True)
            - hat * jnp.mean(grad * hat, axis=-1, keepdims=True)
        )
        store(
            1,
            group,
            (load(1, group).astype(jnp.float32) + grad_rows).astype(jnp.bfloat16),
        )


def run_block(counts, gain, both, weights, pieces):
    frames, _, patches, width = both.shape
    total = frames * patches
    vmem = pl.BlockSpec(memory_space=pltpu.VMEM)
    anywhere = pl.BlockSpec(memory_space=pl.ANY)
    return pl.pallas_call(
        functools.partial(block_kernel, pieces, frames, patches, width),
        out_shape=jax.ShapeDtypeStruct(both.shape, jnp.bfloat16),
        in_specs=[pl.BlockSpec(memory_space=pltpu.SMEM), vmem, vmem]
        + [anywhere] * len(weights),
        out_specs=vmem,
        scratch_shapes=[
            pltpu.VMEM((width, 3 * width), jnp.bfloat16),
            pltpu.VMEM((width, width), jnp.bfloat16),
            pltpu.VMEM((total, width), jnp.bfloat16),
            pltpu.VMEM((total, 3 * width), jnp.bfloat16),
            pltpu.VMEM((total, width), jnp.bfloat16),
            pltpu.VMEM((total, width), jnp.bfloat16),
            pltpu.VMEM((total, 3 * width), jnp.bfloat16),
            pltpu.VMEM((total, 128), jnp.float32),
            pltpu.SemaphoreType.DMA((2,)),
        ],
        compiler_params=pltpu.CompilerParams(vmem_limit_bytes=48 * 1024 * 1024),
        cost_estimate=pl.CostEstimate(
            flops=16 * total * width * width,
            bytes_accessed=8 * width * width + 8 * total * width,
            transcendentals=total * 2048,
        ),
        name="block",
    )(counts, gain, both, *weights)


def swap(array, distance, devices):
    return lax.ppermute(array, "frame", [(f, f ^ distance) for f in range(devices)])


def finish(held, half, devices):
    _, by_x, by_y = held
    top, bottom = swap(by_y[:half], 2, devices), swap(by_x[half:], 4, devices)
    return [array for mine in (*held, top, bottom) for array in (mine, swap(mine, 1, devices))]


def join_kernel(left_ref, right_ref, out_ref, sems):
    width = left_ref.shape[1]
    copies = [
        pltpu.make_async_copy(left_ref, out_ref.at[:, pl.ds(0, width)], sems.at[0]),
        pltpu.make_async_copy(right_ref, out_ref.at[:, pl.ds(width, right_ref.shape[1])], sems.at[1]),
    ]
    for copy in copies:
        copy.start()
    for copy in copies:
        copy.wait()


def join(left, right):
    anywhere = pl.BlockSpec(memory_space=pl.ANY)
    return pl.pallas_call(
        join_kernel,
        out_shape=jax.ShapeDtypeStruct((left.shape[0], left.shape[1] + right.shape[1]), left.dtype),
        in_specs=[anywhere, anywhere],
        out_specs=pl.BlockSpec(memory_space=pltpu.VMEM),
        scratch_shapes=[pltpu.SemaphoreType.DMA((2,))],
        name="join",
    )(left, right)


def gather_weights(input_weights, output_weights, both, clips, devices):
    depth, in_columns = input_weights.shape
    out_columns = output_weights.shape[1]
    fits = in_columns % 128 == 0 and out_columns % 128 == 0 and depth % 32 == 0
    if clips == 4 and devices == 8 and fits:
        joined = join(input_weights, output_weights)
        half = depth // 2
        order = (0, 1, 3, 2)
        held, source = [joined], joined
        for offset in order[1:]:
            held.append(lax.ppermute(source, "clip", [(c, c ^ offset) for c in range(clips)]))
            source, held[-1] = lax.optimization_barrier((source, held[-1]))
        arrays, places, before, earlier = [], [], [], []
        for step, own in enumerate(held):
            if step > 0:
                gate = before + earlier + ([both] if step == 2 else [])
                own, *gate = lax.optimization_barrier((own, *gate))
                if step == 2:
                    both = gate.pop()
                earlier = gate[len(before):]
                arrays += earlier
                before = gate[: len(before)]
            by_x, by_y = swap(own, 2, devices), swap(own, 4, devices)
            if step > 0:
                earlier = finish(before, half, devices)
            before = [own, by_x, by_y]
        arrays += earlier + finish(before, half, devices)

        def pieces():
            clip, frame = lax.axis_index("clip"), lax.axis_index("frame")
            found = ([], [])
            ref = 0
            for offset in order:
                column = clip ^ offset
                for distance, row in ((0, 0), (2, 0), (4, 0), (6, 0), (6, half)):
                    for core in (0, 1):
                        start = (frame ^ (distance + core)) * depth + row
                        part = (ref, 0, half if distance == 6 else depth)
                        found[0].append((*part, (0, in_columns), start, column * in_columns))
                        found[1].append(
                            (*part, (in_columns, out_columns), start, column * out_columns)
                        )
                        ref += 1
            return found

        return arrays, pieces, both
    arrays = []
    for weights in (input_weights, output_weights):
        columns = lax.all_gather(weights, "clip", axis=1, tiled=True)
        arrays.append(lax.all_gather(columns, "frame", axis=0, tiled=True))
    found = tuple([(i, 0, w.shape[0], (0, w.shape[1]), 0, 0)] for i, w in enumerate(arrays))
    return arrays, lambda: found, both


def per_device(clips, devices, tokens, counts, norm_gain, input_weights, output_weights, cotangent):
    _, slots, patches, width = tokens.shape
    share = -(-patches // devices)
    share = -(-share // SUB) * SUB
    extra = devices * share - patches

    def by_destination(source):
        padded = jnp.pad(source[0], ((0, 0), (0, extra), (0, 0)))
        return padded.reshape(slots, devices, share, width).transpose(1, 0, 2, 3)

    both = jnp.stack([by_destination(tokens), by_destination(cotangent)], axis=2)
    both = lax.all_to_all(both, "frame", split_axis=0, concat_axis=0, tiled=True)
    weights, pieces, both = gather_weights(input_weights, output_weights, both, clips, devices)
    both = both.reshape(devices * slots, 2, share, width)
    back = run_block(counts, norm_gain.reshape(1, width), both, weights, pieces)
    back = back.reshape(devices, slots, 2, share, width)
    back = lax.all_to_all(back, "frame", split_axis=0, concat_axis=0, tiled=True)

    def in_order(which):
        rows = back[:, :, which].transpose(1, 0, 2, 3).reshape(slots, devices * share, width)
        return rows[None, :, :patches]

    return in_order(0), in_order(1)


def solution(mesh):
    in_specs = (
        P("clip", "frame", None, None),
        P("clip"),
        P(),
        P("frame", "clip"),
        P("frame", "clip"),
        P("clip", "frame", None, None),
    )
    out_specs = (P("clip", "frame", None, None), P("clip", "frame", None, None))
    body = functools.partial(per_device, mesh.shape["clip"], mesh.shape["frame"])
    return jax.shard_map(body, mesh=mesh, in_specs=in_specs, out_specs=out_specs, check_vma=False)
```

time: 144 us -> 124 us (0.86)
  waiting for transfers between devices: 78.5 us -> 39.7 us
  starting transfers between devices: 5.34 us -> 38.9 us
  between operations: 14.7 us -> 1.54 us
  other arithmetic: 3.04 us -> 1.07 us
    all_gather x1 -> x0, waiting for transfers between devices: 61.9 us -> none  [gather_weights(): whole = lax.all_gather(joined, ('clip', 'frame'), axis=0)]
    ppermute x0 -> x39, waiting for transfers between devices: none -> 39.7 us  [the longest x36 29.8 us: swap(): lax.ppermute(array, 'frame', [(f, f ^ distance) for f in range(devices)])]
    ppermute x0 -> x39, starting transfers between devices: none -> 33.7 us  [the longest x36 21.3 us: swap(): lax.ppermute(array, 'frame', [(f, f ^ distance) for f in range(devices)])]
    all_to_all x1, waiting for transfers between devices: 16.6 us -> 0.01 us  [per_device(): lax.all_to_all(both, 'frame', split_axis=0, concat_axis=0, tiled=True)]
    concatenate x2 -> x0, other arithmetic: 2.94 us -> none  [the longest x1 1.7 us: gather_weights(): joined = jnp.concatenate([input_weights, output_weights], axis=1)]
    pallas_call x1, Pallas kernels: 21.6 us -> 19.2 us  [run_block(): pl.pallas_call(functools.partial(block_kernel, pieces, frames, patches, w...]
    pallas_call x0 -> x1, Pallas kernels: none -> 1.65 us  [join(): pl.pallas_call(join_kernel, out_shape=jax.ShapeDtypeStruct((left.shape[0]...]
  transfers between devices with their start and end apart: 2 -> 40, of which waited for: 2 -> 16; matrix products, arithmetic and copies ran while one was open for 2% -> 0% of each run, Pallas kernels for 0% -> 1%
where the time goes in v3:
time: 124 us
  waiting for transfers between devices  39.7 us (32%)
  starting transfers between devices  38.9 us (31%)
  Pallas kernels  20.9 us (17%)
  blocking collectives  18.8 us (15%)
  local copies, waits for them, and re-layouts  2.97 us (2%)
  between operations  1.54 us (1%)
    ppermute x36, waiting for transfers between devices, swap(): lax.ppermute(array, 'frame', [(f, f ^ distance) for f in range(devices)])  29.8 us
    ppermute x36, starting transfers between devices, swap(): lax.ppermute(array, 'frame', [(f, f ^ distance) for f in range(devices)])  21.3 us
    pallas_call x1, Pallas kernels, run_block(): pl.pallas_call(functools.partial(block_kernel, pieces, frames, patches, w...  19.2 us
    all_to_all x1, blocking collectives, per_device(): lax.all_to_all(back, 'frame', split_axis=0, concat_axis=0, tiled=True)  18.8 us
    ppermute x3, starting transfers between devices, gather_weights(): lax.ppermute(source, 'clip', [(c, c ^ offset) for c in range(clips)])  12.5 us
    ppermute x3, waiting for transfers between devices, gather_weights(): lax.ppermute(source, 'clip', [(c, c ^ offset) for c in range(clips)])  9.89 us
    all_to_all x1, starting transfers between devices, per_device(): lax.all_to_all(both, 'frame', split_axis=0, concat_axis=0, tiled=True)  5.17 us
  transfers between devices with their start and end apart: 40, of which 16 were waited for; matrix products, arithmetic and copies ran while one was open for 0% of the time, Pallas kernels for 1%

profile of v3, /device:TPU:0, one launch (start us, length us, event | category | flops | bytes accessed | tf_op | source)
XLA Modules:
  0.0 123.9 jit_solution(14081976132151024851)
XLA Ops:
  0.6 1.1 pad.7
  1.7 0.0 copy-done.2
  1.8 1.1 pad_maximum_fusion
  2.9 5.2 %all-to-all-start = ((bf16[8,1,2,32,1024]{4,3,2,1,0:T(8,128)(2,1)}), bf16[8,1,2,32,1024]{4,3,2,1,0:T(8,128)(2,1)}, u32[]{:S(2)}, u32[]{:S(2)}) async-start(bf16[8,1,2,32,1024]{4,3,2,1,0:T(8,128)(2,1)} %pad_maximum_fusion), calls=%async_computation | async-start | bytes 2097152 | tf_op jit(solution)/shard_map/all_to_all | solution.py:314
  8.0 1.7 %join.1.rest_0_ = bf16[128,1024]{1,0:T(8,128)(2,1)} custom-call(bf16[128,768]{1,0:T(8,128)(2,1)} %left_ref.1, bf16[128,256]{1,0:T(8,128)(2,1)} %right_ref.1), custom_call_target="tpu_custom_call" | custom-call | tf_op jit(solution)/shard_map/join/pallas_call | solution.py:239
  9.7 0.0 copy-start
  9.7 2.2 %collective-permute-start = (bf16[128,1024]{1,0:T(8,128)(2,1)}, bf16[128,1024]{1,0:T(8,128)(2,1)S(1)}, u32[]{:S(2)}, u32[]{:S(2)}) collective-permute-start(bf16[128,1024]{1,0:T(8,128)(2,1)} %join.1.rest_0_), channel_id=1, source_target_pairs={{0,8},{8,0},{16,24},{24,16},{1,9},{9,1},{17,25},{25,17},{2,10},{10... | collective-permute-start | bytes 786440 | tf_op jit(solution)/shard_map/ppermute | solution.py:259
  11.9 1.9 %collective-permute-start.3 = (bf16[128,1024]{1,0:T(8,128)(2,1)}, bf16[128,1024]{1,0:T(8,128)(2,1)S(1)}, u32[]{:S(2)}, u32[]{:S(2)}) collective-permute-start(bf16[128,1024]{1,0:T(8,128)(2,1)} %join.1.rest_0_), channel_id=1, source_target_pairs={{0,4},{1,5},{2,6},{3,7},{4,0},{5,1},{6,2},{7,3},{8,12},{9,13},{10,... | collective-permute-start | bytes 786440 | tf_op jit(solution)/shard_map/ppermute | solution.py:216
  13.8 1.5 %collective-permute-start.2 = (bf16[128,1024]{1,0:T(8,128)(2,1)}, bf16[128,1024]{1,0:T(8,128)(2,1)S(1)}, u32[]{:S(2)}, u32[]{:S(2)}) collective-permute-start(bf16[128,1024]{1,0:T(8,128)(2,1)} %join.1.rest_0_), channel_id=1, source_target_pairs={{0,2},{1,3},{2,0},{3,1},{4,6},{5,7},{6,4},{7,5},{8,10},{9,11},{10,... | collective-permute-start | bytes 786440 | tf_op jit(solution)/shard_map/ppermute | solution.py:216
  15.3 3.7 %collective-permute-done.rest_10_ = bf16[128,1024]{1,0:T(8,128)(2,1)S(1)} collective-permute-done((bf16[128,1024]{1,0:T(8,128)(2,1)}, bf16[128,1024]{1,0:T(8,128)(2,1)S(1)}, u32[]{:S(2)}, u32[]{:S(2)}) %collective-permute-start) | collective-permute-done | bytes 262176 | tf_op jit(solution)/shard_map/ppermute | solution.py:259
  19.0 9.2 %collective-permute-done.3.rest_4_ = bf16[128,1024]{1,0:T(8,128)(2,1)S(1)} collective-permute-done((bf16[128,1024]{1,0:T(8,128)(2,1)}, bf16[128,1024]{1,0:T(8,128)(2,1)S(1)}, u32[]{:S(2)}, u32[]{:S(2)}) %collective-permute-start.3) | collective-permute-done | bytes 262176 | tf_op jit(solution)/shard_map/ppermute | solution.py:216
  28.1 0.1 collective-permute-done.2.rest_2_
  28.2 1.4 %collective-permute-start.9 = (bf16[64,1024]{1,0:T(8,128)(2,1)S(1)}, bf16[64,1024]{1,0:T(8,128)(2,1)S(1)}, u32[]{:S(2)}, u32[]{:S(2)}) collective-permute-start(bf16[64,1024]{1,0:T(8,128)(2,1)S(1)} %slice.36), channel_id=1, source_target_pairs={{0,2},{1,3},{2,0},{3,1},{4,6},{5,7},{6,4},{7,5},{8,10},{9,11},{10,... | collective-permute-start | bytes 393224 | tf_op jit(solution)/shard_map/ppermute | solution.py:216
  29.7 0.7 collective-permute-start.11
  30.4 4.0 %collective-permute-start.1 = (bf16[128,1024]{1,0:T(8,128)(2,1)S(1)}, bf16[128,1024]{1,0:T(8,128)(2,1)S(1)}, u32[]{:S(2)}, u32[]{:S(2)}) collective-permute-start(bf16[128,1024]{1,0:T(8,128)(2,1)S(1)} %copy-done), channel_id=1, source_target_pairs={{0,24},{8,16},{16,8},{24,0},{1,25},{9,17},{17,9},{25,1},{2,26},{10... | collective-permute-start | bytes 786440 | tf_op jit(solution)/shard_map/ppermute | solution.py:259
  34.4 0.5 collective-permute-done.11.rest_8_
  34.9 0.0 collective-permute-start.12
  34.9 0.5 collective-permute-start.6
  35.5 0.9 collective-permute-start.5
  36.4 1.0 collective-permute-start.4
  37.4 0.0 collective-permute-done.12.rest_9_
  37.4 0.0 collective-permute-start.7
  37.4 2.9 %collective-permute-done.1.rest_20_ = bf16[128,1024]{1,0:T(8,128)(2,1)S(1)} collective-permute-done((bf16[128,1024]{1,0:T(8,128)(2,1)S(1)}, bf16[128,1024]{1,0:T(8,128)(2,1)S(1)}, u32[]{:S(2)}, u32[]{:S(2)}) %collective-permute-start.1) | collective-permute-done | bytes 262176 | tf_op jit(solution)/shard_map/ppermute | solution.py:259
  40.2 0.0 collective-permute-start.8
  40.2 0.0 collective-permute-done.6.rest_1_
  40.2 6.2 %collective-permute-start.13 = (bf16[128,1024]{1,0:T(8,128)(2,1)S(1)}, bf16[128,1024]{1,0:T(8,128)(2,1)S(1)}, u32[]{:S(2)}, u32[]{:S(2)}) collective-permute-start(bf16[128,1024]{1,0:T(8,128)(2,1)S(1)} %copy-done), channel_id=1, source_target_pairs={{0,16},{8,24},{16,0},{24,8},{1,17},{9,25},{17,1},{25,9},{2,18},{10... | collective-permute-start | bytes 786440 | tf_op jit(solution)/shard_map/ppermute | solution.py:259
  46.5 0.0 collective-permute-done.5.rest_14_
  46.5 1.4 %collective-permute-start.19 = (bf16[64,1024]{1,0:T(8,128)(2,1)S(1)}, bf16[64,1024]{1,0:T(8,128)(2,1)S(1)}, u32[]{:S(2)}, u32[]{:S(2)}) collective-permute-start(bf16[64,1024]{1,0:T(8,128)(2,1)S(1)} %slice.38), channel_id=1, source_target_pairs={{0,2},{1,3},{2,0},{3,1},{4,6},{5,7},{6,4},{7,5},{8,10},{9,11},{10,... | collective-permute-start | bytes 393224 | tf_op jit(solution)/shard_map/ppermute | solution.py:216
  47.9 0.7 collective-permute-start.21
  48.6 3.6 %collective-permute-done.19.rest_16_ = bf16[64,1024]{1,0:T(8,128)(2,1)S(1)} collective-permute-done((bf16[64,1024]{1,0:T(8,128)(2,1)S(1)}, bf16[64,1024]{1,0:T(8,128)(2,1)S(1)}, u32[]{:S(2)}, u32[]{:S(2)}) %collective-permute-start.19) | collective-permute-done | bytes 131104 | tf_op jit(solution)/shard_map/ppermute | solution.py:216
  52.2 1.1 collective-permute-done.21.rest_18_
  53.4 1.0 collective-permute-start.15
  54.4 1.3 %collective-permute-start.14 = (bf16[128,1024]{1,0:T(8,128)(2,1)S(1)}, bf16[128,1024]{1,0:T(8,128)(2,1)S(1)}, u32[]{:S(2)}, u32[]{:S(2)}) collective-permute-start(bf16[128,1024]{1,0:T(8,128)(2,1)S(1)} %collective-permute-done.1.rest_20_), channel_id=1, source_target_pairs={{0,2},{1,3},{2,0},{3,1},{4,6},{5,7},{6,4},{7,5},{8,10},{9,11},{10,... | collective-permute-start | bytes 786440 | tf_op jit(solution)/shard_map/ppermute | solution.py:216
  55.7 3.4 %collective-permute-done.13.rest_30_ = bf16[128,1024]{1,0:T(8,128)(2,1)S(1)} collective-permute-done((bf16[128,1024]{1,0:T(8,128)(2,1)S(1)}, bf16[128,1024]{1,0:T(8,128)(2,1)S(1)}, u32[]{:S(2)}, u32[]{:S(2)}) %collective-permute-start.13) | collective-permute-done | bytes 262176 | tf_op jit(solution)/shard_map/ppermute | solution.py:259
  59.1 0.5 collective-permute-start.17
  59.6 0.1 collective-permute-start.18
  59.7 0.9 collective-permute-done.16.rest_11_
  60.6 1.5 %collective-permute-done.15.rest_24_ = bf16[128,1024]{1,0:T(8,128)(2,1)S(1)} collective-permute-done((bf16[128,1024]{1,0:T(8,128)(2,1)S(1)}, bf16[128,1024]{1,0:T(8,128)(2,1)S(1)}, u32[]{:S(2)}, u32[]{:S(2)}) %collective-permute-start.15) | collective-permute-done | bytes 262176 | tf_op jit(solution)/shard_map/ppermute | solution.py:216
  62.1 0.3 collective-permute-done.14.rest_22_
  62.4 1.4 %collective-permute-start.33 = (bf16[128,1024]{1,0:T(8,128)(2,1)S(1)}, bf16[128,1024]{1,0:T(8,128)(2,1)S(1)}, u32[]{:S(2)}, u32[]{:S(2)}) collective-permute-start(bf16[128,1024]{1,0:T(8,128)(2,1)S(1)} %collective-permute-done.13.rest_30_), channel_id=1, source_target_pairs={{0,4},{1,5},{2,6},{3,7},{4,0},{5,1},{6,2},{7,3},{8,12},{9,13},{10,... | collective-permute-start | bytes 786440 | tf_op jit(solution)/shard_map/ppermute | solution.py:216
  63.8 0.7 collective-permute-start.31
  64.6 1.4 %collective-permute-start.26 = (bf16[64,1024]{1,0:T(8,128)(2,1)S(1)}, bf16[64,1024]{1,0:T(8,128)(2,1)S(1)}, u32[]{:S(2)}, u32[]{:S(2)}) collective-permute-start(bf16[64,1024]{1,0:T(8,128)(2,1)S(1)} %slice.40), channel_id=1, source_target_pairs={{0,2},{1,3},{2,0},{3,1},{4,6},{5,7},{6,4},{7,5},{8,10},{9,11},{10,... | collective-permute-start | bytes 393224 | tf_op jit(solution)/shard_map/ppermute | solution.py:216
  65.9 0.7 collective-permute-start.28
  66.6 7.3 %collective-permute-done.26.rest_26_ = bf16[64,1024]{1,0:T(8,128)(2,1)S(1)} collective-permute-done((bf16[64,1024]{1,0:T(8,128)(2,1)S(1)}, bf16[64,1024]{1,0:T(8,128)(2,1)S(1)}, u32[]{:S(2)}, u32[]{:S(2)}) %collective-permute-start.26) | collective-permute-done | bytes 131104 | tf_op jit(solution)/shard_map/ppermute | solution.py:216
  74.0 0.5 collective-permute-start.25
  74.5 0.1 collective-permute-start.27
  74.6 0.4 collective-permute-start.29
  75.0 0.0 copy-start.1
  75.1 1.0 collective-permute-done.27.rest_27_
  76.1 0.1 collective-permute-start.30
  76.2 0.0 collective-permute-done.29.rest_29_
  76.3 1.0 collective-permute-start.35
  77.3 1.4 %collective-permute-start.37 = (bf16[64,1024]{1,0:T(8,128)(2,1)S(1)}, bf16[64,1024]{1,0:T(8,128)(2,1)S(1)}, u32[]{:S(2)}, u32[]{:S(2)}) collective-permute-start(bf16[64,1024]{1,0:T(8,128)(2,1)S(1)} %slice.49), channel_id=1, source_target_pairs={{0,4},{1,5},{2,6},{3,7},{4,0},{5,1},{6,2},{7,3},{8,12},{9,13},{10,... | collective-permute-start | bytes 393224 | tf_op jit(solution)/shard_map/ppermute | solution.py:216
  78.6 0.1 collective-permute-start.34
  78.7 0.5 collective-permute-start.32
  79.3 2.7 %collective-permute-done.35.rest_36_ = bf16[64,1024]{1,0:T(8,128)(2,1)S(1)} collective-permute-done((bf16[64,1024]{1,0:T(8,128)(2,1)S(1)}, bf16[64,1024]{1,0:T(8,128)(2,1)S(1)}, u32[]{:S(2)}, u32[]{:S(2)}) %collective-permute-start.35) | collective-permute-done | bytes 131104 | tf_op jit(solution)/shard_map/ppermute | solution.py:216
  82.0 0.7 collective-permute-done.37.rest_38_
  83.4 0.6 collective-permute-done.38.rest_39_
  84.1 0.1 copy-done.10
  84.2 0.6 copy-done.11
  84.8 19.2 %block.1 = bf16[8,2,32,1024]{3,2,1,0:T(8,128)(2,1)} custom-call(s32[1]{0:T(128)S(6)} %copy.9.counts_ref, f32[1,1024]{1,0:T(1,128)S(1)} %bitcast.15, bf16[8,2,32,1024]{3,2,1,0:T(8,128)(2,1)} %bitcast.5.both_ref, bf16[128,1024]{1,0:T(8,128)(2,1)S(1)} %copy-done, bf16[128,1024]{1,0:T(8,128)(2,1)S(1)} %collective-permute-done.6.rest_1_, ...), custom_call_target="tpu_custom_call" | custom-call | flops 4294967296 | bytes 10485760 | tf_op jit(solution)/shard_map/block/pallas_call | solution.py:188
  104.0 18.8 %all_to_all.10 = bf16[8,1,2,32,1024]{4,3,2,1,0:T(8,128)(2,1)S(1)} all-to-all(bf16[8,1,2,32,1024]{4,3,2,1,0:T(8,128)(2,1)} %bitcast.20), channel_id=1, replica_groups=mesh['clip'=4,'frame'=8] {'frame'}, dimensions={0} | all-to-all | bytes 2097152 | tf_op jit(solution)/shard_map/all_to_all | solution.py:319
  122.9 0.1 fusion
  123.0 0.9 slice_bitcast_fusion
  (56 shorter events, 0.2 us)
Async XLA Ops:
  0.6 1.1 copy-start.2
  2.9 43.6 %all-to-all-start = ((bf16[8,1,2,32,1024]{4,3,2,1,0:T(8,128)(2,1)}), bf16[8,1,2,32,1024]{4,3,2,1,0:T(8,128)(2,1)}, u32[]{:S(2)}, u32[]{:S(2)}) async-start(bf16[8,1,2,32,1024]{4,3,2,1,0:T(8,128)(2,1)} %pad_maximum_fusion), calls=%async_computation | async-start | bytes 2097152 | tf_op jit(solution)/shard_map/all_to_all | solution.py:314
  9.7 20.7 %copy-start = (bf16[128,1024]{1,0:T(8,128)(2,1)S(1)}, bf16[128,1024]{1,0:T(8,128)(2,1)}, u32[]{:S(2)}) copy-start(bf16[128,1024]{1,0:T(8,128)(2,1)} %join.1.rest_0_) | copy-start | bytes 786436
  9.7 9.2 %collective-permute-start = (bf16[128,1024]{1,0:T(8,128)(2,1)}, bf16[128,1024]{1,0:T(8,128)(2,1)S(1)}, u32[]{:S(2)}, u32[]{:S(2)}) collective-permute-start(bf16[128,1024]{1,0:T(8,128)(2,1)} %join.1.rest_0_), channel_id=1, source_target_pairs={{0,8},{8,0},{16,24},{24,16},{1,9},{9,1},{17,25},{25,17},{2,10},{10... | collective-permute-start | bytes 786440 | tf_op jit(solution)/shard_map/ppermute | solution.py:259
  11.9 16.2 %collective-permute-start.3 = (bf16[128,1024]{1,0:T(8,128)(2,1)}, bf16[128,1024]{1,0:T(8,128)(2,1)S(1)}, u32[]{:S(2)}, u32[]{:S(2)}) collective-permute-start(bf16[128,1024]{1,0:T(8,128)(2,1)} %join.1.rest_0_), channel_id=1, source_target_pairs={{0,4},{1,5},{2,6},{3,7},{4,0},{5,1},{6,2},{7,3},{8,12},{9,13},{10,... | collective-permute-start | bytes 786440 | tf_op jit(solution)/shard_map/ppermute | solution.py:216
  13.8 14.4 %collective-permute-start.2 = (bf16[128,1024]{1,0:T(8,128)(2,1)}, bf16[128,1024]{1,0:T(8,128)(2,1)S(1)}, u32[]{:S(2)}, u32[]{:S(2)}) collective-permute-start(bf16[128,1024]{1,0:T(8,128)(2,1)} %join.1.rest_0_), channel_id=1, source_target_pairs={{0,2},{1,3},{2,0},{3,1},{4,6},{5,7},{6,4},{7,5},{8,10},{9,11},{10,... | collective-permute-start | bytes 786440 | tf_op jit(solution)/shard_map/ppermute | solution.py:216
  28.2 6.2 %collective-permute-start.9 = (bf16[64,1024]{1,0:T(8,128)(2,1)S(1)}, bf16[64,1024]{1,0:T(8,128)(2,1)S(1)}, u32[]{:S(2)}, u32[]{:S(2)}) collective-permute-start(bf16[64,1024]{1,0:T(8,128)(2,1)S(1)} %slice.36), channel_id=1, source_target_pairs={{0,2},{1,3},{2,0},{3,1},{4,6},{5,7},{6,4},{7,5},{8,10},{9,11},{10,... | collective-permute-start | bytes 393224 | tf_op jit(solution)/shard_map/ppermute | solution.py:216
  29.7 5.3 %collective-permute-start.11 = (bf16[64,1024]{1,0:T(8,128)(2,1)S(1)}, bf16[64,1024]{1,0:T(8,128)(2,1)S(1)}, u32[]{:S(2)}, u32[]{:S(2)}) collective-permute-start(bf16[64,1024]{1,0:T(8,128)(2,1)S(1)} %slice.37), channel_id=1, source_target_pairs={{0,4},{1,5},{2,6},{3,7},{4,0},{5,1},{6,2},{7,3},{8,12},{9,13},{10,... | collective-permute-start | bytes 393224 | tf_op jit(solution)/shard_map/ppermute | solution.py:216
  30.4 9.8 %collective-permute-start.1 = (bf16[128,1024]{1,0:T(8,128)(2,1)S(1)}, bf16[128,1024]{1,0:T(8,128)(2,1)S(1)}, u32[]{:S(2)}, u32[]{:S(2)}) collective-permute-start(bf16[128,1024]{1,0:T(8,128)(2,1)S(1)} %copy-done), channel_id=1, source_target_pairs={{0,24},{8,16},{16,8},{24,0},{1,25},{9,17},{17,9},{25,1},{2,26},{10... | collective-permute-start | bytes 786440 | tf_op jit(solution)/shard_map/ppermute | solution.py:259
  34.4 2.0 %collective-permute-start.10 = (bf16[64,1024]{1,0:T(8,128)(2,1)S(1)}, bf16[64,1024]{1,0:T(8,128)(2,1)S(1)}, u32[]{:S(2)}, u32[]{:S(2)}) collective-permute-start(bf16[64,1024]{1,0:T(8,128)(2,1)S(1)} %collective-permute-done.9.rest_6_), channel_id=1, source_target_pairs={{0,1},{1,0},{2,3},{3,2},{4,5},{5,4},{6,7},{7,6},{8,9},{9,8},{10,11... | collective-permute-start | bytes 393224 | tf_op jit(solution)/shard_map/ppermute | solution.py:216
  34.9 2.4 %collective-permute-start.12 = (bf16[64,1024]{1,0:T(8,128)(2,1)S(1)}, bf16[64,1024]{1,0:T(8,128)(2,1)S(1)}, u32[]{:S(2)}, u32[]{:S(2)}) collective-permute-start(bf16[64,1024]{1,0:T(8,128)(2,1)S(1)} %collective-permute-done.11.rest_8_), channel_id=1, source_target_pairs={{0,1},{1,0},{2,3},{3,2},{4,5},{5,4},{6,7},{7,6},{8,9},{9,8},{10,11... | collective-permute-start | bytes 393224 | tf_op jit(solution)/shard_map/ppermute | solution.py:216
  34.9 5.3 %collective-permute-start.6 = (bf16[128,1024]{1,0:T(8,128)(2,1)S(1)}, bf16[128,1024]{1,0:T(8,128)(2,1)S(1)}, u32[]{:S(2)}, u32[]{:S(2)}) collective-permute-start(bf16[128,1024]{1,0:T(8,128)(2,1)S(1)} %copy-done), channel_id=1, source_target_pairs={{0,1},{1,0},{2,3},{3,2},{4,5},{5,4},{6,7},{7,6},{8,9},{9,8},{10,11... | collective-permute-start | bytes 786440 | tf_op jit(solution)/shard_map/ppermute | solution.py:216
  35.5 11.0 %collective-permute-start.5 = (bf16[128,1024]{1,0:T(8,128)(2,1)S(1)}, bf16[128,1024]{1,0:T(8,128)(2,1)S(1)}, u32[]{:S(2)}, u32[]{:S(2)}) collective-permute-start(bf16[128,1024]{1,0:T(8,128)(2,1)S(1)} %collective-permute-done.rest_10_), channel_id=1, source_target_pairs={{0,4},{1,5},{2,6},{3,7},{4,0},{5,1},{6,2},{7,3},{8,12},{9,13},{10,... | collective-permute-start | bytes 786440 | tf_op jit(solution)/shard_map/ppermute | solution.py:216
  36.4 10.1 %collective-permute-start.4 = (bf16[128,1024]{1,0:T(8,128)(2,1)S(1)}, bf16[128,1024]{1,0:T(8,128)(2,1)S(1)}, u32[]{:S(2)}, u32[]{:S(2)}) collective-permute-start(bf16[128,1024]{1,0:T(8,128)(2,1)S(1)} %collective-permute-done.rest_10_), channel_id=1, source_target_pairs={{0,2},{1,3},{2,0},{3,1},{4,6},{5,7},{6,4},{7,5},{8,10},{9,11},{10,... | collective-permute-start | bytes 786440 | tf_op jit(solution)/shard_map/ppermute | solution.py:216
  37.4 9.1 %collective-permute-start.7 = (bf16[128,1024]{1,0:T(8,128)(2,1)S(1)}, bf16[128,1024]{1,0:T(8,128)(2,1)S(1)}, u32[]{:S(2)}, u32[]{:S(2)}) collective-permute-start(bf16[128,1024]{1,0:T(8,128)(2,1)S(1)} %collective-permute-done.2.rest_2_), channel_id=1, source_target_pairs={{0,1},{1,0},{2,3},{3,2},{4,5},{5,4},{6,7},{7,6},{8,9},{9,8},{10,11... | collective-permute-start | bytes 786440 | tf_op jit(solution)/shard_map/ppermute | solution.py:216
  40.2 6.3 %collective-permute-start.8 = (bf16[128,1024]{1,0:T(8,128)(2,1)S(1)}, bf16[128,1024]{1,0:T(8,128)(2,1)S(1)}, u32[]{:S(2)}, u32[]{:S(2)}) collective-permute-start(bf16[128,1024]{1,0:T(8,128)(2,1)S(1)} %collective-permute-done.3.rest_4_), channel_id=1, source_target_pairs={{0,1},{1,0},{2,3},{3,2},{4,5},{5,4},{6,7},{7,6},{8,9},{9,8},{10,11... | collective-permute-start | bytes 786440 | tf_op jit(solution)/shard_map/ppermute | solution.py:216
  40.2 18.8 %collective-permute-start.13 = (bf16[128,1024]{1,0:T(8,128)(2,1)S(1)}, bf16[128,1024]{1,0:T(8,128)(2,1)S(1)}, u32[]{:S(2)}, u32[]{:S(2)}) collective-permute-start(bf16[128,1024]{1,0:T(8,128)(2,1)S(1)} %copy-done), channel_id=1, source_target_pairs={{0,16},{8,24},{16,0},{24,8},{1,17},{9,25},{17,1},{25,9},{2,18},{10... | collective-permute-start | bytes 786440 | tf_op jit(solution)/shard_map/ppermute | solution.py:259
  46.5 5.7 %collective-permute-start.19 = (bf16[64,1024]{1,0:T(8,128)(2,1)S(1)}, bf16[64,1024]{1,0:T(8,128)(2,1)S(1)}, u32[]{:S(2)}, u32[]{:S(2)}) collective-permute-start(bf16[64,1024]{1,0:T(8,128)(2,1)S(1)} %slice.38), channel_id=1, source_target_pairs={{0,2},{1,3},{2,0},{3,1},{4,6},{5,7},{6,4},{7,5},{8,10},{9,11},{10,... | collective-permute-start | bytes 393224 | tf_op jit(solution)/shard_map/ppermute | solution.py:216
  47.9 5.4 %collective-permute-start.21 = (bf16[64,1024]{1,0:T(8,128)(2,1)S(1)}, bf16[64,1024]{1,0:T(8,128)(2,1)S(1)}, u32[]{:S(2)}, u32[]{:S(2)}) collective-permute-start(bf16[64,1024]{1,0:T(8,128)(2,1)S(1)} %slice.39), channel_id=1, source_target_pairs={{0,4},{1,5},{2,6},{3,7},{4,0},{5,1},{6,2},{7,3},{8,12},{9,13},{10,... | collective-permute-start | bytes 393224 | tf_op jit(solution)/shard_map/ppermute | solution.py:216
  52.2 6.9 %collective-permute-start.20 = (bf16[64,1024]{1,0:T(8,128)(2,1)S(1)}, bf16[64,1024]{1,0:T(8,128)(2,1)S(1)}, u32[]{:S(2)}, u32[]{:S(2)}) collective-permute-start(bf16[64,1024]{1,0:T(8,128)(2,1)S(1)} %collective-permute-done.19.rest_16_), channel_id=1, source_target_pairs={{0,1},{1,0},{2,3},{3,2},{4,5},{5,4},{6,7},{7,6},{8,9},{9,8},{10,11... | collective-permute-start | bytes 393224 | tf_op jit(solution)/shard_map/ppermute | solution.py:216
  53.4 6.2 %collective-permute-start.22 = (bf16[64,1024]{1,0:T(8,128)(2,1)S(1)}, bf16[64,1024]{1,0:T(8,128)(2,1)S(1)}, u32[]{:S(2)}, u32[]{:S(2)}) collective-permute-start(bf16[64,1024]{1,0:T(8,128)(2,1)S(1)} %collective-permute-done.21.rest_18_), channel_id=1, source_target_pairs={{0,1},{1,0},{2,3},{3,2},{4,5},{5,4},{6,7},{7,6},{8,9},{9,8},{10,11... | collective-permute-start | bytes 393224 | tf_op jit(solution)/shard_map/ppermute | solution.py:216
  53.4 8.7 %collective-permute-start.15 = (bf16[128,1024]{1,0:T(8,128)(2,1)S(1)}, bf16[128,1024]{1,0:T(8,128)(2,1)S(1)}, u32[]{:S(2)}, u32[]{:S(2)}) collective-permute-start(bf16[128,1024]{1,0:T(8,128)(2,1)S(1)} %collective-permute-done.1.rest_20_), channel_id=1, source_target_pairs={{0,4},{1,5},{2,6},{3,7},{4,0},{5,1},{6,2},{7,3},{8,12},{9,13},{10,... | collective-permute-start | bytes 786440 | tf_op jit(solution)/shard_map/ppermute | solution.py:216
  54.4 8.0 %collective-permute-start.14 = (bf16[128,1024]{1,0:T(8,128)(2,1)S(1)}, bf16[128,1024]{1,0:T(8,128)(2,1)S(1)}, u32[]{:S(2)}, u32[]{:S(2)}) collective-permute-start(bf16[128,1024]{1,0:T(8,128)(2,1)S(1)} %collective-permute-done.1.rest_20_), channel_id=1, source_target_pairs={{0,2},{1,3},{2,0},{3,1},{4,6},{5,7},{6,4},{7,5},{8,10},{9,11},{10,... | collective-permute-start | bytes 786440 | tf_op jit(solution)/shard_map/ppermute | solution.py:216
  59.1 17.0 %copy-start.6 = (bf16[128,1024]{1,0:T(8,128)(2,1)}, bf16[128,1024]{1,0:T(8,128)(2,1)S(1)}, u32[]{:S(2)}) copy-start(bf16[128,1024]{1,0:T(8,128)(2,1)S(1)} %collective-permute-done.13.rest_30_) | copy-start | bytes 786436
  59.1 1.5 %collective-permute-start.16 = (bf16[128,1024]{1,0:T(8,128)(2,1)S(1)}, bf16[128,1024]{1,0:T(8,128)(2,1)S(1)}, u32[]{:S(2)}, u32[]{:S(2)}) collective-permute-start(bf16[128,1024]{1,0:T(8,128)(2,1)S(1)} %collective-permute-done.rest_10_), channel_id=1, source_target_pairs={{0,1},{1,0},{2,3},{3,2},{4,5},{5,4},{6,7},{7,6},{8,9},{9,8},{10,11... | collective-permute-start | bytes 786440 | tf_op jit(solution)/shard_map/ppermute | solution.py:216
  59.1 3.3 %collective-permute-start.17 = (bf16[128,1024]{1,0:T(8,128)(2,1)S(1)}, bf16[128,1024]{1,0:T(8,128)(2,1)S(1)}, u32[]{:S(2)}, u32[]{:S(2)}) collective-permute-start(bf16[128,1024]{1,0:T(8,128)(2,1)S(1)} %collective-permute-done.4.rest_12_), channel_id=1, source_target_pairs={{0,1},{1,0},{2,3},{3,2},{4,5},{5,4},{6,7},{7,6},{8,9},{9,8},{10,11... | collective-permute-start | bytes 786440 | tf_op jit(solution)/shard_map/ppermute | solution.py:216
  59.6 2.8 %collective-permute-start.18 = (bf16[128,1024]{1,0:T(8,128)(2,1)S(1)}, bf16[128,1024]{1,0:T(8,128)(2,1)S(1)}, u32[]{:S(2)}, u32[]{:S(2)}) collective-permute-start(bf16[128,1024]{1,0:T(8,128)(2,1)S(1)} %collective-permute-done.5.rest_14_), channel_id=1, source_target_pairs={{0,1},{1,0},{2,3},{3,2},{4,5},{5,4},{6,7},{7,6},{8,9},{9,8},{10,11... | collective-permute-start | bytes 786440 | tf_op jit(solution)/shard_map/ppermute | solution.py:216
  62.1 11.9 %copy-start.3 = (bf16[128,1024]{1,0:T(8,128)(2,1)}, bf16[128,1024]{1,0:T(8,128)(2,1)S(1)}, u32[]{:S(2)}) copy-start(bf16[128,1024]{1,0:T(8,128)(2,1)S(1)} %collective-permute-done.15.rest_24_) | copy-start | bytes 786436
  62.4 12.1 %collective-permute-start.33 = (bf16[128,1024]{1,0:T(8,128)(2,1)S(1)}, bf16[128,1024]{1,0:T(8,128)(2,1)S(1)}, u32[]{:S(2)}, u32[]{:S(2)}) collective-permute-start(bf16[128,1024]{1,0:T(8,128)(2,1)S(1)} %collective-permute-done.13.rest_30_), channel_id=1, source_target_pairs={{0,4},{1,5},{2,6},{3,7},{4,0},{5,1},{6,2},{7,3},{8,12},{9,13},{10,... | collective-permute-start | bytes 786440 | tf_op jit(solution)/shard_map/ppermute | solution.py:216
  63.8 10.8 %collective-permute-start.31 = (bf16[128,1024]{1,0:T(8,128)(2,1)S(1)}, bf16[128,1024]{1,0:T(8,128)(2,1)S(1)}, u32[]{:S(2)}, u32[]{:S(2)}) collective-permute-start(bf16[128,1024]{1,0:T(8,128)(2,1)S(1)} %collective-permute-done.13.rest_30_), channel_id=1, source_target_pairs={{0,2},{1,3},{2,0},{3,1},{4,6},{5,7},{6,4},{7,5},{8,10},{9,11},{10,... | collective-permute-start | bytes 786440 | tf_op jit(solution)/shard_map/ppermute | solution.py:216
  64.6 9.4 %collective-permute-start.26 = (bf16[64,1024]{1,0:T(8,128)(2,1)S(1)}, bf16[64,1024]{1,0:T(8,128)(2,1)S(1)}, u32[]{:S(2)}, u32[]{:S(2)}) collective-permute-start(bf16[64,1024]{1,0:T(8,128)(2,1)S(1)} %slice.40), channel_id=1, source_target_pairs={{0,2},{1,3},{2,0},{3,1},{4,6},{5,7},{6,4},{7,5},{8,10},{9,11},{10,... | collective-permute-start | bytes 393224 | tf_op jit(solution)/shard_map/ppermute | solution.py:216
  65.9 8.0 %collective-permute-start.28 = (bf16[64,1024]{1,0:T(8,128)(2,1)S(1)}, bf16[64,1024]{1,0:T(8,128)(2,1)S(1)}, u32[]{:S(2)}, u32[]{:S(2)}) collective-permute-start(bf16[64,1024]{1,0:T(8,128)(2,1)S(1)} %slice.41), channel_id=1, source_target_pairs={{0,4},{1,5},{2,6},{3,7},{4,0},{5,1},{6,2},{7,3},{8,12},{9,13},{10,... | collective-permute-start | bytes 393224 | tf_op jit(solution)/shard_map/ppermute | solution.py:216
  66.6 10.6 %collective-permute-start.23 = (bf16[128,1024]{1,0:T(8,128)(2,1)S(1)}, bf16[128,1024]{1,0:T(8,128)(2,1)S(1)}, u32[]{:S(2)}, u32[]{:S(2)}) collective-permute-start(bf16[128,1024]{1,0:T(8,128)(2,1)S(1)} %collective-permute-done.1.rest_20_), channel_id=1, source_target_pairs={{0,1},{1,0},{2,3},{3,2},{4,5},{5,4},{6,7},{7,6},{8,9},{9,8},{10,11... | collective-permute-start | bytes 786440 | tf_op jit(solution)/shard_map/ppermute | solution.py:216
  74.0 4.6 %collective-permute-start.24 = (bf16[128,1024]{1,0:T(8,128)(2,1)S(1)}, bf16[128,1024]{1,0:T(8,128)(2,1)S(1)}, u32[]{:S(2)}, u32[]{:S(2)}) collective-permute-start(bf16[128,1024]{1,0:T(8,128)(2,1)S(1)} %collective-permute-done.14.rest_22_), channel_id=1, source_target_pairs={{0,1},{1,0},{2,3},{3,2},{4,5},{5,4},{6,7},{7,6},{8,9},{9,8},{10,11... | collective-permute-start | bytes 786440 | tf_op jit(solution)/shard_map/ppermute | solution.py:216
  74.0 4.7 %collective-permute-start.25 = (bf16[128,1024]{1,0:T(8,128)(2,1)S(1)}, bf16[128,1024]{1,0:T(8,128)(2,1)S(1)}, u32[]{:S(2)}, u32[]{:S(2)}) collective-permute-start(bf16[128,1024]{1,0:T(8,128)(2,1)S(1)} %collective-permute-done.15.rest_24_), channel_id=1, source_target_pairs={{0,1},{1,0},{2,3},{3,2},{4,5},{5,4},{6,7},{7,6},{8,9},{9,8},{10,11... | collective-permute-start | bytes 786440 | tf_op jit(solution)/shard_map/ppermute | solution.py:216
  74.5 4.1 %copy-start.4 = (bf16[128,1024]{1,0:T(8,128)(2,1)}, bf16[128,1024]{1,0:T(8,128)(2,1)S(1)}, u32[]{:S(2)}) copy-start(bf16[128,1024]{1,0:T(8,128)(2,1)S(1)} %collective-permute-done.33.rest_34_) | copy-start | bytes 786436
  74.5 1.6 %collective-permute-start.27 = (bf16[64,1024]{1,0:T(8,128)(2,1)S(1)}, bf16[64,1024]{1,0:T(8,128)(2,1)S(1)}, u32[]{:S(2)}, u32[]{:S(2)}) collective-permute-start(bf16[64,1024]{1,0:T(8,128)(2,1)S(1)} %collective-permute-done.26.rest_26_), channel_id=1, source_target_pairs={{0,1},{1,0},{2,3},{3,2},{4,5},{5,4},{6,7},{7,6},{8,9},{9,8},{10,11... | collective-permute-start | bytes 393224 | tf_op jit(solution)/shard_map/ppermute | solution.py:216
  74.6 4.1 %copy-start.5 = (bf16[128,1024]{1,0:T(8,128)(2,1)}, bf16[128,1024]{1,0:T(8,128)(2,1)S(1)}, u32[]{:S(2)}) copy-start(bf16[128,1024]{1,0:T(8,128)(2,1)S(1)} %collective-permute-done.31.rest_32_) | copy-start | bytes 786436
  74.6 1.7 %collective-permute-start.29 = (bf16[64,1024]{1,0:T(8,128)(2,1)S(1)}, bf16[64,1024]{1,0:T(8,128)(2,1)S(1)}, u32[]{:S(2)}, u32[]{:S(2)}) collective-permute-start(bf16[64,1024]{1,0:T(8,128)(2,1)S(1)} %collective-permute-done.28.rest_28_), channel_id=1, source_target_pairs={{0,1},{1,0},{2,3},{3,2},{4,5},{5,4},{6,7},{7,6},{8,9},{9,8},{10,11... | collective-permute-start | bytes 393224 | tf_op jit(solution)/shard_map/ppermute | solution.py:216
  75.0 9.7 %copy-start.1 = (f32[1024]{0:T(1024)S(1)}, f32[1024]{0:T(1024)}, u32[]{:S(2)}) copy-start(f32[1024]{0:T(1024)} %param.8) | copy-start | bytes 12292
  76.1 7.3 %collective-permute-start.30 = (bf16[128,1024]{1,0:T(8,128)(2,1)S(1)}, bf16[128,1024]{1,0:T(8,128)(2,1)S(1)}, u32[]{:S(2)}, u32[]{:S(2)}) collective-permute-start(bf16[128,1024]{1,0:T(8,128)(2,1)S(1)} %collective-permute-done.13.rest_30_), channel_id=1, source_target_pairs={{0,1},{1,0},{2,3},{3,2},{4,5},{5,4},{6,7},{7,6},{8,9},{9,8},{10,11... | collective-permute-start | bytes 786440 | tf_op jit(solution)/shard_map/ppermute | solution.py:216
  76.3 5.7 %collective-permute-start.35 = (bf16[64,1024]{1,0:T(8,128)(2,1)S(1)}, bf16[64,1024]{1,0:T(8,128)(2,1)S(1)}, u32[]{:S(2)}, u32[]{:S(2)}) collective-permute-start(bf16[64,1024]{1,0:T(8,128)(2,1)S(1)} %slice.48), channel_id=1, source_target_pairs={{0,2},{1,3},{2,0},{3,1},{4,6},{5,7},{6,4},{7,5},{8,10},{9,11},{10,... | collective-permute-start | bytes 393224 | tf_op jit(solution)/shard_map/ppermute | solution.py:216
  77.3 5.5 %collective-permute-start.37 = (bf16[64,1024]{1,0:T(8,128)(2,1)S(1)}, bf16[64,1024]{1,0:T(8,128)(2,1)S(1)}, u32[]{:S(2)}, u32[]{:S(2)}) collective-permute-start(bf16[64,1024]{1,0:T(8,128)(2,1)S(1)} %slice.49), channel_id=1, source_target_pairs={{0,4},{1,5},{2,6},{3,7},{4,0},{5,1},{6,2},{7,3},{8,12},{9,13},{10,... | collective-permute-start | bytes 393224 | tf_op jit(solution)/shard_map/ppermute | solution.py:216
  78.6 5.5 %copy-start.7 = (bf16[128,1024]{1,0:T(8,128)(2,1)}, bf16[128,1024]{1,0:T(8,128)(2,1)S(1)}, u32[]{:S(2)}) copy-start(bf16[128,1024]{1,0:T(8,128)(2,1)S(1)} %collective-permute-done.24.rest_23_) | copy-start | bytes 786436
  78.6 4.8 %collective-permute-start.34 = (bf16[128,1024]{1,0:T(8,128)(2,1)S(1)}, bf16[128,1024]{1,0:T(8,128)(2,1)S(1)}, u32[]{:S(2)}, u32[]{:S(2)}) collective-permute-start(bf16[128,1024]{1,0:T(8,128)(2,1)S(1)} %collective-permute-done.33.rest_34_), channel_id=1, source_target_pairs={{0,1},{1,0},{2,3},{3,2},{4,5},{5,4},{6,7},{7,6},{8,9},{9,8},{10,11... | collective-permute-start | bytes 786440 | tf_op jit(solution)/shard_map/ppermute | solution.py:216
  78.7 5.4 %copy-start.8 = (bf16[128,1024]{1,0:T(8,128)(2,1)}, bf16[128,1024]{1,0:T(8,128)(2,1)S(1)}, u32[]{:S(2)}) copy-start(bf16[128,1024]{1,0:T(8,128)(2,1)S(1)} %collective-permute-done.25.rest_25_) | copy-start | bytes 786436
  78.7 5.3 %collective-permute-start.32 = (bf16[128,1024]{1,0:T(8,128)(2,1)S(1)}, bf16[128,1024]{1,0:T(8,128)(2,1)S(1)}, u32[]{:S(2)}, u32[]{:S(2)}) collective-permute-start(bf16[128,1024]{1,0:T(8,128)(2,1)S(1)} %collective-permute-done.31.rest_32_), channel_id=1, source_target_pairs={{0,1},{1,0},{2,3},{3,2},{4,5},{5,4},{6,7},{7,6},{8,9},{9,8},{10,11... | collective-permute-start | bytes 786440 | tf_op jit(solution)/shard_map/ppermute | solution.py:216
  82.0 1.4 %collective-permute-start.36 = (bf16[64,1024]{1,0:T(8,128)(2,1)S(1)}, bf16[64,1024]{1,0:T(8,128)(2,1)S(1)}, u32[]{:S(2)}, u32[]{:S(2)}) collective-permute-start(bf16[64,1024]{1,0:T(8,128)(2,1)S(1)} %collective-permute-done.35.rest_36_), channel_id=1, source_target_pairs={{0,1},{1,0},{2,3},{3,2},{4,5},{5,4},{6,7},{7,6},{8,9},{9,8},{10,11... | collective-permute-start | bytes 393224 | tf_op jit(solution)/shard_map/ppermute | solution.py:216
  82.7 1.3 %collective-permute-start.38 = (bf16[64,1024]{1,0:T(8,128)(2,1)S(1)}, bf16[64,1024]{1,0:T(8,128)(2,1)S(1)}, u32[]{:S(2)}, u32[]{:S(2)}) collective-permute-start(bf16[64,1024]{1,0:T(8,128)(2,1)S(1)} %collective-permute-done.37.rest_38_), channel_id=1, source_target_pairs={{0,1},{1,0},{2,3},{3,2},{4,5},{5,4},{6,7},{7,6},{8,9},{9,8},{10,11... | collective-permute-start | bytes 393224 | tf_op jit(solution)/shard_map/ppermute | solution.py:216
  83.4 0.7 copy-start.9
  83.4 0.8 copy-start.10
  84.1 0.7 copy-start.11

commit v4 on v3

v4 whole, which is shorter than its diff:
```python
import functools
import math

import jax
import jax.numpy as jnp
from jax import lax
from jax.experimental import pallas as pl
from jax.experimental.pallas import tpu as pltpu
from jax.sharding import PartitionSpec as P

DH = 64
PAIR = 2 * DH
SUB = 16
EPSILON = 1e-06
NEGATIVE = -1e30
NN = (((1,), (0,)), ((), ()))
NT = (((1,), (1,)), ((), ()))
TN = (((0,), (0,)), ((), ()))


def dot(a, b, dims):
    return lax.dot_general(a, b, dims, preferred_element_type=jnp.float32)


def attention_pair(q, k, v, ga, mask, low, high):
    def apart(block):
        return jnp.concatenate([block * low, block * high], axis=0)

    def stacked(block):
        return jnp.concatenate([block[:, :rows], block[:, rows:]], axis=0)

    rows = q.shape[0]
    q_two, k_two, v_two, ga_two = apart(q * DH ** (-0.5)), apart(k), apart(v), apart(ga)
    scores = dot(k, q_two, NT)
    grad_probs = dot(v, ga_two, NT)
    scores = jnp.where(mask, scores, NEGATIVE)
    highest = jnp.max(scores, axis=0, keepdims=True)
    expanded = jnp.exp(scores - highest)
    probs = expanded * (1.0 / jnp.sum(expanded, axis=0, keepdims=True))
    probs_low = probs.astype(jnp.bfloat16)
    weighted = probs * grad_probs
    delta = jnp.sum(weighted, axis=0, keepdims=True)
    grad_scores = (weighted - probs * delta).astype(jnp.bfloat16)
    attended = dot(stacked(probs_low), v_two, TN).astype(jnp.bfloat16)
    grad_values = dot(probs_low, ga_two, NN).astype(jnp.bfloat16)
    grad_query = (dot(stacked(grad_scores), k_two, TN) * DH ** (-0.5)).astype(jnp.bfloat16)
    grad_keys = dot(grad_scores, q_two, NN).astype(jnp.bfloat16)
    return attended, grad_query, grad_keys, grad_values


def block_kernel(
    pieces, xor_order, frames, patches, width,
    counts_ref, gain_ref, both_ref, *rest,
):
    weight_refs = rest[: len(rest) - 11]
    out_ref, w_in, w_out, normed, proj, ga, att, gproj, gnorm, stats, sems = rest[-11:]
    groups = patches // SUB
    rows = frames * SUB
    total = groups * rows
    count = counts_ref[0]
    device = lax.axis_index("frame")

    found = pieces()
    copies = []
    for block, parts in enumerate(found):
        mine = []
        for ref, first, depth, lanes, target, row, column in parts:
            mine.append(
                pltpu.make_async_copy(
                    weight_refs[ref].at[pl.ds(first, depth), pl.ds(*lanes)],
                    (w_in, w_out)[target].at[
                        pl.ds(pl.multiple_of(row, 16), depth),
                        pl.ds(pl.multiple_of(column, 128), lanes[1]),
                    ],
                    sems.at[block],
                )
            )
        copies.append(mine)
    for mine in copies:
        for copy in mine:
            copy.start()

    live = (lax.broadcasted_iota(jnp.int32, (rows, 1), 0) // SUB < count).astype(jnp.float32)
    gain = gain_ref[...]

    def load(which, group):
        return both_ref[:, which, group * SUB : (group + 1) * SUB, :].reshape(rows, width)

    def store(which, group, value):
        for frame in range(frames):
            place = frame ^ device if xor_order else frame
            out_ref[pl.ds(place, 1), which, group * SUB : (group + 1) * SUB, :] = value[
                frame * SUB : (frame + 1) * SUB
            ].reshape(1, SUB, width)

    for group in range(groups):
        here = pl.ds(group * rows, rows)
        wide = load(0, group).astype(jnp.float32)
        average = jnp.mean(wide, axis=-1, keepdims=True)
        centred = wide - average
        variance = jnp.mean(centred * centred, axis=-1, keepdims=True)
        scale = lax.rsqrt(variance + EPSILON)
        normed[here, :] = (centred * scale * gain).astype(jnp.bfloat16)
        stats[here, 0:1] = average
        stats[here, 1:2] = scale

    for parts, mine in zip(found[:-1], copies[:-1]):
        for copy in mine:
            copy.wait()
        column, columns = parts[0][-1], parts[0][3][1]
        step = math.gcd(columns, 768)

        @pl.loop(0, columns // step)
        def _(j):
            here = pl.ds(pl.multiple_of(column + j * step, 128), step)
            proj[:, here] = dot(normed[...], w_in[:, here], NN).astype(jnp.bfloat16)

    for copy in copies[-1]:
        copy.wait()

    for group in range(groups):
        here = pl.ds(group * rows, rows)
        normed[here, :] = (load(1, group).astype(jnp.float32) * live).astype(jnp.bfloat16)

    step = min(width, 256)

    @pl.loop(0, width // step)
    def _(j):
        columns = pl.ds(pl.multiple_of(j * step, step), step)
        ga[:, columns] = dot(w_out[columns, :], normed[...], NT).astype(jnp.bfloat16).T

    key = lax.broadcasted_iota(jnp.int32, (rows, 2 * rows), 0)
    query = lax.broadcasted_iota(jnp.int32, (rows, 2 * rows), 1)
    mask = (query % SUB == key % SUB) & (key // SUB < count)
    lane = lax.broadcasted_iota(jnp.int32, (1, PAIR), 1)
    low, high = (lane < DH).astype(jnp.bfloat16), (lane >= DH).astype(jnp.bfloat16)
    unroll = 4 if rows <= 128 else 1

    for group in range(groups):
        here = pl.ds(group * rows, rows)

        @pl.loop(0, width // (PAIR * unroll))
        def _(step_index):
            for inner in range(unroll):
                pair = step_index * unroll + inner

                def lanes(part):
                    return pl.ds(pl.multiple_of(part * width + pair * PAIR, PAIR), PAIR)

                attended, grad_query, grad_keys, grad_values = attention_pair(
                    proj[here, lanes(0)],
                    proj[here, lanes(1)],
                    proj[here, lanes(2)],
                    ga[here, lanes(0)],
                    mask,
                    low,
                    high,
                )
                att[here, lanes(0)] = attended
                gproj[here, lanes(0)] = grad_query
                gproj[here, lanes(1)] = grad_keys
                gproj[here, lanes(2)] = grad_values

    for group in range(groups):
        here = pl.ds(group * rows, rows)
        mixed = dot(att[here, :], w_out[...], NN)
        store(
            0,
            group,
            (load(0, group).astype(jnp.float32) + live * mixed).astype(jnp.bfloat16),
        )

    @pl.loop(0, width // step)
    def _(j):
        columns = pl.ds(pl.multiple_of(j * step, step), step)
        gnorm[:, columns] = dot(w_in[columns, :], gproj[...], NT).T

    for group in range(groups):
        here = pl.ds(group * rows, rows)
        grad = gnorm[here, :] * gain
        scale = stats[here, 1:2]
        hat = (load(0, group).astype(jnp.float32) - stats[here, 0:1]) * scale
        grad_rows = scale * (
            grad
            - jnp.mean(grad, axis=-1, keepdims=True)
            - hat * jnp.mean(grad * hat, axis=-1, keepdims=True)
        )
        store(
            1,
            group,
            (load(1, group).astype(jnp.float32) + grad_rows).astype(jnp.bfloat16),
        )


def run_block(counts, gain, both, weights, pieces, xor_order):
    frames, _, patches, width = both.shape
    total = frames * patches
    vmem = pl.BlockSpec(memory_space=pltpu.VMEM)
    anywhere = pl.BlockSpec(memory_space=pl.ANY)
    return pl.pallas_call(
        functools.partial(block_kernel, pieces, xor_order, frames, patches, width),
        out_shape=jax.ShapeDtypeStruct(both.shape, jnp.bfloat16),
        in_specs=[pl.BlockSpec(memory_space=pltpu.SMEM), vmem, vmem]
        + [anywhere] * len(weights),
        out_specs=vmem,
        scratch_shapes=[
            pltpu.VMEM((width, 3 * width), jnp.bfloat16),
            pltpu.VMEM((width, width), jnp.bfloat16),
            pltpu.VMEM((total, width), jnp.bfloat16),
            pltpu.VMEM((total, 3 * width), jnp.bfloat16),
            pltpu.VMEM((total, width), jnp.bfloat16),
            pltpu.VMEM((total, width), jnp.bfloat16),
            pltpu.VMEM((total, 3 * width), jnp.bfloat16),
            pltpu.VMEM((total, width), jnp.float32),
            pltpu.VMEM((total, 128), jnp.float32),
            pltpu.SemaphoreType.DMA((8,)),
        ],
        compiler_params=pltpu.CompilerParams(vmem_limit_bytes=48 * 1024 * 1024),
        cost_estimate=pl.CostEstimate(
            flops=16 * total * width * width,
            bytes_accessed=8 * width * width + 8 * total * width,
            transcendentals=total * 2048,
        ),
        name="block",
    )(counts, gain, both, *weights)


def swap(array, distance, devices):
    return lax.ppermute(array, "frame", [(f, f ^ distance) for f in range(devices)])


def join_kernel(axis, *refs):
    *sources, target = refs
    start = 0
    for source in sources:
        end = start + source.shape[axis]
        if axis == 0:
            target[start:end, :] = source[...]
        else:
            target[:, start:end] = source[...]
        start = end


def join(axis, *arrays):
    shape = list(arrays[0].shape)
    shape[axis] = sum(array.shape[axis] for array in arrays)
    vmem = pl.BlockSpec(memory_space=pltpu.VMEM)
    return pl.pallas_call(
        functools.partial(join_kernel, axis),
        out_shape=jax.ShapeDtypeStruct(shape, arrays[0].dtype),
        in_specs=[vmem] * len(arrays),
        out_specs=vmem,
        name="join",
    )(*arrays)


def gather_rounds(input_weights, output_weights, both, devices):
    depth, in_columns = input_weights.shape
    out_columns = output_weights.shape[1]
    joined = join(1, input_weights, output_weights)
    half = depth // 2
    one, three, two = (
        lax.ppermute(joined, "clip", [(c, c ^ offset) for c in range(4)]) for offset in (1, 3, 2)
    )

    def across(own):
        return swap(own, 2, devices), swap(own, 4, devices)

    def diagonal(by_x, by_y):
        middle = by_x.shape[0] // 2
        return swap(by_y[:middle], 2, devices), swap(by_x[middle:], 4, devices)

    def other_core(arrays):
        return [swap(array, 1, devices) for array in arrays]

    first = [joined, *across(joined)]
    first += diagonal(*first[1:])
    both, *gate = lax.optimization_barrier((both, *first[1:3]))
    first[1:3] = gate
    both = lax.all_to_all(both, "frame", split_axis=0, concat_axis=0, tiled=True)
    second = [one, *across(one)]
    second += diagonal(*second[1:])
    first_other = other_core(first)
    three, second[1], second[2] = lax.optimization_barrier((three, second[1], second[2]))
    third, both, *first_other = lax.optimization_barrier((join(0, three, two), both, *first_other))
    third = [third, *across(third)]
    second_other = other_core(second)
    third[1], *second_other = lax.optimization_barrier((third[1], *second_other))
    third += diagonal(*third[1:])
    third_other = other_core(third)
    arrays = first + first_other + second + second_other + third + third_other

    def pieces():
        clip, frame = lax.axis_index("clip"), lax.axis_index("frame")
        found = {offset: [] for offset in (0, 1, 3, 2)}
        outer = []
        ref = 0
        for offsets in ((0,), (1,), (3, 2)):
            for core in (0, 1):
                for distance, part in ((0, None), (2, None), (4, None), (6, 0), (6, 1)):
                    rows = depth * len(offsets)
                    held = (0, rows) if part is None else (part * (rows // 2), rows // 2)
                    for place, offset in enumerate(offsets):
                        start = max(held[0], place * depth)
                        end = min(sum(held), (place + 1) * depth)
                        if end <= start:
                            continue
                        row = (frame ^ (distance + core)) * depth + (start - place * depth)
                        block = clip ^ offset
                        where = (ref, start - held[0], end - start)
                        found[offset].append(
                            (*where, (0, in_columns), 0, row, block * in_columns)
                        )
                        outer.append(
                            (*where, (in_columns, out_columns), 1, row, block * out_columns)
                        )
                    ref += 1
        return [*found.values(), outer]

    return arrays, pieces, both


def gather_plainly(input_weights, output_weights, both):
    arrays = []
    for weights in (input_weights, output_weights):
        columns = lax.all_gather(weights, "clip", axis=1, tiled=True)
        arrays.append(lax.all_gather(columns, "frame", axis=0, tiled=True))
    both = lax.all_to_all(both, "frame", split_axis=0, concat_axis=0, tiled=True)
    found = [[(i, 0, w.shape[0], (0, w.shape[1]), i, 0, 0)] for i, w in enumerate(arrays)]
    return arrays, lambda: found, both


def order_kernel(devices, patches, *refs):
    *sources, result_ref, grad_ref, held = refs
    me = lax.axis_index("frame")
    share = sources[0].shape[1]
    for distance, source in enumerate(sources):
        rows = pl.ds(pl.multiple_of((me ^ distance) * share, share), share)
        held[0, rows, :] = source[0]
        held[1, rows, :] = source[1]
    result_ref[0, 0] = held[0, :patches]
    grad_ref[0, 0] = held[1, :patches]


def bring_back(blocks, devices, patches):
    _, _, share, width = blocks.shape
    vmem = pl.BlockSpec(memory_space=pltpu.VMEM)
    got = [blocks[0]] + [None] * (devices - 1)
    for distance in sorted(range(1, devices), reverse=True):
        pairs = [(f, f ^ distance) for f in range(devices) if f * share < patches]
        got[distance] = lax.ppermute(blocks[distance], "frame", pairs)
    out = jax.ShapeDtypeStruct((1, 1, patches, width), blocks.dtype)
    return pl.pallas_call(
        functools.partial(order_kernel, devices, patches),
        out_shape=(out, out),
        in_specs=[vmem] * devices,
        out_specs=(vmem, vmem),
        scratch_shapes=[pltpu.VMEM((2, devices * share, width), blocks.dtype)],
        name="order",
    )(*got)


def per_device(clips, devices, tokens, counts, norm_gain, input_weights, output_weights, cotangent):
    _, slots, patches, width = tokens.shape
    share = -(-patches // devices)
    share = -(-share // SUB) * SUB
    extra = devices * share - patches

    def by_destination(source):
        padded = jnp.pad(source[0], ((0, 0), (0, extra), (0, 0)))
        return padded.reshape(slots, devices, share, width).transpose(1, 0, 2, 3)

    both = jnp.stack([by_destination(tokens), by_destination(cotangent)], axis=2)
    depth, in_columns = input_weights.shape
    fits = in_columns % 128 == 0 and output_weights.shape[1] % 128 == 0 and depth % 32 == 0
    small = clips == 4 and devices == 8 and slots == 1 and fits
    if small:
        weights, pieces, both = gather_rounds(input_weights, output_weights, both, devices)
    else:
        weights, pieces, both = gather_plainly(input_weights, output_weights, both)
    both = both.reshape(devices * slots, 2, share, width)
    back = run_block(counts, norm_gain.reshape(1, width), both, weights, pieces, small)
    if small:
        return bring_back(back, devices, patches)
    back = back.reshape(devices, slots, 2, share, width)
    back = lax.all_to_all(back, "frame", split_axis=0, concat_axis=0, tiled=True)

    def in_order(which):
        rows = back[:, :, which].transpose(1, 0, 2, 3).reshape(slots, devices * share, width)
        return rows[None, :, :patches]

    return in_order(0), in_order(1)


def solution(mesh):
    in_specs = (
        P("clip", "frame", None, None),
        P("clip"),
        P(),
        P("frame", "clip"),
        P("frame", "clip"),
        P("clip", "frame", None, None),
    )
    out_specs = (P("clip", "frame", None, None), P("clip", "frame", None, None))
    body = functools.partial(per_device, mesh.shape["clip"], mesh.shape["frame"])
    return jax.shard_map(body, mesh=mesh, in_specs=in_specs, out_specs=out_specs, check_vma=False)
```

time: 124 us -> 127 us (1.024)
  blocking collectives: 18.8 us -> 0 us
  starting transfers between devices: 38.9 us -> 48.8 us
  waiting for transfers between devices: 39.7 us -> 45.7 us
  Pallas kernels: 20.9 us -> 24.2 us
  local copies, waits for them, and re-layouts: 2.97 us -> 4.85 us
    all_to_all x1 -> x0, blocking collectives: 18.8 us -> none  [per_device(): lax.all_to_all(back, 'frame', split_axis=0, concat_axis=0, tiled=True)]
    ppermute x3 -> x10, starting transfers between devices: 12.5 us -> 24 us  [the longest x7 19.5 us: bring_back(): got[distance] = lax.ppermute(blocks[distance], 'frame', pairs)]
    ppermute x3 -> x10, waiting for transfers between devices: 9.89 us -> 15.8 us  [the longest x3 13.5 us: gather_rounds(): lax.ppermute(joined, 'clip', [(c, c ^ offset) for c in range(4)])]
    pallas_call x2 -> x4, Pallas kernels: 20.9 us -> 24.2 us  [the longest x1 18.4 us: run_block(): pl.pallas_call(functools.partial(block_kernel, pieces, xor_order, frames,...]
    squeeze x0 -> x1, local copies, waits for them, and re-layouts: none -> 2.04 us  [bring_back(): got[distance] = lax.ppermute(blocks[distance], 'frame', pairs)]
    unnamed x24 -> x38, local copies, waits for them, and re-layouts: 0.72 us -> 2.65 us
    ppermute x36 -> x27, starting transfers between devices: 21.3 us -> 20.6 us  [swap(): lax.ppermute(array, 'frame', [(f, f ^ distance) for f in range(devices)])]
    ppermute x36 -> x27, waiting for transfers between devices: 29.8 us -> 29.9 us  [swap(): lax.ppermute(array, 'frame', [(f, f ^ distance) for f in range(devices)])]
  transfers between devices with their start and end apart: 40 -> 38, of which waited for: 16 -> 11; matrix products, arithmetic and copies ran while one was open for 0% -> 1% of each run, Pallas kernels for 1% -> 1%
where the time goes in v4:
time: 127 us; the launch traced here: 126 us
  starting transfers between devices  48.8 us (38%)
  waiting for transfers between devices  45.7 us (36%)
  Pallas kernels  24.2 us (19%)
  local copies, waits for them, and re-layouts  4.85 us (4%)
  between operations  1.69 us (1%)
    ppermute x27, waiting for transfers between devices, swap(): lax.ppermute(array, 'frame', [(f, f ^ distance) for f in range(devices)])  29.9 us
    ppermute x27, starting transfers between devices, swap(): lax.ppermute(array, 'frame', [(f, f ^ distance) for f in range(devices)])  20.6 us
    ppermute x7, starting transfers between devices, bring_back(): got[distance] = lax.ppermute(blocks[distance], 'frame', pairs)  19.5 us
    pallas_call x1, Pallas kernels, run_block(): pl.pallas_call(functools.partial(block_kernel, pieces, xor_order, frames,...  18.4 us
    ppermute x3, waiting for transfers between devices, gather_rounds(): lax.ppermute(joined, 'clip', [(c, c ^ offset) for c in range(4)])  13.5 us
    ppermute x3, starting transfers between devices, gather_rounds(): lax.ppermute(joined, 'clip', [(c, c ^ offset) for c in range(4)])  4.45 us
    all_to_all x1, starting transfers between devices, gather_rounds(): lax.all_to_all(both, 'frame', split_axis=0, concat_axis=0, tiled=True)  4.26 us
    pallas_call x2, Pallas kernels, join(): pl.pallas_call(functools.partial(join_kernel, axis), out_shape=jax.ShapeD...  3.57 us
  transfers between devices with their start and end apart: 38, of which 11 were waited for; matrix products, arithmetic and copies ran while one was open for 1% of the time, Pallas kernels for 1%

profile of v4, /device:TPU:0, one launch (start us, length us, event | category | flops | bytes accessed | tf_op | source)
XLA Modules:
  0.0 126.4 jit_solution(8166769941701038478)
XLA Ops:
  0.6 1.7 %join.2.rest_0_ = bf16[128,1024]{1,0:T(8,128)(2,1)} custom-call(bf16[128,768]{1,0:T(8,128)(2,1)} %refs_0_.1, bf16[128,256]{1,0:T(8,128)(2,1)} %refs_1_.1), custom_call_target="tpu_custom_call" | custom-call | tf_op jit(solution)/shard_map/join/pallas_call | solution.py:248
  2.3 3.0 %collective-permute-start.6 = (bf16[128,1024]{1,0:T(8,128)(2,1)}, bf16[128,1024]{1,0:T(8,128)(2,1)S(1)}, u32[]{:S(2)}, u32[]{:S(2)}) collective-permute-start(bf16[128,1024]{1,0:T(8,128)(2,1)} %join.2.rest_0_), channel_id=1, source_target_pairs={{0,4},{1,5},{2,6},{3,7},{4,0},{5,1},{6,2},{7,3},{8,12},{9,13},{10,... | collective-permute-start | bytes 786440 | tf_op jit(solution)/shard_map/ppermute | solution.py:229
  5.3 1.5 %collective-permute-start.5 = (bf16[128,1024]{1,0:T(8,128)(2,1)}, bf16[128,1024]{1,0:T(8,128)(2,1)S(1)}, u32[]{:S(2)}, u32[]{:S(2)}) collective-permute-start(bf16[128,1024]{1,0:T(8,128)(2,1)} %join.2.rest_0_), channel_id=1, source_target_pairs={{0,2},{1,3},{2,0},{3,1},{4,6},{5,7},{6,4},{7,5},{8,10},{9,11},{10,... | collective-permute-start | bytes 786440 | tf_op jit(solution)/shard_map/ppermute | solution.py:229
  6.9 0.9 copy-done.4
  7.9 1.1 pad_maximum_fusion
  8.9 2.9 %collective-permute-done.6.rest_2_ = bf16[128,1024]{1,0:T(8,128)(2,1)S(1)} collective-permute-done((bf16[128,1024]{1,0:T(8,128)(2,1)}, bf16[128,1024]{1,0:T(8,128)(2,1)S(1)}, u32[]{:S(2)}, u32[]{:S(2)}) %collective-permute-start.6) | collective-permute-done | bytes 262176 | tf_op jit(solution)/shard_map/ppermute | solution.py:229
  11.8 1.5 %collective-permute-done.5.rest_1_ = bf16[128,1024]{1,0:T(8,128)(2,1)S(1)} collective-permute-done((bf16[128,1024]{1,0:T(8,128)(2,1)}, bf16[128,1024]{1,0:T(8,128)(2,1)S(1)}, u32[]{:S(2)}, u32[]{:S(2)}) %collective-permute-start.5) | collective-permute-done | bytes 262176 | tf_op jit(solution)/shard_map/ppermute | solution.py:229
  13.3 4.3 %all-to-all-start = ((bf16[8,1,2,32,1024]{4,3,2,1,0:T(8,128)(2,1)}), bf16[8,1,2,32,1024]{4,3,2,1,0:T(8,128)(2,1)}, u32[]{:S(2)}, u32[]{:S(2)}) async-start(bf16[8,1,2,32,1024]{4,3,2,1,0:T(8,128)(2,1)} %pad_maximum_fusion), calls=%async_computation | async-start | bytes 2097152 | tf_op jit(solution)/shard_map/all_to_all | solution.py:280
  17.6 1.6 %collective-permute-start.1 = (bf16[128,1024]{1,0:T(8,128)(2,1)S(1)}, bf16[128,1024]{1,0:T(8,128)(2,1)S(1)}, u32[]{:S(2)}, u32[]{:S(2)}) collective-permute-start(bf16[128,1024]{1,0:T(8,128)(2,1)S(1)} %copy-done.1), channel_id=1, source_target_pairs={{0,8},{8,0},{16,24},{24,16},{1,9},{9,1},{17,25},{25,17},{2,10},{10... | collective-permute-start | bytes 786440 | tf_op jit(solution)/shard_map/ppermute | solution.py:263
  19.2 2.6 %collective-permute-start.4 = (bf16[128,1024]{1,0:T(8,128)(2,1)S(1)}, bf16[128,1024]{1,0:T(8,128)(2,1)S(1)}, u32[]{:S(2)}, u32[]{:S(2)}) collective-permute-start(bf16[128,1024]{1,0:T(8,128)(2,1)S(1)} %copy-done.1), channel_id=1, source_target_pairs={{0,16},{8,24},{16,0},{24,8},{1,17},{9,25},{17,1},{25,9},{2,18},{10... | collective-permute-start | bytes 786440 | tf_op jit(solution)/shard_map/ppermute | solution.py:263
  21.8 0.2 collective-permute-start
  22.0 1.9 %collective-permute-start.10 = (bf16[64,1024]{1,0:T(8,128)(2,1)S(1)}, bf16[64,1024]{1,0:T(8,128)(2,1)S(1)}, u32[]{:S(2)}, u32[]{:S(2)}) collective-permute-start(bf16[64,1024]{1,0:T(8,128)(2,1)S(1)} %slice.56), channel_id=1, source_target_pairs={{0,2},{1,3},{2,0},{3,1},{4,6},{5,7},{6,4},{7,5},{8,10},{9,11},{10,... | collective-permute-start | bytes 393224 | tf_op jit(solution)/shard_map/ppermute | solution.py:229
  23.9 7.3 %collective-permute-done.1.rest_10_ = bf16[128,1024]{1,0:T(8,128)(2,1)S(1)} collective-permute-done((bf16[128,1024]{1,0:T(8,128)(2,1)S(1)}, bf16[128,1024]{1,0:T(8,128)(2,1)S(1)}, u32[]{:S(2)}, u32[]{:S(2)}) %collective-permute-start.1) | collective-permute-done | bytes 262176 | tf_op jit(solution)/shard_map/ppermute | solution.py:263
  31.2 1.6 %collective-permute-start.3 = (bf16[128,1024]{1,0:T(8,128)(2,1)S(1)}, bf16[128,1024]{1,0:T(8,128)(2,1)S(1)}, u32[]{:S(2)}, u32[]{:S(2)}) collective-permute-start(bf16[128,1024]{1,0:T(8,128)(2,1)S(1)} %collective-permute-done.1.rest_10_), channel_id=1, source_target_pairs={{0,4},{1,5},{2,6},{3,7},{4,0},{5,1},{6,2},{7,3},{8,12},{9,13},{10,... | collective-permute-start | bytes 786440 | tf_op jit(solution)/shard_map/ppermute | solution.py:229
  32.9 1.5 %collective-permute-start.2 = (bf16[128,1024]{1,0:T(8,128)(2,1)S(1)}, bf16[128,1024]{1,0:T(8,128)(2,1)S(1)}, u32[]{:S(2)}, u32[]{:S(2)}) collective-permute-start(bf16[128,1024]{1,0:T(8,128)(2,1)S(1)} %collective-permute-done.1.rest_10_), channel_id=1, source_target_pairs={{0,2},{1,3},{2,0},{3,1},{4,6},{5,7},{6,4},{7,5},{8,10},{9,11},{10,... | collective-permute-start | bytes 786440 | tf_op jit(solution)/shard_map/ppermute | solution.py:229
  34.3 6.2 %collective-permute-done.4.refs_1_ = bf16[128,1024]{1,0:T(8,128)(2,1)S(1)} collective-permute-done((bf16[128,1024]{1,0:T(8,128)(2,1)S(1)}, bf16[128,1024]{1,0:T(8,128)(2,1)S(1)}, u32[]{:S(2)}, u32[]{:S(2)}) %collective-permute-start.4) | collective-permute-done | bytes 262176 | tf_op jit(solution)/shard_map/ppermute | solution.py:263
  40.6 1.8 %collective-permute-start.12 = (bf16[64,1024]{1,0:T(8,128)(2,1)S(1)}, bf16[64,1024]{1,0:T(8,128)(2,1)S(1)}, u32[]{:S(2)}, u32[]{:S(2)}) collective-permute-start(bf16[64,1024]{1,0:T(8,128)(2,1)S(1)} %slice.57), channel_id=1, source_target_pairs={{0,4},{1,5},{2,6},{3,7},{4,0},{5,1},{6,2},{7,3},{8,12},{9,13},{10,... | collective-permute-start | bytes 393224 | tf_op jit(solution)/shard_map/ppermute | solution.py:229
  42.4 0.0 collective-permute-done.refs_0_
  42.4 0.0 collective-permute-start.7
  42.4 0.5 collective-permute-start.8
  42.9 2.6 %collective-permute-done.12.rest_4_ = bf16[64,1024]{1,0:T(8,128)(2,1)S(1)} collective-permute-done((bf16[64,1024]{1,0:T(8,128)(2,1)S(1)}, bf16[64,1024]{1,0:T(8,128)(2,1)S(1)}, u32[]{:S(2)}, u32[]{:S(2)}) %collective-permute-start.12) | collective-permute-done | bytes 131104 | tf_op jit(solution)/shard_map/ppermute | solution.py:229
  45.5 0.5 collective-permute-start.11
  46.0 0.1 collective-permute-start.13
  46.1 1.9 %join.3.rest_20_ = bf16[256,1024]{1,0:T(8,128)(2,1)} custom-call(bf16[128,1024]{1,0:T(8,128)(2,1)} %copy-done.6, bf16[128,1024]{1,0:T(8,128)(2,1)} %copy-done.5), custom_call_target="tpu_custom_call" | custom-call | tf_op jit(solution)/shard_map/join/pallas_call | solution.py:248
  48.0 0.0 collective-permute-done.13.rest_9_
  48.0 0.0 all-to-all-done
  48.0 1.9 %collective-permute-start.22 = (bf16[256,1024]{1,0:T(8,128)(2,1)}, bf16[256,1024]{1,0:T(8,128)(2,1)S(1)}, u32[]{:S(2)}, u32[]{:S(2)}) collective-permute-start(bf16[256,1024]{1,0:T(8,128)(2,1)} %join.3.rest_20_), channel_id=1, source_target_pairs={{0,4},{1,5},{2,6},{3,7},{4,0},{5,1},{6,2},{7,3},{8,12},{9,13},{10,... | collective-permute-start | bytes 1572872 | tf_op jit(solution)/shard_map/ppermute | solution.py:229
  49.9 0.2 collective-permute-start.17
  50.1 1.5 %collective-permute-start.16 = (bf16[256,1024]{1,0:T(8,128)(2,1)}, bf16[256,1024]{1,0:T(8,128)(2,1)S(1)}, u32[]{:S(2)}, u32[]{:S(2)}) collective-permute-start(bf16[256,1024]{1,0:T(8,128)(2,1)} %join.3.rest_20_), channel_id=1, source_target_pairs={{0,2},{1,3},{2,0},{3,1},{4,6},{5,7},{6,4},{7,5},{8,10},{9,11},{10,... | collective-permute-start | bytes 1572872 | tf_op jit(solution)/shard_map/ppermute | solution.py:229
  51.6 0.6 collective-permute-start.14
  52.2 0.4 collective-permute-start.15
  52.6 0.0 collective-permute-done.17.rest_15_
  52.6 0.0 collective-permute-start.18
  52.6 14.7 %collective-permute-done.14.rest_13_ = bf16[64,1024]{1,0:T(8,128)(2,1)S(1)} collective-permute-done((bf16[64,1024]{1,0:T(8,128)(2,1)S(1)}, bf16[64,1024]{1,0:T(8,128)(2,1)S(1)}, u32[]{:S(2)}, u32[]{:S(2)}) %collective-permute-start.14) | collective-permute-done | bytes 131104 | tf_op jit(solution)/shard_map/ppermute | solution.py:229
  67.3 0.5 collective-permute-start.20
  67.8 0.1 collective-permute-start.21
  67.9 0.0 collective-permute-done.18.rest_16_
  67.9 0.5 collective-permute-start.25
  68.4 0.4 collective-permute-done.19.rest_17_
  68.8 1.5 %collective-permute-start.23 = (bf16[128,1024]{1,0:T(8,128)(2,1)S(1)}, bf16[128,1024]{1,0:T(8,128)(2,1)S(1)}, u32[]{:S(2)}, u32[]{:S(2)}) collective-permute-start(bf16[128,1024]{1,0:T(8,128)(2,1)S(1)} %slice.60), channel_id=1, source_target_pairs={{0,2},{1,3},{2,0},{3,1},{4,6},{5,7},{6,4},{7,5},{8,10},{9,11},{10,... | collective-permute-start | bytes 786440 | tf_op jit(solution)/shard_map/ppermute | solution.py:229
  70.3 0.0 collective-permute-done.16.rest_21_
  70.3 0.0 copy-start.2
  70.4 0.6 collective-permute-start.24
  71.0 0.5 collective-permute-start.26
  71.5 5.7 %collective-permute-done.23.rest_23_ = bf16[128,1024]{1,0:T(8,128)(2,1)S(1)} collective-permute-done((bf16[128,1024]{1,0:T(8,128)(2,1)S(1)}, bf16[128,1024]{1,0:T(8,128)(2,1)S(1)}, u32[]{:S(2)}, u32[]{:S(2)}) %collective-permute-start.23) | collective-permute-done | bytes 262176 | tf_op jit(solution)/shard_map/ppermute | solution.py:229
  77.2 1.3 %collective-permute-done.24.rest_24_ = bf16[128,1024]{1,0:T(8,128)(2,1)S(1)} collective-permute-done((bf16[128,1024]{1,0:T(8,128)(2,1)S(1)}, bf16[128,1024]{1,0:T(8,128)(2,1)S(1)}, u32[]{:S(2)}, u32[]{:S(2)}) %collective-permute-start.24) | collective-permute-done | bytes 262176 | tf_op jit(solution)/shard_map/ppermute | solution.py:229
  78.5 0.0 collective-permute-start.29
  79.2 0.0 collective-permute-done.28.rest_28_
  79.2 0.8 collective-permute-done.29.rest_29_
  80.1 0.8 copy-done.17
  80.8 0.2 copy-done.18
  81.0 18.4 %block.1 = bf16[8,2,32,1024]{3,2,1,0:T(8,128)(2,1)} custom-call(s32[1]{0:T(128)S(6)} %copy.8.counts_ref, f32[1,1024]{1,0:T(1,128)S(1)} %bitcast.22, bf16[8,2,32,1024]{3,2,1,0:T(8,128)(2,1)} %bitcast.5.both_ref, bf16[128,1024]{1,0:T(8,128)(2,1)S(1)} %copy-done.1, bf16[128,1024]{1,0:T(8,128)(2,1)S(1)} %collective-permute-done.5.rest_1_, ...), custom_call_target="tpu_custom_call" | custom-call | flops 4294967296 | bytes 10485760 | tf_op jit(solution)/shard_map/block/pallas_call | solution.py:200
  99.5 2.0 %slice_bitcast_fusion = (bf16[2,32,1024]{2,1,0:T(8,128)(2,1)S(1)}, bf16[2,32,1024]{2,1,0:T(8,128)(2,1)S(1)}, bf16[2,32,1024]{2,1,0:T(8,128)(2,1)S(1)}, bf16[2,32...) fusion(bf16[8,2,32,1024]{3,2,1,0:T(8,128)(2,1)} %block.1), kind=kLoop, calls=%fused_computation.1 | loop fusion | bytes 2097152 | tf_op jit(solution)/shard_map/squeeze | solution.py:351
  101.5 2.2 %collective-permute-start.36 = (bf16[2,32,1024]{2,1,0:T(8,128)(2,1)S(1)}, bf16[2,32,1024]{2,1,0:T(8,128)(2,1)S(1)}, u32[]{:S(2)}, u32[]{:S(2)}) collective-permute-start(bf16[2,32,1024]{2,1,0:T(8,128)(2,1)S(1)} %get-tuple-element.40), channel_id=1, source_target_pairs={{0,7},{1,6},{2,5},{3,4},{4,3},{5,2},{6,1},{8,15},{9,14},{10,13},{1... | collective-permute-start | bytes 393224 | tf_op jit(solution)/shard_map/ppermute | solution.py:351
  103.7 4.2 %collective-permute-start.35 = (bf16[2,32,1024]{2,1,0:T(8,128)(2,1)S(1)}, bf16[2,32,1024]{2,1,0:T(8,128)(2,1)S(1)}, u32[]{:S(2)}, u32[]{:S(2)}) collective-permute-start(bf16[2,32,1024]{2,1,0:T(8,128)(2,1)S(1)} %get-tuple-element.41), channel_id=1, source_target_pairs={{0,6},{1,7},{2,4},{3,5},{4,2},{5,3},{6,0},{8,14},{9,15},{10,12},{1... | collective-permute-start | bytes 393224 | tf_op jit(solution)/shard_map/ppermute | solution.py:351
  108.0 2.1 %collective-permute-start.34 = (bf16[2,32,1024]{2,1,0:T(8,128)(2,1)S(1)}, bf16[2,32,1024]{2,1,0:T(8,128)(2,1)S(1)}, u32[]{:S(2)}, u32[]{:S(2)}) collective-permute-start(bf16[2,32,1024]{2,1,0:T(8,128)(2,1)S(1)} %get-tuple-element.42), channel_id=1, source_target_pairs={{0,5},{1,4},{2,7},{3,6},{4,1},{5,0},{6,3},{8,13},{9,12},{10,15},{1... | collective-permute-start | bytes 393224 | tf_op jit(solution)/shard_map/ppermute | solution.py:351
  110.1 2.2 %collective-permute-start.33 = (bf16[2,32,1024]{2,1,0:T(8,128)(2,1)S(1)}, bf16[2,32,1024]{2,1,0:T(8,128)(2,1)S(1)}, u32[]{:S(2)}, u32[]{:S(2)}) collective-permute-start(bf16[2,32,1024]{2,1,0:T(8,128)(2,1)S(1)} %get-tuple-element.43), channel_id=1, source_target_pairs={{0,4},{1,5},{2,6},{3,7},{4,0},{5,1},{6,2},{8,12},{9,13},{10,14},{1... | collective-permute-start | bytes 393224 | tf_op jit(solution)/shard_map/ppermute | solution.py:351
  112.4 1.9 %collective-permute-start.32 = (bf16[2,32,1024]{2,1,0:T(8,128)(2,1)S(1)}, bf16[2,32,1024]{2,1,0:T(8,128)(2,1)S(1)}, u32[]{:S(2)}, u32[]{:S(2)}) collective-permute-start(bf16[2,32,1024]{2,1,0:T(8,128)(2,1)S(1)} %get-tuple-element.44), channel_id=1, source_target_pairs={{0,3},{1,2},{2,1},{3,0},{4,7},{5,6},{6,5},{8,11},{9,10},{10,9},{11... | collective-permute-start | bytes 393224 | tf_op jit(solution)/shard_map/ppermute | solution.py:351
  114.3 4.8 %collective-permute-start.31 = (bf16[2,32,1024]{2,1,0:T(8,128)(2,1)S(1)}, bf16[2,32,1024]{2,1,0:T(8,128)(2,1)S(1)}, u32[]{:S(2)}, u32[]{:S(2)}) collective-permute-start(bf16[2,32,1024]{2,1,0:T(8,128)(2,1)S(1)} %get-tuple-element.45), channel_id=1, source_target_pairs={{0,2},{1,3},{2,0},{3,1},{4,6},{5,7},{6,4},{8,10},{9,11},{10,8},{11... | collective-permute-start | bytes 393224 | tf_op jit(solution)/shard_map/ppermute | solution.py:351
  119.2 1.9 %collective-permute-start.30 = (bf16[2,32,1024]{2,1,0:T(8,128)(2,1)S(1)}, bf16[2,32,1024]{2,1,0:T(8,128)(2,1)S(1)}, u32[]{:S(2)}, u32[]{:S(2)}) collective-permute-start(bf16[2,32,1024]{2,1,0:T(8,128)(2,1)S(1)} %get-tuple-element.46), channel_id=1, source_target_pairs={{0,1},{1,0},{2,3},{3,2},{4,5},{5,4},{6,7},{8,9},{9,8},{10,11},{11,... | collective-permute-start | bytes 393224 | tf_op jit(solution)/shard_map/ppermute | solution.py:351
  121.2 2.2 %collective-permute-done.31.refs_2_ = bf16[2,32,1024]{2,1,0:T(8,128)(2,1)S(1)} collective-permute-done((bf16[2,32,1024]{2,1,0:T(8,128)(2,1)S(1)}, bf16[2,32,1024]{2,1,0:T(8,128)(2,1)S(1)}, u32[]{:S(2)}, u32[]{:S(2)}) %collective-permute-start.31) | collective-permute-done | bytes 131104 | tf_op jit(solution)/shard_map/ppermute | solution.py:351
  123.5 0.6 copy-done.14
  124.1 0.1 copy-done.15
  124.1 2.3 %order.1 = (bf16[1,1,196,1024]{3,2,1,0:T(8,128)(2,1)}, bf16[1,1,196,1024]{3,2,1,0:T(8,128)(2,1)}) custom-call(bf16[2,32,1024]{2,1,0:T(8,128)(2,1)} %get-tuple-element.47.refs_0_, bf16[2,32,1024]{2,1,0:T(8,128)(2,1)} %copy-done.15, bf16[2,32,1024]{2,1,0:T(8,128)(2,1)} %copy-done.14, bf16[2,32,1024]{2,1,0:T(8,128)(2,1)} %copy-done.13, ...), custom_call_target="tpu_custom_call" | custom-call | tf_op jit(solution)/shard_map/order/pallas_call | solution.py:353
  (64 shorter events, 0.3 us)
Async XLA Ops:
  0.6 6.2 %copy-start.3 = (bf16[1,1,196,1024]{3,2,1,0:T(8,128)(2,1)S(1)}, bf16[1,1,196,1024]{3,2,1,0:T(8,128)(2,1)}, u32[]{:S(2)}) copy-start(bf16[1,1,196,1024]{3,2,1,0:T(8,128)(2,1)} %param.6) | copy-start | bytes 1204228
  2.3 9.5 %collective-permute-start.6 = (bf16[128,1024]{1,0:T(8,128)(2,1)}, bf16[128,1024]{1,0:T(8,128)(2,1)S(1)}, u32[]{:S(2)}, u32[]{:S(2)}) collective-permute-start(bf16[128,1024]{1,0:T(8,128)(2,1)} %join.2.rest_0_), channel_id=1, source_target_pairs={{0,4},{1,5},{2,6},{3,7},{4,0},{5,1},{6,2},{7,3},{8,12},{9,13},{10,... | collective-permute-start | bytes 786440 | tf_op jit(solution)/shard_map/ppermute | solution.py:229
  5.3 8.0 %collective-permute-start.5 = (bf16[128,1024]{1,0:T(8,128)(2,1)}, bf16[128,1024]{1,0:T(8,128)(2,1)S(1)}, u32[]{:S(2)}, u32[]{:S(2)}) collective-permute-start(bf16[128,1024]{1,0:T(8,128)(2,1)} %join.2.rest_0_), channel_id=1, source_target_pairs={{0,2},{1,3},{2,0},{3,1},{4,6},{5,7},{6,4},{7,5},{8,10},{9,11},{10,... | collective-permute-start | bytes 786440 | tf_op jit(solution)/shard_map/ppermute | solution.py:229
  6.8 1.0 copy-start.4
  8.9 8.6 %copy-start.1 = (bf16[128,1024]{1,0:T(8,128)(2,1)S(1)}, bf16[128,1024]{1,0:T(8,128)(2,1)}, u32[]{:S(2)}) copy-start(bf16[128,1024]{1,0:T(8,128)(2,1)} %join.2.rest_0_) | copy-start | bytes 786436
  13.3 34.7 %all-to-all-start = ((bf16[8,1,2,32,1024]{4,3,2,1,0:T(8,128)(2,1)}), bf16[8,1,2,32,1024]{4,3,2,1,0:T(8,128)(2,1)}, u32[]{:S(2)}, u32[]{:S(2)}) async-start(bf16[8,1,2,32,1024]{4,3,2,1,0:T(8,128)(2,1)} %pad_maximum_fusion), calls=%async_computation | async-start | bytes 2097152 | tf_op jit(solution)/shard_map/all_to_all | solution.py:280
  17.6 13.7 %collective-permute-start.1 = (bf16[128,1024]{1,0:T(8,128)(2,1)S(1)}, bf16[128,1024]{1,0:T(8,128)(2,1)S(1)}, u32[]{:S(2)}, u32[]{:S(2)}) collective-permute-start(bf16[128,1024]{1,0:T(8,128)(2,1)S(1)} %copy-done.1), channel_id=1, source_target_pairs={{0,8},{8,0},{16,24},{24,16},{1,9},{9,1},{17,25},{25,17},{2,10},{10... | collective-permute-start | bytes 786440 | tf_op jit(solution)/shard_map/ppermute | solution.py:263
  19.2 21.3 %collective-permute-start.4 = (bf16[128,1024]{1,0:T(8,128)(2,1)S(1)}, bf16[128,1024]{1,0:T(8,128)(2,1)S(1)}, u32[]{:S(2)}, u32[]{:S(2)}) collective-permute-start(bf16[128,1024]{1,0:T(8,128)(2,1)S(1)} %copy-done.1), channel_id=1, source_target_pairs={{0,16},{8,24},{16,0},{24,8},{1,17},{9,25},{17,1},{25,9},{2,18},{10... | collective-permute-start | bytes 786440 | tf_op jit(solution)/shard_map/ppermute | solution.py:263
  21.8 20.6 %collective-permute-start = (bf16[128,1024]{1,0:T(8,128)(2,1)S(1)}, bf16[128,1024]{1,0:T(8,128)(2,1)S(1)}, u32[]{:S(2)}, u32[]{:S(2)}) collective-permute-start(bf16[128,1024]{1,0:T(8,128)(2,1)S(1)} %copy-done.1), channel_id=1, source_target_pairs={{0,24},{8,16},{16,8},{24,0},{1,25},{9,17},{17,9},{25,1},{2,26},{10... | collective-permute-start | bytes 786440 | tf_op jit(solution)/shard_map/ppermute | solution.py:263
  22.0 20.4 %collective-permute-start.10 = (bf16[64,1024]{1,0:T(8,128)(2,1)S(1)}, bf16[64,1024]{1,0:T(8,128)(2,1)S(1)}, u32[]{:S(2)}, u32[]{:S(2)}) collective-permute-start(bf16[64,1024]{1,0:T(8,128)(2,1)S(1)} %slice.56), channel_id=1, source_target_pairs={{0,2},{1,3},{2,0},{3,1},{4,6},{5,7},{6,4},{7,5},{8,10},{9,11},{10,... | collective-permute-start | bytes 393224 | tf_op jit(solution)/shard_map/ppermute | solution.py:229
  31.2 14.3 %collective-permute-start.3 = (bf16[128,1024]{1,0:T(8,128)(2,1)S(1)}, bf16[128,1024]{1,0:T(8,128)(2,1)S(1)}, u32[]{:S(2)}, u32[]{:S(2)}) collective-permute-start(bf16[128,1024]{1,0:T(8,128)(2,1)S(1)} %collective-permute-done.1.rest_10_), channel_id=1, source_target_pairs={{0,4},{1,5},{2,6},{3,7},{4,0},{5,1},{6,2},{7,3},{8,12},{9,13},{10,... | collective-permute-start | bytes 786440 | tf_op jit(solution)/shard_map/ppermute | solution.py:229
  32.9 13.2 %collective-permute-start.2 = (bf16[128,1024]{1,0:T(8,128)(2,1)S(1)}, bf16[128,1024]{1,0:T(8,128)(2,1)S(1)}, u32[]{:S(2)}, u32[]{:S(2)}) collective-permute-start(bf16[128,1024]{1,0:T(8,128)(2,1)S(1)} %collective-permute-done.1.rest_10_), channel_id=1, source_target_pairs={{0,2},{1,3},{2,0},{3,1},{4,6},{5,7},{6,4},{7,5},{8,10},{9,11},{10,... | collective-permute-start | bytes 786440 | tf_op jit(solution)/shard_map/ppermute | solution.py:229
  40.6 5.6 %copy-start.5 = (bf16[128,1024]{1,0:T(8,128)(2,1)}, bf16[128,1024]{1,0:T(8,128)(2,1)S(1)}, u32[]{:S(2)}) copy-start(bf16[128,1024]{1,0:T(8,128)(2,1)S(1)} %collective-permute-done.4.refs_1_) | copy-start | bytes 786436
  40.6 5.0 %collective-permute-start.12 = (bf16[64,1024]{1,0:T(8,128)(2,1)S(1)}, bf16[64,1024]{1,0:T(8,128)(2,1)S(1)}, u32[]{:S(2)}, u32[]{:S(2)}) collective-permute-start(bf16[64,1024]{1,0:T(8,128)(2,1)S(1)} %slice.57), channel_id=1, source_target_pairs={{0,4},{1,5},{2,6},{3,7},{4,0},{5,1},{6,2},{7,3},{8,12},{9,13},{10,... | collective-permute-start | bytes 393224 | tf_op jit(solution)/shard_map/ppermute | solution.py:229
  42.4 3.7 %copy-start.6 = (bf16[128,1024]{1,0:T(8,128)(2,1)}, bf16[128,1024]{1,0:T(8,128)(2,1)S(1)}, u32[]{:S(2)}) copy-start(bf16[128,1024]{1,0:T(8,128)(2,1)S(1)} %collective-permute-done.refs_0_) | copy-start | bytes 786436
  42.4 5.6 %collective-permute-start.7 = (bf16[128,1024]{1,0:T(8,128)(2,1)S(1)}, bf16[128,1024]{1,0:T(8,128)(2,1)S(1)}, u32[]{:S(2)}, u32[]{:S(2)}) collective-permute-start(bf16[128,1024]{1,0:T(8,128)(2,1)S(1)} %copy-done.1), channel_id=1, source_target_pairs={{0,1},{1,0},{2,3},{3,2},{4,5},{5,4},{6,7},{7,6},{8,9},{9,8},{10,11... | collective-permute-start | bytes 786440 | tf_op jit(solution)/shard_map/ppermute | solution.py:229
  42.4 5.6 %collective-permute-start.8 = (bf16[128,1024]{1,0:T(8,128)(2,1)S(1)}, bf16[128,1024]{1,0:T(8,128)(2,1)S(1)}, u32[]{:S(2)}, u32[]{:S(2)}) collective-permute-start(bf16[128,1024]{1,0:T(8,128)(2,1)S(1)} %collective-permute-done.5.rest_1_), channel_id=1, source_target_pairs={{0,1},{1,0},{2,3},{3,2},{4,5},{5,4},{6,7},{7,6},{8,9},{9,8},{10,11... | collective-permute-start | bytes 786440 | tf_op jit(solution)/shard_map/ppermute | solution.py:229
  45.5 2.5 %collective-permute-start.9 = (bf16[128,1024]{1,0:T(8,128)(2,1)S(1)}, bf16[128,1024]{1,0:T(8,128)(2,1)S(1)}, u32[]{:S(2)}, u32[]{:S(2)}) collective-permute-start(bf16[128,1024]{1,0:T(8,128)(2,1)S(1)} %collective-permute-done.6.rest_2_), channel_id=1, source_target_pairs={{0,1},{1,0},{2,3},{3,2},{4,5},{5,4},{6,7},{7,6},{8,9},{9,8},{10,11... | collective-permute-start | bytes 786440 | tf_op jit(solution)/shard_map/ppermute | solution.py:229
  45.5 2.5 %collective-permute-start.11 = (bf16[64,1024]{1,0:T(8,128)(2,1)S(1)}, bf16[64,1024]{1,0:T(8,128)(2,1)S(1)}, u32[]{:S(2)}, u32[]{:S(2)}) collective-permute-start(bf16[64,1024]{1,0:T(8,128)(2,1)S(1)} %collective-permute-done.10.rest_3_), channel_id=1, source_target_pairs={{0,1},{1,0},{2,3},{3,2},{4,5},{5,4},{6,7},{7,6},{8,9},{9,8},{10,11... | collective-permute-start | bytes 393224 | tf_op jit(solution)/shard_map/ppermute | solution.py:229
  46.0 2.0 %collective-permute-start.13 = (bf16[64,1024]{1,0:T(8,128)(2,1)S(1)}, bf16[64,1024]{1,0:T(8,128)(2,1)S(1)}, u32[]{:S(2)}, u32[]{:S(2)}) collective-permute-start(bf16[64,1024]{1,0:T(8,128)(2,1)S(1)} %collective-permute-done.12.rest_4_), channel_id=1, source_target_pairs={{0,1},{1,0},{2,3},{3,2},{4,5},{5,4},{6,7},{7,6},{8,9},{9,8},{10,11... | collective-permute-start | bytes 393224 | tf_op jit(solution)/shard_map/ppermute | solution.py:229
  48.0 19.9 %copy-start = (bf16[256,1024]{1,0:T(8,128)(2,1)S(1)}, bf16[256,1024]{1,0:T(8,128)(2,1)}, u32[]{:S(2)}) copy-start(bf16[256,1024]{1,0:T(8,128)(2,1)} %join.3.rest_20_) | copy-start | bytes 1572868
  48.0 19.8 %collective-permute-start.22 = (bf16[256,1024]{1,0:T(8,128)(2,1)}, bf16[256,1024]{1,0:T(8,128)(2,1)S(1)}, u32[]{:S(2)}, u32[]{:S(2)}) collective-permute-start(bf16[256,1024]{1,0:T(8,128)(2,1)} %join.3.rest_20_), channel_id=1, source_target_pairs={{0,4},{1,5},{2,6},{3,7},{4,0},{5,1},{6,2},{7,3},{8,12},{9,13},{10,... | collective-permute-start | bytes 1572872 | tf_op jit(solution)/shard_map/ppermute | solution.py:229
  49.9 2.7 %collective-permute-start.17 = (bf16[128,1024]{1,0:T(8,128)(2,1)S(1)}, bf16[128,1024]{1,0:T(8,128)(2,1)S(1)}, u32[]{:S(2)}, u32[]{:S(2)}) collective-permute-start(bf16[128,1024]{1,0:T(8,128)(2,1)S(1)} %collective-permute-done.1.rest_10_), channel_id=1, source_target_pairs={{0,1},{1,0},{2,3},{3,2},{4,5},{5,4},{6,7},{7,6},{8,9},{9,8},{10,11... | collective-permute-start | bytes 786440 | tf_op jit(solution)/shard_map/ppermute | solution.py:229
  50.1 20.2 %collective-permute-start.16 = (bf16[256,1024]{1,0:T(8,128)(2,1)}, bf16[256,1024]{1,0:T(8,128)(2,1)S(1)}, u32[]{:S(2)}, u32[]{:S(2)}) collective-permute-start(bf16[256,1024]{1,0:T(8,128)(2,1)} %join.3.rest_20_), channel_id=1, source_target_pairs={{0,2},{1,3},{2,0},{3,1},{4,6},{5,7},{6,4},{7,5},{8,10},{9,11},{10,... | collective-permute-start | bytes 1572872 | tf_op jit(solution)/shard_map/ppermute | solution.py:229
  51.6 15.7 %collective-permute-start.14 = (bf16[64,1024]{1,0:T(8,128)(2,1)S(1)}, bf16[64,1024]{1,0:T(8,128)(2,1)S(1)}, u32[]{:S(2)}, u32[]{:S(2)}) collective-permute-start(bf16[64,1024]{1,0:T(8,128)(2,1)S(1)} %slice.58), channel_id=1, source_target_pairs={{0,2},{1,3},{2,0},{3,1},{4,6},{5,7},{6,4},{7,5},{8,10},{9,11},{10,... | collective-permute-start | bytes 393224 | tf_op jit(solution)/shard_map/ppermute | solution.py:229
  52.2 15.1 %collective-permute-start.15 = (bf16[64,1024]{1,0:T(8,128)(2,1)S(1)}, bf16[64,1024]{1,0:T(8,128)(2,1)S(1)}, u32[]{:S(2)}, u32[]{:S(2)}) collective-permute-start(bf16[64,1024]{1,0:T(8,128)(2,1)S(1)} %slice.59), channel_id=1, source_target_pairs={{0,4},{1,5},{2,6},{3,7},{4,0},{5,1},{6,2},{7,3},{8,12},{9,13},{10,... | collective-permute-start | bytes 393224 | tf_op jit(solution)/shard_map/ppermute | solution.py:229
  52.6 15.3 %collective-permute-start.18 = (bf16[128,1024]{1,0:T(8,128)(2,1)S(1)}, bf16[128,1024]{1,0:T(8,128)(2,1)S(1)}, u32[]{:S(2)}, u32[]{:S(2)}) collective-permute-start(bf16[128,1024]{1,0:T(8,128)(2,1)S(1)} %collective-permute-done.2.rest_11_), channel_id=1, source_target_pairs={{0,1},{1,0},{2,3},{3,2},{4,5},{5,4},{6,7},{7,6},{8,9},{9,8},{10,11... | collective-permute-start | bytes 786440 | tf_op jit(solution)/shard_map/ppermute | solution.py:229
  67.3 1.5 %collective-permute-start.19 = (bf16[128,1024]{1,0:T(8,128)(2,1)S(1)}, bf16[128,1024]{1,0:T(8,128)(2,1)S(1)}, u32[]{:S(2)}, u32[]{:S(2)}) collective-permute-start(bf16[128,1024]{1,0:T(8,128)(2,1)S(1)} %collective-permute-done.3.rest_12_), channel_id=1, source_target_pairs={{0,1},{1,0},{2,3},{3,2},{4,5},{5,4},{6,7},{7,6},{8,9},{9,8},{10,11... | collective-permute-start | bytes 786440 | tf_op jit(solution)/shard_map/ppermute | solution.py:229
  67.3 3.0 %collective-permute-start.20 = (bf16[64,1024]{1,0:T(8,128)(2,1)S(1)}, bf16[64,1024]{1,0:T(8,128)(2,1)S(1)}, u32[]{:S(2)}, u32[]{:S(2)}) collective-permute-start(bf16[64,1024]{1,0:T(8,128)(2,1)S(1)} %collective-permute-done.14.rest_13_), channel_id=1, source_target_pairs={{0,1},{1,0},{2,3},{3,2},{4,5},{5,4},{6,7},{7,6},{8,9},{9,8},{10,11... | collective-permute-start | bytes 393224 | tf_op jit(solution)/shard_map/ppermute | solution.py:229
  67.8 3.2 %copy-start.7 = (bf16[256,1024]{1,0:T(8,128)(2,1)}, bf16[256,1024]{1,0:T(8,128)(2,1)S(1)}, u32[]{:S(2)}) copy-start(bf16[256,1024]{1,0:T(8,128)(2,1)S(1)} %collective-permute-done.22.rest_22_) | copy-start | bytes 1572868
  67.8 2.5 %collective-permute-start.21 = (bf16[64,1024]{1,0:T(8,128)(2,1)S(1)}, bf16[64,1024]{1,0:T(8,128)(2,1)S(1)}, u32[]{:S(2)}, u32[]{:S(2)}) collective-permute-start(bf16[64,1024]{1,0:T(8,128)(2,1)S(1)} %collective-permute-done.15.rest_14_), channel_id=1, source_target_pairs={{0,1},{1,0},{2,3},{3,2},{4,5},{5,4},{6,7},{7,6},{8,9},{9,8},{10,11... | collective-permute-start | bytes 393224 | tf_op jit(solution)/shard_map/ppermute | solution.py:229
  67.9 11.2 %collective-permute-start.25 = (bf16[256,1024]{1,0:T(8,128)(2,1)S(1)}, bf16[256,1024]{1,0:T(8,128)(2,1)S(1)}, u32[]{:S(2)}, u32[]{:S(2)}) collective-permute-start(bf16[256,1024]{1,0:T(8,128)(2,1)S(1)} %copy-done), channel_id=1, source_target_pairs={{0,1},{1,0},{2,3},{3,2},{4,5},{5,4},{6,7},{7,6},{8,9},{9,8},{10,11... | collective-permute-start | bytes 1572872 | tf_op jit(solution)/shard_map/ppermute | solution.py:229
  68.8 8.3 %collective-permute-start.23 = (bf16[128,1024]{1,0:T(8,128)(2,1)S(1)}, bf16[128,1024]{1,0:T(8,128)(2,1)S(1)}, u32[]{:S(2)}, u32[]{:S(2)}) collective-permute-start(bf16[128,1024]{1,0:T(8,128)(2,1)S(1)} %slice.60), channel_id=1, source_target_pairs={{0,2},{1,3},{2,0},{3,1},{4,6},{5,7},{6,4},{7,5},{8,10},{9,11},{10,... | collective-permute-start | bytes 786440 | tf_op jit(solution)/shard_map/ppermute | solution.py:229
  70.3 9.7 %copy-start.8 = (bf16[256,1024]{1,0:T(8,128)(2,1)}, bf16[256,1024]{1,0:T(8,128)(2,1)S(1)}, u32[]{:S(2)}) copy-start(bf16[256,1024]{1,0:T(8,128)(2,1)S(1)} %collective-permute-done.16.rest_21_) | copy-start | bytes 1572868
  70.3 10.7 %copy-start.2 = (f32[1024]{0:T(1024)S(1)}, f32[1024]{0:T(1024)}, u32[]{:S(2)}) copy-start(f32[1024]{0:T(1024)} %param.8) | copy-start | bytes 12292
  70.4 8.1 %collective-permute-start.24 = (bf16[128,1024]{1,0:T(8,128)(2,1)S(1)}, bf16[128,1024]{1,0:T(8,128)(2,1)S(1)}, u32[]{:S(2)}, u32[]{:S(2)}) collective-permute-start(bf16[128,1024]{1,0:T(8,128)(2,1)S(1)} %slice.47), channel_id=1, source_target_pairs={{0,4},{1,5},{2,6},{3,7},{4,0},{5,1},{6,2},{7,3},{8,12},{9,13},{10,... | collective-permute-start | bytes 786440 | tf_op jit(solution)/shard_map/ppermute | solution.py:229
  71.0 9.1 %collective-permute-start.27 = (bf16[256,1024]{1,0:T(8,128)(2,1)S(1)}, bf16[256,1024]{1,0:T(8,128)(2,1)S(1)}, u32[]{:S(2)}, u32[]{:S(2)}) collective-permute-start(bf16[256,1024]{1,0:T(8,128)(2,1)S(1)} %collective-permute-done.22.rest_22_), channel_id=1, source_target_pairs={{0,1},{1,0},{2,3},{3,2},{4,5},{5,4},{6,7},{7,6},{8,9},{9,8},{10,11... | collective-permute-start | bytes 1572872 | tf_op jit(solution)/shard_map/ppermute | solution.py:229
  71.0 9.1 %collective-permute-start.26 = (bf16[256,1024]{1,0:T(8,128)(2,1)S(1)}, bf16[256,1024]{1,0:T(8,128)(2,1)S(1)}, u32[]{:S(2)}, u32[]{:S(2)}) collective-permute-start(bf16[256,1024]{1,0:T(8,128)(2,1)S(1)} %collective-permute-done.16.rest_21_), channel_id=1, source_target_pairs={{0,1},{1,0},{2,3},{3,2},{4,5},{5,4},{6,7},{7,6},{8,9},{9,8},{10,11... | collective-permute-start | bytes 1572872 | tf_op jit(solution)/shard_map/ppermute | solution.py:229
  77.2 2.0 %collective-permute-start.28 = (bf16[128,1024]{1,0:T(8,128)(2,1)S(1)}, bf16[128,1024]{1,0:T(8,128)(2,1)S(1)}, u32[]{:S(2)}, u32[]{:S(2)}) collective-permute-start(bf16[128,1024]{1,0:T(8,128)(2,1)S(1)} %collective-permute-done.23.rest_23_), channel_id=1, source_target_pairs={{0,1},{1,0},{2,3},{3,2},{4,5},{5,4},{6,7},{7,6},{8,9},{9,8},{10,11... | collective-permute-start | bytes 786440 | tf_op jit(solution)/shard_map/ppermute | solution.py:229
  78.5 1.5 %collective-permute-start.29 = (bf16[128,1024]{1,0:T(8,128)(2,1)S(1)}, bf16[128,1024]{1,0:T(8,128)(2,1)S(1)}, u32[]{:S(2)}, u32[]{:S(2)}) collective-permute-start(bf16[128,1024]{1,0:T(8,128)(2,1)S(1)} %collective-permute-done.24.rest_24_), channel_id=1, source_target_pairs={{0,1},{1,0},{2,3},{3,2},{4,5},{5,4},{6,7},{7,6},{8,9},{9,8},{10,11... | collective-permute-start | bytes 786440 | tf_op jit(solution)/shard_map/ppermute | solution.py:229
  79.2 0.9 copy-start.16
  80.0 0.8 copy-start.17
  80.0 1.0 copy-start.18
  101.5 12.8 %collective-permute-start.36 = (bf16[2,32,1024]{2,1,0:T(8,128)(2,1)S(1)}, bf16[2,32,1024]{2,1,0:T(8,128)(2,1)S(1)}, u32[]{:S(2)}, u32[]{:S(2)}) collective-permute-start(bf16[2,32,1024]{2,1,0:T(8,128)(2,1)S(1)} %get-tuple-element.40), channel_id=1, source_target_pairs={{0,7},{1,6},{2,5},{3,4},{4,3},{5,2},{6,1},{8,15},{9,14},{10,13},{1... | collective-permute-start | bytes 393224 | tf_op jit(solution)/shard_map/ppermute | solution.py:351
  103.7 15.4 %collective-permute-start.35 = (bf16[2,32,1024]{2,1,0:T(8,128)(2,1)S(1)}, bf16[2,32,1024]{2,1,0:T(8,128)(2,1)S(1)}, u32[]{:S(2)}, u32[]{:S(2)}) collective-permute-start(bf16[2,32,1024]{2,1,0:T(8,128)(2,1)S(1)} %get-tuple-element.41), channel_id=1, source_target_pairs={{0,6},{1,7},{2,4},{3,5},{4,2},{5,3},{6,0},{8,14},{9,15},{10,12},{1... | collective-permute-start | bytes 393224 | tf_op jit(solution)/shard_map/ppermute | solution.py:351
  108.0 13.1 %collective-permute-start.34 = (bf16[2,32,1024]{2,1,0:T(8,128)(2,1)S(1)}, bf16[2,32,1024]{2,1,0:T(8,128)(2,1)S(1)}, u32[]{:S(2)}, u32[]{:S(2)}) collective-permute-start(bf16[2,32,1024]{2,1,0:T(8,128)(2,1)S(1)} %get-tuple-element.42), channel_id=1, source_target_pairs={{0,5},{1,4},{2,7},{3,6},{4,1},{5,0},{6,3},{8,13},{9,12},{10,15},{1... | collective-permute-start | bytes 393224 | tf_op jit(solution)/shard_map/ppermute | solution.py:351
  110.1 11.0 %collective-permute-start.33 = (bf16[2,32,1024]{2,1,0:T(8,128)(2,1)S(1)}, bf16[2,32,1024]{2,1,0:T(8,128)(2,1)S(1)}, u32[]{:S(2)}, u32[]{:S(2)}) collective-permute-start(bf16[2,32,1024]{2,1,0:T(8,128)(2,1)S(1)} %get-tuple-element.43), channel_id=1, source_target_pairs={{0,4},{1,5},{2,6},{3,7},{4,0},{5,1},{6,2},{8,12},{9,13},{10,14},{1... | collective-permute-start | bytes 393224 | tf_op jit(solution)/shard_map/ppermute | solution.py:351
  112.4 8.8 %collective-permute-start.32 = (bf16[2,32,1024]{2,1,0:T(8,128)(2,1)S(1)}, bf16[2,32,1024]{2,1,0:T(8,128)(2,1)S(1)}, u32[]{:S(2)}, u32[]{:S(2)}) collective-permute-start(bf16[2,32,1024]{2,1,0:T(8,128)(2,1)S(1)} %get-tuple-element.44), channel_id=1, source_target_pairs={{0,3},{1,2},{2,1},{3,0},{4,7},{5,6},{6,5},{8,11},{9,10},{10,9},{11... | collective-permute-start | bytes 393224 | tf_op jit(solution)/shard_map/ppermute | solution.py:351
  114.3 9.1 %copy-start.9 = (bf16[2,32,1024]{2,1,0:T(8,128)(2,1)}, bf16[2,32,1024]{2,1,0:T(8,128)(2,1)S(1)}, u32[]{:S(2)}) copy-start(bf16[2,32,1024]{2,1,0:T(8,128)(2,1)S(1)} %collective-permute-done.36.refs_7_) | copy-start | bytes 393220
  114.3 9.1 %collective-permute-start.31 = (bf16[2,32,1024]{2,1,0:T(8,128)(2,1)S(1)}, bf16[2,32,1024]{2,1,0:T(8,128)(2,1)S(1)}, u32[]{:S(2)}, u32[]{:S(2)}) collective-permute-start(bf16[2,32,1024]{2,1,0:T(8,128)(2,1)S(1)} %get-tuple-element.45), channel_id=1, source_target_pairs={{0,2},{1,3},{2,0},{3,1},{4,6},{5,7},{6,4},{8,10},{9,11},{10,8},{11... | collective-permute-start | bytes 393224 | tf_op jit(solution)/shard_map/ppermute | solution.py:351
  119.2 4.3 %copy-start.10 = (bf16[2,32,1024]{2,1,0:T(8,128)(2,1)}, bf16[2,32,1024]{2,1,0:T(8,128)(2,1)S(1)}, u32[]{:S(2)}) copy-start(bf16[2,32,1024]{2,1,0:T(8,128)(2,1)S(1)} %collective-permute-done.35.refs_6_) | copy-start | bytes 393220
  119.2 4.2 %collective-permute-start.30 = (bf16[2,32,1024]{2,1,0:T(8,128)(2,1)S(1)}, bf16[2,32,1024]{2,1,0:T(8,128)(2,1)S(1)}, u32[]{:S(2)}, u32[]{:S(2)}) collective-permute-start(bf16[2,32,1024]{2,1,0:T(8,128)(2,1)S(1)} %get-tuple-element.46), channel_id=1, source_target_pairs={{0,1},{1,0},{2,3},{3,2},{4,5},{5,4},{6,7},{8,9},{9,8},{10,11},{11,... | collective-permute-start | bytes 393224 | tf_op jit(solution)/shard_map/ppermute | solution.py:351
  121.1 2.3 %copy-start.11 = (bf16[2,32,1024]{2,1,0:T(8,128)(2,1)}, bf16[2,32,1024]{2,1,0:T(8,128)(2,1)S(1)}, u32[]{:S(2)}) copy-start(bf16[2,32,1024]{2,1,0:T(8,128)(2,1)S(1)} %collective-permute-done.34.refs_5_) | copy-start | bytes 393220
  121.1 2.3 %copy-start.12 = (bf16[2,32,1024]{2,1,0:T(8,128)(2,1)}, bf16[2,32,1024]{2,1,0:T(8,128)(2,1)S(1)}, u32[]{:S(2)}) copy-start(bf16[2,32,1024]{2,1,0:T(8,128)(2,1)S(1)} %collective-permute-done.33.refs_4_) | copy-start | bytes 393220
  121.2 2.3 %copy-start.13 = (bf16[2,32,1024]{2,1,0:T(8,128)(2,1)}, bf16[2,32,1024]{2,1,0:T(8,128)(2,1)S(1)}, u32[]{:S(2)}) copy-start(bf16[2,32,1024]{2,1,0:T(8,128)(2,1)S(1)} %collective-permute-done.32.refs_3_) | copy-start | bytes 393220
  123.4 0.7 copy-start.14
  123.4 0.7 copy-start.15

commit v5 on v1

v5 whole, which is shorter than its diff:
```python
import functools
import math

import jax
import jax.numpy as jnp
from jax import lax
from jax.experimental import pallas as pl
from jax.experimental.pallas import tpu as pltpu
from jax.sharding import PartitionSpec as P

DH = 64
PAIR = 2 * DH
SUB = 16
EPSILON = 1e-06
NEGATIVE = -1e30
NN = (((1,), (0,)), ((), ()))
NT = (((1,), (1,)), ((), ()))
TN = (((0,), (0,)), ((), ()))
VMEM_LIMIT = 48 * 1024 * 1024


def dot(a, b, dims):
    return lax.dot_general(a, b, dims, preferred_element_type=jnp.float32)


def fetch(parts, refs, target, sem):
    copies = []
    for ref, index, first, depth, lanes, row, column in parts:
        source = refs[ref] if index is None else refs[ref].at[index]
        copies.append(
            pltpu.make_async_copy(
                source.at[pl.ds(first, depth), pl.ds(*lanes)],
                target.at[
                    pl.ds(pl.multiple_of(row, 16), depth),
                    pl.ds(pl.multiple_of(column, 128), lanes[1]),
                ],
                sem,
            )
        )
    for copy in copies:
        copy.start()
    return copies


def wait(copies):
    for copy in copies:
        copy.wait()


def load_rows(ref, which, group):
    frames, _, _, width = ref.shape
    return ref[:, which, group * SUB : (group + 1) * SUB, :].reshape(frames * SUB, width)


def front_kernel(plan, both_ref, gain_ref, *rest):
    weight_refs = rest[:-5]
    normed_ref, stats_ref, proj_ref, w_front, sems = rest[-5:]
    copies = fetch(plan["front"](), weight_refs, w_front, sems.at[0])
    frames, _, patches, _ = both_ref.shape
    rows = frames * SUB
    for group in range(patches // SUB):
        here = pl.ds(group * rows, rows)
        wide = load_rows(both_ref, 0, group).astype(jnp.float32)
        average = jnp.mean(wide, axis=-1, keepdims=True)
        centred = wide - average
        variance = jnp.mean(centred * centred, axis=-1, keepdims=True)
        scale = lax.rsqrt(variance + EPSILON)
        normed_ref[here, :] = (centred * scale * gain_ref[...]).astype(jnp.bfloat16)
        stats_ref[here, 0:1] = average
        stats_ref[here, 1:2] = scale
    wait(copies)
    columns = w_front.shape[1]
    step = math.gcd(columns, 512)

    @pl.loop(0, columns // step)
    def _(j):
        here = pl.ds(pl.multiple_of(j * step, step), step)
        proj_ref[:, here] = dot(normed_ref[...], w_front[:, here], NN).astype(jnp.bfloat16)


def main_kernel(plan, counts_ref, gain_ref, both_ref, normed_ref, stats_ref, front_ref, *rest):
    weight_refs = rest[:-14]
    out_ref, w_in, w_out, grads, proj, ga, att, gproj, gnorm, bias, scores, gprobs, low, sems = rest[-14:]
    frames, _, patches, width = both_ref.shape
    groups = patches // SUB
    rows = frames * SUB
    count = counts_ref[0]

    place = [
        pltpu.make_async_copy(
            front_ref.at[:, pl.ds(start, size)], proj.at[:, pl.ds(target, size)], sems.at[3]
        )
        for start, target, size in plan["placed"]
    ]
    for copy in place:
        copy.start()
    late = fetch(plan["late"](), weight_refs, w_in, sems.at[0])
    outer = fetch(plan["outer"](), weight_refs, w_out, sems.at[1])
    again = fetch(plan["again"](), weight_refs, w_in, sems.at[2])

    live = (lax.broadcasted_iota(jnp.int32, (rows, 1), 0) // SUB < count).astype(jnp.float32)
    for group in range(groups):
        here = pl.ds(group * rows, rows)
        grads[here, :] = (load_rows(both_ref, 1, group).astype(jnp.float32) * live).astype(
            jnp.bfloat16
        )
    key = lax.broadcasted_iota(jnp.int32, (rows, 2 * rows), 0)
    query = lax.broadcasted_iota(jnp.int32, (rows, 2 * rows), 1)
    bias[...] = jnp.where((query % SUB == key % SUB) & (key // SUB < count), 0.0, NEGATIVE)
    lane = lax.broadcasted_iota(jnp.int32, (1, PAIR), 1)
    low_lanes = (lane < DH).astype(jnp.bfloat16)
    high_lanes = (lane >= DH).astype(jnp.bfloat16)

    wait(late)
    for start, size in plan["missing"]:
        proj[:, start : start + size] = dot(
            normed_ref[...], w_in[:, start : start + size], NN
        ).astype(jnp.bfloat16)

    wait(outer)
    step = min(width, 256)

    @pl.loop(0, width // step)
    def _(j):
        columns = pl.ds(pl.multiple_of(j * step, step), step)
        ga[:, columns] = dot(grads[...], w_out[columns, :], NT).astype(jnp.bfloat16)

    wait(place)

    def apart(block):
        return jnp.concatenate([block * low_lanes, block * high_lanes], axis=0)

    def stacked(block):
        return jnp.concatenate([block[:, :rows], block[:, rows:]], axis=0)

    def lanes(part, pair):
        return pl.ds(pl.multiple_of(part * width + pair * PAIR, PAIR), PAIR)

    chunk = scores.shape[0]
    unroll = min(chunk, 4)

    def each(body):
        @pl.loop(0, chunk // unroll)
        def _(i):
            for inner in range(unroll):
                body(i * unroll + inner)

    for group in range(groups):
        here = pl.ds(group * rows, rows)

        @pl.loop(0, width // (PAIR * chunk))
        def _(part):
            def products(item):
                pair = part * chunk + item
                q_two = apart(proj[here, lanes(0, pair)] * DH ** (-0.5))
                scores[item] = dot(proj[here, lanes(1, pair)], q_two, NT)
                ga_two = apart(ga[here, lanes(0, pair)])
                gprobs[item] = dot(proj[here, lanes(2, pair)], ga_two, NT)

            def softmax(item):
                masked = scores[item] + bias[...]
                expanded = jnp.exp(masked - jnp.max(masked, axis=0, keepdims=True))
                probs = expanded * (1.0 / jnp.sum(expanded, axis=0, keepdims=True))
                low[item, 0] = probs.astype(jnp.bfloat16)
                weighted = probs * gprobs[item]
                delta = jnp.sum(weighted, axis=0, keepdims=True)
                low[item, 1] = (weighted - probs * delta).astype(jnp.bfloat16)

            def results(item):
                pair = part * chunk + item
                probs_low, grad_scores = low[item, 0], low[item, 1]
                q_two = apart(proj[here, lanes(0, pair)] * DH ** (-0.5))
                k_two = apart(proj[here, lanes(1, pair)])
                v_two = apart(proj[here, lanes(2, pair)])
                ga_two = apart(ga[here, lanes(0, pair)])
                att[here, lanes(0, pair)] = dot(stacked(probs_low), v_two, TN).astype(jnp.bfloat16)
                gproj[here, lanes(0, pair)] = (
                    dot(stacked(grad_scores), k_two, TN) * DH ** (-0.5)
                ).astype(jnp.bfloat16)
                gproj[here, lanes(1, pair)] = dot(grad_scores, q_two, NN).astype(jnp.bfloat16)
                gproj[here, lanes(2, pair)] = dot(probs_low, ga_two, NN).astype(jnp.bfloat16)

            each(products)
            each(softmax)
            each(results)

    def store(which, group, value):
        out_ref[:, which, group * SUB : (group + 1) * SUB, :] = value.reshape(frames, SUB, width)

    for group in range(groups):
        here = pl.ds(group * rows, rows)
        mixed = dot(att[here, :], w_out[...], NN)
        wide = load_rows(both_ref, 0, group).astype(jnp.float32)
        store(0, group, (wide + live * mixed).astype(jnp.bfloat16))

    wait(again)

    @pl.loop(0, width // step)
    def _(j):
        columns = pl.ds(pl.multiple_of(j * step, step), step)
        gnorm[:, columns] = dot(gproj[...], w_in[columns, :], NT)

    for group in range(groups):
        here = pl.ds(group * rows, rows)
        grad = gnorm[here, :] * gain_ref[...]
        scale = stats_ref[here, 1:2]
        hat = (load_rows(both_ref, 0, group).astype(jnp.float32) - stats_ref[here, 0:1]) * scale
        grad_rows = scale * (
            grad
            - jnp.mean(grad, axis=-1, keepdims=True)
            - hat * jnp.mean(grad * hat, axis=-1, keepdims=True)
        )
        cot = load_rows(both_ref, 1, group).astype(jnp.float32)
        store(1, group, (cot + grad_rows).astype(jnp.bfloat16))


def run_block(counts, gain, both, front_weights, late_weights, plan):
    frames, _, patches, width = both.shape
    total, rows = frames * patches, frames * SUB
    vmem = pl.BlockSpec(memory_space=pltpu.VMEM)
    smem = pl.BlockSpec(memory_space=pltpu.SMEM)
    anywhere = pl.BlockSpec(memory_space=pl.ANY)
    shape = jax.ShapeDtypeStruct
    params = pltpu.CompilerParams(vmem_limit_bytes=VMEM_LIMIT)
    front_columns = sum(size for _, _, size in plan["placed"])
    normed, stats, front = pl.pallas_call(
        functools.partial(front_kernel, plan),
        out_shape=(
            shape((total, width), jnp.bfloat16),
            shape((total, 128), jnp.float32),
            shape((total, front_columns), jnp.bfloat16),
        ),
        in_specs=[vmem, vmem] + [anywhere] * len(front_weights),
        out_specs=(vmem, vmem, vmem),
        scratch_shapes=[
            pltpu.VMEM((width, front_columns), jnp.bfloat16),
            pltpu.SemaphoreType.DMA((1,)),
        ],
        compiler_params=params,
        cost_estimate=pl.CostEstimate(
            flops=2 * total * width * front_columns,
            bytes_accessed=2 * width * front_columns + 8 * total * width,
            transcendentals=total,
        ),
        name="front",
    )(both, gain, *front_weights)
    chunk = 8 if rows <= 128 else 1
    return pl.pallas_call(
        functools.partial(main_kernel, plan),
        out_shape=shape(both.shape, jnp.bfloat16),
        in_specs=[smem, vmem, vmem, vmem, vmem, anywhere]
        + [anywhere] * (len(front_weights) + len(late_weights)),
        out_specs=vmem,
        scratch_shapes=[
            pltpu.VMEM((width, 3 * width), jnp.bfloat16),
            pltpu.VMEM((width, width), jnp.bfloat16),
            pltpu.VMEM((total, width), jnp.bfloat16),
            pltpu.VMEM((total, 3 * width), jnp.bfloat16),
            pltpu.VMEM((total, width), jnp.bfloat16),
            pltpu.VMEM((total, width), jnp.bfloat16),
            pltpu.VMEM((total, 3 * width), jnp.bfloat16),
            pltpu.VMEM((total, width), jnp.float32),
            pltpu.VMEM((rows, 2 * rows), jnp.float32),
            pltpu.VMEM((chunk, rows, 2 * rows), jnp.float32),
            pltpu.VMEM((chunk, rows, 2 * rows), jnp.float32),
            pltpu.VMEM((chunk, 2, rows, 2 * rows), jnp.bfloat16),
            pltpu.SemaphoreType.DMA((4,)),
        ],
        compiler_params=params,
        cost_estimate=pl.CostEstimate(
            flops=12 * total * width * width,
            bytes_accessed=8 * width * width + 8 * total * width,
            transcendentals=total * 2048,
        ),
        name="main",
    )(counts, gain, both, normed, stats, front, *front_weights, *late_weights)


def swap(array, distance, devices):
    return lax.ppermute(array, "frame", [(f, f ^ distance) for f in range(devices)])


def join_kernel(axis, *refs):
    *sources, target = refs
    start = 0
    for source in sources:
        end = start + source.shape[axis]
        if axis == 0:
            target[start:end, :] = source[...]
        else:
            target[:, start:end] = source[...]
        start = end


def join(axis, *arrays):
    shape = list(arrays[0].shape)
    shape[axis] = sum(array.shape[axis] for array in arrays)
    vmem = pl.BlockSpec(memory_space=pltpu.VMEM)
    return pl.pallas_call(
        functools.partial(join_kernel, axis),
        out_shape=jax.ShapeDtypeStruct(shape, arrays[0].dtype),
        in_specs=[vmem] * len(arrays),
        out_specs=vmem,
        name="join",
    )(*arrays)


def gather_two_ways(input_weights, output_weights, both, devices):
    depth, in_columns = input_weights.shape
    out_columns = output_weights.shape[1]
    early = in_columns * 2 // 3 // 128 * 128
    late = in_columns - early
    late_shard = join(1, output_weights, input_weights[:, early:])
    late_whole = lax.all_gather(late_shard, ("clip", "frame"), axis=0)
    late_whole = late_whole.reshape(4 * devices, depth, out_columns + late)

    shard = input_weights[:, :early]
    offsets = (0, 1, 3, 2)
    held = [shard] + [
        lax.ppermute(shard, "clip", [(c, c ^ offset) for c in range(4)]) for offset in offsets[1:]
    ]
    both, held[1] = lax.optimization_barrier((both, held[1]))
    both = lax.all_to_all(both, "frame", split_axis=0, concat_axis=0, tiled=True)
    own = join(0, *held)
    by_x, by_y = swap(own, 2, devices), swap(own, 4, devices)
    by_x, both = lax.optimization_barrier((by_x, both))
    middle = 2 * depth
    arrays = [own, by_x, by_y, swap(by_y[:middle], 2, devices), swap(by_x[middle:], 4, devices)]
    arrays += [swap(array, 1, devices) for array in arrays]

    def front(stride=early):
        clip, frame = lax.axis_index("clip"), lax.axis_index("frame")
        found = []
        for ref in range(10):
            distance = (0, 2, 4, 6, 6)[ref % 5] ^ (ref // 5)
            places = {3: (0, 1), 4: (2, 3)}.get(ref % 5, range(4))
            for order, place in enumerate(places):
                row = (frame ^ distance) * depth
                column = (clip ^ offsets[place]) * stride
                found.append((ref, None, order * depth, depth, (0, early), row, column))
        return found

    def pieces(first, size, stride, offset):
        return [
            (10, c * devices + f, 0, depth, (first, size), f * depth, c * stride + offset)
            for c in range(4)
            for f in range(devices)
        ]

    plan = {
        "front": front,
        "again": lambda: front(in_columns),
        "late": lambda: pieces(out_columns, late, in_columns, early),
        "outer": lambda: pieces(0, out_columns, out_columns, 0),
        "placed": [(c * early, c * in_columns, early) for c in range(4)],
        "missing": [(c * in_columns + early, late) for c in range(4)],
    }
    return arrays, [late_whole], plan, both


def gather_plainly(input_weights, output_weights, both):
    whole = []
    for weights in (input_weights, output_weights):
        columns = lax.all_gather(weights, "clip", axis=1, tiled=True)
        whole.append(lax.all_gather(columns, "frame", axis=0, tiled=True))
    both = lax.all_to_all(both, "frame", split_axis=0, concat_axis=0, tiled=True)
    inner, outer = [[(i, None, 0, w.shape[0], (0, w.shape[1]), 0, 0)] for i, w in enumerate(whole)]
    plan = {
        "front": lambda: inner,
        "again": lambda: inner,
        "late": lambda: [],
        "outer": lambda: outer,
        "placed": [(0, 0, whole[0].shape[1])],
        "missing": [],
    }
    return whole[:1], whole[1:], plan, both


def per_device(clips, devices, tokens, counts, norm_gain, input_weights, output_weights, cotangent):
    _, slots, patches, width = tokens.shape
    share = -(-patches // devices)
    share = -(-share // SUB) * SUB
    extra = devices * share - patches

    def by_destination(source):
        padded = jnp.pad(source[0], ((0, 0), (0, extra), (0, 0)))
        return padded.reshape(slots, devices, share, width).transpose(1, 0, 2, 3)

    both = jnp.stack([by_destination(tokens), by_destination(cotangent)], axis=2)
    depth, in_columns = input_weights.shape
    fits = in_columns % 384 == 0 and output_weights.shape[1] % 128 == 0 and depth % 16 == 0
    if clips == 4 and devices == 8 and fits:
        front, late, plan, both = gather_two_ways(input_weights, output_weights, both, devices)
    else:
        front, late, plan, both = gather_plainly(input_weights, output_weights, both)
    both = both.reshape(devices * slots, 2, share, width)
    back = run_block(counts, norm_gain.reshape(1, width), both, front, late, plan)
    back = back.reshape(devices, slots, 2, share, width)
    back = lax.all_to_all(back, "frame", split_axis=0, concat_axis=0, tiled=True)

    def in_order(which):
        rows = back[:, :, which].transpose(1, 0, 2, 3).reshape(slots, devices * share, width)
        return rows[None, :, :patches]

    return in_order(0), in_order(1)


def solution(mesh):
    in_specs = (
        P("clip", "frame", None, None),
        P("clip"),
        P(),
        P("frame", "clip"),
        P("frame", "clip"),
        P("clip", "frame", None, None),
    )
    out_specs = (P("clip", "frame", None, None), P("clip", "frame", None, None))
    body = functools.partial(per_device, mesh.shape["clip"], mesh.shape["frame"])
    return jax.shard_map(body, mesh=mesh, in_specs=in_specs, out_specs=out_specs, check_vma=False)
```

time: 144 us -> 130 us (0.903)
  waiting for transfers between devices: 78.5 us -> 41.3 us
  local copies, waits for them, and re-layouts: 2.37 us -> 16.4 us
  starting transfers between devices: 5.34 us -> 17.1 us
  other arithmetic: 3.04 us -> 1.09 us
    all_gather x1, waiting for transfers between devices: 61.9 us -> 6.62 us  [gather_two_ways(): late_whole = lax.all_gather(late_shard, ('clip', 'frame'), axis=0)]
    ppermute x0 -> x12, waiting for transfers between devices: none -> 34.7 us  [the longest x9 23.5 us: swap(): lax.ppermute(array, 'frame', [(f, f ^ distance) for f in range(devices)])]
    all_to_all x1, waiting for transfers between devices: 16.6 us -> 0.01 us  [gather_two_ways(): lax.all_to_all(both, 'frame', split_axis=0, concat_axis=0, tiled=True)]
    ppermute x0 -> x12, starting transfers between devices: none -> 12.8 us  [the longest x3 7.26 us: gather_two_ways(): lax.ppermute(shard, 'clip', [(c, c ^ offset) for c in range(4)])]
    unnamed x3 -> x32, local copies, waits for them, and re-layouts: 0.94 us -> 10.1 us
    slice x0 -> x5, local copies, waits for them, and re-layouts: none -> 3.22 us  [the longest x1 1.48 us: gather_two_ways(): late_shard = join(1, output_weights, input_weights[:, early:])]
    concatenate x2 -> x0, other arithmetic: 2.94 us -> none  [the longest x1 1.7 us: gather_weights(): joined = jnp.concatenate([input_weights, output_weights], axis=1)]
    pad x0 -> x2, local copies, waits for them, and re-layouts: none -> 2.1 us  [by_destination(): padded = jnp.pad(source[0], ((0, 0), (0, extra), (0, 0)))]
  transfers between devices with their start and end apart: 2 -> 14, of which waited for: 2 -> 8; matrix products, arithmetic and copies ran while one was open for 2% -> 4% of each run, Pallas kernels for 0% -> 4%
where the time goes in v5:
time: 130 us; the launch traced here: 129 us
  waiting for transfers between devices  41.3 us (32%)
  Pallas kernels  20.6 us (16%)
  blocking collectives  17.8 us (14%)
  starting transfers between devices  17.1 us (13%)
  local copies, waits for them, and re-layouts  16.4 us (13%)
  between operations  14.8 us (11%)
    ppermute x9, waiting for transfers between devices, swap(): lax.ppermute(array, 'frame', [(f, f ^ distance) for f in range(devices)])  23.5 us
    all_to_all x1, blocking collectives, per_device(): lax.all_to_all(back, 'frame', split_axis=0, concat_axis=0, tiled=True)  17.8 us
    pallas_call x1, Pallas kernels, run_block(): pl.pallas_call(functools.partial(main_kernel, plan), out_shape=shape(both...  13.3 us
    ppermute x3, waiting for transfers between devices, gather_two_ways(): lax.ppermute(shard, 'clip', [(c, c ^ offset) for c in range(4)])  11.2 us
    unnamed x32, local copies, waits for them, and re-layouts  10.1 us
    ppermute x3, starting transfers between devices, gather_two_ways(): lax.ppermute(shard, 'clip', [(c, c ^ offset) for c in range(4)])  7.26 us
    all_gather x1, waiting for transfers between devices, gather_two_ways(): late_whole = lax.all_gather(late_shard, ('clip', 'frame'), axis=0)  6.62 us
    ppermute x9, starting transfers between devices, swap(): lax.ppermute(array, 'frame', [(f, f ^ distance) for f in range(devices)])  5.54 us
  transfers between devices with their start and end apart: 14, of which 8 were waited for; matrix products, arithmetic and copies ran while one was open for 4% of the time, Pallas kernels for 4%

profile of v5, /device:TPU:0, one launch (start us, length us, event | category | flops | bytes accessed | tf_op | source)
XLA Modules:
  0.0 129.0 jit_solution(14437931970818315188)
XLA Ops:
  7.2 0.0 all-gather.3.cloned.1.call-start
  7.2 1.5 %slice.27.refs_1_ = bf16[128,256]{1,0:T(8,128)(2,1)} slice(bf16[128,768]{1,0:T(8,128)(2,1)} %param.9), slice={[0:128], [512:768]} | slice | bytes 131072 | tf_op jit(solution)/shard_map/slice | solution.py:313
  8.7 1.5 %join.3 = bf16[128,512]{1,0:T(8,128)(2,1)} custom-call(bf16[128,256]{1,0:T(8,128)(2,1)} %refs_0_.1, bf16[128,256]{1,0:T(8,128)(2,1)} %slice.27.refs_1_), custom_call_target="tpu_custom_call" | custom-call | tf_op jit(solution)/shard_map/join/pallas_call | solution.py:299
  10.2 0.0 all-gather.3.cloned.1.call-update
  10.2 0.0 copy-start.11
  10.2 0.9 slice.24.refs_0_
  11.2 0.0 copy-start.12
  11.2 3.1 %collective-permute-start = (bf16[128,512]{1,0:T(8,128)(2,1)S(1)}, bf16[128,512]{1,0:T(8,128)(2,1)S(1)}, u32[]{:S(2)}, u32[]{:S(2)}) collective-permute-start(bf16[128,512]{1,0:T(8,128)(2,1)S(1)} %slice.24.refs_0_), channel_id=1, source_target_pairs={{0,8},{8,0},{16,24},{24,16},{1,9},{9,1},{17,25},{25,17},{2,10},{10... | collective-permute-start | bytes 393224 | tf_op jit(solution)/shard_map/ppermute | solution.py:320
  14.3 1.0 pad.7
  15.3 1.1 pad.8
  16.4 1.1 pad_maximum_fusion
  17.5 0.3 collective-permute-done.refs_1_
  17.8 0.0 copy-start.13
  17.8 4.2 %all-to-all-start = ((bf16[8,1,2,32,1024]{4,3,2,1,0:T(8,128)(2,1)}), bf16[8,1,2,32,1024]{4,3,2,1,0:T(8,128)(2,1)}, u32[]{:S(2)}, u32[]{:S(2)}) async-start(bf16[8,1,2,32,1024]{4,3,2,1,0:T(8,128)(2,1)} %pad_maximum_fusion), calls=%async_computation | async-start | bytes 2097152 | tf_op jit(solution)/shard_map/all_to_all | solution.py:323
  22.0 2.8 %collective-permute-start.2 = (bf16[128,512]{1,0:T(8,128)(2,1)S(1)}, bf16[128,512]{1,0:T(8,128)(2,1)S(1)}, u32[]{:S(2)}, u32[]{:S(2)}) collective-permute-start(bf16[128,512]{1,0:T(8,128)(2,1)S(1)} %slice.24.refs_0_), channel_id=1, source_target_pairs={{0,16},{8,24},{16,0},{24,8},{1,17},{9,25},{17,1},{25,9},{2,18},{10... | collective-permute-start | bytes 393224 | tf_op jit(solution)/shard_map/ppermute | solution.py:320
  24.8 1.3 %collective-permute-start.1 = (bf16[128,512]{1,0:T(8,128)(2,1)S(1)}, bf16[128,512]{1,0:T(8,128)(2,1)S(1)}, u32[]{:S(2)}, u32[]{:S(2)}) collective-permute-start(bf16[128,512]{1,0:T(8,128)(2,1)S(1)} %slice.24.refs_0_), channel_id=1, source_target_pairs={{0,24},{8,16},{16,8},{24,0},{1,25},{9,17},{17,9},{25,1},{2,26},{10... | collective-permute-start | bytes 393224 | tf_op jit(solution)/shard_map/ppermute | solution.py:320
  26.2 10.9 %collective-permute-done.2.refs_3_ = bf16[128,512]{1,0:T(8,128)(2,1)S(1)} collective-permute-done((bf16[128,512]{1,0:T(8,128)(2,1)S(1)}, bf16[128,512]{1,0:T(8,128)(2,1)S(1)}, u32[]{:S(2)}, u32[]{:S(2)}) %collective-permute-start.2) | collective-permute-done | bytes 131104 | tf_op jit(solution)/shard_map/ppermute | solution.py:320
  37.1 0.0 copy-start.14
  37.1 0.0 collective-permute-done.1.refs_2_
  37.1 0.0 copy-done.12
  37.1 0.0 copy-done.13
  37.1 0.6 copy-done.14
  37.7 0.0 copy-start.15
  37.7 0.6 copy-done.15
  38.4 1.9 %join.2.rest_0_ = bf16[512,512]{1,0:T(8,128)(2,1)} custom-call(bf16[128,512]{1,0:T(8,128)(2,1)} %copy-done.12, bf16[128,512]{1,0:T(8,128)(2,1)} %copy-done.13, bf16[128,512]{1,0:T(8,128)(2,1)} %copy-done.15, bf16[128,512]{1,0:T(8,128)(2,1)} %copy-done.14), custom_call_target="tpu_custom_call" | custom-call | tf_op jit(solution)/shard_map/join/pallas_call | solution.py:299
  40.3 1.8 %collective-permute-start.4 = (bf16[512,512]{1,0:T(8,128)(2,1)}, bf16[512,512]{1,0:T(8,128)(2,1)S(1)}, u32[]{:S(2)}, u32[]{:S(2)}) collective-permute-start(bf16[512,512]{1,0:T(8,128)(2,1)} %join.2.rest_0_), channel_id=1, source_target_pairs={{0,4},{1,5},{2,6},{3,7},{4,0},{5,1},{6,2},{7,3},{8,12},{9,13},{10,... | collective-permute-start | bytes 1572872 | tf_op jit(solution)/shard_map/ppermute | solution.py:280
  42.1 1.5 %collective-permute-start.3 = (bf16[512,512]{1,0:T(8,128)(2,1)}, bf16[512,512]{1,0:T(8,128)(2,1)S(1)}, u32[]{:S(2)}, u32[]{:S(2)}) collective-permute-start(bf16[512,512]{1,0:T(8,128)(2,1)} %join.2.rest_0_), channel_id=1, source_target_pairs={{0,2},{1,3},{2,0},{3,1},{4,6},{5,7},{6,4},{7,5},{8,10},{9,11},{10,... | collective-permute-start | bytes 1572872 | tf_op jit(solution)/shard_map/ppermute | solution.py:280
  43.6 0.0 collective-permute-start.7
  43.6 12.5 %collective-permute-done.4.rest_2_ = bf16[512,512]{1,0:T(8,128)(2,1)S(1)} collective-permute-done((bf16[512,512]{1,0:T(8,128)(2,1)}, bf16[512,512]{1,0:T(8,128)(2,1)S(1)}, u32[]{:S(2)}, u32[]{:S(2)}) %collective-permute-start.4) | collective-permute-done | bytes 524320 | tf_op jit(solution)/shard_map/ppermute | solution.py:280
  56.1 0.7 slice.32
  56.8 1.3 %collective-permute-start.5 = (bf16[256,512]{1,0:T(8,128)(2,1)}, bf16[256,512]{1,0:T(8,128)(2,1)S(1)}, u32[]{:S(2)}, u32[]{:S(2)}) collective-permute-start(bf16[256,512]{1,0:T(8,128)(2,1)} %slice.32), channel_id=1, source_target_pairs={{0,2},{1,3},{2,0},{3,1},{4,6},{5,7},{6,4},{7,5},{8,10},{9,11},{10,... | collective-permute-start | bytes 786440 | tf_op jit(solution)/shard_map/ppermute | solution.py:280
  58.1 0.0 collective-permute-start.9
  58.2 1.3 %collective-permute-done.3.rest_1_ = bf16[512,512]{1,0:T(8,128)(2,1)S(1)} collective-permute-done((bf16[512,512]{1,0:T(8,128)(2,1)}, bf16[512,512]{1,0:T(8,128)(2,1)S(1)}, u32[]{:S(2)}, u32[]{:S(2)}) %collective-permute-start.3) | collective-permute-done | bytes 524320 | tf_op jit(solution)/shard_map/ppermute | solution.py:280
  59.4 0.0 all-to-all-done
  59.5 0.1 collective-permute-start.8
  59.5 0.9 collective-permute-start.6
  60.4 4.3 %collective-permute-done.5.rest_3_ = bf16[256,512]{1,0:T(8,128)(2,1)S(1)} collective-permute-done((bf16[256,512]{1,0:T(8,128)(2,1)}, bf16[256,512]{1,0:T(8,128)(2,1)S(1)}, u32[]{:S(2)}, u32[]{:S(2)}) %collective-permute-start.5) | collective-permute-done | bytes 262176 | tf_op jit(solution)/shard_map/ppermute | solution.py:280
  64.7 0.0 collective-permute-start.10
  64.7 4.5 %collective-permute-done.6.rest_4_ = bf16[256,512]{1,0:T(8,128)(2,1)S(1)} collective-permute-done((bf16[256,512]{1,0:T(8,128)(2,1)S(1)}, bf16[256,512]{1,0:T(8,128)(2,1)S(1)}, u32[]{:S(2)}, u32[]{:S(2)}) %collective-permute-start.6) | collective-permute-done | bytes 262176 | tf_op jit(solution)/shard_map/ppermute | solution.py:280
  69.2 0.0 collective-permute-start.11
  69.9 0.0 collective-permute-done.7.rest_5_
  69.9 0.0 collective-permute-done.9.rest_7_
  69.9 0.0 collective-permute-done.10.rest_8_
  69.9 0.0 collective-permute-done.8.rest_6_
  69.9 0.8 collective-permute-done.11.rest_9_
  70.8 0.0 copy-done.11
  70.8 1.1 copy-done
  71.8 3.8 %front.1 = (bf16[256,1024]{1,0:T(8,128)(2,1)S(1)}, f32[256,128]{1,0:T(8,128)S(1)}, bf16[256,2048]{1,0:T(8,128)(2,1)S(1)}) custom-call(bf16[8,2,32,1024]{3,2,1,0:T(8,128)(2,1)} %bitcast.5.both_ref, f32[1,1024]{1,0:T(1,128)S(1)} %bitcast.17, bf16[512,512]{1,0:T(8,128)(2,1)S(1)} %copy-done, bf16[512,512]{1,0:T(8,128)(2,1)S(1)} %collective-permute-done.3.rest_1_, ...), custom_call_target="tpu_custom_call" | custom-call | flops 1073741824 | bytes 6291456 | tf_op jit(solution)/shard_map/front/pallas_call | solution.py:226
  75.7 0.0 copy-start.2
  75.7 1.0 copy-done.2
  76.7 0.7 copy-done.3
  77.4 0.7 copy-done.5
  78.1 0.7 copy-done.7
  78.8 0.8 copy-done.9
  79.6 6.6 %all-gather.3.cloned.1.call-done = bf16[4096,512]{1,0:T(8,128)(2,1)} async-done(((bf16[128,512]{1,0:T(8,128)(2,1)}), bf16[4096,512]{1,0:T(8,128)(2,1)}) %all-gather.3.cloned.1.call-update) | async-done | bytes 4194320 | tf_op jit(solution)/shard_map/all_gather | solution.py:314
  86.2 0.0 copy-done.1
  86.2 0.9 copy-done.4
  87.1 0.9 copy-done.6
  88.1 0.9 copy-done.8
  89.0 1.0 copy-done.10
  90.1 13.3 %main.1 = bf16[8,2,32,1024]{3,2,1,0:T(8,128)(2,1)S(1)} custom-call(s32[1]{0:T(128)S(6)} %copy.9.counts_ref, f32[1,1024]{1,0:T(1,128)S(1)} %bitcast.18, bf16[8,2,32,1024]{3,2,1,0:T(8,128)(2,1)} %bitcast.5.both_ref, bf16[256,1024]{1,0:T(8,128)(2,1)S(1)} %copy-done.10, f32[256,128]{1,0:T(8,128)S(1)} %get-tuple-element.14.stats_ref, ...), custom_call_target="tpu_custom_call" | custom-call | flops 3221225472 | bytes 10485760 | tf_op jit(solution)/shard_map/main/pallas_call | solution.py:248
  103.4 17.8 %all_to_all.10 = bf16[8,1,2,32,1024]{4,3,2,1,0:T(8,128)(2,1)S(1)} all-to-all(bf16[8,1,2,32,1024]{4,3,2,1,0:T(8,128)(2,1)S(1)} %bitcast.16), channel_id=1, replica_groups=mesh['clip'=4,'frame'=8] {'frame'}, dimensions={0} | all-to-all | bytes 2097152 | tf_op jit(solution)/shard_map/all_to_all | solution.py:399
  121.1 0.1 fusion
  121.2 0.9 slice_bitcast_fusion
  (11 shorter events, 0.0 us)
Async XLA Ops:
  7.2 79.0 %all-gather.3.cloned.1.call-start = ((), (), s32[]{:S(2)}) async-start(), calls=%async_computation.2 | async-start | bytes 4325376 | tf_op jit(solution)/shard_map/all_gather | solution.py:314
  10.2 60.5 %copy-start.11 = (f32[1024]{0:T(1024)S(1)}, f32[1024]{0:T(1024)}, u32[]{:S(2)}) copy-start(f32[1024]{0:T(1024)} %param.8) | copy-start | bytes 12292
  11.2 25.9 %copy-start.12 = (bf16[128,512]{1,0:T(8,128)(2,1)}, bf16[128,512]{1,0:T(8,128)(2,1)S(1)}, u32[]{:S(2)}) copy-start(bf16[128,512]{1,0:T(8,128)(2,1)S(1)} %slice.24.refs_0_) | copy-start | bytes 393220
  11.2 6.6 %collective-permute-start = (bf16[128,512]{1,0:T(8,128)(2,1)S(1)}, bf16[128,512]{1,0:T(8,128)(2,1)S(1)}, u32[]{:S(2)}, u32[]{:S(2)}) collective-permute-start(bf16[128,512]{1,0:T(8,128)(2,1)S(1)} %slice.24.refs_0_), channel_id=1, source_target_pairs={{0,8},{8,0},{16,24},{24,16},{1,9},{9,1},{17,25},{25,17},{2,10},{10... | collective-permute-start | bytes 393224 | tf_op jit(solution)/shard_map/ppermute | solution.py:320
  17.8 19.3 %copy-start.13 = (bf16[128,512]{1,0:T(8,128)(2,1)}, bf16[128,512]{1,0:T(8,128)(2,1)S(1)}, u32[]{:S(2)}) copy-start(bf16[128,512]{1,0:T(8,128)(2,1)S(1)} %collective-permute-done.refs_1_) | copy-start | bytes 393220
  17.8 41.7 %all-to-all-start = ((bf16[8,1,2,32,1024]{4,3,2,1,0:T(8,128)(2,1)}), bf16[8,1,2,32,1024]{4,3,2,1,0:T(8,128)(2,1)}, u32[]{:S(2)}, u32[]{:S(2)}) async-start(bf16[8,1,2,32,1024]{4,3,2,1,0:T(8,128)(2,1)} %pad_maximum_fusion), calls=%async_computation | async-start | bytes 2097152 | tf_op jit(solution)/shard_map/all_to_all | solution.py:323
  22.0 15.1 %collective-permute-start.2 = (bf16[128,512]{1,0:T(8,128)(2,1)S(1)}, bf16[128,512]{1,0:T(8,128)(2,1)S(1)}, u32[]{:S(2)}, u32[]{:S(2)}) collective-permute-start(bf16[128,512]{1,0:T(8,128)(2,1)S(1)} %slice.24.refs_0_), channel_id=1, source_target_pairs={{0,16},{8,24},{16,0},{24,8},{1,17},{9,25},{17,1},{25,9},{2,18},{10... | collective-permute-start | bytes 393224 | tf_op jit(solution)/shard_map/ppermute | solution.py:320
  24.8 12.3 %collective-permute-start.1 = (bf16[128,512]{1,0:T(8,128)(2,1)S(1)}, bf16[128,512]{1,0:T(8,128)(2,1)S(1)}, u32[]{:S(2)}, u32[]{:S(2)}) collective-permute-start(bf16[128,512]{1,0:T(8,128)(2,1)S(1)} %slice.24.refs_0_), channel_id=1, source_target_pairs={{0,24},{8,16},{16,8},{24,0},{1,25},{9,17},{17,9},{25,1},{2,26},{10... | collective-permute-start | bytes 393224 | tf_op jit(solution)/shard_map/ppermute | solution.py:320
  37.1 0.6 copy-start.14
  37.7 0.6 copy-start.15
  40.3 45.9 %copy-start.1 = (bf16[512,512]{1,0:T(8,128)(2,1)S(1)}, bf16[512,512]{1,0:T(8,128)(2,1)}, u32[]{:S(2)}) copy-start(bf16[512,512]{1,0:T(8,128)(2,1)} %join.2.rest_0_) | copy-start | bytes 1572868
  40.3 15.8 %collective-permute-start.4 = (bf16[512,512]{1,0:T(8,128)(2,1)}, bf16[512,512]{1,0:T(8,128)(2,1)S(1)}, u32[]{:S(2)}, u32[]{:S(2)}) collective-permute-start(bf16[512,512]{1,0:T(8,128)(2,1)} %join.2.rest_0_), channel_id=1, source_target_pairs={{0,4},{1,5},{2,6},{3,7},{4,0},{5,1},{6,2},{7,3},{8,12},{9,13},{10,... | collective-permute-start | bytes 1572872 | tf_op jit(solution)/shard_map/ppermute | solution.py:280
  42.1 17.4 %collective-permute-start.3 = (bf16[512,512]{1,0:T(8,128)(2,1)}, bf16[512,512]{1,0:T(8,128)(2,1)S(1)}, u32[]{:S(2)}, u32[]{:S(2)}) collective-permute-start(bf16[512,512]{1,0:T(8,128)(2,1)} %join.2.rest_0_), channel_id=1, source_target_pairs={{0,2},{1,3},{2,0},{3,1},{4,6},{5,7},{6,4},{7,5},{8,10},{9,11},{10,... | collective-permute-start | bytes 1572872 | tf_op jit(solution)/shard_map/ppermute | solution.py:280
  43.6 26.3 %collective-permute-start.7 = (bf16[512,512]{1,0:T(8,128)(2,1)}, bf16[512,512]{1,0:T(8,128)(2,1)S(1)}, u32[]{:S(2)}, u32[]{:S(2)}) collective-permute-start(bf16[512,512]{1,0:T(8,128)(2,1)} %join.2.rest_0_), channel_id=1, source_target_pairs={{0,1},{1,0},{2,3},{3,2},{4,5},{5,4},{6,7},{7,6},{8,9},{9,8},{10,11... | collective-permute-start | bytes 1572872 | tf_op jit(solution)/shard_map/ppermute | solution.py:280
  56.8 7.9 %collective-permute-start.5 = (bf16[256,512]{1,0:T(8,128)(2,1)}, bf16[256,512]{1,0:T(8,128)(2,1)S(1)}, u32[]{:S(2)}, u32[]{:S(2)}) collective-permute-start(bf16[256,512]{1,0:T(8,128)(2,1)} %slice.32), channel_id=1, source_target_pairs={{0,2},{1,3},{2,0},{3,1},{4,6},{5,7},{6,4},{7,5},{8,10},{9,11},{10,... | collective-permute-start | bytes 786440 | tf_op jit(solution)/shard_map/ppermute | solution.py:280
  58.1 11.7 %collective-permute-start.9 = (bf16[512,512]{1,0:T(8,128)(2,1)S(1)}, bf16[512,512]{1,0:T(8,128)(2,1)S(1)}, u32[]{:S(2)}, u32[]{:S(2)}) collective-permute-start(bf16[512,512]{1,0:T(8,128)(2,1)S(1)} %collective-permute-done.4.rest_2_), channel_id=1, source_target_pairs={{0,1},{1,0},{2,3},{3,2},{4,5},{5,4},{6,7},{7,6},{8,9},{9,8},{10,11... | collective-permute-start | bytes 1572872 | tf_op jit(solution)/shard_map/ppermute | solution.py:280
  59.5 10.4 %collective-permute-start.8 = (bf16[512,512]{1,0:T(8,128)(2,1)S(1)}, bf16[512,512]{1,0:T(8,128)(2,1)S(1)}, u32[]{:S(2)}, u32[]{:S(2)}) collective-permute-start(bf16[512,512]{1,0:T(8,128)(2,1)S(1)} %collective-permute-done.3.rest_1_), channel_id=1, source_target_pairs={{0,1},{1,0},{2,3},{3,2},{4,5},{5,4},{6,7},{7,6},{8,9},{9,8},{10,11... | collective-permute-start | bytes 1572872 | tf_op jit(solution)/shard_map/ppermute | solution.py:280
  59.5 9.7 %collective-permute-start.6 = (bf16[256,512]{1,0:T(8,128)(2,1)S(1)}, bf16[256,512]{1,0:T(8,128)(2,1)S(1)}, u32[]{:S(2)}, u32[]{:S(2)}) collective-permute-start(bf16[256,512]{1,0:T(8,128)(2,1)S(1)} %slice.26), channel_id=1, source_target_pairs={{0,4},{1,5},{2,6},{3,7},{4,0},{5,1},{6,2},{7,3},{8,12},{9,13},{10,... | collective-permute-start | bytes 786440 | tf_op jit(solution)/shard_map/ppermute | solution.py:280
  64.7 5.2 %collective-permute-start.10 = (bf16[256,512]{1,0:T(8,128)(2,1)S(1)}, bf16[256,512]{1,0:T(8,128)(2,1)S(1)}, u32[]{:S(2)}, u32[]{:S(2)}) collective-permute-start(bf16[256,512]{1,0:T(8,128)(2,1)S(1)} %collective-permute-done.5.rest_3_), channel_id=1, source_target_pairs={{0,1},{1,0},{2,3},{3,2},{4,5},{5,4},{6,7},{7,6},{8,9},{9,8},{10,11... | collective-permute-start | bytes 786440 | tf_op jit(solution)/shard_map/ppermute | solution.py:280
  69.2 1.5 %collective-permute-start.11 = (bf16[256,512]{1,0:T(8,128)(2,1)S(1)}, bf16[256,512]{1,0:T(8,128)(2,1)S(1)}, u32[]{:S(2)}, u32[]{:S(2)}) collective-permute-start(bf16[256,512]{1,0:T(8,128)(2,1)S(1)} %collective-permute-done.6.rest_4_), channel_id=1, source_target_pairs={{0,1},{1,0},{2,3},{3,2},{4,5},{5,4},{6,7},{7,6},{8,9},{9,8},{10,11... | collective-permute-start | bytes 786440 | tf_op jit(solution)/shard_map/ppermute | solution.py:280
  70.8 1.1 copy-start
  75.7 1.0 copy-start.2
  76.7 0.7 copy-start.3
  77.4 0.7 copy-start.5
  78.1 0.7 copy-start.7
  78.8 0.8 copy-start.9
  86.2 1.0 copy-start.4
  87.1 0.9 copy-start.6
  88.1 0.9 copy-start.8
  89.0 1.0 copy-start.10
Sparse Core Ops, SparseCore 0:
  10.9 75.2 all-gather.2

commit v6 on v5

--- a/solution.py
+++ b/solution.py
@@ -16,7 +16,7 @@
 NN = (((1,), (0,)), ((), ()))
 NT = (((1,), (1,)), ((), ()))
 TN = (((0,), (0,)), ((), ()))
-VMEM_LIMIT = 48 * 1024 * 1024
+VMEM_LIMIT = 27 * 1024 * 1024
 
 
 def dot(a, b, dims):
@@ -52,10 +52,11 @@
     return ref[:, which, group * SUB : (group + 1) * SUB, :].reshape(frames * SUB, width)
 
 
-def front_kernel(plan, both_ref, gain_ref, *rest):
-    weight_refs = rest[:-5]
-    normed_ref, stats_ref, proj_ref, w_front, sems = rest[-5:]
-    copies = fetch(plan["front"](), weight_refs, w_front, sems.at[0])
+def front_kernel(plan, *refs):
+    gain_ref, *sources = refs[:-6]
+    both_ref, normed_ref, stats_ref, proj_ref, w_front, sems = refs[-6:]
+    copies = fetch(plan["front"](), sources, w_front, sems.at[0])
+    plan["tokens"](sources, both_ref)
     frames, _, patches, _ = both_ref.shape
     rows = frames * SUB
     for group in range(patches // SUB):
@@ -86,11 +87,14 @@
     rows = frames * SUB
     count = counts_ref[0]
 
+    device = plan["device"]()
     place = [
         pltpu.make_async_copy(
-            front_ref.at[:, pl.ds(start, size)], proj.at[:, pl.ds(target, size)], sems.at[3]
+            front_ref.at[:, pl.ds(start, size)],
+            proj.at[:, pl.ds(pl.multiple_of(target, 128), size)],
+            sems.at[3],
         )
-        for start, target, size in plan["placed"]
+        for start, target, size in plan["placed"]()
     ]
     for copy in place:
         copy.start()
@@ -98,7 +102,10 @@
     outer = fetch(plan["outer"](), weight_refs, w_out, sems.at[1])
     again = fetch(plan["again"](), weight_refs, w_in, sems.at[2])
 
-    live = (lax.broadcasted_iota(jnp.int32, (rows, 1), 0) // SUB < count).astype(jnp.float32)
+    def real(index):
+        return ((index // SUB) ^ device) < count
+
+    live = real(lax.broadcasted_iota(jnp.int32, (rows, 1), 0)).astype(jnp.float32)
     for group in range(groups):
         here = pl.ds(group * rows, rows)
         grads[here, :] = (load_rows(both_ref, 1, group).astype(jnp.float32) * live).astype(
@@ -106,16 +113,15 @@
         )
     key = lax.broadcasted_iota(jnp.int32, (rows, 2 * rows), 0)
     query = lax.broadcasted_iota(jnp.int32, (rows, 2 * rows), 1)
-    bias[...] = jnp.where((query % SUB == key % SUB) & (key // SUB < count), 0.0, NEGATIVE)
+    bias[...] = jnp.where((query % SUB == key % SUB) & real(key), 0.0, NEGATIVE)
     lane = lax.broadcasted_iota(jnp.int32, (1, PAIR), 1)
     low_lanes = (lane < DH).astype(jnp.bfloat16)
     high_lanes = (lane >= DH).astype(jnp.bfloat16)
 
     wait(late)
-    for start, size in plan["missing"]:
-        proj[:, start : start + size] = dot(
-            normed_ref[...], w_in[:, start : start + size], NN
-        ).astype(jnp.bfloat16)
+    for start, size in plan["missing"]():
+        columns = pl.ds(pl.multiple_of(start, 128), size)
+        proj[:, columns] = dot(normed_ref[...], w_in[:, columns], NN).astype(jnp.bfloat16)
 
     wait(outer)
     step = min(width, 256)
@@ -185,7 +191,10 @@
             each(results)
 
     def store(which, group, value):
-        out_ref[:, which, group * SUB : (group + 1) * SUB, :] = value.reshape(frames, SUB, width)
+        for frame in range(frames):
+            out_ref[pl.ds(frame ^ device, 1), which, group * SUB : (group + 1) * SUB, :] = value[
+                frame * SUB : (frame + 1) * SUB
+            ].reshape(1, SUB, width)
 
     for group in range(groups):
         here = pl.ds(group * rows, rows)
@@ -214,42 +223,50 @@
         store(1, group, (cot + grad_rows).astype(jnp.bfloat16))
 
 
-def run_block(counts, gain, both, front_weights, late_weights, plan):
+def run_front(gain, shape, sources, plan):
+    frames, _, patches, width = shape
+    total = frames * patches
+    vmem = pl.BlockSpec(memory_space=pltpu.VMEM)
+    anywhere = pl.BlockSpec(memory_space=pl.ANY)
+    columns = plan["columns"]
+    return pl.pallas_call(
+        functools.partial(front_kernel, plan),
+        out_shape=(
+            jax.ShapeDtypeStruct(shape, jnp.bfloat16),
+            jax.ShapeDtypeStruct((total, width), jnp.bfloat16),
+            jax.ShapeDtypeStruct((total, 128), jnp.float32),
+            jax.ShapeDtypeStruct((total, columns), jnp.bfloat16),
+        ),
+        in_specs=[vmem] + [anywhere if wide else vmem for wide in plan["spread"]],
+        out_specs=(vmem, vmem, vmem, vmem),
+        scratch_shapes=[
+            pltpu.VMEM((width, columns), jnp.bfloat16),
+            pltpu.SemaphoreType.DMA((1,)),
+        ],
+        compiler_params=pltpu.CompilerParams(vmem_limit_bytes=VMEM_LIMIT),
+        cost_estimate=pl.CostEstimate(
+            flops=2 * total * width * columns,
+            bytes_accessed=2 * width * columns + 8 * total * width,
+            transcendentals=total,
+        ),
+        name="front",
+    )(gain, *sources)
+
+
+def run_main(counts, gain, fronted, weights, plan):
+    both, normed, stats, front = fronted
     frames, _, patches, width = both.shape
     total, rows = frames * patches, frames * SUB
     vmem = pl.BlockSpec(memory_space=pltpu.VMEM)
     smem = pl.BlockSpec(memory_space=pltpu.SMEM)
     anywhere = pl.BlockSpec(memory_space=pl.ANY)
-    shape = jax.ShapeDtypeStruct
-    params = pltpu.CompilerParams(vmem_limit_bytes=VMEM_LIMIT)
-    front_columns = sum(size for _, _, size in plan["placed"])
-    normed, stats, front = pl.pallas_call(
-        functools.partial(front_kernel, plan),
-        out_shape=(
-            shape((total, width), jnp.bfloat16),
-            shape((total, 128), jnp.float32),
-            shape((total, front_columns), jnp.bfloat16),
-        ),
-        in_specs=[vmem, vmem] + [anywhere] * len(front_weights),
-        out_specs=(vmem, vmem, vmem),
-        scratch_shapes=[
-            pltpu.VMEM((width, front_columns), jnp.bfloat16),
-            pltpu.SemaphoreType.DMA((1,)),
-        ],
-        compiler_params=params,
-        cost_estimate=pl.CostEstimate(
-            flops=2 * total * width * front_columns,
-            bytes_accessed=2 * width * front_columns + 8 * total * width,
-            transcendentals=total,
-        ),
-        name="front",
-    )(both, gain, *front_weights)
+    params = pltpu.CompilerParams(vmem_limit_bytes=VMEM_LIMIT if rows <= 128 else 2 * VMEM_LIMIT)
     chunk = 8 if rows <= 128 else 1
     return pl.pallas_call(
         functools.partial(main_kernel, plan),
-        out_shape=shape(both.shape, jnp.bfloat16),
+        out_shape=jax.ShapeDtypeStruct(both.shape, jnp.bfloat16),
         in_specs=[smem, vmem, vmem, vmem, vmem, anywhere]
-        + [anywhere] * (len(front_weights) + len(late_weights)),
+        + [anywhere] * len(weights),
         out_specs=vmem,
         scratch_shapes=[
             pltpu.VMEM((width, 3 * width), jnp.bfloat16),
@@ -273,7 +290,7 @@
             transcendentals=total * 2048,
         ),
         name="main",
-    )(counts, gain, both, normed, stats, front, *front_weights, *late_weights)
+    )(counts, gain, both, normed, stats, front, *weights)
 
 
 def swap(array, distance, devices):
@@ -305,96 +322,214 @@
     )(*arrays)
 
 
-def gather_two_ways(input_weights, output_weights, both, devices):
+def pack_kernel(patches, share, w_in, w_out, tokens, cot, joined, own, mine, to_x, to_y, held):
+    depth = w_in.shape[0]
+    half, block = depth // 2, 2 * share
+    device = lax.axis_index("frame")
+    chip, core = device // 2, device % 2
+    joined[:, : w_in.shape[1]] = w_in[...]
+    joined[:, w_in.shape[1] :] = w_out[...]
+    held[...] = jnp.zeros_like(held)
+    held[0, :patches] = tokens[0, 0]
+    held[1, :patches] = cot[0, 0]
+
+    def put(target, row, owner):
+        rows = pl.ds(pl.multiple_of(owner * share, share), share)
+        target[row : row + share, :] = held[0, rows, :]
+        target[row + share : row + block, :] = held[1, rows, :]
+
+    put(mine, 0, device)
+    own[:depth, :] = joined[...]
+    put(own, depth, device ^ 1)
+    for target, first, last, away, core_by in ((to_x, 0, half, 1, 0), (to_y, half, 0, 2, 1)):
+        target[:half, :] = joined[first : first + half, :]
+        put(target, half, (chip ^ away) * 2)
+        put(target, half + block, (chip ^ away) * 2 + 1)
+        target[half + 2 * block : depth + 2 * block, :] = joined[last : last + half, :]
+        put(target, depth + 2 * block, (chip ^ 3) * 2 + core_by)
+
+
+def turn_kernel(half, by_x, by_y, pair_x, pair_y, to_dx, to_dy):
+    to_dx[:half, :] = by_y[:half, :]
+    to_dx[half:, :] = pair_y[: 2 * half, :]
+    to_dy[:half, :] = by_x[half:, :]
+    to_dy[half:, :] = pair_x[2 * half :, :]
+
+
+def gather_in_rounds(input_weights, output_weights, tokens, cotangent, gain, share, devices):
     depth, in_columns = input_weights.shape
     out_columns = output_weights.shape[1]
-    early = in_columns * 2 // 3 // 128 * 128
-    late = in_columns - early
-    late_shard = join(1, output_weights, input_weights[:, early:])
-    late_whole = lax.all_gather(late_shard, ("clip", "frame"), axis=0)
-    late_whole = late_whole.reshape(4 * devices, depth, out_columns + late)
-
-    shard = input_weights[:, :early]
-    offsets = (0, 1, 3, 2)
-    held = [shard] + [
-        lax.ppermute(shard, "clip", [(c, c ^ offset) for c in range(4)]) for offset in offsets[1:]
+    _, _, patches, width = tokens.shape
+    half, block = depth // 2, 2 * share
+    vmem = pl.BlockSpec(memory_space=pltpu.VMEM)
+
+    def rows_of(count):
+        return jax.ShapeDtypeStruct((count, width), jnp.bfloat16)
+
+    joined, own, mine, to_x, to_y = pl.pallas_call(
+        functools.partial(pack_kernel, patches, share),
+        out_shape=tuple(
+            map(rows_of, (depth, depth + block, block, depth + 3 * block, depth + 3 * block))
+        ),
+        in_specs=[vmem] * 4,
+        out_specs=(vmem,) * 5,
+        scratch_shapes=[pltpu.VMEM((2, devices * share, width), jnp.bfloat16)],
+        name="pack",
+    )(input_weights, output_weights, tokens, cotangent)
+
+    def by_clip(array, offset):
+        return lax.ppermute(array, "clip", [(c, c ^ offset) for c in range(4)])
+
+    def across(array):
+        return [swap(array, 2, devices), swap(array, 4, devices)]
+
+    def other_core(arrays):
+        return [swap(array, 1, devices) for array in arrays]
+
+    one = by_clip(joined, 1)
+    first = [swap(to_x, 2, devices), swap(to_y, 4, devices)]
+    tail = half + 2 * block
+    first += [swap(first[1][tail:], 2, devices), swap(first[0][tail:], 4, devices)]
+    third = [by_clip(join(0, joined, one), 2)]
+    second = [one, *across(one)]
+    third[0], second[1], second[2] = lax.optimization_barrier((third[0], second[1], second[2]))
+    first_other = other_core([own, *first])
+    second_other = other_core(second)
+    third[0], first[2], first[3] = lax.optimization_barrier((third[0], first[2], first[3]))
+    ready = [joined, *first, *first_other, *second, *second_other]
+    third += across(third[0])
+
+    def tokens_in(sources, both_ref):
+        core = lax.axis_index("frame") % 2
+        mine_ref, _, x_ref, y_ref, dx_ref, dy_ref, own2, x2, y2, dx2, dy2 = sources[:11]
+        rows = pl.ds(pl.multiple_of(half + core * block, block), block)
+        behind = slice(half, half + block)
+
+        def diagonal(by_x, by_y):
+            return jnp.where(core == 0, by_y[behind, :], by_x[behind, :])
+
+        found = (
+            mine_ref[...], own2[depth : depth + block, :],
+            x_ref[rows, :], x2[rows, :], y_ref[rows, :], y2[rows, :],
+            diagonal(dx_ref, dy_ref), diagonal(dx2, dy2),
+        )
+        for distance, value in enumerate(found):
+            both_ref[distance] = value.reshape(2, share, width)
+
+    table = [
+        [(0, 0, 0, depth, 0)],
+        [(0, 2, 0, half, 0), (0, 2, tail, half, half)],
+        [(0, 4, 0, half, half), (0, 4, tail, half, 0)],
+        [(0, 6, 0, half, 0)],
+        [(0, 6, 0, half, half)],
     ]
-    both, held[1] = lax.optimization_barrier((both, held[1]))
-    both = lax.all_to_all(both, "frame", split_axis=0, concat_axis=0, tiled=True)
-    own = join(0, *held)
-    by_x, by_y = swap(own, 2, devices), swap(own, 4, devices)
-    by_x, both = lax.optimization_barrier((by_x, both))
-    middle = 2 * depth
-    arrays = [own, by_x, by_y, swap(by_y[:middle], 2, devices), swap(by_x[middle:], 4, devices)]
-    arrays += [swap(array, 1, devices) for array in arrays]
-
-    def front(stride=early):
+    others = [[(1, d, 0, depth, 0)] for d in (0, 2, 4)]
+    pairs = [[(2, d, 0, depth, 0), (3, d, depth, depth, 0)] for d in (0, 2, 4)]
+    pairs += [
+        [(1, 6, 0, half, 0), (2, 6, half, depth, 0)],
+        [(1, 6, 0, half, half), (3, 6, half, depth, 0)],
+    ]
+    arrays = []
+    for group in (table, others, pairs):
+        arrays += [(core, parts) for core in (0, 1) for parts in group]
+
+    def pieces(offsets, lanes, base):
         clip, frame = lax.axis_index("clip"), lax.axis_index("frame")
         found = []
-        for ref in range(10):
-            distance = (0, 2, 4, 6, 6)[ref % 5] ^ (ref // 5)
-            places = {3: (0, 1), 4: (2, 3)}.get(ref % 5, range(4))
-            for order, place in enumerate(places):
-                row = (frame ^ distance) * depth
-                column = (clip ^ offsets[place]) * stride
-                found.append((ref, None, order * depth, depth, (0, early), row, column))
+        for ref, (core, parts) in enumerate(arrays):
+            for offset, distance, first, rows, inside in parts:
+                if offset in offsets:
+                    row = (frame ^ distance ^ core) * depth + inside
+                    found.append((base + ref, None, first, rows, lanes, row, clip ^ offset))
         return found
 
-    def pieces(first, size, stride, offset):
-        return [
-            (10, c * devices + f, 0, depth, (first, size), f * depth, c * stride + offset)
-            for c in range(4)
-            for f in range(devices)
-        ]
+    def placed(parts, stride):
+        return [(*part[:-1], part[-1] * stride) for part in parts]
+
+    def compact():
+        return [(*part[:-1], 0) for part in pieces((0,), (0, in_columns), 1)]
+
+    inner, outer = (0, in_columns), (in_columns, out_columns)
+
+    def columns_of(offsets):
+        clip = lax.axis_index("clip")
+        return [(clip ^ offset) * in_columns for offset in offsets]
 
     plan = {
-        "front": front,
-        "again": lambda: front(in_columns),
-        "late": lambda: pieces(out_columns, late, in_columns, early),
-        "outer": lambda: pieces(0, out_columns, out_columns, 0),
-        "placed": [(c * early, c * in_columns, early) for c in range(4)],
-        "missing": [(c * in_columns + early, late) for c in range(4)],
+        "front": compact,
+        "tokens": tokens_in,
+        "columns": in_columns,
+        "spread": [False] * 11,
+        "device": lambda: lax.axis_index("frame"),
+        "late": lambda: placed(pieces((1, 2, 3), inner, 0), in_columns),
+        "again": lambda: placed(pieces((0,), inner, 0), in_columns),
+        "outer": lambda: placed(pieces((0, 1, 2, 3), outer, 0), out_columns),
+        "placed": lambda: [
+            (0, start, in_columns) for start in columns_of((0,))
+        ],
+        "missing": lambda: [(start, in_columns) for start in columns_of((1, 2, 3))],
     }
-    return arrays, [late_whole], plan, both
-
-
-def gather_plainly(input_weights, output_weights, both):
+    fronted = run_front(gain, (devices, 2, share, width), [mine, *ready[:10]], plan)
+    third[1], *fronted = lax.optimization_barrier((third[1], *fronted))
+    to_dx, to_dy = pl.pallas_call(
+        functools.partial(turn_kernel, half),
+        out_shape=(rows_of(depth + half), rows_of(depth + half)),
+        in_specs=[vmem] * 4,
+        out_specs=(vmem, vmem),
+        name="turn",
+    )(second[1], second[2], third[1], third[2])
+    third += [swap(to_dx, 2, devices), swap(to_dy, 4, devices)]
+    third += other_core(third)
+    return fronted, [*ready, *third], plan
+
+
+def gather_plainly(input_weights, output_weights, tokens, cotangent, gain, share, devices):
+    _, slots, patches, width = tokens.shape
     whole = []
     for weights in (input_weights, output_weights):
         columns = lax.all_gather(weights, "clip", axis=1, tiled=True)
         whole.append(lax.all_gather(columns, "frame", axis=0, tiled=True))
+
+    def by_destination(source):
+        padded = jnp.pad(source[0], ((0, 0), (0, devices * share - patches), (0, 0)))
+        return padded.reshape(slots, devices, share, width).transpose(1, 0, 2, 3)
+
+    both = jnp.stack([by_destination(tokens), by_destination(cotangent)], axis=2)
     both = lax.all_to_all(both, "frame", split_axis=0, concat_axis=0, tiled=True)
+    both = both.reshape(devices * slots, 2, share, width)
+
+    def tokens_in(sources, both_ref):
+        both_ref[...] = sources[1][...]
+
     inner, outer = [[(i, None, 0, w.shape[0], (0, w.shape[1]), 0, 0)] for i, w in enumerate(whole)]
     plan = {
         "front": lambda: inner,
+        "tokens": tokens_in,
+        "columns": whole[0].shape[1],
+        "spread": [True, False],
+        "device": lambda: 0,
+        "late": lambda: [],
         "again": lambda: inner,
-        "late": lambda: [],
         "outer": lambda: outer,
-        "placed": [(0, 0, whole[0].shape[1])],
-        "missing": [],
+        "placed": lambda: [(0, 0, whole[0].shape[1])],
+        "missing": lambda: [],
     }
-    return whole[:1], whole[1:], plan, both
+    return run_front(gain, both.shape, [whole[0], both], plan), whole, plan
 
 
 def per_device(clips, devices, tokens, counts, norm_gain, input_weights, output_weights, cotangent):
     _, slots, patches, width = tokens.shape
     share = -(-patches // devices)
     share = -(-share // SUB) * SUB
-    extra = devices * share - patches
-
-    def by_destination(source):
-        padded = jnp.pad(source[0], ((0, 0), (0, extra), (0, 0)))
-        return padded.reshape(slots, devices, share, width).transpose(1, 0, 2, 3)
-
-    both = jnp.stack([by_destination(tokens), by_destination(cotangent)], axis=2)
     depth, in_columns = input_weights.shape
-    fits = in_columns % 384 == 0 and output_weights.shape[1] % 128 == 0 and depth % 16 == 0
-    if clips == 4 and devices == 8 and fits:
-        front, late, plan, both = gather_two_ways(input_weights, output_weights, both, devices)
-    else:
-        front, late, plan, both = gather_plainly(input_weights, output_weights, both)
-    both = both.reshape(devices * slots, 2, share, width)
-    back = run_block(counts, norm_gain.reshape(1, width), both, front, late, plan)
+    fits = in_columns % 128 == 0 and output_weights.shape[1] % 128 == 0 and depth % 32 == 0
+    small = clips == 4 and devices == 8 and slots == 1 and fits
+    gather = gather_in_rounds if small else gather_plainly
+    gain = norm_gain.reshape(1, width)
+    fronted, weights, plan = gather(
+        input_weights, output_weights, tokens, cotangent, gain, share, devices
+    )
+    back = run_main(counts, gain, fronted, weights, plan)
     back = back.reshape(devices, slots, 2, share, width)
     back = lax.all_to_all(back, "frame", split_axis=0, concat_axis=0, tiled=True)
 

time: 130 us -> 115 us (0.88)
  between operations: 14.8 us -> 1.47 us
  local copies, waits for them, and re-layouts: 16.4 us -> 14.2 us
    ppermute x9 -> x23, starting transfers between devices: 5.54 us -> 13.5 us  [swap(): lax.ppermute(array, 'frame', [(f, f ^ distance) for f in range(devices)])]
    ppermute x3 -> x2, waiting for transfers between devices: 11.2 us -> 18.1 us  [by_clip(): return lax.ppermute(array, 'clip', [(c, c ^ offset) for c in range(4)])]
    all_gather x1 -> x0, waiting for transfers between devices: 6.62 us -> none  [gather_two_ways(): late_whole = lax.all_gather(late_shard, ('clip', 'frame'), axis=0)]
    all_to_all x1 -> x0, starting transfers between devices: 4.23 us -> none  [gather_two_ways(): lax.all_to_all(both, 'frame', split_axis=0, concat_axis=0, tiled=True)]
    slice x4 -> x2, local copies, waits for them, and re-layouts: 3.13 us -> 0.04 us  [the longest x1 0.02 us: gather_in_rounds(): first[1][tail:]]
    ppermute x3 -> x2, starting transfers between devices: 7.26 us -> 4.17 us  [by_clip(): return lax.ppermute(array, 'clip', [(c, c ^ offset) for c in range(4)])]
    unnamed x32 -> x46, local copies, waits for them, and re-layouts: 10.1 us -> 13.1 us
    pad x2 -> x0, local copies, waits for them, and re-layouts: 2.1 us -> none  [by_destination(): padded = jnp.pad(source[0], ((0, 0), (0, extra), (0, 0)))]
  transfers between devices with their start and end apart: 14 -> 25, of which waited for: 8 -> 14; matrix products, arithmetic and copies ran while one was open for 4% -> 0% of each run, Pallas kernels for 4% -> 5%
where the time goes in v6:
time: 115 us; the launch traced here: 114 us
  waiting for transfers between devices  41.8 us (36%)
  Pallas kernels  21 us (18%)
  blocking collectives  17.8 us (15%)
  starting transfers between devices  17.7 us (15%)
  local copies, waits for them, and re-layouts  14.2 us (12%)
  between operations  1.47 us (1%)
    ppermute x23, waiting for transfers between devices, swap(): lax.ppermute(array, 'frame', [(f, f ^ distance) for f in range(devices)])  23.7 us
    ppermute x2, waiting for transfers between devices, by_clip(): return lax.ppermute(array, 'clip', [(c, c ^ offset) for c in range(4)])  18.1 us
    all_to_all x1, blocking collectives, per_device(): lax.all_to_all(back, 'frame', split_axis=0, concat_axis=0, tiled=True)  17.8 us
    ppermute x23, starting transfers between devices, swap(): lax.ppermute(array, 'frame', [(f, f ^ distance) for f in range(devices)])  13.5 us
    unnamed x46, local copies, waits for them, and re-layouts  13.1 us
    pallas_call x1, Pallas kernels, run_main(): pl.pallas_call(functools.partial(main_kernel, plan), out_shape=jax.ShapeD...  12.6 us
    ppermute x2, starting transfers between devices, by_clip(): return lax.ppermute(array, 'clip', [(c, c ^ offset) for c in range(4)])  4.17 us
    pallas_call x1, Pallas kernels, gather_in_rounds(): pl.pallas_call(functools.partial(pack_kernel, patches, share), out_shape=...  2.61 us
  transfers between devices with their start and end apart: 25, of which 14 were waited for; matrix products, arithmetic and copies ran while one was open for 0% of the time, Pallas kernels for 5%

profile of v6, /device:TPU:0, one launch (start us, length us, event | category | flops | bytes accessed | tf_op | source)
XLA Modules:
  0.0 113.9 jit_solution(13088708590593532200)
XLA Ops:
  0.6 2.6 %pack.1 = (bf16[128,1024]{1,0:T(8,128)(2,1)}, bf16[192,1024]{1,0:T(8,128)(2,1)}, bf16[64,1024]{1,0:T(8,128)(2,1)}, bf16[320,1024]{1,0:T(8,128)(2,1)}, bf16[320,1024]{1,0:T(8,128)(2,1)}) custom-call(bf16[128,768]{1,0:T(8,128)(2,1)} %w_in.1, bf16[128,256]{1,0:T(8,128)(2,1)} %w_out.1, bf16[1,1,196,1024]{3,2,1,0:T(8,128)(2,1)} %tokens.1, ...), custom_call_target="tpu_custom_call" | custom-call | tf_op jit(solution)/shard_map/pack/pallas_call | solution.py:369
  3.2 3.0 %collective-permute-start.4 = (bf16[320,1024]{1,0:T(8,128)(2,1)}, bf16[320,1024]{1,0:T(8,128)(2,1)S(1)}, u32[]{:S(2)}, u32[]{:S(2)}) collective-permute-start(bf16[320,1024]{1,0:T(8,128)(2,1)} %get-tuple-element.26), channel_id=1, source_target_pairs={{0,4},{1,5},{2,6},{3,7},{4,0},{5,1},{6,2},{7,3},{8,12},{9,13},{10,... | collective-permute-start | bytes 1966088 | tf_op jit(solution)/shard_map/ppermute | solution.py:297
  6.2 1.5 %collective-permute-start.6 = (bf16[320,1024]{1,0:T(8,128)(2,1)}, bf16[320,1024]{1,0:T(8,128)(2,1)S(1)}, u32[]{:S(2)}, u32[]{:S(2)}) collective-permute-start(bf16[320,1024]{1,0:T(8,128)(2,1)} %get-tuple-element.27), channel_id=1, source_target_pairs={{0,2},{1,3},{2,0},{3,1},{4,6},{5,7},{6,4},{7,5},{8,10},{9,11},{10,... | collective-permute-start | bytes 1966088 | tf_op jit(solution)/shard_map/ppermute | solution.py:297
  7.7 1.6 %collective-permute-start = (bf16[128,1024]{1,0:T(8,128)(2,1)}, bf16[128,1024]{1,0:T(8,128)(2,1)}, u32[]{:S(2)}, u32[]{:S(2)}) collective-permute-start(bf16[128,1024]{1,0:T(8,128)(2,1)} %get-tuple-element.24.refs_0_.refs_2_.rest_0_), channel_id=1, source_target_pairs={{0,8},{8,0},{16,24},{24,16},{1,9},{9,1},{17,25},{25,17},{2,10},{10... | collective-permute-start | bytes 786440 | tf_op jit(solution)/shard_map/ppermute | solution.py:381
  9.3 6.2 %collective-permute-done.refs_1_.rest_10_ = bf16[128,1024]{1,0:T(8,128)(2,1)} collective-permute-done((bf16[128,1024]{1,0:T(8,128)(2,1)}, bf16[128,1024]{1,0:T(8,128)(2,1)}, u32[]{:S(2)}, u32[]{:S(2)}) %collective-permute-start) | collective-permute-done | bytes 262176 | tf_op jit(solution)/shard_map/ppermute | solution.py:381
  15.5 1.9 %join.1 = bf16[256,1024]{1,0:T(8,128)(2,1)} custom-call(bf16[128,1024]{1,0:T(8,128)(2,1)} %get-tuple-element.24.refs_0_.refs_2_.rest_0_, bf16[128,1024]{1,0:T(8,128)(2,1)} %collective-permute-done.refs_1_.rest_10_), custom_call_target="tpu_custom_call" | custom-call | tf_op jit(solution)/shard_map/join/pallas_call | solution.py:316
  17.4 2.6 %collective-permute-start.1 = (bf16[256,1024]{1,0:T(8,128)(2,1)}, bf16[256,1024]{1,0:T(8,128)(2,1)S(1)}, u32[]{:S(2)}, u32[]{:S(2)}) collective-permute-start(bf16[256,1024]{1,0:T(8,128)(2,1)} %join.1), channel_id=1, source_target_pairs={{0,16},{8,24},{16,0},{24,8},{1,17},{9,25},{17,1},{25,9},{2,18},{10... | collective-permute-start | bytes 1572872 | tf_op jit(solution)/shard_map/ppermute | solution.py:381
  19.9 0.5 collective-permute-start.3
  20.5 0.5 collective-permute-start.2
  21.0 0.7 collective-permute-done.4.refs_4_.rest_2_
  21.7 2.4 %collective-permute-done.6.refs_3_.rest_1_ = bf16[320,1024]{1,0:T(8,128)(2,1)S(1)} collective-permute-done((bf16[320,1024]{1,0:T(8,128)(2,1)}, bf16[320,1024]{1,0:T(8,128)(2,1)S(1)}, u32[]{:S(2)}, u32[]{:S(2)}) %collective-permute-start.6) | collective-permute-done | bytes 655392 | tf_op jit(solution)/shard_map/ppermute | solution.py:297
  24.1 1.5 %collective-permute-start.5 = (bf16[128,1024]{1,0:T(8,128)(2,1)S(1)}, bf16[128,1024]{1,0:T(8,128)(2,1)S(1)}, u32[]{:S(2)}, u32[]{:S(2)}) collective-permute-start(bf16[128,1024]{1,0:T(8,128)(2,1)S(1)} %slice.24), channel_id=1, source_target_pairs={{0,2},{1,3},{2,0},{3,1},{4,6},{5,7},{6,4},{7,5},{8,10},{9,11},{10,... | collective-permute-start | bytes 786440 | tf_op jit(solution)/shard_map/ppermute | solution.py:297
  25.6 1.3 %collective-permute-done.3.by_y.rest_12_ = bf16[128,1024]{1,0:T(8,128)(2,1)} collective-permute-done((bf16[128,1024]{1,0:T(8,128)(2,1)}, bf16[128,1024]{1,0:T(8,128)(2,1)}, u32[]{:S(2)}, u32[]{:S(2)}) %collective-permute-start.3) | collective-permute-done | bytes 262176 | tf_op jit(solution)/shard_map/ppermute | solution.py:297
  26.9 1.7 %collective-permute-start.7 = (bf16[128,1024]{1,0:T(8,128)(2,1)S(1)}, bf16[128,1024]{1,0:T(8,128)(2,1)S(1)}, u32[]{:S(2)}, u32[]{:S(2)}) collective-permute-start(bf16[128,1024]{1,0:T(8,128)(2,1)S(1)} %slice.25), channel_id=1, source_target_pairs={{0,4},{1,5},{2,6},{3,7},{4,0},{5,1},{6,2},{7,3},{8,12},{9,13},{10,... | collective-permute-start | bytes 786440 | tf_op jit(solution)/shard_map/ppermute | solution.py:297
  28.6 1.4 %collective-permute-done.2.by_x.rest_11_ = bf16[128,1024]{1,0:T(8,128)(2,1)} collective-permute-done((bf16[128,1024]{1,0:T(8,128)(2,1)}, bf16[128,1024]{1,0:T(8,128)(2,1)}, u32[]{:S(2)}, u32[]{:S(2)}) %collective-permute-start.2) | collective-permute-done | bytes 262176 | tf_op jit(solution)/shard_map/ppermute | solution.py:297
  30.0 11.9 %collective-permute-done.1.rest_16_ = bf16[256,1024]{1,0:T(8,128)(2,1)S(1)} collective-permute-done((bf16[256,1024]{1,0:T(8,128)(2,1)}, bf16[256,1024]{1,0:T(8,128)(2,1)S(1)}, u32[]{:S(2)}, u32[]{:S(2)}) %collective-permute-start.1) | collective-permute-done | bytes 524320 | tf_op jit(solution)/shard_map/ppermute | solution.py:381
  41.9 0.5 collective-permute-start.12
  42.4 0.0 collective-permute-done.7.refs_6_.rest_4_
  42.4 0.5 collective-permute-start.8
  42.9 0.6 collective-permute-start.17
  43.6 0.8 collective-permute-done.12.refs_10_.rest_8_
  44.4 0.1 collective-permute-start.13
  44.5 1.4 %collective-permute-done.13.refs_11_.rest_9_ = bf16[128,1024]{1,0:T(8,128)(2,1)S(1)} collective-permute-done((bf16[128,1024]{1,0:T(8,128)(2,1)S(1)}, bf16[128,1024]{1,0:T(8,128)(2,1)S(1)}, u32[]{:S(2)}, u32[]{:S(2)}) %collective-permute-start.13) | collective-permute-done | bytes 262176 | tf_op jit(solution)/shard_map/ppermute | solution.py:297
  45.9 0.1 collective-permute-start.14
  46.0 0.4 collective-permute-start.15
  46.4 0.0 collective-permute-done.10.refs_8_.rest_6_
  46.4 0.1 collective-permute-start.16
  46.6 1.6 %front.1 = (bf16[8,2,32,1024]{3,2,1,0:T(8,128)(2,1)S(1)}, bf16[256,1024]{1,0:T(8,128)(2,1)S(1)}, f32[256,128]{1,0:T(8,128)S(1)}, bf16[256,768]{1,0:T(8,128)(2,1)S(1)}) custom-call(f32[1,1024]{1,0:T(1,128)S(1)} %bitcast.11, bf16[64,1024]{1,0:T(8,128)(2,1)S(1)} %copy-done.21, bf16[128,1024]{1,0:T(8,128)(2,1)S(1)} %copy-done, ...), custom_call_target="tpu_custom_call" | custom-call | flops 402653184 | bytes 3670016 | tf_op jit(solution)/shard_map/front/pallas_call | solution.py:232
  48.3 1.0 copy-done.5
  49.3 0.8 copy-done.17
  50.0 0.7 copy-done.19
  50.8 5.5 %collective-permute-done.8.pair_x.rest_17_ = bf16[256,1024]{1,0:T(8,128)(2,1)S(1)} collective-permute-done((bf16[256,1024]{1,0:T(8,128)(2,1)S(1)}, bf16[256,1024]{1,0:T(8,128)(2,1)S(1)}, u32[]{:S(2)}, u32[]{:S(2)}) %collective-permute-start.8) | collective-permute-done | bytes 524320 | tf_op jit(solution)/shard_map/ppermute | solution.py:297
  56.3 0.4 collective-permute-done.17.pair_y.rest_18_
  56.7 0.4 copy-done.1
  57.1 2.3 %turn.1 = (bf16[192,1024]{1,0:T(8,128)(2,1)}, bf16[192,1024]{1,0:T(8,128)(2,1)}) custom-call(bf16[128,1024]{1,0:T(8,128)(2,1)} %collective-permute-done.2.by_x.rest_11_, bf16[128,1024]{1,0:T(8,128)(2,1)} %collective-permute-done.3.by_y.rest_12_, bf16[256,1024]{1,0:T(8,128)(2,1)} %copy-done.1, bf16[256,1024]{1,0:T(8,128)(2,1)} %collective-permute-done.17.pair_y.rest_18_), custom_call_target="tpu_custom_call" | custom-call | tf_op jit(solution)/shard_map/turn/pallas_call | solution.py:474
  59.4 1.1 collective-permute-start.18
  60.5 0.5 collective-permute-start.19
  61.0 0.0 collective-permute-done.14.rest_13_
  61.0 0.0 collective-permute-start.20
  61.0 0.0 collective-permute-done.15.rest_14_
  61.0 0.5 collective-permute-start.22
  61.5 0.0 collective-permute-done.16.rest_15_
  61.5 0.1 collective-permute-start.21
  61.6 8.4 %collective-permute-done.18.rest_19_ = bf16[192,1024]{1,0:T(8,128)(2,1)S(1)} collective-permute-done((bf16[192,1024]{1,0:T(8,128)(2,1)}, bf16[192,1024]{1,0:T(8,128)(2,1)S(1)}, u32[]{:S(2)}, u32[]{:S(2)}) %collective-permute-start.18) | collective-permute-done | bytes 393248 | tf_op jit(solution)/shard_map/ppermute | solution.py:297
  70.0 0.0 collective-permute-start.23
  70.0 0.4 collective-permute-done.19.rest_20_
  70.3 0.1 collective-permute-start.24
  71.2 0.0 collective-permute-done.22.rest_23_
  71.2 0.5 collective-permute-done.23.rest_24_
  71.7 0.6 collective-permute-done.24.rest_25_
  72.3 1.0 copy-done.2
  73.3 1.0 copy-done.4
  74.3 1.2 %copy-done.6 = bf16[8,2,32,1024]{3,2,1,0:T(8,128)(2,1)S(1)} copy-done((bf16[8,2,32,1024]{3,2,1,0:T(8,128)(2,1)S(1)}, bf16[8,2,32,1024]{3,2,1,0:T(8,128)(2,1)}, u32[]{:S(2)}) %copy-start.6) | copy-done | bytes 1048600
  75.5 0.9 copy-done.8
  76.5 0.9 copy-done.10
  77.4 0.9 copy-done.12
  78.4 0.9 copy-done.14
  79.3 1.0 copy-done.16
  80.4 1.0 copy-done.18
  81.4 1.0 copy-done.20
  82.4 12.6 %main.1 = bf16[8,2,32,1024]{3,2,1,0:T(8,128)(2,1)S(1)} custom-call(s32[1]{0:T(128)S(6)} %copy.9.counts_ref, f32[1,1024]{1,0:T(1,128)S(1)} %bitcast.12, bf16[8,2,32,1024]{3,2,1,0:T(8,128)(2,1)S(1)} %copy-done.6, bf16[256,1024]{1,0:T(8,128)(2,1)S(1)} %copy-done.18, f32[256,128]{1,0:T(8,128)S(1)} %get-tuple-element.39.stats_ref, ...), custom_call_target="tpu_custom_call" | custom-call | flops 3221225472 | bytes 10485760 | tf_op jit(solution)/shard_map/main/pallas_call | solution.py:265
  95.1 17.8 %all_to_all.5 = bf16[8,1,2,32,1024]{4,3,2,1,0:T(8,128)(2,1)S(1)} all-to-all(bf16[8,1,2,32,1024]{4,3,2,1,0:T(8,128)(2,1)S(1)} %bitcast.10), channel_id=1, replica_groups=mesh['clip'=4,'frame'=8] {'frame'}, dimensions={0} | all-to-all | bytes 2097152 | tf_op jit(solution)/shard_map/all_to_all | solution.py:534
  112.8 0.1 fusion
  112.9 0.9 slice_bitcast_fusion
  (42 shorter events, 0.1 us)
Async XLA Ops:
  3.2 18.4 %collective-permute-start.4 = (bf16[320,1024]{1,0:T(8,128)(2,1)}, bf16[320,1024]{1,0:T(8,128)(2,1)S(1)}, u32[]{:S(2)}, u32[]{:S(2)}) collective-permute-start(bf16[320,1024]{1,0:T(8,128)(2,1)} %get-tuple-element.26), channel_id=1, source_target_pairs={{0,4},{1,5},{2,6},{3,7},{4,0},{5,1},{6,2},{7,3},{8,12},{9,13},{10,... | collective-permute-start | bytes 1966088 | tf_op jit(solution)/shard_map/ppermute | solution.py:297
  6.2 17.9 %collective-permute-start.6 = (bf16[320,1024]{1,0:T(8,128)(2,1)}, bf16[320,1024]{1,0:T(8,128)(2,1)S(1)}, u32[]{:S(2)}, u32[]{:S(2)}) collective-permute-start(bf16[320,1024]{1,0:T(8,128)(2,1)} %get-tuple-element.27), channel_id=1, source_target_pairs={{0,2},{1,3},{2,0},{3,1},{4,6},{5,7},{6,4},{7,5},{8,10},{9,11},{10,... | collective-permute-start | bytes 1966088 | tf_op jit(solution)/shard_map/ppermute | solution.py:297
  7.7 7.8 %collective-permute-start = (bf16[128,1024]{1,0:T(8,128)(2,1)}, bf16[128,1024]{1,0:T(8,128)(2,1)}, u32[]{:S(2)}, u32[]{:S(2)}) collective-permute-start(bf16[128,1024]{1,0:T(8,128)(2,1)} %get-tuple-element.24.refs_0_.refs_2_.rest_0_), channel_id=1, source_target_pairs={{0,8},{8,0},{16,24},{24,16},{1,9},{9,1},{17,25},{25,17},{2,10},{10... | collective-permute-start | bytes 786440 | tf_op jit(solution)/shard_map/ppermute | solution.py:381
  17.4 24.5 %collective-permute-start.1 = (bf16[256,1024]{1,0:T(8,128)(2,1)}, bf16[256,1024]{1,0:T(8,128)(2,1)S(1)}, u32[]{:S(2)}, u32[]{:S(2)}) collective-permute-start(bf16[256,1024]{1,0:T(8,128)(2,1)} %join.1), channel_id=1, source_target_pairs={{0,16},{8,24},{16,0},{24,8},{1,17},{9,25},{17,1},{25,9},{2,18},{10... | collective-permute-start | bytes 1572872 | tf_op jit(solution)/shard_map/ppermute | solution.py:381
  19.9 6.9 %collective-permute-start.3 = (bf16[128,1024]{1,0:T(8,128)(2,1)}, bf16[128,1024]{1,0:T(8,128)(2,1)}, u32[]{:S(2)}, u32[]{:S(2)}) collective-permute-start(bf16[128,1024]{1,0:T(8,128)(2,1)} %collective-permute-done.refs_1_.rest_10_), channel_id=1, source_target_pairs={{0,4},{1,5},{2,6},{3,7},{4,0},{5,1},{6,2},{7,3},{8,12},{9,13},{10,... | collective-permute-start | bytes 786440 | tf_op jit(solution)/shard_map/ppermute | solution.py:297
  20.5 9.6 %collective-permute-start.2 = (bf16[128,1024]{1,0:T(8,128)(2,1)}, bf16[128,1024]{1,0:T(8,128)(2,1)}, u32[]{:S(2)}, u32[]{:S(2)}) collective-permute-start(bf16[128,1024]{1,0:T(8,128)(2,1)} %collective-permute-done.refs_1_.rest_10_), channel_id=1, source_target_pairs={{0,2},{1,3},{2,0},{3,1},{4,6},{5,7},{6,4},{7,5},{8,10},{9,11},{10,... | collective-permute-start | bytes 786440 | tf_op jit(solution)/shard_map/ppermute | solution.py:297
  21.7 21.3 %collective-permute-start.9 = (bf16[192,1024]{1,0:T(8,128)(2,1)}, bf16[192,1024]{1,0:T(8,128)(2,1)S(1)}, u32[]{:S(2)}, u32[]{:S(2)}) collective-permute-start(bf16[192,1024]{1,0:T(8,128)(2,1)} %get-tuple-element.32), channel_id=1, source_target_pairs={{0,1},{1,0},{2,3},{3,2},{4,5},{5,4},{6,7},{7,6},{8,9},{9,8},{10,11... | collective-permute-start | bytes 1179656 | tf_op jit(solution)/shard_map/ppermute | solution.py:297
  21.7 24.9 %copy-start = (bf16[128,1024]{1,0:T(8,128)(2,1)S(1)}, bf16[128,1024]{1,0:T(8,128)(2,1)}, u32[]{:S(2)}) copy-start(bf16[128,1024]{1,0:T(8,128)(2,1)} %get-tuple-element.24.refs_0_.refs_2_.rest_0_) | copy-start | bytes 786436
  21.7 24.9 %copy-start.21 = (bf16[64,1024]{1,0:T(8,128)(2,1)S(1)}, bf16[64,1024]{1,0:T(8,128)(2,1)}, u32[]{:S(2)}) copy-start(bf16[64,1024]{1,0:T(8,128)(2,1)} %get-tuple-element.29.refs_1_) | copy-start | bytes 393220
  24.1 17.8 %collective-permute-start.5 = (bf16[128,1024]{1,0:T(8,128)(2,1)S(1)}, bf16[128,1024]{1,0:T(8,128)(2,1)S(1)}, u32[]{:S(2)}, u32[]{:S(2)}) collective-permute-start(bf16[128,1024]{1,0:T(8,128)(2,1)S(1)} %slice.24), channel_id=1, source_target_pairs={{0,2},{1,3},{2,0},{3,1},{4,6},{5,7},{6,4},{7,5},{8,10},{9,11},{10,... | collective-permute-start | bytes 786440 | tf_op jit(solution)/shard_map/ppermute | solution.py:297
  25.6 21.0 %copy-start.22 = (f32[1024]{0:T(1024)S(1)}, f32[1024]{0:T(1024)}, u32[]{:S(2)}) copy-start(f32[1024]{0:T(1024)} %param.8) | copy-start | bytes 12292
  26.9 15.5 %collective-permute-start.7 = (bf16[128,1024]{1,0:T(8,128)(2,1)S(1)}, bf16[128,1024]{1,0:T(8,128)(2,1)S(1)}, u32[]{:S(2)}, u32[]{:S(2)}) collective-permute-start(bf16[128,1024]{1,0:T(8,128)(2,1)S(1)} %slice.25), channel_id=1, source_target_pairs={{0,4},{1,5},{2,6},{3,7},{4,0},{5,1},{6,2},{7,3},{8,12},{9,13},{10,... | collective-permute-start | bytes 786440 | tf_op jit(solution)/shard_map/ppermute | solution.py:297
  30.0 16.0 %collective-permute-start.11 = (bf16[320,1024]{1,0:T(8,128)(2,1)S(1)}, bf16[320,1024]{1,0:T(8,128)(2,1)S(1)}, u32[]{:S(2)}, u32[]{:S(2)}) collective-permute-start(bf16[320,1024]{1,0:T(8,128)(2,1)S(1)} %collective-permute-done.4.refs_4_.rest_2_), channel_id=1, source_target_pairs={{0,1},{1,0},{2,3},{3,2},{4,5},{5,4},{6,7},{7,6},{8,9},{9,8},{10,11... | collective-permute-start | bytes 1966088 | tf_op jit(solution)/shard_map/ppermute | solution.py:297
  41.9 6.3 %copy-start.15 = (bf16[256,1024]{1,0:T(8,128)(2,1)}, bf16[256,1024]{1,0:T(8,128)(2,1)S(1)}, u32[]{:S(2)}) copy-start(bf16[256,1024]{1,0:T(8,128)(2,1)S(1)} %collective-permute-done.1.rest_16_) | copy-start | bytes 1572868
  41.9 4.5 %collective-permute-start.10 = (bf16[320,1024]{1,0:T(8,128)(2,1)S(1)}, bf16[320,1024]{1,0:T(8,128)(2,1)S(1)}, u32[]{:S(2)}, u32[]{:S(2)}) collective-permute-start(bf16[320,1024]{1,0:T(8,128)(2,1)S(1)} %collective-permute-done.6.refs_3_.rest_1_), channel_id=1, source_target_pairs={{0,1},{1,0},{2,3},{3,2},{4,5},{5,4},{6,7},{7,6},{8,9},{9,8},{10,11... | collective-permute-start | bytes 1966088 | tf_op jit(solution)/shard_map/ppermute | solution.py:297
  41.9 6.3 %copy-start.7 = (bf16[128,1024]{1,0:T(8,128)(2,1)}, bf16[128,1024]{1,0:T(8,128)(2,1)S(1)}, u32[]{:S(2)}) copy-start(bf16[128,1024]{1,0:T(8,128)(2,1)S(1)} %collective-permute-done.5.refs_5_.rest_3_) | copy-start | bytes 786436
  41.9 2.5 %collective-permute-start.12 = (bf16[128,1024]{1,0:T(8,128)(2,1)S(1)}, bf16[128,1024]{1,0:T(8,128)(2,1)S(1)}, u32[]{:S(2)}, u32[]{:S(2)}) collective-permute-start(bf16[128,1024]{1,0:T(8,128)(2,1)S(1)} %collective-permute-done.5.refs_5_.rest_3_), channel_id=1, source_target_pairs={{0,1},{1,0},{2,3},{3,2},{4,5},{5,4},{6,7},{7,6},{8,9},{9,8},{10,11... | collective-permute-start | bytes 786440 | tf_op jit(solution)/shard_map/ppermute | solution.py:297
  42.4 5.8 %copy-start.9 = (bf16[128,1024]{1,0:T(8,128)(2,1)}, bf16[128,1024]{1,0:T(8,128)(2,1)S(1)}, u32[]{:S(2)}) copy-start(bf16[128,1024]{1,0:T(8,128)(2,1)S(1)} %collective-permute-done.7.refs_6_.rest_4_) | copy-start | bytes 786436
  42.4 13.9 %collective-permute-start.8 = (bf16[256,1024]{1,0:T(8,128)(2,1)S(1)}, bf16[256,1024]{1,0:T(8,128)(2,1)S(1)}, u32[]{:S(2)}, u32[]{:S(2)}) collective-permute-start(bf16[256,1024]{1,0:T(8,128)(2,1)S(1)} %collective-permute-done.1.rest_16_), channel_id=1, source_target_pairs={{0,2},{1,3},{2,0},{3,1},{4,6},{5,7},{6,4},{7,5},{8,10},{9,11},{10,... | collective-permute-start | bytes 1572872 | tf_op jit(solution)/shard_map/ppermute | solution.py:297
  42.9 5.3 %copy-start.3 = (bf16[192,1024]{1,0:T(8,128)(2,1)}, bf16[192,1024]{1,0:T(8,128)(2,1)S(1)}, u32[]{:S(2)}) copy-start(bf16[192,1024]{1,0:T(8,128)(2,1)S(1)} %collective-permute-done.9.refs_7_.rest_5_) | copy-start | bytes 1179652
  42.9 13.7 %collective-permute-start.17 = (bf16[256,1024]{1,0:T(8,128)(2,1)S(1)}, bf16[256,1024]{1,0:T(8,128)(2,1)}, u32[]{:S(2)}, u32[]{:S(2)}) collective-permute-start(bf16[256,1024]{1,0:T(8,128)(2,1)S(1)} %collective-permute-done.1.rest_16_), channel_id=1, source_target_pairs={{0,4},{1,5},{2,6},{3,7},{4,0},{5,1},{6,2},{7,3},{8,12},{9,13},{10,... | collective-permute-start | bytes 1572872 | tf_op jit(solution)/shard_map/ppermute | solution.py:297
  44.4 3.9 %copy-start.11 = (bf16[128,1024]{1,0:T(8,128)(2,1)}, bf16[128,1024]{1,0:T(8,128)(2,1)S(1)}, u32[]{:S(2)}) copy-start(bf16[128,1024]{1,0:T(8,128)(2,1)S(1)} %collective-permute-done.12.refs_10_.rest_8_) | copy-start | bytes 786436
  44.4 1.5 %collective-permute-start.13 = (bf16[128,1024]{1,0:T(8,128)(2,1)S(1)}, bf16[128,1024]{1,0:T(8,128)(2,1)S(1)}, u32[]{:S(2)}, u32[]{:S(2)}) collective-permute-start(bf16[128,1024]{1,0:T(8,128)(2,1)S(1)} %collective-permute-done.7.refs_6_.rest_4_), channel_id=1, source_target_pairs={{0,1},{1,0},{2,3},{3,2},{4,5},{5,4},{6,7},{7,6},{8,9},{9,8},{10,11... | collective-permute-start | bytes 786440 | tf_op jit(solution)/shard_map/ppermute | solution.py:297
  45.9 2.3 %copy-start.13 = (bf16[128,1024]{1,0:T(8,128)(2,1)}, bf16[128,1024]{1,0:T(8,128)(2,1)S(1)}, u32[]{:S(2)}) copy-start(bf16[128,1024]{1,0:T(8,128)(2,1)S(1)} %collective-permute-done.13.refs_11_.rest_9_) | copy-start | bytes 786436
  45.9 15.1 %collective-permute-start.14 = (bf16[128,1024]{1,0:T(8,128)(2,1)}, bf16[128,1024]{1,0:T(8,128)(2,1)}, u32[]{:S(2)}, u32[]{:S(2)}) collective-permute-start(bf16[128,1024]{1,0:T(8,128)(2,1)} %collective-permute-done.refs_1_.rest_10_), channel_id=1, source_target_pairs={{0,1},{1,0},{2,3},{3,2},{4,5},{5,4},{6,7},{7,6},{8,9},{9,8},{10,11... | collective-permute-start | bytes 786440 | tf_op jit(solution)/shard_map/ppermute | solution.py:297
  46.0 14.9 %collective-permute-start.15 = (bf16[128,1024]{1,0:T(8,128)(2,1)}, bf16[128,1024]{1,0:T(8,128)(2,1)}, u32[]{:S(2)}, u32[]{:S(2)}) collective-permute-start(bf16[128,1024]{1,0:T(8,128)(2,1)} %collective-permute-done.2.by_x.rest_11_), channel_id=1, source_target_pairs={{0,1},{1,0},{2,3},{3,2},{4,5},{5,4},{6,7},{7,6},{8,9},{9,8},{10,11... | collective-permute-start | bytes 786440 | tf_op jit(solution)/shard_map/ppermute | solution.py:297
  46.4 15.1 %collective-permute-start.16 = (bf16[128,1024]{1,0:T(8,128)(2,1)}, bf16[128,1024]{1,0:T(8,128)(2,1)}, u32[]{:S(2)}, u32[]{:S(2)}) collective-permute-start(bf16[128,1024]{1,0:T(8,128)(2,1)} %collective-permute-done.3.by_y.rest_12_), channel_id=1, source_target_pairs={{0,1},{1,0},{2,3},{3,2},{4,5},{5,4},{6,7},{7,6},{8,9},{9,8},{10,11... | collective-permute-start | bytes 786440 | tf_op jit(solution)/shard_map/ppermute | solution.py:297
  48.2 1.0 copy-start.5
  49.3 0.8 copy-start.17
  50.0 0.7 copy-start.19
  56.3 0.8 copy-start.1
  59.4 10.6 %collective-permute-start.18 = (bf16[192,1024]{1,0:T(8,128)(2,1)}, bf16[192,1024]{1,0:T(8,128)(2,1)S(1)}, u32[]{:S(2)}, u32[]{:S(2)}) collective-permute-start(bf16[192,1024]{1,0:T(8,128)(2,1)} %get-tuple-element.44), channel_id=1, source_target_pairs={{0,2},{1,3},{2,0},{3,1},{4,6},{5,7},{6,4},{7,5},{8,10},{9,11},{10,... | collective-permute-start | bytes 1179656 | tf_op jit(solution)/shard_map/ppermute | solution.py:297
  60.5 9.9 %collective-permute-start.19 = (bf16[192,1024]{1,0:T(8,128)(2,1)}, bf16[192,1024]{1,0:T(8,128)(2,1)S(1)}, u32[]{:S(2)}, u32[]{:S(2)}) collective-permute-start(bf16[192,1024]{1,0:T(8,128)(2,1)} %get-tuple-element.45), channel_id=1, source_target_pairs={{0,4},{1,5},{2,6},{3,7},{4,0},{5,1},{6,2},{7,3},{8,12},{9,13},{10,... | collective-permute-start | bytes 1179656 | tf_op jit(solution)/shard_map/ppermute | solution.py:297
  61.0 10.2 %collective-permute-start.20 = (bf16[256,1024]{1,0:T(8,128)(2,1)}, bf16[256,1024]{1,0:T(8,128)(2,1)S(1)}, u32[]{:S(2)}, u32[]{:S(2)}) collective-permute-start(bf16[256,1024]{1,0:T(8,128)(2,1)} %copy-done.15), channel_id=1, source_target_pairs={{0,1},{1,0},{2,3},{3,2},{4,5},{5,4},{6,7},{7,6},{8,9},{9,8},{10,11... | collective-permute-start | bytes 1572872 | tf_op jit(solution)/shard_map/ppermute | solution.py:297
  61.0 10.2 %collective-permute-start.22 = (bf16[256,1024]{1,0:T(8,128)(2,1)}, bf16[256,1024]{1,0:T(8,128)(2,1)S(1)}, u32[]{:S(2)}, u32[]{:S(2)}) collective-permute-start(bf16[256,1024]{1,0:T(8,128)(2,1)} %collective-permute-done.17.pair_y.rest_18_), channel_id=1, source_target_pairs={{0,1},{1,0},{2,3},{3,2},{4,5},{5,4},{6,7},{7,6},{8,9},{9,8},{10,11... | collective-permute-start | bytes 1572872 | tf_op jit(solution)/shard_map/ppermute | solution.py:297
  61.5 9.7 %collective-permute-start.21 = (bf16[256,1024]{1,0:T(8,128)(2,1)}, bf16[256,1024]{1,0:T(8,128)(2,1)S(1)}, u32[]{:S(2)}, u32[]{:S(2)}) collective-permute-start(bf16[256,1024]{1,0:T(8,128)(2,1)} %copy-done.1), channel_id=1, source_target_pairs={{0,1},{1,0},{2,3},{3,2},{4,5},{5,4},{6,7},{7,6},{8,9},{9,8},{10,11... | collective-permute-start | bytes 1572872 | tf_op jit(solution)/shard_map/ppermute | solution.py:297
  70.0 1.7 %collective-permute-start.23 = (bf16[192,1024]{1,0:T(8,128)(2,1)S(1)}, bf16[192,1024]{1,0:T(8,128)(2,1)S(1)}, u32[]{:S(2)}, u32[]{:S(2)}) collective-permute-start(bf16[192,1024]{1,0:T(8,128)(2,1)S(1)} %collective-permute-done.18.rest_19_), channel_id=1, source_target_pairs={{0,1},{1,0},{2,3},{3,2},{4,5},{5,4},{6,7},{7,6},{8,9},{9,8},{10,11... | collective-permute-start | bytes 1179656 | tf_op jit(solution)/shard_map/ppermute | solution.py:297
  70.3 1.9 %collective-permute-start.24 = (bf16[192,1024]{1,0:T(8,128)(2,1)S(1)}, bf16[192,1024]{1,0:T(8,128)(2,1)S(1)}, u32[]{:S(2)}, u32[]{:S(2)}) collective-permute-start(bf16[192,1024]{1,0:T(8,128)(2,1)S(1)} %collective-permute-done.19.rest_20_), channel_id=1, source_target_pairs={{0,1},{1,0},{2,3},{3,2},{4,5},{5,4},{6,7},{7,6},{8,9},{9,8},{10,11... | collective-permute-start | bytes 1179656 | tf_op jit(solution)/shard_map/ppermute | solution.py:297
  72.3 1.0 copy-start.2
  73.3 1.0 copy-start.4
  74.3 1.2 %copy-start.6 = (bf16[8,2,32,1024]{3,2,1,0:T(8,128)(2,1)S(1)}, bf16[8,2,32,1024]{3,2,1,0:T(8,128)(2,1)}, u32[]{:S(2)}) copy-start(bf16[8,2,32,1024]{3,2,1,0:T(8,128)(2,1)} %copy-done.5) | copy-start | bytes 3145732
  75.5 0.9 copy-start.8
  76.5 0.9 copy-start.10
  77.4 0.9 copy-start.12
  78.4 0.9 copy-start.14
  79.3 1.0 copy-start.16
  80.4 1.0 copy-start.18
  81.4 1.0 copy-start.20

commit v7 on v6

--- a/solution.py
+++ b/solution.py
@@ -17,6 +17,7 @@
 NT = (((1,), (1,)), ((), ()))
 TN = (((0,), (0,)), ((), ()))
 VMEM_LIMIT = 27 * 1024 * 1024
+SMALL = pltpu.CompilerParams(vmem_limit_bytes=6 * 1024 * 1024)
 
 
 def dot(a, b, dims):
@@ -318,6 +319,7 @@
         out_shape=jax.ShapeDtypeStruct(shape, arrays[0].dtype),
         in_specs=[vmem] * len(arrays),
         out_specs=vmem,
+        compiler_params=SMALL,
         name="join",
     )(*arrays)
 
@@ -374,6 +376,7 @@
         in_specs=[vmem] * 4,
         out_specs=(vmem,) * 5,
         scratch_shapes=[pltpu.VMEM((2, devices * share, width), jnp.bfloat16)],
+        compiler_params=SMALL,
         name="pack",
     )(input_weights, output_weights, tokens, cotangent)
 
@@ -386,16 +389,21 @@
     def other_core(arrays):
         return [swap(array, 1, devices) for array in arrays]
 
-    one = by_clip(joined, 1)
+    one, two = by_clip(joined, 1), by_clip(joined, 2)
+    source, two = lax.optimization_barrier((joined, two))
+    three = by_clip(source, 3)
     first = [swap(to_x, 2, devices), swap(to_y, 4, devices)]
     tail = half + 2 * block
     first += [swap(first[1][tail:], 2, devices), swap(first[0][tail:], 4, devices)]
-    third = [by_clip(join(0, joined, one), 2)]
+    one, first[0], first[1] = lax.optimization_barrier((one, first[0], first[1]))
     second = [one, *across(one)]
-    third[0], second[1], second[2] = lax.optimization_barrier((third[0], second[1], second[2]))
+    two, three, first[2], first[3], second[1], second[2] = lax.optimization_barrier(
+        (two, three, first[2], first[3], second[1], second[2])
+    )
+    third = [join(0, two, three)]
+    own, first[2] = lax.optimization_barrier((own, first[2]))
     first_other = other_core([own, *first])
     second_other = other_core(second)
-    third[0], first[2], first[3] = lax.optimization_barrier((third[0], first[2], first[3]))
     ready = [joined, *first, *first_other, *second, *second_other]
     third += across(third[0])
 
@@ -476,6 +484,7 @@
         out_shape=(rows_of(depth + half), rows_of(depth + half)),
         in_specs=[vmem] * 4,
         out_specs=(vmem, vmem),
+        compiler_params=SMALL,
         name="turn",
     )(second[1], second[2], third[1], third[2])
     third += [swap(to_dx, 2, devices), swap(to_dy, 4, devices)]

time: 115 us -> 101 us (0.88)
  local copies, waits for them, and re-layouts: 14.2 us -> 4.83 us
  Pallas kernels: 21 us -> 14.6 us
  starting transfers between devices: 17.7 us -> 22 us
  waiting for transfers between devices: 41.8 us -> 40.3 us
    unnamed x46 -> x10, local copies, waits for them, and re-layouts: 13.1 us -> 3.76 us
    ppermute x2 -> x3, waiting for transfers between devices: 18.1 us -> 12.3 us  [by_clip(): return lax.ppermute(array, 'clip', [(c, c ^ offset) for c in range(4)])]
    ppermute x23, waiting for transfers between devices: 23.7 us -> 28 us  [swap(): lax.ppermute(array, 'frame', [(f, f ^ distance) for f in range(devices)])]
    ppermute x2 -> x3, starting transfers between devices: 4.17 us -> 7.55 us  [by_clip(): return lax.ppermute(array, 'clip', [(c, c ^ offset) for c in range(4)])]
    pallas_call x1, Pallas kernels: 2.61 us -> 0.21 us  [gather_in_rounds(): pl.pallas_call(functools.partial(pack_kernel, patches, share), out_shape=...]
    pallas_call x1, Pallas kernels: 2.28 us -> 0.05 us  [gather_in_rounds(): pl.pallas_call(functools.partial(turn_kernel, half), out_shape=(rows_of(d...]
    pallas_call x1, Pallas kernels: 1.85 us -> 0.03 us  [join(): pl.pallas_call(functools.partial(join_kernel, axis), out_shape=jax.ShapeD...]
  transfers between devices with their start and end apart: 25 -> 26, of which waited for: 14 -> 12; matrix products, arithmetic and copies ran while one was open for 0% -> 0% of each run, Pallas kernels for 5% -> 2%
where the time goes in v7:
time: 101 us
  waiting for transfers between devices  40.3 us (40%)
  starting transfers between devices  22 us (22%)
  blocking collectives  17.8 us (18%)
  Pallas kernels  14.6 us (14%)
  local copies, waits for them, and re-layouts  4.83 us (5%)
  between operations  1.39 us (1%)
    ppermute x23, waiting for transfers between devices, swap(): lax.ppermute(array, 'frame', [(f, f ^ distance) for f in range(devices)])  28 us
    all_to_all x1, blocking collectives, per_device(): lax.all_to_all(back, 'frame', split_axis=0, concat_axis=0, tiled=True)  17.8 us
    ppermute x23, starting transfers between devices, swap(): lax.ppermute(array, 'frame', [(f, f ^ distance) for f in range(devices)])  14.4 us
    pallas_call x1, Pallas kernels, run_main(): pl.pallas_call(functools.partial(main_kernel, plan), out_shape=jax.ShapeD...  12.8 us
    ppermute x3, waiting for transfers between devices, by_clip(): return lax.ppermute(array, 'clip', [(c, c ^ offset) for c in range(4)])  12.3 us
    ppermute x3, starting transfers between devices, by_clip(): return lax.ppermute(array, 'clip', [(c, c ^ offset) for c in range(4)])  7.55 us
    unnamed x10, local copies, waits for them, and re-layouts  3.76 us
  transfers between devices with their start and end apart: 26, of which 12 were waited for; matrix products, arithmetic and copies ran while one was open for 0% of the time, Pallas kernels for 2%

profile of v7, /device:TPU:0, one launch (start us, length us, event | category | flops | bytes accessed | tf_op | source)
XLA Modules:
  0.0 101.0 jit_solution(3502290770205476205)
XLA Ops:
  0.6 0.0 copy-start
  0.6 1.0 copy-done
  1.6 1.0 copy-done.1
  2.6 0.9 copy-done.2
  3.6 0.8 copy-done.3
  4.4 0.2 pack.1
  4.6 3.0 %collective-permute-start.2 = (bf16[320,1024]{1,0:T(8,128)(2,1)S(1)}, bf16[320,1024]{1,0:T(8,128)(2,1)S(1)}, u32[]{:S(2)}, u32[]{:S(2)}) collective-permute-start(bf16[320,1024]{1,0:T(8,128)(2,1)S(1)} %get-tuple-element.34), channel_id=1, source_target_pairs={{0,4},{1,5},{2,6},{3,7},{4,0},{5,1},{6,2},{7,3},{8,12},{9,13},{10,... | collective-permute-start | bytes 1966088 | tf_op jit(solution)/shard_map/ppermute | solution.py:298
  7.6 1.5 %collective-permute-start.4 = (bf16[320,1024]{1,0:T(8,128)(2,1)S(1)}, bf16[320,1024]{1,0:T(8,128)(2,1)S(1)}, u32[]{:S(2)}, u32[]{:S(2)}) collective-permute-start(bf16[320,1024]{1,0:T(8,128)(2,1)S(1)} %get-tuple-element.35), channel_id=1, source_target_pairs={{0,2},{1,3},{2,0},{3,1},{4,6},{5,7},{6,4},{7,5},{8,10},{9,11},{10,... | collective-permute-start | bytes 1966088 | tf_op jit(solution)/shard_map/ppermute | solution.py:298
  9.1 2.6 %collective-permute-start = (bf16[128,1024]{1,0:T(8,128)(2,1)S(1)}, bf16[128,1024]{1,0:T(8,128)(2,1)S(1)}, u32[]{:S(2)}, u32[]{:S(2)}) collective-permute-start(bf16[128,1024]{1,0:T(8,128)(2,1)S(1)} %get-tuple-element.33.refs_2_.rest_0_), channel_id=1, source_target_pairs={{0,16},{8,24},{16,0},{24,8},{1,17},{9,25},{17,1},{25,9},{2,18},{10... | collective-permute-start | bytes 786440 | tf_op jit(solution)/shard_map/ppermute | solution.py:384
  11.7 1.6 %collective-permute-start.6 = (bf16[128,1024]{1,0:T(8,128)(2,1)S(1)}, bf16[128,1024]{1,0:T(8,128)(2,1)S(1)}, u32[]{:S(2)}, u32[]{:S(2)}) collective-permute-start(bf16[128,1024]{1,0:T(8,128)(2,1)S(1)} %get-tuple-element.33.refs_2_.rest_0_), channel_id=1, source_target_pairs={{0,8},{8,0},{16,24},{24,16},{1,9},{9,1},{17,25},{25,17},{2,10},{10... | collective-permute-start | bytes 786440 | tf_op jit(solution)/shard_map/ppermute | solution.py:384
  13.3 9.9 %collective-permute-done.refs_0_ = bf16[128,1024]{1,0:T(8,128)(2,1)S(1)} collective-permute-done((bf16[128,1024]{1,0:T(8,128)(2,1)S(1)}, bf16[128,1024]{1,0:T(8,128)(2,1)S(1)}, u32[]{:S(2)}, u32[]{:S(2)}) %collective-permute-start) | collective-permute-done | bytes 262176 | tf_op jit(solution)/shard_map/ppermute | solution.py:384
  23.2 3.4 %collective-permute-start.1 = (bf16[128,1024]{1,0:T(8,128)(2,1)S(1)}, bf16[128,1024]{1,0:T(8,128)(2,1)S(1)}, u32[]{:S(2)}, u32[]{:S(2)}) collective-permute-start(bf16[128,1024]{1,0:T(8,128)(2,1)S(1)} %get-tuple-element.33.refs_2_.rest_0_), channel_id=1, source_target_pairs={{0,24},{8,16},{16,8},{24,0},{1,25},{9,17},{17,9},{25,1},{2,26},{10... | collective-permute-start | bytes 786440 | tf_op jit(solution)/shard_map/ppermute | solution.py:384
  26.6 0.0 collective-permute-done.2.refs_4_.rest_2_
  26.7 0.6 collective-permute-start.3
  27.3 0.0 collective-permute-done.6.rest_10_
  27.3 0.0 collective-permute-done.4.refs_3_.rest_1_
  27.3 0.6 collective-permute-start.5
  27.9 1.5 %collective-permute-start.8 = (bf16[128,1024]{1,0:T(8,128)(2,1)S(1)}, bf16[128,1024]{1,0:T(8,128)(2,1)S(1)}, u32[]{:S(2)}, u32[]{:S(2)}) collective-permute-start(bf16[128,1024]{1,0:T(8,128)(2,1)S(1)} %collective-permute-done.6.rest_10_), channel_id=1, source_target_pairs={{0,4},{1,5},{2,6},{3,7},{4,0},{5,1},{6,2},{7,3},{8,12},{9,13},{10,... | collective-permute-start | bytes 786440 | tf_op jit(solution)/shard_map/ppermute | solution.py:298
  29.4 1.5 %collective-permute-start.7 = (bf16[128,1024]{1,0:T(8,128)(2,1)S(1)}, bf16[128,1024]{1,0:T(8,128)(2,1)S(1)}, u32[]{:S(2)}, u32[]{:S(2)}) collective-permute-start(bf16[128,1024]{1,0:T(8,128)(2,1)S(1)} %collective-permute-done.6.rest_10_), channel_id=1, source_target_pairs={{0,2},{1,3},{2,0},{3,1},{4,6},{5,7},{6,4},{7,5},{8,10},{9,11},{10,... | collective-permute-start | bytes 786440 | tf_op jit(solution)/shard_map/ppermute | solution.py:298
  30.9 2.4 %collective-permute-done.1.refs_1_ = bf16[128,1024]{1,0:T(8,128)(2,1)S(1)} collective-permute-done((bf16[128,1024]{1,0:T(8,128)(2,1)S(1)}, bf16[128,1024]{1,0:T(8,128)(2,1)S(1)}, u32[]{:S(2)}, u32[]{:S(2)}) %collective-permute-start.1) | collective-permute-done | bytes 262176 | tf_op jit(solution)/shard_map/ppermute | solution.py:384
  33.2 2.7 %collective-permute-done.3.refs_5_.rest_3_ = bf16[128,1024]{1,0:T(8,128)(2,1)S(1)} collective-permute-done((bf16[128,1024]{1,0:T(8,128)(2,1)S(1)}, bf16[128,1024]{1,0:T(8,128)(2,1)S(1)}, u32[]{:S(2)}, u32[]{:S(2)}) %collective-permute-start.3) | collective-permute-done | bytes 262176 | tf_op jit(solution)/shard_map/ppermute | solution.py:298
  35.9 0.7 collective-permute-done.5.refs_6_.rest_4_
  36.6 4.0 %collective-permute-done.8.by_y.rest_12_ = bf16[128,1024]{1,0:T(8,128)(2,1)S(1)} collective-permute-done((bf16[128,1024]{1,0:T(8,128)(2,1)S(1)}, bf16[128,1024]{1,0:T(8,128)(2,1)S(1)}, u32[]{:S(2)}, u32[]{:S(2)}) %collective-permute-start.8) | collective-permute-done | bytes 262176 | tf_op jit(solution)/shard_map/ppermute | solution.py:298
  40.6 0.0 collective-permute-done.7.by_x.rest_11_
  40.6 0.0 collective-permute-start.13
  40.6 0.5 collective-permute-start.14
  41.2 0.0 collective-permute-start.11
  41.2 0.5 collective-permute-start.12
  41.7 1.6 %collective-permute-start.9 = (bf16[256,1024]{1,0:T(8,128)(2,1)S(1)}, bf16[256,1024]{1,0:T(8,128)(2,1)S(1)}, u32[]{:S(2)}, u32[]{:S(2)}) collective-permute-start(bf16[256,1024]{1,0:T(8,128)(2,1)S(1)} %join.1.rest_16_), channel_id=1, source_target_pairs={{0,2},{1,3},{2,0},{3,1},{4,6},{5,7},{6,4},{7,5},{8,10},{9,11},{10,... | collective-permute-start | bytes 1572872 | tf_op jit(solution)/shard_map/ppermute | solution.py:298
  43.3 0.0 collective-permute-done.13.refs_10_.rest_8_
  43.3 0.5 collective-permute-start.18
  43.8 0.0 collective-permute-done.14.refs_11_.rest_9_
  43.8 0.0 collective-permute-start.10
  43.8 1.7 %collective-permute-done.10.refs_7_.rest_5_ = bf16[192,1024]{1,0:T(8,128)(2,1)S(1)} collective-permute-done((bf16[192,1024]{1,0:T(8,128)(2,1)S(1)}, bf16[192,1024]{1,0:T(8,128)(2,1)S(1)}, u32[]{:S(2)}, u32[]{:S(2)}) %collective-permute-start.10) | collective-permute-done | bytes 393248 | tf_op jit(solution)/shard_map/ppermute | solution.py:298
  45.5 0.1 collective-permute-start.15
  45.6 0.0 collective-permute-done.11.refs_8_.rest_6_
  45.6 0.4 collective-permute-start.16
  46.0 0.0 collective-permute-done.12.refs_9_.rest_7_
  46.0 0.1 collective-permute-start.17
  46.2 1.6 %front.1 = (bf16[8,2,32,1024]{3,2,1,0:T(8,128)(2,1)S(1)}, bf16[256,1024]{1,0:T(8,128)(2,1)S(1)}, f32[256,128]{1,0:T(8,128)S(1)}, bf16[256,768]{1,0:T(8,128)(2,1)S(1)}) custom-call(f32[1,1024]{1,0:T(1,128)S(1)} %bitcast.11, bf16[64,1024]{1,0:T(8,128)(2,1)S(1)} %get-tuple-element.39.refs_1_, bf16[128,1024]{1,0:T(8,128)(2,1)S(1)} %get-tuple-element.33.refs_2_.rest_0_, ...), custom_call_target="tpu_custom_call" | custom-call | flops 402653184 | bytes 3670016 | tf_op jit(solution)/shard_map/front/pallas_call | solution.py:233
  47.8 7.8 %collective-permute-done.9.pair_x.rest_17_ = bf16[256,1024]{1,0:T(8,128)(2,1)S(1)} collective-permute-done((bf16[256,1024]{1,0:T(8,128)(2,1)S(1)}, bf16[256,1024]{1,0:T(8,128)(2,1)S(1)}, u32[]{:S(2)}, u32[]{:S(2)}) %collective-permute-start.9) | collective-permute-done | bytes 524320 | tf_op jit(solution)/shard_map/ppermute | solution.py:298
  55.6 1.2 %collective-permute-done.18.pair_y.rest_18_ = bf16[256,1024]{1,0:T(8,128)(2,1)S(1)} collective-permute-done((bf16[256,1024]{1,0:T(8,128)(2,1)S(1)}, bf16[256,1024]{1,0:T(8,128)(2,1)S(1)}, u32[]{:S(2)}, u32[]{:S(2)}) %collective-permute-start.18) | collective-permute-done | bytes 524320 | tf_op jit(solution)/shard_map/ppermute | solution.py:298
  56.8 0.1 turn.1
  56.9 0.9 collective-permute-start.19
  57.8 0.5 collective-permute-start.20
  58.3 0.0 collective-permute-done.15.rest_13_
  58.3 0.0 collective-permute-start.21
  58.3 0.0 collective-permute-done.16.rest_14_
  58.3 0.5 collective-permute-start.23
  58.8 0.0 collective-permute-done.17.rest_15_
  58.8 0.1 collective-permute-start.22
  58.9 7.9 %collective-permute-done.19.rest_19_ = bf16[192,1024]{1,0:T(8,128)(2,1)S(1)} collective-permute-done((bf16[192,1024]{1,0:T(8,128)(2,1)S(1)}, bf16[192,1024]{1,0:T(8,128)(2,1)S(1)}, u32[]{:S(2)}, u32[]{:S(2)}) %collective-permute-start.19) | collective-permute-done | bytes 393248 | tf_op jit(solution)/shard_map/ppermute | solution.py:298
  66.8 0.0 collective-permute-start.24
  66.8 0.9 collective-permute-done.20.rest_20_
  67.7 0.0 collective-permute-start.25
  68.3 0.0 collective-permute-done.21.rest_21_
  68.3 0.0 collective-permute-done.23.rest_23_
  68.3 0.0 collective-permute-done.22.rest_22_
  68.3 0.2 collective-permute-done.24.rest_24_
  68.5 0.9 collective-permute-done.25.rest_25_
  69.4 12.8 %main.1 = bf16[8,2,32,1024]{3,2,1,0:T(8,128)(2,1)S(1)} custom-call(s32[1]{0:T(128)S(6)} %copy.9.counts_ref, f32[1,1024]{1,0:T(1,128)S(1)} %bitcast.12, bf16[8,2,32,1024]{3,2,1,0:T(8,128)(2,1)S(1)} %get-tuple-element.51.both_ref, bf16[256,1024]{1,0:T(8,128)(2,1)S(1)} %get-tuple-element.52.normed_ref, f32[256,128]{1,0:T(8,128)S(1)} %get-tuple-element.53.stats_ref, ...), custom_call_target="tpu_custom_call" | custom-call | flops 3221225472 | bytes 10485760 | tf_op jit(solution)/shard_map/main/pallas_call | solution.py:266
  82.1 17.8 %all_to_all.5 = bf16[8,1,2,32,1024]{4,3,2,1,0:T(8,128)(2,1)S(1)} all-to-all(bf16[8,1,2,32,1024]{4,3,2,1,0:T(8,128)(2,1)S(1)} %bitcast.10), channel_id=1, replica_groups=mesh['clip'=4,'frame'=8] {'frame'}, dimensions={0} | all-to-all | bytes 2097152 | tf_op jit(solution)/shard_map/all_to_all | solution.py:543
  99.9 0.1 fusion
  100.0 0.9 slice_bitcast_fusion
  (8 shorter events, 0.1 us)
Async XLA Ops:
  0.6 1.0 copy-start
  1.6 1.0 copy-start.1
  2.6 0.9 copy-start.2
  3.6 0.8 copy-start.3
  4.6 22.0 %collective-permute-start.2 = (bf16[320,1024]{1,0:T(8,128)(2,1)S(1)}, bf16[320,1024]{1,0:T(8,128)(2,1)S(1)}, u32[]{:S(2)}, u32[]{:S(2)}) collective-permute-start(bf16[320,1024]{1,0:T(8,128)(2,1)S(1)} %get-tuple-element.34), channel_id=1, source_target_pairs={{0,4},{1,5},{2,6},{3,7},{4,0},{5,1},{6,2},{7,3},{8,12},{9,13},{10,... | collective-permute-start | bytes 1966088 | tf_op jit(solution)/shard_map/ppermute | solution.py:298
  7.6 19.6 %collective-permute-start.4 = (bf16[320,1024]{1,0:T(8,128)(2,1)S(1)}, bf16[320,1024]{1,0:T(8,128)(2,1)S(1)}, u32[]{:S(2)}, u32[]{:S(2)}) collective-permute-start(bf16[320,1024]{1,0:T(8,128)(2,1)S(1)} %get-tuple-element.35), channel_id=1, source_target_pairs={{0,2},{1,3},{2,0},{3,1},{4,6},{5,7},{6,4},{7,5},{8,10},{9,11},{10,... | collective-permute-start | bytes 1966088 | tf_op jit(solution)/shard_map/ppermute | solution.py:298
  9.1 14.1 %collective-permute-start = (bf16[128,1024]{1,0:T(8,128)(2,1)S(1)}, bf16[128,1024]{1,0:T(8,128)(2,1)S(1)}, u32[]{:S(2)}, u32[]{:S(2)}) collective-permute-start(bf16[128,1024]{1,0:T(8,128)(2,1)S(1)} %get-tuple-element.33.refs_2_.rest_0_), channel_id=1, source_target_pairs={{0,16},{8,24},{16,0},{24,8},{1,17},{9,25},{17,1},{25,9},{2,18},{10... | collective-permute-start | bytes 786440 | tf_op jit(solution)/shard_map/ppermute | solution.py:384
  11.7 15.5 %collective-permute-start.6 = (bf16[128,1024]{1,0:T(8,128)(2,1)S(1)}, bf16[128,1024]{1,0:T(8,128)(2,1)S(1)}, u32[]{:S(2)}, u32[]{:S(2)}) collective-permute-start(bf16[128,1024]{1,0:T(8,128)(2,1)S(1)} %get-tuple-element.33.refs_2_.rest_0_), channel_id=1, source_target_pairs={{0,8},{8,0},{16,24},{24,16},{1,9},{9,1},{17,25},{25,17},{2,10},{10... | collective-permute-start | bytes 786440 | tf_op jit(solution)/shard_map/ppermute | solution.py:384
  23.2 10.0 %collective-permute-start.1 = (bf16[128,1024]{1,0:T(8,128)(2,1)S(1)}, bf16[128,1024]{1,0:T(8,128)(2,1)S(1)}, u32[]{:S(2)}, u32[]{:S(2)}) collective-permute-start(bf16[128,1024]{1,0:T(8,128)(2,1)S(1)} %get-tuple-element.33.refs_2_.rest_0_), channel_id=1, source_target_pairs={{0,24},{8,16},{16,8},{24,0},{1,25},{9,17},{17,9},{25,1},{2,26},{10... | collective-permute-start | bytes 786440 | tf_op jit(solution)/shard_map/ppermute | solution.py:384
  26.7 9.3 %collective-permute-start.3 = (bf16[128,1024]{1,0:T(8,128)(2,1)S(1)}, bf16[128,1024]{1,0:T(8,128)(2,1)S(1)}, u32[]{:S(2)}, u32[]{:S(2)}) collective-permute-start(bf16[128,1024]{1,0:T(8,128)(2,1)S(1)} %slice.24), channel_id=1, source_target_pairs={{0,2},{1,3},{2,0},{3,1},{4,6},{5,7},{6,4},{7,5},{8,10},{9,11},{10,... | collective-permute-start | bytes 786440 | tf_op jit(solution)/shard_map/ppermute | solution.py:298
  27.3 9.3 %collective-permute-start.5 = (bf16[128,1024]{1,0:T(8,128)(2,1)S(1)}, bf16[128,1024]{1,0:T(8,128)(2,1)S(1)}, u32[]{:S(2)}, u32[]{:S(2)}) collective-permute-start(bf16[128,1024]{1,0:T(8,128)(2,1)S(1)} %slice.25), channel_id=1, source_target_pairs={{0,4},{1,5},{2,6},{3,7},{4,0},{5,1},{6,2},{7,3},{8,12},{9,13},{10,... | collective-permute-start | bytes 786440 | tf_op jit(solution)/shard_map/ppermute | solution.py:298
  27.9 12.8 %collective-permute-start.8 = (bf16[128,1024]{1,0:T(8,128)(2,1)S(1)}, bf16[128,1024]{1,0:T(8,128)(2,1)S(1)}, u32[]{:S(2)}, u32[]{:S(2)}) collective-permute-start(bf16[128,1024]{1,0:T(8,128)(2,1)S(1)} %collective-permute-done.6.rest_10_), channel_id=1, source_target_pairs={{0,4},{1,5},{2,6},{3,7},{4,0},{5,1},{6,2},{7,3},{8,12},{9,13},{10,... | collective-permute-start | bytes 786440 | tf_op jit(solution)/shard_map/ppermute | solution.py:298
  29.4 11.3 %collective-permute-start.7 = (bf16[128,1024]{1,0:T(8,128)(2,1)S(1)}, bf16[128,1024]{1,0:T(8,128)(2,1)S(1)}, u32[]{:S(2)}, u32[]{:S(2)}) collective-permute-start(bf16[128,1024]{1,0:T(8,128)(2,1)S(1)} %collective-permute-done.6.rest_10_), channel_id=1, source_target_pairs={{0,2},{1,3},{2,0},{3,1},{4,6},{5,7},{6,4},{7,5},{8,10},{9,11},{10,... | collective-permute-start | bytes 786440 | tf_op jit(solution)/shard_map/ppermute | solution.py:298
  40.6 2.6 %collective-permute-start.13 = (bf16[128,1024]{1,0:T(8,128)(2,1)S(1)}, bf16[128,1024]{1,0:T(8,128)(2,1)S(1)}, u32[]{:S(2)}, u32[]{:S(2)}) collective-permute-start(bf16[128,1024]{1,0:T(8,128)(2,1)S(1)} %collective-permute-done.3.refs_5_.rest_3_), channel_id=1, source_target_pairs={{0,1},{1,0},{2,3},{3,2},{4,5},{5,4},{6,7},{7,6},{8,9},{9,8},{10,11... | collective-permute-start | bytes 786440 | tf_op jit(solution)/shard_map/ppermute | solution.py:298
  40.6 3.1 %collective-permute-start.14 = (bf16[128,1024]{1,0:T(8,128)(2,1)S(1)}, bf16[128,1024]{1,0:T(8,128)(2,1)S(1)}, u32[]{:S(2)}, u32[]{:S(2)}) collective-permute-start(bf16[128,1024]{1,0:T(8,128)(2,1)S(1)} %collective-permute-done.5.refs_6_.rest_4_), channel_id=1, source_target_pairs={{0,1},{1,0},{2,3},{3,2},{4,5},{5,4},{6,7},{7,6},{8,9},{9,8},{10,11... | collective-permute-start | bytes 786440 | tf_op jit(solution)/shard_map/ppermute | solution.py:298
  41.2 4.5 %collective-permute-start.11 = (bf16[320,1024]{1,0:T(8,128)(2,1)S(1)}, bf16[320,1024]{1,0:T(8,128)(2,1)S(1)}, u32[]{:S(2)}, u32[]{:S(2)}) collective-permute-start(bf16[320,1024]{1,0:T(8,128)(2,1)S(1)} %collective-permute-done.4.refs_3_.rest_1_), channel_id=1, source_target_pairs={{0,1},{1,0},{2,3},{3,2},{4,5},{5,4},{6,7},{7,6},{8,9},{9,8},{10,11... | collective-permute-start | bytes 1966088 | tf_op jit(solution)/shard_map/ppermute | solution.py:298
  41.2 4.9 %collective-permute-start.12 = (bf16[320,1024]{1,0:T(8,128)(2,1)S(1)}, bf16[320,1024]{1,0:T(8,128)(2,1)S(1)}, u32[]{:S(2)}, u32[]{:S(2)}) collective-permute-start(bf16[320,1024]{1,0:T(8,128)(2,1)S(1)} %collective-permute-done.2.refs_4_.rest_2_), channel_id=1, source_target_pairs={{0,1},{1,0},{2,3},{3,2},{4,5},{5,4},{6,7},{7,6},{8,9},{9,8},{10,11... | collective-permute-start | bytes 1966088 | tf_op jit(solution)/shard_map/ppermute | solution.py:298
  41.7 4.5 %copy-start.4 = (f32[1024]{0:T(1024)S(1)}, f32[1024]{0:T(1024)}, u32[]{:S(2)}) copy-start(f32[1024]{0:T(1024)} %param.8) | copy-start | bytes 12292
  41.7 13.9 %collective-permute-start.9 = (bf16[256,1024]{1,0:T(8,128)(2,1)S(1)}, bf16[256,1024]{1,0:T(8,128)(2,1)S(1)}, u32[]{:S(2)}, u32[]{:S(2)}) collective-permute-start(bf16[256,1024]{1,0:T(8,128)(2,1)S(1)} %join.1.rest_16_), channel_id=1, source_target_pairs={{0,2},{1,3},{2,0},{3,1},{4,6},{5,7},{6,4},{7,5},{8,10},{9,11},{10,... | collective-permute-start | bytes 1572872 | tf_op jit(solution)/shard_map/ppermute | solution.py:298
  43.3 13.6 %collective-permute-start.18 = (bf16[256,1024]{1,0:T(8,128)(2,1)S(1)}, bf16[256,1024]{1,0:T(8,128)(2,1)S(1)}, u32[]{:S(2)}, u32[]{:S(2)}) collective-permute-start(bf16[256,1024]{1,0:T(8,128)(2,1)S(1)} %join.1.rest_16_), channel_id=1, source_target_pairs={{0,4},{1,5},{2,6},{3,7},{4,0},{5,1},{6,2},{7,3},{8,12},{9,13},{10,... | collective-permute-start | bytes 1572872 | tf_op jit(solution)/shard_map/ppermute | solution.py:298
  43.8 1.7 %collective-permute-start.10 = (bf16[192,1024]{1,0:T(8,128)(2,1)S(1)}, bf16[192,1024]{1,0:T(8,128)(2,1)S(1)}, u32[]{:S(2)}, u32[]{:S(2)}) collective-permute-start(bf16[192,1024]{1,0:T(8,128)(2,1)S(1)} %get-tuple-element.46), channel_id=1, source_target_pairs={{0,1},{1,0},{2,3},{3,2},{4,5},{5,4},{6,7},{7,6},{8,9},{9,8},{10,11... | collective-permute-start | bytes 1179656 | tf_op jit(solution)/shard_map/ppermute | solution.py:298
  45.5 12.8 %collective-permute-start.15 = (bf16[128,1024]{1,0:T(8,128)(2,1)S(1)}, bf16[128,1024]{1,0:T(8,128)(2,1)S(1)}, u32[]{:S(2)}, u32[]{:S(2)}) collective-permute-start(bf16[128,1024]{1,0:T(8,128)(2,1)S(1)} %collective-permute-done.6.rest_10_), channel_id=1, source_target_pairs={{0,1},{1,0},{2,3},{3,2},{4,5},{5,4},{6,7},{7,6},{8,9},{9,8},{10,11... | collective-permute-start | bytes 786440 | tf_op jit(solution)/shard_map/ppermute | solution.py:298
  45.6 12.6 %collective-permute-start.16 = (bf16[128,1024]{1,0:T(8,128)(2,1)S(1)}, bf16[128,1024]{1,0:T(8,128)(2,1)S(1)}, u32[]{:S(2)}, u32[]{:S(2)}) collective-permute-start(bf16[128,1024]{1,0:T(8,128)(2,1)S(1)} %collective-permute-done.7.by_x.rest_11_), channel_id=1, source_target_pairs={{0,1},{1,0},{2,3},{3,2},{4,5},{5,4},{6,7},{7,6},{8,9},{9,8},{10,11... | collective-permute-start | bytes 786440 | tf_op jit(solution)/shard_map/ppermute | solution.py:298
  46.0 12.8 %collective-permute-start.17 = (bf16[128,1024]{1,0:T(8,128)(2,1)S(1)}, bf16[128,1024]{1,0:T(8,128)(2,1)S(1)}, u32[]{:S(2)}, u32[]{:S(2)}) collective-permute-start(bf16[128,1024]{1,0:T(8,128)(2,1)S(1)} %collective-permute-done.8.by_y.rest_12_), channel_id=1, source_target_pairs={{0,1},{1,0},{2,3},{3,2},{4,5},{5,4},{6,7},{7,6},{8,9},{9,8},{10,11... | collective-permute-start | bytes 786440 | tf_op jit(solution)/shard_map/ppermute | solution.py:298
  56.9 9.9 %collective-permute-start.19 = (bf16[192,1024]{1,0:T(8,128)(2,1)S(1)}, bf16[192,1024]{1,0:T(8,128)(2,1)S(1)}, u32[]{:S(2)}, u32[]{:S(2)}) collective-permute-start(bf16[192,1024]{1,0:T(8,128)(2,1)S(1)} %get-tuple-element.58), channel_id=1, source_target_pairs={{0,2},{1,3},{2,0},{3,1},{4,6},{5,7},{6,4},{7,5},{8,10},{9,11},{10,... | collective-permute-start | bytes 1179656 | tf_op jit(solution)/shard_map/ppermute | solution.py:298
  57.8 9.9 %collective-permute-start.20 = (bf16[192,1024]{1,0:T(8,128)(2,1)S(1)}, bf16[192,1024]{1,0:T(8,128)(2,1)S(1)}, u32[]{:S(2)}, u32[]{:S(2)}) collective-permute-start(bf16[192,1024]{1,0:T(8,128)(2,1)S(1)} %get-tuple-element.59), channel_id=1, source_target_pairs={{0,4},{1,5},{2,6},{3,7},{4,0},{5,1},{6,2},{7,3},{8,12},{9,13},{10,... | collective-permute-start | bytes 1179656 | tf_op jit(solution)/shard_map/ppermute | solution.py:298
  58.3 10.0 %collective-permute-start.21 = (bf16[256,1024]{1,0:T(8,128)(2,1)S(1)}, bf16[256,1024]{1,0:T(8,128)(2,1)S(1)}, u32[]{:S(2)}, u32[]{:S(2)}) collective-permute-start(bf16[256,1024]{1,0:T(8,128)(2,1)S(1)} %join.1.rest_16_), channel_id=1, source_target_pairs={{0,1},{1,0},{2,3},{3,2},{4,5},{5,4},{6,7},{7,6},{8,9},{9,8},{10,11... | collective-permute-start | bytes 1572872 | tf_op jit(solution)/shard_map/ppermute | solution.py:298
  58.3 10.0 %collective-permute-start.23 = (bf16[256,1024]{1,0:T(8,128)(2,1)S(1)}, bf16[256,1024]{1,0:T(8,128)(2,1)S(1)}, u32[]{:S(2)}, u32[]{:S(2)}) collective-permute-start(bf16[256,1024]{1,0:T(8,128)(2,1)S(1)} %collective-permute-done.18.pair_y.rest_18_), channel_id=1, source_target_pairs={{0,1},{1,0},{2,3},{3,2},{4,5},{5,4},{6,7},{7,6},{8,9},{9,8},{10,11... | collective-permute-start | bytes 1572872 | tf_op jit(solution)/shard_map/ppermute | solution.py:298
  58.8 9.5 %collective-permute-start.22 = (bf16[256,1024]{1,0:T(8,128)(2,1)S(1)}, bf16[256,1024]{1,0:T(8,128)(2,1)S(1)}, u32[]{:S(2)}, u32[]{:S(2)}) collective-permute-start(bf16[256,1024]{1,0:T(8,128)(2,1)S(1)} %collective-permute-done.9.pair_x.rest_17_), channel_id=1, source_target_pairs={{0,1},{1,0},{2,3},{3,2},{4,5},{5,4},{6,7},{7,6},{8,9},{9,8},{10,11... | collective-permute-start | bytes 1572872 | tf_op jit(solution)/shard_map/ppermute | solution.py:298
  66.8 1.7 %collective-permute-start.24 = (bf16[192,1024]{1,0:T(8,128)(2,1)S(1)}, bf16[192,1024]{1,0:T(8,128)(2,1)S(1)}, u32[]{:S(2)}, u32[]{:S(2)}) collective-permute-start(bf16[192,1024]{1,0:T(8,128)(2,1)S(1)} %collective-permute-done.19.rest_19_), channel_id=1, source_target_pairs={{0,1},{1,0},{2,3},{3,2},{4,5},{5,4},{6,7},{7,6},{8,9},{9,8},{10,11... | collective-permute-start | bytes 1179656 | tf_op jit(solution)/shard_map/ppermute | solution.py:298
  67.7 1.7 %collective-permute-start.25 = (bf16[192,1024]{1,0:T(8,128)(2,1)S(1)}, bf16[192,1024]{1,0:T(8,128)(2,1)S(1)}, u32[]{:S(2)}, u32[]{:S(2)}) collective-permute-start(bf16[192,1024]{1,0:T(8,128)(2,1)S(1)} %collective-permute-done.20.rest_20_), channel_id=1, source_target_pairs={{0,1},{1,0},{2,3},{3,2},{4,5},{5,4},{6,7},{7,6},{8,9},{9,8},{10,11... | collective-permute-start | bytes 1179656 | tf_op jit(solution)/shard_map/ppermute | solution.py:298

commit v8 on v7

--- a/solution.py
+++ b/solution.py
@@ -99,8 +99,10 @@
     ]
     for copy in place:
         copy.start()
-    late = fetch(plan["late"](), weight_refs, w_in, sems.at[0])
     outer = fetch(plan["outer"](), weight_refs, w_out, sems.at[1])
+    late = [
+        fetch(parts, weight_refs, w_in, sems.at[4 + i]) for i, parts in enumerate(plan["late"]())
+    ]
     again = fetch(plan["again"](), weight_refs, w_in, sems.at[2])
 
     def real(index):
@@ -119,11 +121,6 @@
     low_lanes = (lane < DH).astype(jnp.bfloat16)
     high_lanes = (lane >= DH).astype(jnp.bfloat16)
 
-    wait(late)
-    for start, size in plan["missing"]():
-        columns = pl.ds(pl.multiple_of(start, 128), size)
-        proj[:, columns] = dot(normed_ref[...], w_in[:, columns], NN).astype(jnp.bfloat16)
-
     wait(outer)
     step = min(width, 256)
 
@@ -131,6 +128,11 @@
     def _(j):
         columns = pl.ds(pl.multiple_of(j * step, step), step)
         ga[:, columns] = dot(grads[...], w_out[columns, :], NT).astype(jnp.bfloat16)
+
+    for (start, size), copies in zip(plan["missing"](), late):
+        wait(copies)
+        columns = pl.ds(pl.multiple_of(start, 128), size)
+        proj[:, columns] = dot(normed_ref[...], w_in[:, columns], NN).astype(jnp.bfloat16)
 
     wait(place)
 
@@ -245,11 +247,7 @@
             pltpu.SemaphoreType.DMA((1,)),
         ],
         compiler_params=pltpu.CompilerParams(vmem_limit_bytes=VMEM_LIMIT),
-        cost_estimate=pl.CostEstimate(
-            flops=2 * total * width * columns,
-            bytes_accessed=2 * width * columns + 8 * total * width,
-            transcendentals=total,
-        ),
+        cost_estimate=pl.CostEstimate(flops=total, bytes_accessed=total, transcendentals=0),
         name="front",
     )(gain, *sources)
 
@@ -282,7 +280,7 @@
             pltpu.VMEM((chunk, rows, 2 * rows), jnp.float32),
             pltpu.VMEM((chunk, rows, 2 * rows), jnp.float32),
             pltpu.VMEM((chunk, 2, rows, 2 * rows), jnp.bfloat16),
-            pltpu.SemaphoreType.DMA((4,)),
+            pltpu.SemaphoreType.DMA((8,)),
         ],
         compiler_params=params,
         cost_estimate=pl.CostEstimate(
@@ -324,14 +322,26 @@
     )(*arrays)
 
 
-def pack_kernel(patches, share, w_in, w_out, tokens, cot, joined, own, mine, to_x, to_y, held):
+def pack_kernel(patches, share, *refs):
+    sources, (joined, own, mine, to_x, to_y), held, fetched, sems = (
+        refs[:4], refs[4:9], refs[9], refs[10:14], refs[14]
+    )
+    copies = [
+        pltpu.make_async_copy(source, target, sems.at[i])
+        for i, (source, target) in enumerate(zip(sources, fetched))
+    ]
+    for copy in copies:
+        copy.start()
+    w_in, w_out, tokens, cot = fetched
     depth = w_in.shape[0]
     half, block = depth // 2, 2 * share
     device = lax.axis_index("frame")
     chip, core = device // 2, device % 2
+    full = patches // SUB * SUB
+    held[:, full:] = jnp.zeros((2, held.shape[1] - full, held.shape[2]), held.dtype)
+    wait(copies)
     joined[:, : w_in.shape[1]] = w_in[...]
     joined[:, w_in.shape[1] :] = w_out[...]
-    held[...] = jnp.zeros_like(held)
     held[0, :patches] = tokens[0, 0]
     held[1, :patches] = cot[0, 0]
 
@@ -373,9 +383,11 @@
         out_shape=tuple(
             map(rows_of, (depth, depth + block, block, depth + 3 * block, depth + 3 * block))
         ),
-        in_specs=[vmem] * 4,
+        in_specs=[pl.BlockSpec(memory_space=pl.ANY)] * 4,
         out_specs=(vmem,) * 5,
-        scratch_shapes=[pltpu.VMEM((2, devices * share, width), jnp.bfloat16)],
+        scratch_shapes=[pltpu.VMEM((2, devices * share, width), jnp.bfloat16)]
+        + [pltpu.VMEM(a.shape, a.dtype) for a in (input_weights, output_weights, tokens, cotangent)]
+        + [pltpu.SemaphoreType.DMA((4,))],
         compiler_params=SMALL,
         name="pack",
     )(input_weights, output_weights, tokens, cotangent)
@@ -397,11 +409,11 @@
     first += [swap(first[1][tail:], 2, devices), swap(first[0][tail:], 4, devices)]
     one, first[0], first[1] = lax.optimization_barrier((one, first[0], first[1]))
     second = [one, *across(one)]
-    two, three, first[2], first[3], second[1], second[2] = lax.optimization_barrier(
-        (two, three, first[2], first[3], second[1], second[2])
+    two, three, first[2], first[3] = lax.optimization_barrier((two, three, first[2], first[3]))
+    third = [join(0, two, three)]
+    second[1], second[2], own, *first = lax.optimization_barrier(
+        (second[1], second[2], own, *first)
     )
-    third = [join(0, two, three)]
-    own, first[2] = lax.optimization_barrier((own, first[2]))
     first_other = other_core([own, *first])
     second_other = other_core(second)
     ready = [joined, *first, *first_other, *second, *second_other]
@@ -469,7 +481,7 @@
         "columns": in_columns,
         "spread": [False] * 11,
         "device": lambda: lax.axis_index("frame"),
-        "late": lambda: placed(pieces((1, 2, 3), inner, 0), in_columns),
+        "late": lambda: [placed(pieces((i,), inner, 0), in_columns) for i in (1, 2, 3)],
         "again": lambda: placed(pieces((0,), inner, 0), in_columns),
         "outer": lambda: placed(pieces((0, 1, 2, 3), outer, 0), out_columns),
         "placed": lambda: [
@@ -478,7 +490,6 @@
         "missing": lambda: [(start, in_columns) for start in columns_of((1, 2, 3))],
     }
     fronted = run_front(gain, (devices, 2, share, width), [mine, *ready[:10]], plan)
-    third[1], *fronted = lax.optimization_barrier((third[1], *fronted))
     to_dx, to_dy = pl.pallas_call(
         functools.partial(turn_kernel, half),
         out_shape=(rows_of(depth + half), rows_of(depth + half)),
@@ -488,6 +499,7 @@
         name="turn",
     )(second[1], second[2], third[1], third[2])
     third += [swap(to_dx, 2, devices), swap(to_dy, 4, devices)]
+    third[3], *fronted = lax.optimization_barrier((third[3], *fronted))
     third += other_core(third)
     return fronted, [*ready, *third], plan
 

time: 101 us -> 101 us (level)
  waiting for transfers between devices: 40.3 us -> 38.5 us
  Pallas kernels: 14.6 us -> 16 us
    ppermute x23, waiting for transfers between devices: 28 us -> 26.2 us  [swap(): lax.ppermute(array, 'frame', [(f, f ^ distance) for f in range(devices)])]
  transfers between devices with their start and end apart: 26 -> 26, of which waited for: 12 -> 13; matrix products, arithmetic and copies ran while one was open for 0% -> 0% of each run, Pallas kernels for 2% -> 2%
where the time goes in v8:
time: 101 us
  waiting for transfers between devices  38.5 us (38%)
  starting transfers between devices  22.1 us (22%)
  blocking collectives  18 us (18%)
  Pallas kernels  16 us (16%)
  local copies, waits for them, and re-layouts  4.83 us (5%)
  between operations  1.42 us (1%)
    ppermute x23, waiting for transfers between devices, swap(): lax.ppermute(array, 'frame', [(f, f ^ distance) for f in range(devices)])  26.2 us
    all_to_all x1, blocking collectives, per_device(): lax.all_to_all(back, 'frame', split_axis=0, concat_axis=0, tiled=True)  18 us
    ppermute x23, starting transfers between devices, swap(): lax.ppermute(array, 'frame', [(f, f ^ distance) for f in range(devices)])  14.5 us
    pallas_call x1, Pallas kernels, run_main(): pl.pallas_call(functools.partial(main_kernel, plan), out_shape=jax.ShapeD...  13.4 us
    ppermute x3, waiting for transfers between devices, by_clip(): return lax.ppermute(array, 'clip', [(c, c ^ offset) for c in range(4)])  12.3 us
    ppermute x3, starting transfers between devices, by_clip(): return lax.ppermute(array, 'clip', [(c, c ^ offset) for c in range(4)])  7.55 us
    unnamed x10, local copies, waits for them, and re-layouts  3.77 us
  transfers between devices with their start and end apart: 26, of which 13 were waited for; matrix products, arithmetic and copies ran while one was open for 0% of the time, Pallas kernels for 2%

profile of v8, /device:TPU:0, one launch (start us, length us, event | category | flops | bytes accessed | tf_op | source)
XLA Modules:
  0.0 100.8 jit_solution(6351085796773441578)
XLA Ops:
  0.6 1.0 copy-done
  1.6 1.0 copy-done.1
  2.6 0.9 copy-done.2
  3.6 0.8 copy-done.3
  4.4 1.0 pack.1
  5.4 3.0 %collective-permute-start.1 = (bf16[320,1024]{1,0:T(8,128)(2,1)S(1)}, bf16[320,1024]{1,0:T(8,128)(2,1)S(1)}, u32[]{:S(2)}, u32[]{:S(2)}) collective-permute-start(bf16[320,1024]{1,0:T(8,128)(2,1)S(1)} %get-tuple-element.35), channel_id=1, source_target_pairs={{0,2},{1,3},{2,0},{3,1},{4,6},{5,7},{6,4},{7,5},{8,10},{9,11},{10,... | collective-permute-start | bytes 1966088 | tf_op jit(solution)/shard_map/ppermute | solution.py:296
  8.4 1.5 %collective-permute-start.2 = (bf16[320,1024]{1,0:T(8,128)(2,1)S(1)}, bf16[320,1024]{1,0:T(8,128)(2,1)S(1)}, u32[]{:S(2)}, u32[]{:S(2)}) collective-permute-start(bf16[320,1024]{1,0:T(8,128)(2,1)S(1)} %get-tuple-element.36), channel_id=1, source_target_pairs={{0,4},{1,5},{2,6},{3,7},{4,0},{5,1},{6,2},{7,3},{8,12},{9,13},{10,... | collective-permute-start | bytes 1966088 | tf_op jit(solution)/shard_map/ppermute | solution.py:296
  9.9 2.6 %collective-permute-start.5 = (bf16[128,1024]{1,0:T(8,128)(2,1)S(1)}, bf16[128,1024]{1,0:T(8,128)(2,1)S(1)}, u32[]{:S(2)}, u32[]{:S(2)}) collective-permute-start(bf16[128,1024]{1,0:T(8,128)(2,1)S(1)} %get-tuple-element.42.refs_2_.rest_0_), channel_id=1, source_target_pairs={{0,16},{8,24},{16,0},{24,8},{1,17},{9,25},{17,1},{25,9},{2,18},{10... | collective-permute-start | bytes 786440 | tf_op jit(solution)/shard_map/ppermute | solution.py:396
  12.5 1.6 %collective-permute-start = (bf16[128,1024]{1,0:T(8,128)(2,1)S(1)}, bf16[128,1024]{1,0:T(8,128)(2,1)S(1)}, u32[]{:S(2)}, u32[]{:S(2)}) collective-permute-start(bf16[128,1024]{1,0:T(8,128)(2,1)S(1)} %get-tuple-element.42.refs_2_.rest_0_), channel_id=1, source_target_pairs={{0,8},{8,0},{16,24},{24,16},{1,9},{9,1},{17,25},{25,17},{2,10},{10... | collective-permute-start | bytes 786440 | tf_op jit(solution)/shard_map/ppermute | solution.py:396
  14.1 9.9 %collective-permute-done.5.refs_0_ = bf16[128,1024]{1,0:T(8,128)(2,1)S(1)} collective-permute-done((bf16[128,1024]{1,0:T(8,128)(2,1)S(1)}, bf16[128,1024]{1,0:T(8,128)(2,1)S(1)}, u32[]{:S(2)}, u32[]{:S(2)}) %collective-permute-start.5) | collective-permute-done | bytes 262176 | tf_op jit(solution)/shard_map/ppermute | solution.py:396
  24.0 3.4 %collective-permute-start.6 = (bf16[128,1024]{1,0:T(8,128)(2,1)S(1)}, bf16[128,1024]{1,0:T(8,128)(2,1)S(1)}, u32[]{:S(2)}, u32[]{:S(2)}) collective-permute-start(bf16[128,1024]{1,0:T(8,128)(2,1)S(1)} %get-tuple-element.42.refs_2_.rest_0_), channel_id=1, source_target_pairs={{0,24},{8,16},{16,8},{24,0},{1,25},{9,17},{17,9},{25,1},{2,26},{10... | collective-permute-start | bytes 786440 | tf_op jit(solution)/shard_map/ppermute | solution.py:396
  27.4 0.0 collective-permute-done.1.refs_3_.rest_1_
  27.4 0.6 collective-permute-start.8
  28.0 0.0 collective-permute-done.2.refs_4_.rest_2_
  28.0 0.6 collective-permute-start.7
  28.6 0.0 collective-permute-done.rest_10_
  28.6 1.5 %collective-permute-start.4 = (bf16[128,1024]{1,0:T(8,128)(2,1)S(1)}, bf16[128,1024]{1,0:T(8,128)(2,1)S(1)}, u32[]{:S(2)}, u32[]{:S(2)}) collective-permute-start(bf16[128,1024]{1,0:T(8,128)(2,1)S(1)} %collective-permute-done.rest_10_), channel_id=1, source_target_pairs={{0,4},{1,5},{2,6},{3,7},{4,0},{5,1},{6,2},{7,3},{8,12},{9,13},{10,... | collective-permute-start | bytes 786440 | tf_op jit(solution)/shard_map/ppermute | solution.py:296
  30.1 1.5 %collective-permute-start.3 = (bf16[128,1024]{1,0:T(8,128)(2,1)S(1)}, bf16[128,1024]{1,0:T(8,128)(2,1)S(1)}, u32[]{:S(2)}, u32[]{:S(2)}) collective-permute-start(bf16[128,1024]{1,0:T(8,128)(2,1)S(1)} %collective-permute-done.rest_10_), channel_id=1, source_target_pairs={{0,2},{1,3},{2,0},{3,1},{4,6},{5,7},{6,4},{7,5},{8,10},{9,11},{10,... | collective-permute-start | bytes 786440 | tf_op jit(solution)/shard_map/ppermute | solution.py:296
  31.6 2.4 %collective-permute-done.6.refs_1_ = bf16[128,1024]{1,0:T(8,128)(2,1)S(1)} collective-permute-done((bf16[128,1024]{1,0:T(8,128)(2,1)S(1)}, bf16[128,1024]{1,0:T(8,128)(2,1)S(1)}, u32[]{:S(2)}, u32[]{:S(2)}) %collective-permute-start.6) | collective-permute-done | bytes 262176 | tf_op jit(solution)/shard_map/ppermute | solution.py:396
  34.0 2.7 %collective-permute-done.8.refs_6_.rest_4_ = bf16[128,1024]{1,0:T(8,128)(2,1)S(1)} collective-permute-done((bf16[128,1024]{1,0:T(8,128)(2,1)S(1)}, bf16[128,1024]{1,0:T(8,128)(2,1)S(1)}, u32[]{:S(2)}, u32[]{:S(2)}) %collective-permute-start.8) | collective-permute-done | bytes 262176 | tf_op jit(solution)/shard_map/ppermute | solution.py:296
  36.7 0.6 collective-permute-done.7.refs_5_.rest_3_
  37.4 1.6 %collective-permute-start.10 = (bf16[256,1024]{1,0:T(8,128)(2,1)S(1)}, bf16[256,1024]{1,0:T(8,128)(2,1)S(1)}, u32[]{:S(2)}, u32[]{:S(2)}) collective-permute-start(bf16[256,1024]{1,0:T(8,128)(2,1)S(1)} %join.1.rest_16_), channel_id=1, source_target_pairs={{0,4},{1,5},{2,6},{3,7},{4,0},{5,1},{6,2},{7,3},{8,12},{9,13},{10,... | collective-permute-start | bytes 1572872 | tf_op jit(solution)/shard_map/ppermute | solution.py:296
  39.0 0.5 collective-permute-start.9
  39.5 0.0 collective-permute-start.17
  39.5 2.8 %collective-permute-done.4.by_y.rest_12_ = bf16[128,1024]{1,0:T(8,128)(2,1)S(1)} collective-permute-done((bf16[128,1024]{1,0:T(8,128)(2,1)S(1)}, bf16[128,1024]{1,0:T(8,128)(2,1)S(1)}, u32[]{:S(2)}, u32[]{:S(2)}) %collective-permute-start.4) | collective-permute-done | bytes 262176 | tf_op jit(solution)/shard_map/ppermute | solution.py:296
  42.3 0.6 collective-permute-done.3.by_x.rest_11_
  42.9 0.0 collective-permute-start.18
  43.0 0.5 collective-permute-start.13
  43.5 0.0 collective-permute-done.17.rest_13_
  43.5 0.0 collective-permute-start.14
  43.5 1.0 %collective-permute-done.18.rest_14_ = bf16[128,1024]{1,0:T(8,128)(2,1)S(1)} collective-permute-done((bf16[128,1024]{1,0:T(8,128)(2,1)S(1)}, bf16[128,1024]{1,0:T(8,128)(2,1)S(1)}, u32[]{:S(2)}, u32[]{:S(2)}) %collective-permute-start.18) | collective-permute-done | bytes 262176 | tf_op jit(solution)/shard_map/ppermute | solution.py:296
  44.5 0.1 collective-permute-start.15
  44.6 7.7 %collective-permute-done.10.pair_y.rest_18_ = bf16[256,1024]{1,0:T(8,128)(2,1)S(1)} collective-permute-done((bf16[256,1024]{1,0:T(8,128)(2,1)S(1)}, bf16[256,1024]{1,0:T(8,128)(2,1)S(1)}, u32[]{:S(2)}, u32[]{:S(2)}) %collective-permute-start.10) | collective-permute-done | bytes 524320 | tf_op jit(solution)/shard_map/ppermute | solution.py:296
  52.3 0.0 collective-permute-start.16
  52.3 0.3 collective-permute-done.9.pair_x.rest_17_
  52.6 0.2 collective-permute-start.12
  52.8 0.1 turn.1
  52.9 0.0 copy-start.4
  52.9 0.0 collective-permute-done.15.refs_10_.rest_8_
  52.9 0.6 collective-permute-start.11
  53.5 0.3 collective-permute-done.16.refs_11_.rest_9_
  53.8 1.0 collective-permute-start.20
  54.8 0.0 collective-permute-done.12.refs_7_.rest_5_
  54.8 0.0 collective-permute-start.19
  54.8 0.0 collective-permute-done.13.refs_8_.rest_6_
  54.8 0.5 collective-permute-start.21
  55.3 0.0 collective-permute-done.14.refs_9_.rest_7_
  55.3 0.1 collective-permute-start.23
  55.4 8.9 %collective-permute-done.11.rest_19_ = bf16[192,1024]{1,0:T(8,128)(2,1)S(1)} collective-permute-done((bf16[192,1024]{1,0:T(8,128)(2,1)S(1)}, bf16[192,1024]{1,0:T(8,128)(2,1)S(1)}, u32[]{:S(2)}, u32[]{:S(2)}) %collective-permute-start.11) | collective-permute-done | bytes 393248 | tf_op jit(solution)/shard_map/ppermute | solution.py:296
  64.3 0.0 collective-permute-start.22
  64.3 1.6 %front.1 = (bf16[8,2,32,1024]{3,2,1,0:T(8,128)(2,1)S(1)}, bf16[256,1024]{1,0:T(8,128)(2,1)S(1)}, f32[256,128]{1,0:T(8,128)S(1)}, bf16[256,768]{1,0:T(8,128)(2,1)S(1)}) custom-call(f32[1,1024]{1,0:T(1,128)S(1)} %bitcast.11, bf16[64,1024]{1,0:T(8,128)(2,1)S(1)} %get-tuple-element.50.refs_1_, bf16[128,1024]{1,0:T(8,128)(2,1)S(1)} %get-tuple-element.42.refs_2_.rest_0_, ...), custom_call_target="tpu_custom_call" | custom-call | flops 256 | bytes 256 | tf_op jit(solution)/shard_map/front/pallas_call | solution.py:235
  65.9 0.0 collective-permute-done.20.rest_20_
  65.9 0.6 collective-permute-start.25
  66.5 0.0 collective-permute-done.19.rest_15_
  66.5 0.1 collective-permute-start.24
  67.2 0.0 collective-permute-done.21.rest_21_
  67.2 0.0 collective-permute-done.23.rest_23_
  67.2 0.0 collective-permute-done.22.rest_22_
  67.3 0.6 collective-permute-done.25.rest_25_
  67.8 0.6 collective-permute-done.24.rest_24_
  68.4 13.4 %main.1 = bf16[8,2,32,1024]{3,2,1,0:T(8,128)(2,1)S(1)} custom-call(s32[1]{0:T(128)S(6)} %copy.9.counts_ref, f32[1,1024]{1,0:T(1,128)S(1)} %bitcast.12, bf16[8,2,32,1024]{3,2,1,0:T(8,128)(2,1)S(1)} %get-tuple-element.60.both_ref, bf16[256,1024]{1,0:T(8,128)(2,1)S(1)} %get-tuple-element.61.normed_ref, f32[256,128]{1,0:T(8,128)S(1)} %get-tuple-element.62.stats_ref, ...), custom_call_target="tpu_custom_call" | custom-call | flops 3221225472 | bytes 10485760 | tf_op jit(solution)/shard_map/main/pallas_call | solution.py:264
  81.8 18.0 %all_to_all.5 = bf16[8,1,2,32,1024]{4,3,2,1,0:T(8,128)(2,1)S(1)} all-to-all(bf16[8,1,2,32,1024]{4,3,2,1,0:T(8,128)(2,1)S(1)} %bitcast.10), channel_id=1, replica_groups=mesh['clip'=4,'frame'=8] {'frame'}, dimensions={0} | all-to-all | bytes 2097152 | tf_op jit(solution)/shard_map/all_to_all | solution.py:555
  99.7 0.1 fusion
  99.8 0.9 slice_bitcast_fusion
  (8 shorter events, 0.1 us)
Async XLA Ops:
  0.6 1.0 copy-start
  1.6 1.0 copy-start.1
  2.6 0.9 copy-start.2
  3.6 0.8 copy-start.3
  5.4 22.0 %collective-permute-start.1 = (bf16[320,1024]{1,0:T(8,128)(2,1)S(1)}, bf16[320,1024]{1,0:T(8,128)(2,1)S(1)}, u32[]{:S(2)}, u32[]{:S(2)}) collective-permute-start(bf16[320,1024]{1,0:T(8,128)(2,1)S(1)} %get-tuple-element.35), channel_id=1, source_target_pairs={{0,2},{1,3},{2,0},{3,1},{4,6},{5,7},{6,4},{7,5},{8,10},{9,11},{10,... | collective-permute-start | bytes 1966088 | tf_op jit(solution)/shard_map/ppermute | solution.py:296
  8.4 19.6 %collective-permute-start.2 = (bf16[320,1024]{1,0:T(8,128)(2,1)S(1)}, bf16[320,1024]{1,0:T(8,128)(2,1)S(1)}, u32[]{:S(2)}, u32[]{:S(2)}) collective-permute-start(bf16[320,1024]{1,0:T(8,128)(2,1)S(1)} %get-tuple-element.36), channel_id=1, source_target_pairs={{0,4},{1,5},{2,6},{3,7},{4,0},{5,1},{6,2},{7,3},{8,12},{9,13},{10,... | collective-permute-start | bytes 1966088 | tf_op jit(solution)/shard_map/ppermute | solution.py:296
  9.9 14.1 %collective-permute-start.5 = (bf16[128,1024]{1,0:T(8,128)(2,1)S(1)}, bf16[128,1024]{1,0:T(8,128)(2,1)S(1)}, u32[]{:S(2)}, u32[]{:S(2)}) collective-permute-start(bf16[128,1024]{1,0:T(8,128)(2,1)S(1)} %get-tuple-element.42.refs_2_.rest_0_), channel_id=1, source_target_pairs={{0,16},{8,24},{16,0},{24,8},{1,17},{9,25},{17,1},{25,9},{2,18},{10... | collective-permute-start | bytes 786440 | tf_op jit(solution)/shard_map/ppermute | solution.py:396
  12.5 16.1 %collective-permute-start = (bf16[128,1024]{1,0:T(8,128)(2,1)S(1)}, bf16[128,1024]{1,0:T(8,128)(2,1)S(1)}, u32[]{:S(2)}, u32[]{:S(2)}) collective-permute-start(bf16[128,1024]{1,0:T(8,128)(2,1)S(1)} %get-tuple-element.42.refs_2_.rest_0_), channel_id=1, source_target_pairs={{0,8},{8,0},{16,24},{24,16},{1,9},{9,1},{17,25},{25,17},{2,10},{10... | collective-permute-start | bytes 786440 | tf_op jit(solution)/shard_map/ppermute | solution.py:396
  24.0 10.0 %collective-permute-start.6 = (bf16[128,1024]{1,0:T(8,128)(2,1)S(1)}, bf16[128,1024]{1,0:T(8,128)(2,1)S(1)}, u32[]{:S(2)}, u32[]{:S(2)}) collective-permute-start(bf16[128,1024]{1,0:T(8,128)(2,1)S(1)} %get-tuple-element.42.refs_2_.rest_0_), channel_id=1, source_target_pairs={{0,24},{8,16},{16,8},{24,0},{1,25},{9,17},{17,9},{25,1},{2,26},{10... | collective-permute-start | bytes 786440 | tf_op jit(solution)/shard_map/ppermute | solution.py:396
  27.4 9.3 %collective-permute-start.8 = (bf16[128,1024]{1,0:T(8,128)(2,1)S(1)}, bf16[128,1024]{1,0:T(8,128)(2,1)S(1)}, u32[]{:S(2)}, u32[]{:S(2)}) collective-permute-start(bf16[128,1024]{1,0:T(8,128)(2,1)S(1)} %slice.25), channel_id=1, source_target_pairs={{0,4},{1,5},{2,6},{3,7},{4,0},{5,1},{6,2},{7,3},{8,12},{9,13},{10,... | collective-permute-start | bytes 786440 | tf_op jit(solution)/shard_map/ppermute | solution.py:296
  28.0 9.3 %collective-permute-start.7 = (bf16[128,1024]{1,0:T(8,128)(2,1)S(1)}, bf16[128,1024]{1,0:T(8,128)(2,1)S(1)}, u32[]{:S(2)}, u32[]{:S(2)}) collective-permute-start(bf16[128,1024]{1,0:T(8,128)(2,1)S(1)} %slice.24), channel_id=1, source_target_pairs={{0,2},{1,3},{2,0},{3,1},{4,6},{5,7},{6,4},{7,5},{8,10},{9,11},{10,... | collective-permute-start | bytes 786440 | tf_op jit(solution)/shard_map/ppermute | solution.py:296
  28.6 13.7 %collective-permute-start.4 = (bf16[128,1024]{1,0:T(8,128)(2,1)S(1)}, bf16[128,1024]{1,0:T(8,128)(2,1)S(1)}, u32[]{:S(2)}, u32[]{:S(2)}) collective-permute-start(bf16[128,1024]{1,0:T(8,128)(2,1)S(1)} %collective-permute-done.rest_10_), channel_id=1, source_target_pairs={{0,4},{1,5},{2,6},{3,7},{4,0},{5,1},{6,2},{7,3},{8,12},{9,13},{10,... | collective-permute-start | bytes 786440 | tf_op jit(solution)/shard_map/ppermute | solution.py:296
  30.1 12.8 %collective-permute-start.3 = (bf16[128,1024]{1,0:T(8,128)(2,1)S(1)}, bf16[128,1024]{1,0:T(8,128)(2,1)S(1)}, u32[]{:S(2)}, u32[]{:S(2)}) collective-permute-start(bf16[128,1024]{1,0:T(8,128)(2,1)S(1)} %collective-permute-done.rest_10_), channel_id=1, source_target_pairs={{0,2},{1,3},{2,0},{3,1},{4,6},{5,7},{6,4},{7,5},{8,10},{9,11},{10,... | collective-permute-start | bytes 786440 | tf_op jit(solution)/shard_map/ppermute | solution.py:296
  37.4 14.9 %collective-permute-start.10 = (bf16[256,1024]{1,0:T(8,128)(2,1)S(1)}, bf16[256,1024]{1,0:T(8,128)(2,1)S(1)}, u32[]{:S(2)}, u32[]{:S(2)}) collective-permute-start(bf16[256,1024]{1,0:T(8,128)(2,1)S(1)} %join.1.rest_16_), channel_id=1, source_target_pairs={{0,4},{1,5},{2,6},{3,7},{4,0},{5,1},{6,2},{7,3},{8,12},{9,13},{10,... | collective-permute-start | bytes 1572872 | tf_op jit(solution)/shard_map/ppermute | solution.py:296
  39.0 13.7 %collective-permute-start.9 = (bf16[256,1024]{1,0:T(8,128)(2,1)S(1)}, bf16[256,1024]{1,0:T(8,128)(2,1)S(1)}, u32[]{:S(2)}, u32[]{:S(2)}) collective-permute-start(bf16[256,1024]{1,0:T(8,128)(2,1)S(1)} %join.1.rest_16_), channel_id=1, source_target_pairs={{0,2},{1,3},{2,0},{3,1},{4,6},{5,7},{6,4},{7,5},{8,10},{9,11},{10,... | collective-permute-start | bytes 1572872 | tf_op jit(solution)/shard_map/ppermute | solution.py:296
  39.5 4.0 %collective-permute-start.17 = (bf16[128,1024]{1,0:T(8,128)(2,1)S(1)}, bf16[128,1024]{1,0:T(8,128)(2,1)S(1)}, u32[]{:S(2)}, u32[]{:S(2)}) collective-permute-start(bf16[128,1024]{1,0:T(8,128)(2,1)S(1)} %collective-permute-done.rest_10_), channel_id=1, source_target_pairs={{0,1},{1,0},{2,3},{3,2},{4,5},{5,4},{6,7},{7,6},{8,9},{9,8},{10,11... | collective-permute-start | bytes 786440 | tf_op jit(solution)/shard_map/ppermute | solution.py:296
  42.9 1.5 %collective-permute-start.18 = (bf16[128,1024]{1,0:T(8,128)(2,1)S(1)}, bf16[128,1024]{1,0:T(8,128)(2,1)S(1)}, u32[]{:S(2)}, u32[]{:S(2)}) collective-permute-start(bf16[128,1024]{1,0:T(8,128)(2,1)S(1)} %collective-permute-done.3.by_x.rest_11_), channel_id=1, source_target_pairs={{0,1},{1,0},{2,3},{3,2},{4,5},{5,4},{6,7},{7,6},{8,9},{9,8},{10,11... | collective-permute-start | bytes 786440 | tf_op jit(solution)/shard_map/ppermute | solution.py:296
  43.0 11.9 %collective-permute-start.13 = (bf16[320,1024]{1,0:T(8,128)(2,1)S(1)}, bf16[320,1024]{1,0:T(8,128)(2,1)S(1)}, u32[]{:S(2)}, u32[]{:S(2)}) collective-permute-start(bf16[320,1024]{1,0:T(8,128)(2,1)S(1)} %collective-permute-done.1.refs_3_.rest_1_), channel_id=1, source_target_pairs={{0,1},{1,0},{2,3},{3,2},{4,5},{5,4},{6,7},{7,6},{8,9},{9,8},{10,11... | collective-permute-start | bytes 1966088 | tf_op jit(solution)/shard_map/ppermute | solution.py:296
  43.5 11.9 %collective-permute-start.14 = (bf16[320,1024]{1,0:T(8,128)(2,1)S(1)}, bf16[320,1024]{1,0:T(8,128)(2,1)S(1)}, u32[]{:S(2)}, u32[]{:S(2)}) collective-permute-start(bf16[320,1024]{1,0:T(8,128)(2,1)S(1)} %collective-permute-done.2.refs_4_.rest_2_), channel_id=1, source_target_pairs={{0,1},{1,0},{2,3},{3,2},{4,5},{5,4},{6,7},{7,6},{8,9},{9,8},{10,11... | collective-permute-start | bytes 1966088 | tf_op jit(solution)/shard_map/ppermute | solution.py:296
  44.5 8.4 %collective-permute-start.15 = (bf16[128,1024]{1,0:T(8,128)(2,1)S(1)}, bf16[128,1024]{1,0:T(8,128)(2,1)S(1)}, u32[]{:S(2)}, u32[]{:S(2)}) collective-permute-start(bf16[128,1024]{1,0:T(8,128)(2,1)S(1)} %collective-permute-done.7.refs_5_.rest_3_), channel_id=1, source_target_pairs={{0,1},{1,0},{2,3},{3,2},{4,5},{5,4},{6,7},{7,6},{8,9},{9,8},{10,11... | collective-permute-start | bytes 786440 | tf_op jit(solution)/shard_map/ppermute | solution.py:296
  52.3 1.5 %collective-permute-start.16 = (bf16[128,1024]{1,0:T(8,128)(2,1)S(1)}, bf16[128,1024]{1,0:T(8,128)(2,1)S(1)}, u32[]{:S(2)}, u32[]{:S(2)}) collective-permute-start(bf16[128,1024]{1,0:T(8,128)(2,1)S(1)} %collective-permute-done.8.refs_6_.rest_4_), channel_id=1, source_target_pairs={{0,1},{1,0},{2,3},{3,2},{4,5},{5,4},{6,7},{7,6},{8,9},{9,8},{10,11... | collective-permute-start | bytes 786440 | tf_op jit(solution)/shard_map/ppermute | solution.py:296
  52.6 2.2 %collective-permute-start.12 = (bf16[192,1024]{1,0:T(8,128)(2,1)S(1)}, bf16[192,1024]{1,0:T(8,128)(2,1)S(1)}, u32[]{:S(2)}, u32[]{:S(2)}) collective-permute-start(bf16[192,1024]{1,0:T(8,128)(2,1)S(1)} %get-tuple-element.55), channel_id=1, source_target_pairs={{0,1},{1,0},{2,3},{3,2},{4,5},{5,4},{6,7},{7,6},{8,9},{9,8},{10,11... | collective-permute-start | bytes 1179656 | tf_op jit(solution)/shard_map/ppermute | solution.py:296
  52.9 11.4 %copy-start.4 = (f32[1024]{0:T(1024)S(1)}, f32[1024]{0:T(1024)}, u32[]{:S(2)}) copy-start(f32[1024]{0:T(1024)} %param.8) | copy-start | bytes 12292
  52.9 11.4 %collective-permute-start.11 = (bf16[192,1024]{1,0:T(8,128)(2,1)S(1)}, bf16[192,1024]{1,0:T(8,128)(2,1)S(1)}, u32[]{:S(2)}, u32[]{:S(2)}) collective-permute-start(bf16[192,1024]{1,0:T(8,128)(2,1)S(1)} %get-tuple-element.49), channel_id=1, source_target_pairs={{0,2},{1,3},{2,0},{3,1},{4,6},{5,7},{6,4},{7,5},{8,10},{9,11},{10,... | collective-permute-start | bytes 1179656 | tf_op jit(solution)/shard_map/ppermute | solution.py:296
  53.8 12.1 %collective-permute-start.20 = (bf16[192,1024]{1,0:T(8,128)(2,1)S(1)}, bf16[192,1024]{1,0:T(8,128)(2,1)S(1)}, u32[]{:S(2)}, u32[]{:S(2)}) collective-permute-start(bf16[192,1024]{1,0:T(8,128)(2,1)S(1)} %get-tuple-element.65), channel_id=1, source_target_pairs={{0,4},{1,5},{2,6},{3,7},{4,0},{5,1},{6,2},{7,3},{8,12},{9,13},{10,... | collective-permute-start | bytes 1179656 | tf_op jit(solution)/shard_map/ppermute | solution.py:296
  54.8 11.7 %collective-permute-start.19 = (bf16[128,1024]{1,0:T(8,128)(2,1)S(1)}, bf16[128,1024]{1,0:T(8,128)(2,1)S(1)}, u32[]{:S(2)}, u32[]{:S(2)}) collective-permute-start(bf16[128,1024]{1,0:T(8,128)(2,1)S(1)} %collective-permute-done.4.by_y.rest_12_), channel_id=1, source_target_pairs={{0,1},{1,0},{2,3},{3,2},{4,5},{5,4},{6,7},{7,6},{8,9},{9,8},{10,11... | collective-permute-start | bytes 786440 | tf_op jit(solution)/shard_map/ppermute | solution.py:296
  54.8 12.4 %collective-permute-start.21 = (bf16[256,1024]{1,0:T(8,128)(2,1)S(1)}, bf16[256,1024]{1,0:T(8,128)(2,1)S(1)}, u32[]{:S(2)}, u32[]{:S(2)}) collective-permute-start(bf16[256,1024]{1,0:T(8,128)(2,1)S(1)} %join.1.rest_16_), channel_id=1, source_target_pairs={{0,1},{1,0},{2,3},{3,2},{4,5},{5,4},{6,7},{7,6},{8,9},{9,8},{10,11... | collective-permute-start | bytes 1572872 | tf_op jit(solution)/shard_map/ppermute | solution.py:296
  55.3 11.9 %collective-permute-start.23 = (bf16[256,1024]{1,0:T(8,128)(2,1)S(1)}, bf16[256,1024]{1,0:T(8,128)(2,1)S(1)}, u32[]{:S(2)}, u32[]{:S(2)}) collective-permute-start(bf16[256,1024]{1,0:T(8,128)(2,1)S(1)} %collective-permute-done.10.pair_y.rest_18_), channel_id=1, source_target_pairs={{0,1},{1,0},{2,3},{3,2},{4,5},{5,4},{6,7},{7,6},{8,9},{9,8},{10,11... | collective-permute-start | bytes 1572872 | tf_op jit(solution)/shard_map/ppermute | solution.py:296
  64.3 3.0 %collective-permute-start.22 = (bf16[256,1024]{1,0:T(8,128)(2,1)S(1)}, bf16[256,1024]{1,0:T(8,128)(2,1)S(1)}, u32[]{:S(2)}, u32[]{:S(2)}) collective-permute-start(bf16[256,1024]{1,0:T(8,128)(2,1)S(1)} %collective-permute-done.9.pair_x.rest_17_), channel_id=1, source_target_pairs={{0,1},{1,0},{2,3},{3,2},{4,5},{5,4},{6,7},{7,6},{8,9},{9,8},{10,11... | collective-permute-start | bytes 1572872 | tf_op jit(solution)/shard_map/ppermute | solution.py:296
  65.9 1.9 %collective-permute-start.25 = (bf16[192,1024]{1,0:T(8,128)(2,1)S(1)}, bf16[192,1024]{1,0:T(8,128)(2,1)S(1)}, u32[]{:S(2)}, u32[]{:S(2)}) collective-permute-start(bf16[192,1024]{1,0:T(8,128)(2,1)S(1)} %collective-permute-done.20.rest_20_), channel_id=1, source_target_pairs={{0,1},{1,0},{2,3},{3,2},{4,5},{5,4},{6,7},{7,6},{8,9},{9,8},{10,11... | collective-permute-start | bytes 1179656 | tf_op jit(solution)/shard_map/ppermute | solution.py:296
  66.5 1.9 %collective-permute-start.24 = (bf16[192,1024]{1,0:T(8,128)(2,1)S(1)}, bf16[192,1024]{1,0:T(8,128)(2,1)S(1)}, u32[]{:S(2)}, u32[]{:S(2)}) collective-permute-start(bf16[192,1024]{1,0:T(8,128)(2,1)S(1)} %collective-permute-done.11.rest_19_), channel_id=1, source_target_pairs={{0,1},{1,0},{2,3},{3,2},{4,5},{5,4},{6,7},{7,6},{8,9},{9,8},{10,11... | collective-permute-start | bytes 1179656 | tf_op jit(solution)/shard_map/ppermute | solution.py:296

commit v9 on v8

--- a/solution.py
+++ b/solution.py
@@ -17,30 +17,12 @@
 NT = (((1,), (1,)), ((), ()))
 TN = (((0,), (0,)), ((), ()))
 VMEM_LIMIT = 27 * 1024 * 1024
+PACK_LIMIT = 58 * 1024 * 1024
 SMALL = pltpu.CompilerParams(vmem_limit_bytes=6 * 1024 * 1024)
 
 
 def dot(a, b, dims):
     return lax.dot_general(a, b, dims, preferred_element_type=jnp.float32)
-
-
-def fetch(parts, refs, target, sem):
-    copies = []
-    for ref, index, first, depth, lanes, row, column in parts:
-        source = refs[ref] if index is None else refs[ref].at[index]
-        copies.append(
-            pltpu.make_async_copy(
-                source.at[pl.ds(first, depth), pl.ds(*lanes)],
-                target.at[
-                    pl.ds(pl.multiple_of(row, 16), depth),
-                    pl.ds(pl.multiple_of(column, 128), lanes[1]),
-                ],
-                sem,
-            )
-        )
-    for copy in copies:
-        copy.start()
-    return copies
 
 
 def wait(copies):
@@ -53,11 +35,39 @@
     return ref[:, which, group * SUB : (group + 1) * SUB, :].reshape(frames * SUB, width)
 
 
-def front_kernel(plan, *refs):
-    gain_ref, *sources = refs[:-6]
-    both_ref, normed_ref, stats_ref, proj_ref, w_front, sems = refs[-6:]
-    copies = fetch(plan["front"](), sources, w_front, sems.at[0])
-    plan["tokens"](sources, both_ref)
+def beside(ref, starts, size):
+    return jnp.concatenate(
+        [ref[:, pl.ds(pl.multiple_of(start, 128), size)] for start in starts], axis=1
+    )
+
+
+def chunks(columns):
+    step = math.gcd(columns, 256)
+    return [(start, step) for start in range(0, columns, step)]
+
+
+def stack_rows(view, refs, block, lanes):
+    return jnp.concatenate(
+        [view.piece(refs, block, *part, lanes) for parts in view.rows for part in parts], axis=0
+    )
+
+
+def stack_columns(view, refs, parts, start, size):
+    return jnp.concatenate(
+        [
+            jnp.concatenate(
+                [view.piece(refs, block, *part, (start, size)) for part in parts], axis=0
+            )
+            for block in range(view.blocks)
+        ],
+        axis=1,
+    )
+
+
+def front_kernel(view, gain_ref, *refs):
+    sources = refs[:-5]
+    both_ref, normed_ref, stats_ref, proj_ref, natural = refs[-5:]
+    view.tokens(sources, both_ref)
     frames, _, patches, _ = both_ref.shape
     rows = frames * SUB
     for group in range(patches // SUB):
@@ -67,43 +77,36 @@
         centred = wide - average
         variance = jnp.mean(centred * centred, axis=-1, keepdims=True)
         scale = lax.rsqrt(variance + EPSILON)
-        normed_ref[here, :] = (centred * scale * gain_ref[...]).astype(jnp.bfloat16)
+        natural[here, :] = (centred * scale * gain_ref[...]).astype(jnp.bfloat16)
         stats_ref[here, 0:1] = average
         stats_ref[here, 1:2] = scale
-    wait(copies)
-    columns = w_front.shape[1]
-    step = math.gcd(columns, 512)
-
-    @pl.loop(0, columns // step)
-    def _(j):
-        here = pl.ds(pl.multiple_of(j * step, step), step)
-        proj_ref[:, here] = dot(normed_ref[...], w_front[:, here], NN).astype(jnp.bfloat16)
-
-
-def main_kernel(plan, counts_ref, gain_ref, both_ref, normed_ref, stats_ref, front_ref, *rest):
-    weight_refs = rest[:-14]
-    out_ref, w_in, w_out, grads, proj, ga, att, gproj, gnorm, bias, scores, gprobs, low, sems = rest[-14:]
+    normed_ref[...] = beside(natural, *view.row_order())
+    for start, size in chunks(proj_ref.shape[1]):
+        weight = stack_rows(view, sources, 0, (start, size))
+        proj_ref[:, start : start + size] = dot(normed_ref[...], weight, NN).astype(jnp.bfloat16)
+
+
+def main_kernel(view, counts_ref, gain_ref, both_ref, normed_ref, stats_ref, front_ref, *rest):
+    weights = rest[:-11]
+    out_ref, grads, proj, ga, att, gproj, wide_sum, bias, scores, gprobs, low = rest[-11:]
     frames, _, patches, width = both_ref.shape
     groups = patches // SUB
     rows = frames * SUB
     count = counts_ref[0]
-
-    device = plan["device"]()
-    place = [
-        pltpu.make_async_copy(
-            front_ref.at[:, pl.ds(start, size)],
-            proj.at[:, pl.ds(pl.multiple_of(target, 128), size)],
-            sems.at[3],
-        )
-        for start, target, size in plan["placed"]()
-    ]
-    for copy in place:
-        copy.start()
-    outer = fetch(plan["outer"](), weight_refs, w_out, sems.at[1])
-    late = [
-        fetch(parts, weight_refs, w_in, sems.at[4 + i]) for i, parts in enumerate(plan["late"]())
-    ]
-    again = fetch(plan["again"](), weight_refs, w_in, sems.at[2])
+    device = view.device()
+    in_columns, out_columns = view.in_columns, view.out_columns
+    row_starts, row_size = view.row_order()
+    block_order = view.block_order()
+
+    def column(block, stride, start=0):
+        return pl.multiple_of(block_order[block] * stride + start, 128)
+
+    def put_rows(target, parts, value):
+        done = 0
+        for index, first, depth in parts:
+            start = pl.multiple_of(row_starts[index] + first, 128)
+            target[:, pl.ds(start, depth)] = value[:, done : done + depth]
+            done += depth
 
     def real(index):
         return ((index // SUB) ^ device) < count
@@ -121,20 +124,18 @@
     low_lanes = (lane < DH).astype(jnp.bfloat16)
     high_lanes = (lane >= DH).astype(jnp.bfloat16)
 
-    wait(outer)
-    step = min(width, 256)
-
-    @pl.loop(0, width // step)
-    def _(j):
-        columns = pl.ds(pl.multiple_of(j * step, step), step)
-        ga[:, columns] = dot(grads[...], w_out[columns, :], NT).astype(jnp.bfloat16)
-
-    for (start, size), copies in zip(plan["missing"](), late):
-        wait(copies)
-        columns = pl.ds(pl.multiple_of(start, 128), size)
-        proj[:, columns] = dot(normed_ref[...], w_in[:, columns], NN).astype(jnp.bfloat16)
-
-    wait(place)
+    grads_ordered = beside(grads, [column(i, out_columns) for i in range(view.blocks)], out_columns)
+    for parts in view.rows:
+        weight = stack_columns(view, weights, parts, in_columns, out_columns)
+        put_rows(ga, parts, dot(grads_ordered, weight, NT).astype(jnp.bfloat16))
+
+    proj[:, pl.ds(column(0, in_columns), in_columns)] = front_ref[...]
+    for block in range(1, view.blocks):
+        for start, size in chunks(in_columns):
+            weight = stack_rows(view, weights, block, (start, size))
+            proj[:, pl.ds(column(block, in_columns, start), size)] = dot(
+                normed_ref[...], weight, NN
+            ).astype(jnp.bfloat16)
 
     def apart(block):
         return jnp.concatenate([block * low_lanes, block * high_lanes], axis=0)
@@ -199,22 +200,27 @@
                 frame * SUB : (frame + 1) * SUB
             ].reshape(1, SUB, width)
 
+    att_ordered = beside(att, row_starts, row_size)
+    for block in range(view.blocks):
+        for start, size in chunks(out_columns):
+            weight = stack_rows(view, weights, block, (in_columns + start, size))
+            wide_sum[:, pl.ds(column(block, out_columns, start), size)] = dot(
+                att_ordered, weight, NN
+            )
+
     for group in range(groups):
         here = pl.ds(group * rows, rows)
-        mixed = dot(att[here, :], w_out[...], NN)
         wide = load_rows(both_ref, 0, group).astype(jnp.float32)
-        store(0, group, (wide + live * mixed).astype(jnp.bfloat16))
-
-    wait(again)
-
-    @pl.loop(0, width // step)
-    def _(j):
-        columns = pl.ds(pl.multiple_of(j * step, step), step)
-        gnorm[:, columns] = dot(gproj[...], w_in[columns, :], NT)
+        store(0, group, (wide + live * wide_sum[here, :]).astype(jnp.bfloat16))
+
+    gproj_ordered = beside(gproj, [column(i, in_columns) for i in range(view.blocks)], in_columns)
+    for parts in view.rows:
+        weight = stack_columns(view, weights, parts, 0, in_columns)
+        put_rows(wide_sum, parts, dot(gproj_ordered, weight, NT))
 
     for group in range(groups):
         here = pl.ds(group * rows, rows)
-        grad = gnorm[here, :] * gain_ref[...]
+        grad = wide_sum[here, :] * gain_ref[...]
         scale = stats_ref[here, 1:2]
         hat = (load_rows(both_ref, 0, group).astype(jnp.float32) - stats_ref[here, 0:1]) * scale
         grad_rows = scale * (
@@ -226,50 +232,40 @@
         store(1, group, (cot + grad_rows).astype(jnp.bfloat16))
 
 
-def run_front(gain, shape, sources, plan):
+def run_front(gain, shape, sources, view):
     frames, _, patches, width = shape
     total = frames * patches
     vmem = pl.BlockSpec(memory_space=pltpu.VMEM)
-    anywhere = pl.BlockSpec(memory_space=pl.ANY)
-    columns = plan["columns"]
     return pl.pallas_call(
-        functools.partial(front_kernel, plan),
+        functools.partial(front_kernel, view),
         out_shape=(
             jax.ShapeDtypeStruct(shape, jnp.bfloat16),
             jax.ShapeDtypeStruct((total, width), jnp.bfloat16),
             jax.ShapeDtypeStruct((total, 128), jnp.float32),
-            jax.ShapeDtypeStruct((total, columns), jnp.bfloat16),
+            jax.ShapeDtypeStruct((total, view.in_columns), jnp.bfloat16),
         ),
-        in_specs=[vmem] + [anywhere if wide else vmem for wide in plan["spread"]],
-        out_specs=(vmem, vmem, vmem, vmem),
-        scratch_shapes=[
-            pltpu.VMEM((width, columns), jnp.bfloat16),
-            pltpu.SemaphoreType.DMA((1,)),
-        ],
+        in_specs=[vmem] * (1 + len(sources)),
+        out_specs=(vmem,) * 4,
+        scratch_shapes=[pltpu.VMEM((total, width), jnp.bfloat16)],
         compiler_params=pltpu.CompilerParams(vmem_limit_bytes=VMEM_LIMIT),
         cost_estimate=pl.CostEstimate(flops=total, bytes_accessed=total, transcendentals=0),
         name="front",
     )(gain, *sources)
 
 
-def run_main(counts, gain, fronted, weights, plan):
+def run_main(counts, gain, fronted, weights, view):
     both, normed, stats, front = fronted
     frames, _, patches, width = both.shape
     total, rows = frames * patches, frames * SUB
     vmem = pl.BlockSpec(memory_space=pltpu.VMEM)
     smem = pl.BlockSpec(memory_space=pltpu.SMEM)
-    anywhere = pl.BlockSpec(memory_space=pl.ANY)
-    params = pltpu.CompilerParams(vmem_limit_bytes=VMEM_LIMIT if rows <= 128 else 2 * VMEM_LIMIT)
     chunk = 8 if rows <= 128 else 1
     return pl.pallas_call(
-        functools.partial(main_kernel, plan),
+        functools.partial(main_kernel, view),
         out_shape=jax.ShapeDtypeStruct(both.shape, jnp.bfloat16),
-        in_specs=[smem, vmem, vmem, vmem, vmem, anywhere]
-        + [anywhere] * len(weights),
+        in_specs=[smem] + [vmem] * (5 + len(weights)),
         out_specs=vmem,
         scratch_shapes=[
-            pltpu.VMEM((width, 3 * width), jnp.bfloat16),
-            pltpu.VMEM((width, width), jnp.bfloat16),
             pltpu.VMEM((total, width), jnp.bfloat16),
             pltpu.VMEM((total, 3 * width), jnp.bfloat16),
             pltpu.VMEM((total, width), jnp.bfloat16),
@@ -280,9 +276,10 @@
             pltpu.VMEM((chunk, rows, 2 * rows), jnp.float32),
             pltpu.VMEM((chunk, rows, 2 * rows), jnp.float32),
             pltpu.VMEM((chunk, 2, rows, 2 * rows), jnp.bfloat16),
-            pltpu.SemaphoreType.DMA((8,)),
         ],
-        compiler_params=params,
+        compiler_params=pltpu.CompilerParams(
+            vmem_limit_bytes=VMEM_LIMIT if rows <= 128 else 2 * VMEM_LIMIT
+        ),
         cost_estimate=pl.CostEstimate(
             flops=12 * total * width * width,
             bytes_accessed=8 * width * width + 8 * total * width,
@@ -290,6 +287,14 @@
         ),
         name="main",
     )(counts, gain, both, normed, stats, front, *weights)
+
+
+class View:
+    def __init__(self, blocks, rows, in_columns, out_columns, piece, tokens, device, row_order, block_order):
+        self.blocks, self.rows = blocks, rows
+        self.in_columns, self.out_columns = in_columns, out_columns
+        self.piece, self.tokens, self.device = piece, tokens, device
+        self.row_order, self.block_order = row_order, block_order
 
 
 def swap(array, distance, devices):
@@ -383,12 +388,12 @@
         out_shape=tuple(
             map(rows_of, (depth, depth + block, block, depth + 3 * block, depth + 3 * block))
         ),
-        in_specs=[pl.BlockSpec(memory_space=pl.ANY)] * 4,
+        in_specs=[pl.BlockSpec(memory_space=pltpu.HBM)] * 4,
         out_specs=(vmem,) * 5,
         scratch_shapes=[pltpu.VMEM((2, devices * share, width), jnp.bfloat16)]
         + [pltpu.VMEM(a.shape, a.dtype) for a in (input_weights, output_weights, tokens, cotangent)]
         + [pltpu.SemaphoreType.DMA((4,))],
-        compiler_params=SMALL,
+        compiler_params=pltpu.CompilerParams(vmem_limit_bytes=PACK_LIMIT),
         name="pack",
     )(input_weights, output_weights, tokens, cotangent)
 
@@ -401,9 +406,7 @@
     def other_core(arrays):
         return [swap(array, 1, devices) for array in arrays]
 
-    one, two = by_clip(joined, 1), by_clip(joined, 2)
-    source, two = lax.optimization_barrier((joined, two))
-    three = by_clip(source, 3)
+    one, two, three = by_clip(joined, 1), by_clip(joined, 2), by_clip(joined, 3)
     first = [swap(to_x, 2, devices), swap(to_y, 4, devices)]
     tail = half + 2 * block
     first += [swap(first[1][tail:], 2, devices), swap(first[0][tail:], 4, devices)]
@@ -453,43 +456,32 @@
     for group in (table, others, pairs):
         arrays += [(core, parts) for core in (0, 1) for parts in group]
 
-    def pieces(offsets, lanes, base):
-        clip, frame = lax.axis_index("clip"), lax.axis_index("frame")
-        found = []
-        for ref, (core, parts) in enumerate(arrays):
-            for offset, distance, first, rows, inside in parts:
-                if offset in offsets:
-                    row = (frame ^ distance ^ core) * depth + inside
-                    found.append((base + ref, None, first, rows, lanes, row, clip ^ offset))
-        return found
-
-    def placed(parts, stride):
-        return [(*part[:-1], part[-1] * stride) for part in parts]
-
-    def compact():
-        return [(*part[:-1], 0) for part in pieces((0,), (0, in_columns), 1)]
-
-    inner, outer = (0, in_columns), (in_columns, out_columns)
-
-    def columns_of(offsets):
-        clip = lax.axis_index("clip")
-        return [(clip ^ offset) * in_columns for offset in offsets]
-
-    plan = {
-        "front": compact,
-        "tokens": tokens_in,
-        "columns": in_columns,
-        "spread": [False] * 11,
-        "device": lambda: lax.axis_index("frame"),
-        "late": lambda: [placed(pieces((i,), inner, 0), in_columns) for i in (1, 2, 3)],
-        "again": lambda: placed(pieces((0,), inner, 0), in_columns),
-        "outer": lambda: placed(pieces((0, 1, 2, 3), outer, 0), out_columns),
-        "placed": lambda: [
-            (0, start, in_columns) for start in columns_of((0,))
-        ],
-        "missing": lambda: [(start, in_columns) for start in columns_of((1, 2, 3))],
-    }
-    fronted = run_front(gain, (devices, 2, share, width), [mine, *ready[:10]], plan)
+    def piece(base):
+        def value(refs, offset, distance, first, depth, lanes):
+            found = [
+                (inside, refs[base + ref][start : start + size, lanes[0] : lanes[0] + lanes[1]])
+                for ref, (core, parts) in enumerate(arrays)
+                for source, away, start, size, inside in parts
+                if (source, away ^ core) == (offset, distance)
+            ]
+            return jnp.concatenate([held for _, held in sorted(found, key=lambda f: f[0])], axis=0)
+
+        return value
+
+    def view(base):
+        return View(
+            4,
+            [[(d, 0, depth), (d + 1, 0, depth)] for d in range(0, devices, 2)],
+            in_columns,
+            out_columns,
+            piece(base),
+            tokens_in,
+            lambda: lax.axis_index("frame"),
+            lambda: ([(lax.axis_index("frame") ^ d) * depth for d in range(devices)], depth),
+            lambda: [lax.axis_index("clip") ^ offset for offset in range(4)],
+        )
+
+    fronted = run_front(gain, (devices, 2, share, width), [mine, *ready[:10]], view(1))
     to_dx, to_dy = pl.pallas_call(
         functools.partial(turn_kernel, half),
         out_shape=(rows_of(depth + half), rows_of(depth + half)),
@@ -501,7 +493,7 @@
     third += [swap(to_dx, 2, devices), swap(to_dy, 4, devices)]
     third[3], *fronted = lax.optimization_barrier((third[3], *fronted))
     third += other_core(third)
-    return fronted, [*ready, *third], plan
+    return fronted, [*ready, *third], view(0)
 
 
 def gather_plainly(input_weights, output_weights, tokens, cotangent, gain, share, devices):
@@ -520,22 +512,28 @@
     both = both.reshape(devices * slots, 2, share, width)
 
     def tokens_in(sources, both_ref):
-        both_ref[...] = sources[1][...]
-
-    inner, outer = [[(i, None, 0, w.shape[0], (0, w.shape[1]), 0, 0)] for i, w in enumerate(whole)]
-    plan = {
-        "front": lambda: inner,
-        "tokens": tokens_in,
-        "columns": whole[0].shape[1],
-        "spread": [True, False],
-        "device": lambda: 0,
-        "late": lambda: [],
-        "again": lambda: inner,
-        "outer": lambda: outer,
-        "placed": lambda: [(0, 0, whole[0].shape[1])],
-        "missing": lambda: [],
-    }
-    return run_front(gain, both.shape, [whole[0], both], plan), whole, plan
+        both_ref[...] = sources[2][...]
+
+    in_columns, out_columns = whole[0].shape[1], whole[1].shape[1]
+
+    def piece(refs, block, index, first, depth, lanes):
+        outer = lanes[0] >= in_columns
+        start = lanes[0] - in_columns * outer
+        return refs[int(outer)][first : first + depth, start : start + lanes[1]]
+
+    step = math.gcd(width, 256)
+    view = View(
+        1,
+        [[(0, first, step)] for first in range(0, width, step)],
+        in_columns,
+        out_columns,
+        piece,
+        tokens_in,
+        lambda: 0,
+        lambda: ([0], width),
+        lambda: [0],
+    )
+    return run_front(gain, both.shape, [*whole, both], view), whole, view
 
 
 def per_device(clips, devices, tokens, counts, norm_gain, input_weights, output_weights, cotangent):
@@ -547,10 +545,10 @@
     small = clips == 4 and devices == 8 and slots == 1 and fits
     gather = gather_in_rounds if small else gather_plainly
     gain = norm_gain.reshape(1, width)
-    fronted, weights, plan = gather(
+    fronted, weights, view = gather(
         input_weights, output_weights, tokens, cotangent, gain, share, devices
     )
-    back = run_main(counts, gain, fronted, weights, plan)
+    back = run_main(counts, gain, fronted, weights, view)
     back = back.reshape(devices, slots, 2, share, width)
     back = lax.all_to_all(back, "frame", split_axis=0, concat_axis=0, tiled=True)
 

time: 101 us -> 91.5 us (0.906)
  local copies, waits for them, and re-layouts: 4.83 us -> 1.08 us
  starting transfers between devices: 22.1 us -> 19.2 us
  Pallas kernels: 16 us -> 13.8 us
    ppermute x3, waiting for transfers between devices: 12.3 us -> 8.19 us  [by_clip(): return lax.ppermute(array, 'clip', [(c, c ^ offset) for c in range(4)])]
    pallas_call x2, Pallas kernels: 15 us -> 11 us  [the longest x1 9.91 us: run_main(): pl.pallas_call(functools.partial(main_kernel, view), out_shape=jax.ShapeD...]
    unnamed x10 -> x8, local copies, waits for them, and re-layouts: 3.77 us -> 0.02 us
    ppermute x23, waiting for transfers between devices: 26.2 us -> 29.6 us  [swap(): lax.ppermute(array, 'frame', [(f, f ^ distance) for f in range(devices)])]
    ppermute x3, starting transfers between devices: 7.55 us -> 4.17 us  [by_clip(): return lax.ppermute(array, 'clip', [(c, c ^ offset) for c in range(4)])]
    pallas_call x1, Pallas kernels: 0.97 us -> 2.68 us  [gather_in_rounds(): pl.pallas_call(functools.partial(pack_kernel, patches, share), out_shape=...]
  transfers between devices with their start and end apart: 26 -> 26, of which waited for: 13 -> 9; matrix products, arithmetic and copies ran while one was open for 0% -> 0% of each run, Pallas kernels for 2% -> 1%
where the time goes in v9:
time: 91.5 us; the launch traced here: 91.3 us
  waiting for transfers between devices  37.8 us (41%)
  starting transfers between devices  19.2 us (21%)
  blocking collectives  18 us (20%)
  Pallas kernels  13.8 us (15%)
  between operations  1.44 us (2%)
  local copies, waits for them, and re-layouts  1.08 us (1%)
    ppermute x23, waiting for transfers between devices, swap(): lax.ppermute(array, 'frame', [(f, f ^ distance) for f in range(devices)])  29.6 us
    all_to_all x1, blocking collectives, per_device(): lax.all_to_all(back, 'frame', split_axis=0, concat_axis=0, tiled=True)  18 us
    ppermute x23, starting transfers between devices, swap(): lax.ppermute(array, 'frame', [(f, f ^ distance) for f in range(devices)])  15 us
    pallas_call x1, Pallas kernels, run_main(): pl.pallas_call(functools.partial(main_kernel, view), out_shape=jax.ShapeD...  9.91 us
    ppermute x3, waiting for transfers between devices, by_clip(): return lax.ppermute(array, 'clip', [(c, c ^ offset) for c in range(4)])  8.19 us
    ppermute x3, starting transfers between devices, by_clip(): return lax.ppermute(array, 'clip', [(c, c ^ offset) for c in range(4)])  4.17 us
    pallas_call x1, Pallas kernels, gather_in_rounds(): pl.pallas_call(functools.partial(pack_kernel, patches, share), out_shape=...  2.68 us
  transfers between devices with their start and end apart: 26, of which 9 were waited for; matrix products, arithmetic and copies ran while one was open for 0% of the time, Pallas kernels for 1%

profile of v9, /device:TPU:0, one launch (start us, length us, event | category | flops | bytes accessed | tf_op | source)
XLA Modules:
  0.0 91.3 jit_solution(15218092679373139899)
XLA Ops:
  0.6 2.7 %pack.1 = (bf16[128,1024]{1,0:T(8,128)(2,1)}, bf16[192,1024]{1,0:T(8,128)(2,1)}, bf16[64,1024]{1,0:T(8,128)(2,1)}, bf16[320,1024]{1,0:T(8,128)(2,1)}, bf16[320,1024]{1,0:T(8,128)(2,1)}) custom-call(bf16[128,768]{1,0:T(8,128)(2,1)} %refs_0_.1, bf16[128,256]{1,0:T(8,128)(2,1)} %refs_1_.1, bf16[1,1,196,1024]{3,2,1,0:T(8,128)(2,1)} %refs_2_.1, ...), custom_call_target="tpu_custom_call" | custom-call | tf_op jit(solution)/shard_map/pack/pallas_call | solution.py:386
  3.3 3.0 %collective-permute-start.1 = (bf16[320,1024]{1,0:T(8,128)(2,1)}, bf16[320,1024]{1,0:T(8,128)(2,1)S(1)}, u32[]{:S(2)}, u32[]{:S(2)}) collective-permute-start(bf16[320,1024]{1,0:T(8,128)(2,1)} %get-tuple-element.33), channel_id=1, source_target_pairs={{0,2},{1,3},{2,0},{3,1},{4,6},{5,7},{6,4},{7,5},{8,10},{9,11},{10,... | collective-permute-start | bytes 1966088 | tf_op jit(solution)/shard_map/ppermute | solution.py:301
  6.3 1.5 %collective-permute-start.2 = (bf16[320,1024]{1,0:T(8,128)(2,1)}, bf16[320,1024]{1,0:T(8,128)(2,1)S(1)}, u32[]{:S(2)}, u32[]{:S(2)}) collective-permute-start(bf16[320,1024]{1,0:T(8,128)(2,1)} %get-tuple-element.34), channel_id=1, source_target_pairs={{0,4},{1,5},{2,6},{3,7},{4,0},{5,1},{6,2},{7,3},{8,12},{9,13},{10,... | collective-permute-start | bytes 1966088 | tf_op jit(solution)/shard_map/ppermute | solution.py:301
  7.8 1.6 %collective-permute-start = (bf16[128,1024]{1,0:T(8,128)(2,1)}, bf16[128,1024]{1,0:T(8,128)(2,1)S(1)}, u32[]{:S(2)}, u32[]{:S(2)}) collective-permute-start(bf16[128,1024]{1,0:T(8,128)(2,1)} %get-tuple-element.32.refs_1_.rest_0_), channel_id=1, source_target_pairs={{0,8},{8,0},{16,24},{24,16},{1,9},{9,1},{17,25},{25,17},{2,10},{10... | collective-permute-start | bytes 786440 | tf_op jit(solution)/shard_map/ppermute | solution.py:401
  9.4 2.5 %collective-permute-start.6 = (bf16[128,1024]{1,0:T(8,128)(2,1)}, bf16[128,1024]{1,0:T(8,128)(2,1)S(1)}, u32[]{:S(2)}, u32[]{:S(2)}) collective-permute-start(bf16[128,1024]{1,0:T(8,128)(2,1)} %get-tuple-element.32.refs_1_.rest_0_), channel_id=1, source_target_pairs={{0,24},{8,16},{16,8},{24,0},{1,25},{9,17},{17,9},{25,1},{2,26},{10... | collective-permute-start | bytes 786440 | tf_op jit(solution)/shard_map/ppermute | solution.py:401
  11.9 0.1 collective-permute-start.5
  12.0 9.3 %collective-permute-done.1.refs_2_.rest_1_ = bf16[320,1024]{1,0:T(8,128)(2,1)S(1)} collective-permute-done((bf16[320,1024]{1,0:T(8,128)(2,1)}, bf16[320,1024]{1,0:T(8,128)(2,1)S(1)}, u32[]{:S(2)}, u32[]{:S(2)}) %collective-permute-start.1) | collective-permute-done | bytes 655392 | tf_op jit(solution)/shard_map/ppermute | solution.py:301
  21.3 1.8 %collective-permute-start.8 = (bf16[128,1024]{1,0:T(8,128)(2,1)S(1)}, bf16[128,1024]{1,0:T(8,128)(2,1)S(1)}, u32[]{:S(2)}, u32[]{:S(2)}) collective-permute-start(bf16[128,1024]{1,0:T(8,128)(2,1)S(1)} %slice.25), channel_id=1, source_target_pairs={{0,4},{1,5},{2,6},{3,7},{4,0},{5,1},{6,2},{7,3},{8,12},{9,13},{10,... | collective-permute-start | bytes 786440 | tf_op jit(solution)/shard_map/ppermute | solution.py:301
  23.1 0.0 collective-permute-done.2.refs_3_.rest_2_
  23.2 0.0 copy-start.3
  23.2 1.6 %collective-permute-start.7 = (bf16[128,1024]{1,0:T(8,128)(2,1)S(1)}, bf16[128,1024]{1,0:T(8,128)(2,1)S(1)}, u32[]{:S(2)}, u32[]{:S(2)}) collective-permute-start(bf16[128,1024]{1,0:T(8,128)(2,1)S(1)} %slice.24), channel_id=1, source_target_pairs={{0,2},{1,3},{2,0},{3,1},{4,6},{5,7},{6,4},{7,5},{8,10},{9,11},{10,... | collective-permute-start | bytes 786440 | tf_op jit(solution)/shard_map/ppermute | solution.py:301
  24.7 0.0 collective-permute-done.rest_10_
  24.7 0.5 collective-permute-start.4
  25.2 0.0 collective-permute-done.6.refs_1_
  25.2 1.1 %collective-permute-start.3 = (bf16[128,1024]{1,0:T(8,128)(2,1)S(1)}, bf16[128,1024]{1,0:T(8,128)(2,1)S(1)}, u32[]{:S(2)}, u32[]{:S(2)}) collective-permute-start(bf16[128,1024]{1,0:T(8,128)(2,1)S(1)} %collective-permute-done.rest_10_), channel_id=1, source_target_pairs={{0,2},{1,3},{2,0},{3,1},{4,6},{5,7},{6,4},{7,5},{8,10},{9,11},{10,... | collective-permute-start | bytes 786440 | tf_op jit(solution)/shard_map/ppermute | solution.py:301
  26.4 8.2 %collective-permute-done.5.refs_0_ = bf16[128,1024]{1,0:T(8,128)(2,1)S(1)} collective-permute-done((bf16[128,1024]{1,0:T(8,128)(2,1)}, bf16[128,1024]{1,0:T(8,128)(2,1)S(1)}, u32[]{:S(2)}, u32[]{:S(2)}) %collective-permute-start.5) | collective-permute-done | bytes 262176 | tf_op jit(solution)/shard_map/ppermute | solution.py:401
  34.6 0.0 collective-permute-done.8.refs_5_.rest_4_
  34.6 0.0 collective-permute-done.7.refs_4_.rest_3_
  34.6 0.6 collective-permute-start.10
  35.2 0.5 collective-permute-start.9
  35.7 0.0 collective-permute-start.17
  35.7 0.0 collective-permute-done.4.by_y.rest_12_
  35.7 0.0 collective-permute-done.3.by_x.rest_11_
  35.8 0.0 copy-start.1
  35.8 0.6 collective-permute-start.18
  36.3 0.1 collective-permute-start.13
  36.4 0.9 collective-permute-done.17.rest_13_
  37.3 0.1 collective-permute-start.14
  37.4 0.2 collective-permute-done.18.rest_14_
  37.6 0.2 collective-permute-start.15
  37.9 9.0 %collective-permute-done.10.pair_y.rest_18_ = bf16[256,1024]{1,0:T(8,128)(2,1)S(1)} collective-permute-done((bf16[256,1024]{1,0:T(8,128)(2,1)S(1)}, bf16[256,1024]{1,0:T(8,128)(2,1)S(1)}, u32[]{:S(2)}, u32[]{:S(2)}) %collective-permute-start.10) | collective-permute-done | bytes 524320 | tf_op jit(solution)/shard_map/ppermute | solution.py:301
  46.9 0.0 collective-permute-start.16
  46.9 0.2 collective-permute-done.9.pair_x.rest_17_
  47.1 0.0 copy-done.3
  47.1 0.3 collective-permute-start.12
  47.4 0.1 turn.1
  47.4 0.0 copy-start.2
  47.4 0.0 collective-permute-done.15.refs_9_.rest_8_
  47.5 1.2 %collective-permute-start.11 = (bf16[192,1024]{1,0:T(8,128)(2,1)S(1)}, bf16[192,1024]{1,0:T(8,128)(2,1)S(1)}, u32[]{:S(2)}, u32[]{:S(2)}) collective-permute-start(bf16[192,1024]{1,0:T(8,128)(2,1)S(1)} %get-tuple-element.45), channel_id=1, source_target_pairs={{0,2},{1,3},{2,0},{3,1},{4,6},{5,7},{6,4},{7,5},{8,10},{9,11},{10,... | collective-permute-start | bytes 1179656 | tf_op jit(solution)/shard_map/ppermute | solution.py:301
  48.6 0.0 collective-permute-done.16.refs_10_.rest_9_
  48.6 0.7 collective-permute-start.20
  49.3 0.0 collective-permute-done.12.refs_6_.rest_5_
  49.3 0.0 collective-permute-start.19
  49.3 0.0 collective-permute-done.13.refs_7_.rest_6_
  49.3 0.5 collective-permute-start.21
  49.8 0.0 collective-permute-done.14.refs_8_.rest_7_
  49.8 0.1 collective-permute-start.23
  49.9 8.9 %collective-permute-done.11.rest_19_ = bf16[192,1024]{1,0:T(8,128)(2,1)S(1)} collective-permute-done((bf16[192,1024]{1,0:T(8,128)(2,1)S(1)}, bf16[192,1024]{1,0:T(8,128)(2,1)S(1)}, u32[]{:S(2)}, u32[]{:S(2)}) %collective-permute-start.11) | collective-permute-done | bytes 393248 | tf_op jit(solution)/shard_map/ppermute | solution.py:301
  58.8 0.0 collective-permute-start.22
  58.8 0.0 copy-done
  58.8 1.1 %front.1 = (bf16[8,2,32,1024]{3,2,1,0:T(8,128)(2,1)S(1)}, bf16[256,1024]{1,0:T(8,128)(2,1)S(1)}, f32[256,128]{1,0:T(8,128)S(1)}, bf16[256,768]{1,0:T(8,128)(2,1)S(1)}) custom-call(f32[1,1024]{1,0:T(1,128)S(1)} %bitcast.11, bf16[64,1024]{1,0:T(8,128)(2,1)S(1)} %copy-done.1, bf16[128,1024]{1,0:T(8,128)(2,1)S(1)} %copy-done, ...), custom_call_target="tpu_custom_call" | custom-call | flops 256 | bytes 256 | tf_op jit(solution)/shard_map/front/pallas_call | solution.py:239
  59.9 0.0 collective-permute-done.20.rest_20_
  59.9 0.6 collective-permute-start.25
  60.5 0.0 collective-permute-done.19.rest_15_
  60.5 0.1 collective-permute-start.24
  61.2 0.0 collective-permute-done.21.rest_21_
  61.2 0.0 collective-permute-done.23.rest_23_
  61.2 0.0 collective-permute-done.22.rest_22_
  61.3 0.6 collective-permute-done.25.rest_25_
  61.8 0.6 collective-permute-done.24.rest_24_
  62.4 9.9 %main.1 = bf16[8,2,32,1024]{3,2,1,0:T(8,128)(2,1)S(1)} custom-call(s32[1]{0:T(128)S(6)} %copy.9.counts_ref, f32[1,1024]{1,0:T(1,128)S(1)} %bitcast.12, bf16[8,2,32,1024]{3,2,1,0:T(8,128)(2,1)S(1)} %get-tuple-element.56.both_ref, bf16[256,1024]{1,0:T(8,128)(2,1)S(1)} %get-tuple-element.57.normed_ref, f32[256,128]{1,0:T(8,128)S(1)} %get-tuple-element.58.stats_ref, ...), custom_call_target="tpu_custom_call" | custom-call | flops 3221225472 | bytes 10485760 | tf_op jit(solution)/shard_map/main/pallas_call | solution.py:263
  72.3 18.0 %all_to_all.5 = bf16[8,1,2,32,1024]{4,3,2,1,0:T(8,128)(2,1)S(1)} all-to-all(bf16[8,1,2,32,1024]{4,3,2,1,0:T(8,128)(2,1)S(1)} %bitcast.10), channel_id=1, replica_groups=mesh['clip'=4,'frame'=8] {'frame'}, dimensions={0} | all-to-all | bytes 2097152 | tf_op jit(solution)/shard_map/all_to_all | solution.py:553
  90.3 0.1 fusion
  90.4 0.9 %slice_bitcast_fusion = (bf16[1,1,196,1024]{3,2,1,0:T(8,128)(2,1)}, bf16[1,1,196,1024]{3,2,1,0:T(8,128)(2,1)}) fusion(bf16[1,256,1024]{2,1,0:T(8,128)(2,1)S(1)} %bitcast.13, bf16[1,256,1024]{2,1,0:T(8,128)(2,1)S(1)} %bitcast.14), kind=kLoop, calls=%fused_computation | loop fusion | bytes 1605632 | tf_op jit(solution)/shard_map/broadcast_in_dim | solution.py:557
  (6 shorter events, 0.1 us)
Async XLA Ops:
  3.3 17.9 %collective-permute-start.1 = (bf16[320,1024]{1,0:T(8,128)(2,1)}, bf16[320,1024]{1,0:T(8,128)(2,1)S(1)}, u32[]{:S(2)}, u32[]{:S(2)}) collective-permute-start(bf16[320,1024]{1,0:T(8,128)(2,1)} %get-tuple-element.33), channel_id=1, source_target_pairs={{0,2},{1,3},{2,0},{3,1},{4,6},{5,7},{6,4},{7,5},{8,10},{9,11},{10,... | collective-permute-start | bytes 1966088 | tf_op jit(solution)/shard_map/ppermute | solution.py:301
  6.3 16.8 %collective-permute-start.2 = (bf16[320,1024]{1,0:T(8,128)(2,1)}, bf16[320,1024]{1,0:T(8,128)(2,1)S(1)}, u32[]{:S(2)}, u32[]{:S(2)}) collective-permute-start(bf16[320,1024]{1,0:T(8,128)(2,1)} %get-tuple-element.34), channel_id=1, source_target_pairs={{0,4},{1,5},{2,6},{3,7},{4,0},{5,1},{6,2},{7,3},{8,12},{9,13},{10,... | collective-permute-start | bytes 1966088 | tf_op jit(solution)/shard_map/ppermute | solution.py:301
  7.8 16.9 %collective-permute-start = (bf16[128,1024]{1,0:T(8,128)(2,1)}, bf16[128,1024]{1,0:T(8,128)(2,1)S(1)}, u32[]{:S(2)}, u32[]{:S(2)}) collective-permute-start(bf16[128,1024]{1,0:T(8,128)(2,1)} %get-tuple-element.32.refs_1_.rest_0_), channel_id=1, source_target_pairs={{0,8},{8,0},{16,24},{24,16},{1,9},{9,1},{17,25},{25,17},{2,10},{10... | collective-permute-start | bytes 786440 | tf_op jit(solution)/shard_map/ppermute | solution.py:401
  9.4 15.8 %collective-permute-start.6 = (bf16[128,1024]{1,0:T(8,128)(2,1)}, bf16[128,1024]{1,0:T(8,128)(2,1)S(1)}, u32[]{:S(2)}, u32[]{:S(2)}) collective-permute-start(bf16[128,1024]{1,0:T(8,128)(2,1)} %get-tuple-element.32.refs_1_.rest_0_), channel_id=1, source_target_pairs={{0,24},{8,16},{16,8},{24,0},{1,25},{9,17},{17,9},{25,1},{2,26},{10... | collective-permute-start | bytes 786440 | tf_op jit(solution)/shard_map/ppermute | solution.py:401
  11.9 22.7 %collective-permute-start.5 = (bf16[128,1024]{1,0:T(8,128)(2,1)}, bf16[128,1024]{1,0:T(8,128)(2,1)S(1)}, u32[]{:S(2)}, u32[]{:S(2)}) collective-permute-start(bf16[128,1024]{1,0:T(8,128)(2,1)} %get-tuple-element.32.refs_1_.rest_0_), channel_id=1, source_target_pairs={{0,16},{8,24},{16,0},{24,8},{1,17},{9,25},{17,1},{25,9},{2,18},{10... | collective-permute-start | bytes 786440 | tf_op jit(solution)/shard_map/ppermute | solution.py:401
  21.3 13.3 %collective-permute-start.8 = (bf16[128,1024]{1,0:T(8,128)(2,1)S(1)}, bf16[128,1024]{1,0:T(8,128)(2,1)S(1)}, u32[]{:S(2)}, u32[]{:S(2)}) collective-permute-start(bf16[128,1024]{1,0:T(8,128)(2,1)S(1)} %slice.25), channel_id=1, source_target_pairs={{0,4},{1,5},{2,6},{3,7},{4,0},{5,1},{6,2},{7,3},{8,12},{9,13},{10,... | collective-permute-start | bytes 786440 | tf_op jit(solution)/shard_map/ppermute | solution.py:301
  23.2 23.9 %copy-start.3 = (bf16[192,1024]{1,0:T(8,128)(2,1)S(1)}, bf16[192,1024]{1,0:T(8,128)(2,1)}, u32[]{:S(2)}) copy-start(bf16[192,1024]{1,0:T(8,128)(2,1)} %get-tuple-element.51) | copy-start | bytes 1179652
  23.2 11.4 %collective-permute-start.7 = (bf16[128,1024]{1,0:T(8,128)(2,1)S(1)}, bf16[128,1024]{1,0:T(8,128)(2,1)S(1)}, u32[]{:S(2)}, u32[]{:S(2)}) collective-permute-start(bf16[128,1024]{1,0:T(8,128)(2,1)S(1)} %slice.24), channel_id=1, source_target_pairs={{0,2},{1,3},{2,0},{3,1},{4,6},{5,7},{6,4},{7,5},{8,10},{9,11},{10,... | collective-permute-start | bytes 786440 | tf_op jit(solution)/shard_map/ppermute | solution.py:301
  24.7 11.0 %collective-permute-start.4 = (bf16[128,1024]{1,0:T(8,128)(2,1)S(1)}, bf16[128,1024]{1,0:T(8,128)(2,1)S(1)}, u32[]{:S(2)}, u32[]{:S(2)}) collective-permute-start(bf16[128,1024]{1,0:T(8,128)(2,1)S(1)} %collective-permute-done.rest_10_), channel_id=1, source_target_pairs={{0,4},{1,5},{2,6},{3,7},{4,0},{5,1},{6,2},{7,3},{8,12},{9,13},{10,... | collective-permute-start | bytes 786440 | tf_op jit(solution)/shard_map/ppermute | solution.py:301
  25.2 10.5 %collective-permute-start.3 = (bf16[128,1024]{1,0:T(8,128)(2,1)S(1)}, bf16[128,1024]{1,0:T(8,128)(2,1)S(1)}, u32[]{:S(2)}, u32[]{:S(2)}) collective-permute-start(bf16[128,1024]{1,0:T(8,128)(2,1)S(1)} %collective-permute-done.rest_10_), channel_id=1, source_target_pairs={{0,2},{1,3},{2,0},{3,1},{4,6},{5,7},{6,4},{7,5},{8,10},{9,11},{10,... | collective-permute-start | bytes 786440 | tf_op jit(solution)/shard_map/ppermute | solution.py:301
  34.6 12.2 %collective-permute-start.10 = (bf16[256,1024]{1,0:T(8,128)(2,1)S(1)}, bf16[256,1024]{1,0:T(8,128)(2,1)S(1)}, u32[]{:S(2)}, u32[]{:S(2)}) collective-permute-start(bf16[256,1024]{1,0:T(8,128)(2,1)S(1)} %join.1.rest_16_), channel_id=1, source_target_pairs={{0,4},{1,5},{2,6},{3,7},{4,0},{5,1},{6,2},{7,3},{8,12},{9,13},{10,... | collective-permute-start | bytes 1572872 | tf_op jit(solution)/shard_map/ppermute | solution.py:301
  35.2 11.9 %collective-permute-start.9 = (bf16[256,1024]{1,0:T(8,128)(2,1)S(1)}, bf16[256,1024]{1,0:T(8,128)(2,1)S(1)}, u32[]{:S(2)}, u32[]{:S(2)}) collective-permute-start(bf16[256,1024]{1,0:T(8,128)(2,1)S(1)} %join.1.rest_16_), channel_id=1, source_target_pairs={{0,2},{1,3},{2,0},{3,1},{4,6},{5,7},{6,4},{7,5},{8,10},{9,11},{10,... | collective-permute-start | bytes 1572872 | tf_op jit(solution)/shard_map/ppermute | solution.py:301
  35.7 1.5 %collective-permute-start.17 = (bf16[128,1024]{1,0:T(8,128)(2,1)S(1)}, bf16[128,1024]{1,0:T(8,128)(2,1)S(1)}, u32[]{:S(2)}, u32[]{:S(2)}) collective-permute-start(bf16[128,1024]{1,0:T(8,128)(2,1)S(1)} %collective-permute-done.rest_10_), channel_id=1, source_target_pairs={{0,1},{1,0},{2,3},{3,2},{4,5},{5,4},{6,7},{7,6},{8,9},{9,8},{10,11... | collective-permute-start | bytes 786440 | tf_op jit(solution)/shard_map/ppermute | solution.py:301
  35.7 23.0 %copy-start = (bf16[128,1024]{1,0:T(8,128)(2,1)S(1)}, bf16[128,1024]{1,0:T(8,128)(2,1)}, u32[]{:S(2)}) copy-start(bf16[128,1024]{1,0:T(8,128)(2,1)} %get-tuple-element.32.refs_1_.rest_0_) | copy-start | bytes 786436
  35.8 23.0 %copy-start.1 = (bf16[64,1024]{1,0:T(8,128)(2,1)S(1)}, bf16[64,1024]{1,0:T(8,128)(2,1)}, u32[]{:S(2)}) copy-start(bf16[64,1024]{1,0:T(8,128)(2,1)} %get-tuple-element.46.refs_0_) | copy-start | bytes 393220
  35.8 1.9 %collective-permute-start.18 = (bf16[128,1024]{1,0:T(8,128)(2,1)S(1)}, bf16[128,1024]{1,0:T(8,128)(2,1)S(1)}, u32[]{:S(2)}, u32[]{:S(2)}) collective-permute-start(bf16[128,1024]{1,0:T(8,128)(2,1)S(1)} %collective-permute-done.3.by_x.rest_11_), channel_id=1, source_target_pairs={{0,1},{1,0},{2,3},{3,2},{4,5},{5,4},{6,7},{7,6},{8,9},{9,8},{10,11... | collective-permute-start | bytes 786440 | tf_op jit(solution)/shard_map/ppermute | solution.py:301
  36.3 13.0 %collective-permute-start.13 = (bf16[320,1024]{1,0:T(8,128)(2,1)S(1)}, bf16[320,1024]{1,0:T(8,128)(2,1)S(1)}, u32[]{:S(2)}, u32[]{:S(2)}) collective-permute-start(bf16[320,1024]{1,0:T(8,128)(2,1)S(1)} %collective-permute-done.1.refs_2_.rest_1_), channel_id=1, source_target_pairs={{0,1},{1,0},{2,3},{3,2},{4,5},{5,4},{6,7},{7,6},{8,9},{9,8},{10,11... | collective-permute-start | bytes 1966088 | tf_op jit(solution)/shard_map/ppermute | solution.py:301
  37.3 12.6 %collective-permute-start.14 = (bf16[320,1024]{1,0:T(8,128)(2,1)S(1)}, bf16[320,1024]{1,0:T(8,128)(2,1)S(1)}, u32[]{:S(2)}, u32[]{:S(2)}) collective-permute-start(bf16[320,1024]{1,0:T(8,128)(2,1)S(1)} %collective-permute-done.2.refs_3_.rest_2_), channel_id=1, source_target_pairs={{0,1},{1,0},{2,3},{3,2},{4,5},{5,4},{6,7},{7,6},{8,9},{9,8},{10,11... | collective-permute-start | bytes 1966088 | tf_op jit(solution)/shard_map/ppermute | solution.py:301
  37.6 9.8 %collective-permute-start.15 = (bf16[128,1024]{1,0:T(8,128)(2,1)S(1)}, bf16[128,1024]{1,0:T(8,128)(2,1)S(1)}, u32[]{:S(2)}, u32[]{:S(2)}) collective-permute-start(bf16[128,1024]{1,0:T(8,128)(2,1)S(1)} %collective-permute-done.7.refs_4_.rest_3_), channel_id=1, source_target_pairs={{0,1},{1,0},{2,3},{3,2},{4,5},{5,4},{6,7},{7,6},{8,9},{9,8},{10,11... | collective-permute-start | bytes 786440 | tf_op jit(solution)/shard_map/ppermute | solution.py:301
  46.9 1.8 %collective-permute-start.16 = (bf16[128,1024]{1,0:T(8,128)(2,1)S(1)}, bf16[128,1024]{1,0:T(8,128)(2,1)S(1)}, u32[]{:S(2)}, u32[]{:S(2)}) collective-permute-start(bf16[128,1024]{1,0:T(8,128)(2,1)S(1)} %collective-permute-done.8.refs_5_.rest_4_), channel_id=1, source_target_pairs={{0,1},{1,0},{2,3},{3,2},{4,5},{5,4},{6,7},{7,6},{8,9},{9,8},{10,11... | collective-permute-start | bytes 786440 | tf_op jit(solution)/shard_map/ppermute | solution.py:301
  47.1 2.2 %collective-permute-start.12 = (bf16[192,1024]{1,0:T(8,128)(2,1)S(1)}, bf16[192,1024]{1,0:T(8,128)(2,1)S(1)}, u32[]{:S(2)}, u32[]{:S(2)}) collective-permute-start(bf16[192,1024]{1,0:T(8,128)(2,1)S(1)} %copy-done.3), channel_id=1, source_target_pairs={{0,1},{1,0},{2,3},{3,2},{4,5},{5,4},{6,7},{7,6},{8,9},{9,8},{10,11... | collective-permute-start | bytes 1179656 | tf_op jit(solution)/shard_map/ppermute | solution.py:301
  47.4 11.3 %copy-start.2 = (f32[1024]{0:T(1024)S(1)}, f32[1024]{0:T(1024)}, u32[]{:S(2)}) copy-start(f32[1024]{0:T(1024)} %param.8) | copy-start | bytes 12292
  47.5 11.3 %collective-permute-start.11 = (bf16[192,1024]{1,0:T(8,128)(2,1)S(1)}, bf16[192,1024]{1,0:T(8,128)(2,1)S(1)}, u32[]{:S(2)}, u32[]{:S(2)}) collective-permute-start(bf16[192,1024]{1,0:T(8,128)(2,1)S(1)} %get-tuple-element.45), channel_id=1, source_target_pairs={{0,2},{1,3},{2,0},{3,1},{4,6},{5,7},{6,4},{7,5},{8,10},{9,11},{10,... | collective-permute-start | bytes 1179656 | tf_op jit(solution)/shard_map/ppermute | solution.py:301
  48.6 11.3 %collective-permute-start.20 = (bf16[192,1024]{1,0:T(8,128)(2,1)S(1)}, bf16[192,1024]{1,0:T(8,128)(2,1)S(1)}, u32[]{:S(2)}, u32[]{:S(2)}) collective-permute-start(bf16[192,1024]{1,0:T(8,128)(2,1)S(1)} %get-tuple-element.61), channel_id=1, source_target_pairs={{0,4},{1,5},{2,6},{3,7},{4,0},{5,1},{6,2},{7,3},{8,12},{9,13},{10,... | collective-permute-start | bytes 1179656 | tf_op jit(solution)/shard_map/ppermute | solution.py:301
  49.3 11.2 %collective-permute-start.19 = (bf16[128,1024]{1,0:T(8,128)(2,1)S(1)}, bf16[128,1024]{1,0:T(8,128)(2,1)S(1)}, u32[]{:S(2)}, u32[]{:S(2)}) collective-permute-start(bf16[128,1024]{1,0:T(8,128)(2,1)S(1)} %collective-permute-done.4.by_y.rest_12_), channel_id=1, source_target_pairs={{0,1},{1,0},{2,3},{3,2},{4,5},{5,4},{6,7},{7,6},{8,9},{9,8},{10,11... | collective-permute-start | bytes 786440 | tf_op jit(solution)/shard_map/ppermute | solution.py:301
  49.3 11.9 %collective-permute-start.21 = (bf16[256,1024]{1,0:T(8,128)(2,1)S(1)}, bf16[256,1024]{1,0:T(8,128)(2,1)S(1)}, u32[]{:S(2)}, u32[]{:S(2)}) collective-permute-start(bf16[256,1024]{1,0:T(8,128)(2,1)S(1)} %join.1.rest_16_), channel_id=1, source_target_pairs={{0,1},{1,0},{2,3},{3,2},{4,5},{5,4},{6,7},{7,6},{8,9},{9,8},{10,11... | collective-permute-start | bytes 1572872 | tf_op jit(solution)/shard_map/ppermute | solution.py:301
  49.8 11.4 %collective-permute-start.23 = (bf16[256,1024]{1,0:T(8,128)(2,1)S(1)}, bf16[256,1024]{1,0:T(8,128)(2,1)S(1)}, u32[]{:S(2)}, u32[]{:S(2)}) collective-permute-start(bf16[256,1024]{1,0:T(8,128)(2,1)S(1)} %collective-permute-done.10.pair_y.rest_18_), channel_id=1, source_target_pairs={{0,1},{1,0},{2,3},{3,2},{4,5},{5,4},{6,7},{7,6},{8,9},{9,8},{10,11... | collective-permute-start | bytes 1572872 | tf_op jit(solution)/shard_map/ppermute | solution.py:301
  58.8 2.5 %collective-permute-start.22 = (bf16[256,1024]{1,0:T(8,128)(2,1)S(1)}, bf16[256,1024]{1,0:T(8,128)(2,1)S(1)}, u32[]{:S(2)}, u32[]{:S(2)}) collective-permute-start(bf16[256,1024]{1,0:T(8,128)(2,1)S(1)} %collective-permute-done.9.pair_x.rest_17_), channel_id=1, source_target_pairs={{0,1},{1,0},{2,3},{3,2},{4,5},{5,4},{6,7},{7,6},{8,9},{9,8},{10,11... | collective-permute-start | bytes 1572872 | tf_op jit(solution)/shard_map/ppermute | solution.py:301
  59.9 1.9 %collective-permute-start.25 = (bf16[192,1024]{1,0:T(8,128)(2,1)S(1)}, bf16[192,1024]{1,0:T(8,128)(2,1)S(1)}, u32[]{:S(2)}, u32[]{:S(2)}) collective-permute-start(bf16[192,1024]{1,0:T(8,128)(2,1)S(1)} %collective-permute-done.20.rest_20_), channel_id=1, source_target_pairs={{0,1},{1,0},{2,3},{3,2},{4,5},{5,4},{6,7},{7,6},{8,9},{9,8},{10,11... | collective-permute-start | bytes 1179656 | tf_op jit(solution)/shard_map/ppermute | solution.py:301
  60.5 1.9 %collective-permute-start.24 = (bf16[192,1024]{1,0:T(8,128)(2,1)S(1)}, bf16[192,1024]{1,0:T(8,128)(2,1)S(1)}, u32[]{:S(2)}, u32[]{:S(2)}) collective-permute-start(bf16[192,1024]{1,0:T(8,128)(2,1)S(1)} %collective-permute-done.11.rest_19_), channel_id=1, source_target_pairs={{0,1},{1,0},{2,3},{3,2},{4,5},{5,4},{6,7},{7,6},{8,9},{9,8},{10,11... | collective-permute-start | bytes 1179656 | tf_op jit(solution)/shard_map/ppermute | solution.py:301

commit v10 on v9

--- a/solution.py
+++ b/solution.py
@@ -81,9 +81,11 @@
         stats_ref[here, 0:1] = average
         stats_ref[here, 1:2] = scale
     normed_ref[...] = beside(natural, *view.row_order())
-    for start, size in chunks(proj_ref.shape[1]):
-        weight = stack_rows(view, sources, 0, (start, size))
-        proj_ref[:, start : start + size] = dot(normed_ref[...], weight, NN).astype(jnp.bfloat16)
+    for block in range(view.early):
+        for start, size in chunks(view.in_columns):
+            weight = stack_rows(view, sources, block, (start, size))
+            here = pl.ds(block * view.in_columns + start, size)
+            proj_ref[:, here] = dot(normed_ref[...], weight, NN).astype(jnp.bfloat16)
 
 
 def main_kernel(view, counts_ref, gain_ref, both_ref, normed_ref, stats_ref, front_ref, *rest):
@@ -129,8 +131,10 @@
         weight = stack_columns(view, weights, parts, in_columns, out_columns)
         put_rows(ga, parts, dot(grads_ordered, weight, NT).astype(jnp.bfloat16))
 
-    proj[:, pl.ds(column(0, in_columns), in_columns)] = front_ref[...]
-    for block in range(1, view.blocks):
+    for block in range(view.early):
+        held = front_ref[:, block * in_columns : (block + 1) * in_columns]
+        proj[:, pl.ds(column(block, in_columns), in_columns)] = held
+    for block in range(view.early, view.blocks):
         for start, size in chunks(in_columns):
             weight = stack_rows(view, weights, block, (start, size))
             proj[:, pl.ds(column(block, in_columns, start), size)] = dot(
@@ -242,7 +246,7 @@
             jax.ShapeDtypeStruct(shape, jnp.bfloat16),
             jax.ShapeDtypeStruct((total, width), jnp.bfloat16),
             jax.ShapeDtypeStruct((total, 128), jnp.float32),
-            jax.ShapeDtypeStruct((total, view.in_columns), jnp.bfloat16),
+            jax.ShapeDtypeStruct((total, view.early * view.in_columns), jnp.bfloat16),
         ),
         in_specs=[vmem] * (1 + len(sources)),
         out_specs=(vmem,) * 4,
@@ -290,8 +294,8 @@
 
 
 class View:
-    def __init__(self, blocks, rows, in_columns, out_columns, piece, tokens, device, row_order, block_order):
-        self.blocks, self.rows = blocks, rows
+    def __init__(self, blocks, early, rows, in_columns, out_columns, piece, tokens, device, row_order, block_order):
+        self.blocks, self.early, self.rows = blocks, early, rows
         self.in_columns, self.out_columns = in_columns, out_columns
         self.piece, self.tokens, self.device = piece, tokens, device
         self.row_order, self.block_order = row_order, block_order
@@ -366,11 +370,9 @@
         put(target, depth + 2 * block, (chip ^ 3) * 2 + core_by)
 
 
-def turn_kernel(half, by_x, by_y, pair_x, pair_y, to_dx, to_dy):
-    to_dx[:half, :] = by_y[:half, :]
-    to_dx[half:, :] = pair_y[: 2 * half, :]
-    to_dy[:half, :] = by_x[half:, :]
-    to_dy[half:, :] = pair_x[2 * half :, :]
+def pick_kernel(half, top_ref, bottom_ref, out_ref):
+    out_ref[:half, :] = top_ref[:half, :]
+    out_ref[half:, :] = bottom_ref[:half, :]
 
 
 def gather_in_rounds(input_weights, output_weights, tokens, cotangent, gain, share, devices):
@@ -403,8 +405,9 @@
     def across(array):
         return [swap(array, 2, devices), swap(array, 4, devices)]
 
-    def other_core(arrays):
-        return [swap(array, 1, devices) for array in arrays]
+    def both_cores(arrays):
+        packed = join(0, *arrays)
+        return [packed, swap(packed, 1, devices)]
 
     one, two, three = by_clip(joined, 1), by_clip(joined, 2), by_clip(joined, 3)
     first = [swap(to_x, 2, devices), swap(to_y, 4, devices)]
@@ -414,47 +417,61 @@
     second = [one, *across(one)]
     two, three, first[2], first[3] = lax.optimization_barrier((two, three, first[2], first[3]))
     third = [join(0, two, three)]
+    diagonal_own = pl.pallas_call(
+        functools.partial(pick_kernel, half),
+        out_shape=rows_of(depth),
+        in_specs=[vmem] * 2,
+        out_specs=vmem,
+        compiler_params=SMALL,
+        name="pick",
+    )(first[2], first[3])
+    by_diagonal = [by_clip(diagonal_own, 2), by_clip(diagonal_own, 1)]
     second[1], second[2], own, *first = lax.optimization_barrier(
         (second[1], second[2], own, *first)
     )
-    first_other = other_core([own, *first])
-    second_other = other_core(second)
-    ready = [joined, *first, *first_other, *second, *second_other]
+    ready = both_cores([own, *first]) + both_cores(second)
     third += across(third[0])
+
+    bounds = [0]
+    for array in (own, *first):
+        bounds.append(bounds[-1] + array.shape[0])
 
     def tokens_in(sources, both_ref):
         core = lax.axis_index("frame") % 2
-        mine_ref, _, x_ref, y_ref, dx_ref, dy_ref, own2, x2, y2, dx2, dy2 = sources[:11]
-        rows = pl.ds(pl.multiple_of(half + core * block, block), block)
-        behind = slice(half, half + block)
-
-        def diagonal(by_x, by_y):
-            return jnp.where(core == 0, by_y[behind, :], by_x[behind, :])
+        mine_ref, here, there = sources[:3]
+
+        def straight(ref, which):
+            start = bounds[which] + half + core * block
+            return ref[pl.ds(pl.multiple_of(start, SUB), block), :]
+
+        def diagonal(ref):
+            by_x, by_y = (
+                ref[bounds[which] + half : bounds[which] + half + block, :] for which in (3, 4)
+            )
+            return jnp.where(core == 0, by_y, by_x)
 
         found = (
-            mine_ref[...], own2[depth : depth + block, :],
-            x_ref[rows, :], x2[rows, :], y_ref[rows, :], y2[rows, :],
-            diagonal(dx_ref, dy_ref), diagonal(dx2, dy2),
+            mine_ref[...], there[depth : depth + block, :],
+            straight(here, 1), straight(there, 1), straight(here, 2), straight(there, 2),
+            diagonal(here), diagonal(there),
         )
         for distance, value in enumerate(found):
             both_ref[distance] = value.reshape(2, share, width)
 
+    x_row, y_row, dx_row, dy_row = bounds[1:5]
     table = [
-        [(0, 0, 0, depth, 0)],
-        [(0, 2, 0, half, 0), (0, 2, tail, half, half)],
-        [(0, 4, 0, half, half), (0, 4, tail, half, 0)],
-        [(0, 6, 0, half, 0)],
-        [(0, 6, 0, half, half)],
+        [
+            (0, 0, 0, depth, 0),
+            (0, 2, x_row, half, 0), (0, 2, x_row + tail, half, half),
+            (0, 4, y_row, half, half), (0, 4, y_row + tail, half, 0),
+            (0, 6, dx_row, half, 0), (0, 6, dy_row, half, half),
+        ],
+        [(1, d, d // 2 * depth, depth, 0) for d in (0, 2, 4)],
+        [(2 + i, d, (d + i) * depth, depth, 0) for d in (0, 2, 4) for i in (0, 1)]
+        + [(2, 6, 6 * depth, depth, 0), (1, 6, 7 * depth, depth, 0)],
+        [(3, 6, 0, half, 0), (3, 6, half, half, half)],
     ]
-    others = [[(1, d, 0, depth, 0)] for d in (0, 2, 4)]
-    pairs = [[(2, d, 0, depth, 0), (3, d, depth, depth, 0)] for d in (0, 2, 4)]
-    pairs += [
-        [(1, 6, 0, half, 0), (2, 6, half, depth, 0)],
-        [(1, 6, 0, half, half), (3, 6, half, depth, 0)],
-    ]
-    arrays = []
-    for group in (table, others, pairs):
-        arrays += [(core, parts) for core in (0, 1) for parts in group]
+    arrays = [(core, parts) for parts in table for core in (0, 1)]
 
     def piece(base):
         def value(refs, offset, distance, first, depth, lanes):
@@ -471,6 +488,7 @@
     def view(base):
         return View(
             4,
+            1,
             [[(d, 0, depth), (d + 1, 0, depth)] for d in range(0, devices, 2)],
             in_columns,
             out_columns,
@@ -481,19 +499,14 @@
             lambda: [lax.axis_index("clip") ^ offset for offset in range(4)],
         )
 
-    fronted = run_front(gain, (devices, 2, share, width), [mine, *ready[:10]], view(1))
-    to_dx, to_dy = pl.pallas_call(
-        functools.partial(turn_kernel, half),
-        out_shape=(rows_of(depth + half), rows_of(depth + half)),
-        in_specs=[vmem] * 4,
-        out_specs=(vmem, vmem),
-        compiler_params=SMALL,
-        name="turn",
-    )(second[1], second[2], third[1], third[2])
-    third += [swap(to_dx, 2, devices), swap(to_dy, 4, devices)]
-    third[3], *fronted = lax.optimization_barrier((third[3], *fronted))
-    third += other_core(third)
-    return fronted, [*ready, *third], view(0)
+    fronted = run_front(gain, (devices, 2, share, width), [mine, *ready[:2]], view(1))
+    third[1], third[2], *fronted = lax.optimization_barrier((third[1], third[2], *fronted))
+    last = [
+        swap(third[2][depth : depth + half], 2, devices),
+        swap(third[1][depth + half :], 4, devices),
+    ]
+    weights = [*ready, *both_cores([*third, *by_diagonal]), *both_cores(last)]
+    return fronted, weights, view(0)
 
 
 def gather_plainly(input_weights, output_weights, tokens, cotangent, gain, share, devices):
@@ -523,6 +536,7 @@
 
     step = math.gcd(width, 256)
     view = View(
+        1,
         1,
         [[(0, first, step)] for first in range(0, width, step)],
         in_columns,

time: 91.5 us -> 93.3 us (1.020)
  starting transfers between devices: 19.2 us -> 22.4 us
  waiting for transfers between devices: 37.8 us -> 35.3 us
  local copies, waits for them, and re-layouts: 1.08 us -> 2.09 us
    ppermute x23 -> x14, waiting for transfers between devices: 29.6 us -> 24.5 us  [swap(): lax.ppermute(array, 'frame', [(f, f ^ distance) for f in range(devices)])]
    ppermute x3 -> x5, starting transfers between devices: 4.17 us -> 8.4 us  [by_clip(): return lax.ppermute(array, 'clip', [(c, c ^ offset) for c in range(4)])]
    ppermute x3 -> x5, waiting for transfers between devices: 8.19 us -> 10.8 us  [by_clip(): return lax.ppermute(array, 'clip', [(c, c ^ offset) for c in range(4)])]
    ppermute x23 -> x14, starting transfers between devices: 15 us -> 14 us  [swap(): lax.ppermute(array, 'frame', [(f, f ^ distance) for f in range(devices)])]
    unnamed x8 -> x6, local copies, waits for them, and re-layouts: 0.02 us -> 1 us
  transfers between devices with their start and end apart: 26 -> 19, of which waited for: 9 -> 10; matrix products, arithmetic and copies ran while one was open for 0% -> 0% of each run, Pallas kernels for 1% -> 1%
where the time goes in v10:
time: 93.3 us; the launch traced here: 93.1 us
  waiting for transfers between devices  35.3 us (38%)
  starting transfers between devices  22.4 us (24%)
  blocking collectives  17.8 us (19%)
  Pallas kernels  14.1 us (15%)
  local copies, waits for them, and re-layouts  2.09 us (2%)
  between operations  1.41 us (2%)
    ppermute x14, waiting for transfers between devices, swap(): lax.ppermute(array, 'frame', [(f, f ^ distance) for f in range(devices)])  24.5 us
    all_to_all x1, blocking collectives, per_device(): lax.all_to_all(back, 'frame', split_axis=0, concat_axis=0, tiled=True)  17.8 us
    ppermute x14, starting transfers between devices, swap(): lax.ppermute(array, 'frame', [(f, f ^ distance) for f in range(devices)])  14 us
    ppermute x5, waiting for transfers between devices, by_clip(): return lax.ppermute(array, 'clip', [(c, c ^ offset) for c in range(4)])  10.8 us
    pallas_call x1, Pallas kernels, run_main(): pl.pallas_call(functools.partial(main_kernel, view), out_shape=jax.ShapeD...  9.89 us
    ppermute x5, starting transfers between devices, by_clip(): return lax.ppermute(array, 'clip', [(c, c ^ offset) for c in range(4)])  8.4 us
    pallas_call x1, Pallas kernels, gather_in_rounds(): pl.pallas_call(functools.partial(pack_kernel, patches, share), out_shape=...  2.67 us
  transfers between devices with their start and end apart: 19, of which 10 were waited for; matrix products, arithmetic and copies ran while one was open for 0% of the time, Pallas kernels for 1%

profile of v10, /device:TPU:0, one launch (start us, length us, event | category | flops | bytes accessed | tf_op | source)
XLA Modules:
  0.0 93.1 jit_solution(18314442156224882964)
XLA Ops:
  0.6 2.7 %pack.1 = (bf16[128,1024]{1,0:T(8,128)(2,1)}, bf16[192,1024]{1,0:T(8,128)(2,1)}, bf16[64,1024]{1,0:T(8,128)(2,1)}, bf16[320,1024]{1,0:T(8,128)(2,1)}, bf16[320,1024]{1,0:T(8,128)(2,1)}) custom-call(bf16[128,768]{1,0:T(8,128)(2,1)} %refs_0_.1, bf16[128,256]{1,0:T(8,128)(2,1)} %refs_1_.1, bf16[1,1,196,1024]{3,2,1,0:T(8,128)(2,1)} %refs_2_.1, ...), custom_call_target="tpu_custom_call" | custom-call | tf_op jit(solution)/shard_map/pack/pallas_call | solution.py:388
  3.3 3.0 %collective-permute-start.2 = (bf16[320,1024]{1,0:T(8,128)(2,1)}, bf16[320,1024]{1,0:T(8,128)(2,1)S(1)}, u32[]{:S(2)}, u32[]{:S(2)}) collective-permute-start(bf16[320,1024]{1,0:T(8,128)(2,1)} %get-tuple-element.32), channel_id=1, source_target_pairs={{0,4},{1,5},{2,6},{3,7},{4,0},{5,1},{6,2},{7,3},{8,12},{9,13},{10,... | collective-permute-start | bytes 1966088 | tf_op jit(solution)/shard_map/ppermute | solution.py:305
  6.3 1.5 %collective-permute-start.4 = (bf16[320,1024]{1,0:T(8,128)(2,1)}, bf16[320,1024]{1,0:T(8,128)(2,1)S(1)}, u32[]{:S(2)}, u32[]{:S(2)}) collective-permute-start(bf16[320,1024]{1,0:T(8,128)(2,1)} %get-tuple-element.33), channel_id=1, source_target_pairs={{0,2},{1,3},{2,0},{3,1},{4,6},{5,7},{6,4},{7,5},{8,10},{9,11},{10,... | collective-permute-start | bytes 1966088 | tf_op jit(solution)/shard_map/ppermute | solution.py:305
  7.8 1.6 %collective-permute-start.8 = (bf16[128,1024]{1,0:T(8,128)(2,1)}, bf16[128,1024]{1,0:T(8,128)(2,1)S(1)}, u32[]{:S(2)}, u32[]{:S(2)}) collective-permute-start(bf16[128,1024]{1,0:T(8,128)(2,1)} %get-tuple-element.31), channel_id=1, source_target_pairs={{0,8},{8,0},{16,24},{24,16},{1,9},{9,1},{17,25},{25,17},{2,10},{10... | collective-permute-start | bytes 786440 | tf_op jit(solution)/shard_map/ppermute | solution.py:403
  9.4 2.5 %collective-permute-start.1 = (bf16[128,1024]{1,0:T(8,128)(2,1)}, bf16[128,1024]{1,0:T(8,128)(2,1)S(1)}, u32[]{:S(2)}, u32[]{:S(2)}) collective-permute-start(bf16[128,1024]{1,0:T(8,128)(2,1)} %get-tuple-element.31), channel_id=1, source_target_pairs={{0,24},{8,16},{16,8},{24,0},{1,25},{9,17},{17,9},{25,1},{2,26},{10... | collective-permute-start | bytes 786440 | tf_op jit(solution)/shard_map/ppermute | solution.py:403
  11.9 0.1 collective-permute-start
  12.0 9.3 %collective-permute-done.2.refs_2_ = bf16[320,1024]{1,0:T(8,128)(2,1)S(1)} collective-permute-done((bf16[320,1024]{1,0:T(8,128)(2,1)}, bf16[320,1024]{1,0:T(8,128)(2,1)S(1)}, u32[]{:S(2)}, u32[]{:S(2)}) %collective-permute-start.2) | collective-permute-done | bytes 655392 | tf_op jit(solution)/shard_map/ppermute | solution.py:305
  21.3 1.8 %collective-permute-start.3 = (bf16[128,1024]{1,0:T(8,128)(2,1)S(1)}, bf16[128,1024]{1,0:T(8,128)(2,1)S(1)}, u32[]{:S(2)}, u32[]{:S(2)}) collective-permute-start(bf16[128,1024]{1,0:T(8,128)(2,1)S(1)} %slice.32), channel_id=1, source_target_pairs={{0,2},{1,3},{2,0},{3,1},{4,6},{5,7},{6,4},{7,5},{8,10},{9,11},{10,... | collective-permute-start | bytes 786440 | tf_op jit(solution)/shard_map/ppermute | solution.py:305
  23.1 0.0 collective-permute-done.8.refs_0_
  23.1 0.0 collective-permute-done.4.refs_1_
  23.1 1.6 %collective-permute-start.5 = (bf16[128,1024]{1,0:T(8,128)(2,1)S(1)}, bf16[128,1024]{1,0:T(8,128)(2,1)S(1)}, u32[]{:S(2)}, u32[]{:S(2)}) collective-permute-start(bf16[128,1024]{1,0:T(8,128)(2,1)S(1)} %slice.33), channel_id=1, source_target_pairs={{0,4},{1,5},{2,6},{3,7},{4,0},{5,1},{6,2},{7,3},{8,12},{9,13},{10,... | collective-permute-start | bytes 786440 | tf_op jit(solution)/shard_map/ppermute | solution.py:305
  24.7 0.5 collective-permute-start.10
  25.2 0.0 collective-permute-done.1.refs_1_
  25.2 1.1 %collective-permute-start.9 = (bf16[128,1024]{1,0:T(8,128)(2,1)S(1)}, bf16[128,1024]{1,0:T(8,128)(2,1)S(1)}, u32[]{:S(2)}, u32[]{:S(2)}) collective-permute-start(bf16[128,1024]{1,0:T(8,128)(2,1)S(1)} %collective-permute-done.8.refs_0_), channel_id=1, source_target_pairs={{0,2},{1,3},{2,0},{3,1},{4,6},{5,7},{6,4},{7,5},{8,10},{9,11},{10,... | collective-permute-start | bytes 786440 | tf_op jit(solution)/shard_map/ppermute | solution.py:305
  26.4 8.2 %collective-permute-done.refs_0_ = bf16[128,1024]{1,0:T(8,128)(2,1)S(1)} collective-permute-done((bf16[128,1024]{1,0:T(8,128)(2,1)}, bf16[128,1024]{1,0:T(8,128)(2,1)S(1)}, u32[]{:S(2)}, u32[]{:S(2)}) %collective-permute-start) | collective-permute-done | bytes 262176 | tf_op jit(solution)/shard_map/ppermute | solution.py:403
  34.6 0.0 collective-permute-done.3.refs_3_.top_ref
  34.6 0.0 collective-permute-done.5.refs_4_.bottom_ref
  34.6 1.1 %collective-permute-done.10.refs_2_ = bf16[128,1024]{1,0:T(8,128)(2,1)S(1)} collective-permute-done((bf16[128,1024]{1,0:T(8,128)(2,1)S(1)}, bf16[128,1024]{1,0:T(8,128)(2,1)S(1)}, u32[]{:S(2)}, u32[]{:S(2)}) %collective-permute-start.10) | collective-permute-done | bytes 262176 | tf_op jit(solution)/shard_map/ppermute | solution.py:305
  35.7 0.0 collective-permute-done.9.refs_1_
  35.7 0.0 copy-start
  35.7 1.0 %copy-done = bf16[192,1024]{1,0:T(8,128)(2,1)S(1)} copy-done((bf16[192,1024]{1,0:T(8,128)(2,1)S(1)}, bf16[192,1024]{1,0:T(8,128)(2,1)}, u32[]{:S(2)}) %copy-start) | copy-done | bytes 393240
  36.7 0.0 copy-start.1
  36.7 0.0 copy-start.2
  36.7 0.1 join.6.refs_1_.rest_0_
  36.8 0.1 collective-permute-start.11
  37.0 1.6 %collective-permute-start.7 = (bf16[256,1024]{1,0:T(8,128)(2,1)S(1)}, bf16[256,1024]{1,0:T(8,128)(2,1)S(1)}, u32[]{:S(2)}, u32[]{:S(2)}) collective-permute-start(bf16[256,1024]{1,0:T(8,128)(2,1)S(1)} %join.5.refs_0_), channel_id=1, source_target_pairs={{0,4},{1,5},{2,6},{3,7},{4,0},{5,1},{6,2},{7,3},{8,12},{9,13},{10,... | collective-permute-start | bytes 1572872 | tf_op jit(solution)/shard_map/ppermute | solution.py:305
  38.6 0.5 collective-permute-start.6
  39.1 1.6 %collective-permute-start.14 = (bf16[128,1024]{1,0:T(8,128)(2,1)S(1)}, bf16[128,1024]{1,0:T(8,128)(2,1)S(1)}, u32[]{:S(2)}, u32[]{:S(2)}) collective-permute-start(bf16[128,1024]{1,0:T(8,128)(2,1)S(1)} %pick.1), channel_id=1, source_target_pairs={{0,8},{8,0},{16,24},{24,16},{1,9},{9,1},{17,25},{25,17},{2,10},{10... | collective-permute-start | bytes 786440 | tf_op jit(solution)/shard_map/ppermute | solution.py:403
  40.8 2.6 %collective-permute-start.13 = (bf16[128,1024]{1,0:T(8,128)(2,1)S(1)}, bf16[128,1024]{1,0:T(8,128)(2,1)S(1)}, u32[]{:S(2)}, u32[]{:S(2)}) collective-permute-start(bf16[128,1024]{1,0:T(8,128)(2,1)S(1)} %pick.1), channel_id=1, source_target_pairs={{0,16},{8,24},{16,0},{24,8},{1,17},{9,25},{17,1},{25,9},{2,18},{10... | collective-permute-start | bytes 786440 | tf_op jit(solution)/shard_map/ppermute | solution.py:403
  43.3 0.0 collective-permute-done.11.refs_2_.rest_1_
  43.3 0.0 copy-done.1
  43.3 0.0 copy-done.2
  43.4 1.1 %front.1 = (bf16[8,2,32,1024]{3,2,1,0:T(8,128)(2,1)S(1)}, bf16[256,1024]{1,0:T(8,128)(2,1)S(1)}, f32[256,128]{1,0:T(8,128)S(1)}, bf16[256,768]{1,0:T(8,128)(2,1)S(1)}) custom-call(f32[1,1024]{1,0:T(1,128)S(1)} %bitcast.11, bf16[64,1024]{1,0:T(8,128)(2,1)S(1)} %copy-done.1, bf16[1088,1024]{1,0:T(8,128)(2,1)S(1)} %join.6.refs_1_.rest_0_, ...), custom_call_target="tpu_custom_call" | custom-call | flops 256 | bytes 256 | tf_op jit(solution)/shard_map/front/pallas_call | solution.py:243
  44.5 6.9 %collective-permute-done.7.refs_2_ = bf16[256,1024]{1,0:T(8,128)(2,1)S(1)} collective-permute-done((bf16[256,1024]{1,0:T(8,128)(2,1)S(1)}, bf16[256,1024]{1,0:T(8,128)(2,1)S(1)}, u32[]{:S(2)}, u32[]{:S(2)}) %collective-permute-start.7) | collective-permute-done | bytes 524320 | tf_op jit(solution)/shard_map/ppermute | solution.py:305
  51.4 1.2 %collective-permute-done.6.refs_1_ = bf16[256,1024]{1,0:T(8,128)(2,1)S(1)} collective-permute-done((bf16[256,1024]{1,0:T(8,128)(2,1)S(1)}, bf16[256,1024]{1,0:T(8,128)(2,1)S(1)}, u32[]{:S(2)}, u32[]{:S(2)}) %collective-permute-start.6) | collective-permute-done | bytes 524320 | tf_op jit(solution)/shard_map/ppermute | solution.py:305
  52.6 0.2 collective-permute-done.14.refs_4_
  52.8 2.4 %collective-permute-done.13.refs_3_ = bf16[128,1024]{1,0:T(8,128)(2,1)S(1)} collective-permute-done((bf16[128,1024]{1,0:T(8,128)(2,1)S(1)}, bf16[128,1024]{1,0:T(8,128)(2,1)S(1)}, u32[]{:S(2)}, u32[]{:S(2)}) %collective-permute-start.13) | collective-permute-done | bytes 262176 | tf_op jit(solution)/shard_map/ppermute | solution.py:403
  55.2 0.1 join.8.rest_4_
  55.3 0.1 collective-permute-start.15
  55.4 0.1 join.7.rest_2_
  55.5 0.6 collective-permute-start.12
  56.0 1.6 %collective-permute-start.16 = (bf16[64,1024]{1,0:T(8,128)(2,1)S(1)}, bf16[64,1024]{1,0:T(8,128)(2,1)S(1)}, u32[]{:S(2)}, u32[]{:S(2)}) collective-permute-start(bf16[64,1024]{1,0:T(8,128)(2,1)S(1)} %slice.26), channel_id=1, source_target_pairs={{0,2},{1,3},{2,0},{3,1},{4,6},{5,7},{6,4},{7,5},{8,10},{9,11},{10,... | collective-permute-start | bytes 393224 | tf_op jit(solution)/shard_map/ppermute | solution.py:305
  57.6 0.0 collective-permute-start.17
  57.6 3.9 %collective-permute-done.16.refs_0_ = bf16[64,1024]{1,0:T(8,128)(2,1)S(1)} collective-permute-done((bf16[64,1024]{1,0:T(8,128)(2,1)S(1)}, bf16[64,1024]{1,0:T(8,128)(2,1)S(1)}, u32[]{:S(2)}, u32[]{:S(2)}) %collective-permute-start.16) | collective-permute-done | bytes 131104 | tf_op jit(solution)/shard_map/ppermute | solution.py:305
  61.5 1.2 %collective-permute-done.17.refs_1_ = bf16[64,1024]{1,0:T(8,128)(2,1)S(1)} collective-permute-done((bf16[64,1024]{1,0:T(8,128)(2,1)S(1)}, bf16[64,1024]{1,0:T(8,128)(2,1)S(1)}, u32[]{:S(2)}, u32[]{:S(2)}) %collective-permute-start.17) | collective-permute-done | bytes 131104 | tf_op jit(solution)/shard_map/ppermute | solution.py:305
  62.8 0.1 collective-permute-start.18
  63.5 0.0 collective-permute-done.12.rest_3_
  63.5 0.9 collective-permute-done.18.rest_7_
  64.4 0.0 collective-permute-done.15.rest_5_
  64.4 9.9 %main.1 = bf16[8,2,32,1024]{3,2,1,0:T(8,128)(2,1)S(1)} custom-call(s32[1]{0:T(128)S(6)} %copy.9.counts_ref, f32[1,1024]{1,0:T(1,128)S(1)} %bitcast.12, bf16[8,2,32,1024]{3,2,1,0:T(8,128)(2,1)S(1)} %get-tuple-element.52.both_ref, bf16[256,1024]{1,0:T(8,128)(2,1)S(1)} %get-tuple-element.53.normed_ref, f32[256,128]{1,0:T(8,128)S(1)} %get-tuple-element.54.stats_ref, ...), custom_call_target="tpu_custom_call" | custom-call | flops 3221225472 | bytes 10485760 | tf_op jit(solution)/shard_map/main/pallas_call | solution.py:267
  74.3 17.8 %all_to_all.5 = bf16[8,1,2,32,1024]{4,3,2,1,0:T(8,128)(2,1)S(1)} all-to-all(bf16[8,1,2,32,1024]{4,3,2,1,0:T(8,128)(2,1)S(1)} %bitcast.10), channel_id=1, replica_groups=mesh['clip'=4,'frame'=8] {'frame'}, dimensions={0} | all-to-all | bytes 2097152 | tf_op jit(solution)/shard_map/all_to_all | solution.py:567
  92.1 0.1 fusion
  92.1 0.9 %slice_bitcast_fusion = (bf16[1,1,196,1024]{3,2,1,0:T(8,128)(2,1)}, bf16[1,1,196,1024]{3,2,1,0:T(8,128)(2,1)}) fusion(bf16[1,256,1024]{2,1,0:T(8,128)(2,1)S(1)} %bitcast.13, bf16[1,256,1024]{2,1,0:T(8,128)(2,1)S(1)} %bitcast.14), kind=kLoop, calls=%fused_computation | loop fusion | bytes 1605632 | tf_op jit(solution)/shard_map/broadcast_in_dim | solution.py:571
  (7 shorter events, 0.1 us)
Async XLA Ops:
  3.3 18.0 %collective-permute-start.2 = (bf16[320,1024]{1,0:T(8,128)(2,1)}, bf16[320,1024]{1,0:T(8,128)(2,1)S(1)}, u32[]{:S(2)}, u32[]{:S(2)}) collective-permute-start(bf16[320,1024]{1,0:T(8,128)(2,1)} %get-tuple-element.32), channel_id=1, source_target_pairs={{0,4},{1,5},{2,6},{3,7},{4,0},{5,1},{6,2},{7,3},{8,12},{9,13},{10,... | collective-permute-start | bytes 1966088 | tf_op jit(solution)/shard_map/ppermute | solution.py:305
  6.3 16.7 %collective-permute-start.4 = (bf16[320,1024]{1,0:T(8,128)(2,1)}, bf16[320,1024]{1,0:T(8,128)(2,1)S(1)}, u32[]{:S(2)}, u32[]{:S(2)}) collective-permute-start(bf16[320,1024]{1,0:T(8,128)(2,1)} %get-tuple-element.33), channel_id=1, source_target_pairs={{0,2},{1,3},{2,0},{3,1},{4,6},{5,7},{6,4},{7,5},{8,10},{9,11},{10,... | collective-permute-start | bytes 1966088 | tf_op jit(solution)/shard_map/ppermute | solution.py:305
  7.8 15.3 %collective-permute-start.8 = (bf16[128,1024]{1,0:T(8,128)(2,1)}, bf16[128,1024]{1,0:T(8,128)(2,1)S(1)}, u32[]{:S(2)}, u32[]{:S(2)}) collective-permute-start(bf16[128,1024]{1,0:T(8,128)(2,1)} %get-tuple-element.31), channel_id=1, source_target_pairs={{0,8},{8,0},{16,24},{24,16},{1,9},{9,1},{17,25},{25,17},{2,10},{10... | collective-permute-start | bytes 786440 | tf_op jit(solution)/shard_map/ppermute | solution.py:403
  9.4 15.8 %collective-permute-start.1 = (bf16[128,1024]{1,0:T(8,128)(2,1)}, bf16[128,1024]{1,0:T(8,128)(2,1)S(1)}, u32[]{:S(2)}, u32[]{:S(2)}) collective-permute-start(bf16[128,1024]{1,0:T(8,128)(2,1)} %get-tuple-element.31), channel_id=1, source_target_pairs={{0,24},{8,16},{16,8},{24,0},{1,25},{9,17},{17,9},{25,1},{2,26},{10... | collective-permute-start | bytes 786440 | tf_op jit(solution)/shard_map/ppermute | solution.py:403
  11.9 22.7 %collective-permute-start = (bf16[128,1024]{1,0:T(8,128)(2,1)}, bf16[128,1024]{1,0:T(8,128)(2,1)S(1)}, u32[]{:S(2)}, u32[]{:S(2)}) collective-permute-start(bf16[128,1024]{1,0:T(8,128)(2,1)} %get-tuple-element.31), channel_id=1, source_target_pairs={{0,16},{8,24},{16,0},{24,8},{1,17},{9,25},{17,1},{25,9},{2,18},{10... | collective-permute-start | bytes 786440 | tf_op jit(solution)/shard_map/ppermute | solution.py:403
  21.3 13.3 %collective-permute-start.3 = (bf16[128,1024]{1,0:T(8,128)(2,1)S(1)}, bf16[128,1024]{1,0:T(8,128)(2,1)S(1)}, u32[]{:S(2)}, u32[]{:S(2)}) collective-permute-start(bf16[128,1024]{1,0:T(8,128)(2,1)S(1)} %slice.32), channel_id=1, source_target_pairs={{0,2},{1,3},{2,0},{3,1},{4,6},{5,7},{6,4},{7,5},{8,10},{9,11},{10,... | collective-permute-start | bytes 786440 | tf_op jit(solution)/shard_map/ppermute | solution.py:305
  23.1 11.5 %collective-permute-start.5 = (bf16[128,1024]{1,0:T(8,128)(2,1)S(1)}, bf16[128,1024]{1,0:T(8,128)(2,1)S(1)}, u32[]{:S(2)}, u32[]{:S(2)}) collective-permute-start(bf16[128,1024]{1,0:T(8,128)(2,1)S(1)} %slice.33), channel_id=1, source_target_pairs={{0,4},{1,5},{2,6},{3,7},{4,0},{5,1},{6,2},{7,3},{8,12},{9,13},{10,... | collective-permute-start | bytes 786440 | tf_op jit(solution)/shard_map/ppermute | solution.py:305
  24.7 11.0 %collective-permute-start.10 = (bf16[128,1024]{1,0:T(8,128)(2,1)S(1)}, bf16[128,1024]{1,0:T(8,128)(2,1)S(1)}, u32[]{:S(2)}, u32[]{:S(2)}) collective-permute-start(bf16[128,1024]{1,0:T(8,128)(2,1)S(1)} %collective-permute-done.8.refs_0_), channel_id=1, source_target_pairs={{0,4},{1,5},{2,6},{3,7},{4,0},{5,1},{6,2},{7,3},{8,12},{9,13},{10,... | collective-permute-start | bytes 786440 | tf_op jit(solution)/shard_map/ppermute | solution.py:305
  25.2 10.5 %collective-permute-start.9 = (bf16[128,1024]{1,0:T(8,128)(2,1)S(1)}, bf16[128,1024]{1,0:T(8,128)(2,1)S(1)}, u32[]{:S(2)}, u32[]{:S(2)}) collective-permute-start(bf16[128,1024]{1,0:T(8,128)(2,1)S(1)} %collective-permute-done.8.refs_0_), channel_id=1, source_target_pairs={{0,2},{1,3},{2,0},{3,1},{4,6},{5,7},{6,4},{7,5},{8,10},{9,11},{10,... | collective-permute-start | bytes 786440 | tf_op jit(solution)/shard_map/ppermute | solution.py:305
  35.7 1.0 %copy-start = (bf16[192,1024]{1,0:T(8,128)(2,1)S(1)}, bf16[192,1024]{1,0:T(8,128)(2,1)}, u32[]{:S(2)}) copy-start(bf16[192,1024]{1,0:T(8,128)(2,1)} %get-tuple-element.43.refs_0_) | copy-start | bytes 1179652
  36.7 6.7 %copy-start.1 = (bf16[64,1024]{1,0:T(8,128)(2,1)S(1)}, bf16[64,1024]{1,0:T(8,128)(2,1)}, u32[]{:S(2)}) copy-start(bf16[64,1024]{1,0:T(8,128)(2,1)} %get-tuple-element.36.refs_0_) | copy-start | bytes 393220
  36.7 6.7 %copy-start.2 = (f32[1024]{0:T(1024)S(1)}, f32[1024]{0:T(1024)}, u32[]{:S(2)}) copy-start(f32[1024]{0:T(1024)} %param.8) | copy-start | bytes 12292
  36.8 6.5 %collective-permute-start.11 = (bf16[1088,1024]{1,0:T(8,128)(2,1)S(1)}, bf16[1088,1024]{1,0:T(8,128)(2,1)S(1)}, u32[]{:S(2)}, u32[]{:S(2)}) collective-permute-start(bf16[1088,1024]{1,0:T(8,128)(2,1)S(1)} %join.6.refs_1_.rest_0_), channel_id=1, source_target_pairs={{0,1},{1,0},{2,3},{3,2},{4,5},{5,4},{6,7},{7,6},{8,9},{9,8},{10,11... | collective-permute-start | bytes 6684680 | tf_op jit(solution)/shard_map/ppermute | solution.py:305
  37.0 14.4 %collective-permute-start.7 = (bf16[256,1024]{1,0:T(8,128)(2,1)S(1)}, bf16[256,1024]{1,0:T(8,128)(2,1)S(1)}, u32[]{:S(2)}, u32[]{:S(2)}) collective-permute-start(bf16[256,1024]{1,0:T(8,128)(2,1)S(1)} %join.5.refs_0_), channel_id=1, source_target_pairs={{0,4},{1,5},{2,6},{3,7},{4,0},{5,1},{6,2},{7,3},{8,12},{9,13},{10,... | collective-permute-start | bytes 1572872 | tf_op jit(solution)/shard_map/ppermute | solution.py:305
  38.6 14.0 %collective-permute-start.6 = (bf16[256,1024]{1,0:T(8,128)(2,1)S(1)}, bf16[256,1024]{1,0:T(8,128)(2,1)S(1)}, u32[]{:S(2)}, u32[]{:S(2)}) collective-permute-start(bf16[256,1024]{1,0:T(8,128)(2,1)S(1)} %join.5.refs_0_), channel_id=1, source_target_pairs={{0,2},{1,3},{2,0},{3,1},{4,6},{5,7},{6,4},{7,5},{8,10},{9,11},{10,... | collective-permute-start | bytes 1572872 | tf_op jit(solution)/shard_map/ppermute | solution.py:305
  39.1 13.7 %collective-permute-start.14 = (bf16[128,1024]{1,0:T(8,128)(2,1)S(1)}, bf16[128,1024]{1,0:T(8,128)(2,1)S(1)}, u32[]{:S(2)}, u32[]{:S(2)}) collective-permute-start(bf16[128,1024]{1,0:T(8,128)(2,1)S(1)} %pick.1), channel_id=1, source_target_pairs={{0,8},{8,0},{16,24},{24,16},{1,9},{9,1},{17,25},{25,17},{2,10},{10... | collective-permute-start | bytes 786440 | tf_op jit(solution)/shard_map/ppermute | solution.py:403
  40.8 14.4 %collective-permute-start.13 = (bf16[128,1024]{1,0:T(8,128)(2,1)S(1)}, bf16[128,1024]{1,0:T(8,128)(2,1)S(1)}, u32[]{:S(2)}, u32[]{:S(2)}) collective-permute-start(bf16[128,1024]{1,0:T(8,128)(2,1)S(1)} %pick.1), channel_id=1, source_target_pairs={{0,16},{8,24},{16,0},{24,8},{1,17},{9,25},{17,1},{25,9},{2,18},{10... | collective-permute-start | bytes 786440 | tf_op jit(solution)/shard_map/ppermute | solution.py:403
  55.3 9.1 %collective-permute-start.15 = (bf16[1024,1024]{1,0:T(8,128)(2,1)S(1)}, bf16[1024,1024]{1,0:T(8,128)(2,1)S(1)}, u32[]{:S(2)}, u32[]{:S(2)}) collective-permute-start(bf16[1024,1024]{1,0:T(8,128)(2,1)S(1)} %join.8.rest_4_), channel_id=1, source_target_pairs={{0,1},{1,0},{2,3},{3,2},{4,5},{5,4},{6,7},{7,6},{8,9},{9,8},{10,11... | collective-permute-start | bytes 6291464 | tf_op jit(solution)/shard_map/ppermute | solution.py:305
  55.5 8.0 %collective-permute-start.12 = (bf16[384,1024]{1,0:T(8,128)(2,1)S(1)}, bf16[384,1024]{1,0:T(8,128)(2,1)S(1)}, u32[]{:S(2)}, u32[]{:S(2)}) collective-permute-start(bf16[384,1024]{1,0:T(8,128)(2,1)S(1)} %join.7.rest_2_), channel_id=1, source_target_pairs={{0,1},{1,0},{2,3},{3,2},{4,5},{5,4},{6,7},{7,6},{8,9},{9,8},{10,11... | collective-permute-start | bytes 2359304 | tf_op jit(solution)/shard_map/ppermute | solution.py:305
  56.0 5.5 %collective-permute-start.16 = (bf16[64,1024]{1,0:T(8,128)(2,1)S(1)}, bf16[64,1024]{1,0:T(8,128)(2,1)S(1)}, u32[]{:S(2)}, u32[]{:S(2)}) collective-permute-start(bf16[64,1024]{1,0:T(8,128)(2,1)S(1)} %slice.26), channel_id=1, source_target_pairs={{0,2},{1,3},{2,0},{3,1},{4,6},{5,7},{6,4},{7,5},{8,10},{9,11},{10,... | collective-permute-start | bytes 393224 | tf_op jit(solution)/shard_map/ppermute | solution.py:305
  57.6 5.1 %collective-permute-start.17 = (bf16[64,1024]{1,0:T(8,128)(2,1)S(1)}, bf16[64,1024]{1,0:T(8,128)(2,1)S(1)}, u32[]{:S(2)}, u32[]{:S(2)}) collective-permute-start(bf16[64,1024]{1,0:T(8,128)(2,1)S(1)} %slice.27), channel_id=1, source_target_pairs={{0,4},{1,5},{2,6},{3,7},{4,0},{5,1},{6,2},{7,3},{8,12},{9,13},{10,... | collective-permute-start | bytes 393224 | tf_op jit(solution)/shard_map/ppermute | solution.py:305
  62.8 1.6 %collective-permute-start.18 = (bf16[128,1024]{1,0:T(8,128)(2,1)S(1)}, bf16[128,1024]{1,0:T(8,128)(2,1)S(1)}, u32[]{:S(2)}, u32[]{:S(2)}) collective-permute-start(bf16[128,1024]{1,0:T(8,128)(2,1)S(1)} %join.9.rest_6_), channel_id=1, source_target_pairs={{0,1},{1,0},{2,3},{3,2},{4,5},{5,4},{6,7},{7,6},{8,9},{9,8},{10,11... | collective-permute-start | bytes 786440 | tf_op jit(solution)/shard_map/ppermute | solution.py:305

commit v11 on v9

--- a/solution.py
+++ b/solution.py
@@ -46,9 +46,10 @@
     return [(start, step) for start in range(0, columns, step)]
 
 
-def stack_rows(view, refs, block, lanes):
+def stack_rows(view, refs, block, lanes, groups=None):
+    groups = view.rows if groups is None else groups
     return jnp.concatenate(
-        [view.piece(refs, block, *part, lanes) for parts in view.rows for part in parts], axis=0
+        [view.piece(refs, block, *part, lanes) for parts in groups for part in parts], axis=0
     )
 
 
@@ -81,14 +82,66 @@
         stats_ref[here, 0:1] = average
         stats_ref[here, 1:2] = scale
     normed_ref[...] = beside(natural, *view.row_order())
-    for start, size in chunks(proj_ref.shape[1]):
-        weight = stack_rows(view, sources, 0, (start, size))
-        proj_ref[:, start : start + size] = dot(normed_ref[...], weight, NN).astype(jnp.bfloat16)
+    for block in range(view.early):
+        for start, size in chunks(view.in_columns):
+            weight = stack_rows(view, sources, block, (start, size))
+            here = pl.ds(block * view.in_columns + start, size)
+            proj_ref[:, here] = dot(normed_ref[...], weight, NN).astype(jnp.bfloat16)
+
+
+def put_rows(view, target, parts, value):
+    row_starts, _ = view.row_order()
+    done = 0
+    for index, first, depth in parts:
+        start = pl.multiple_of(row_starts[index] + first, 128)
+        target[:, pl.ds(start, depth)] = value[:, done : done + depth]
+        done += depth
+
+
+def live_rows(view, counts_ref, rows):
+    frame = (lax.broadcasted_iota(jnp.int32, (rows, 1), 0) // SUB) ^ view.device()
+    return (frame < counts_ref[0]).astype(jnp.float32)
+
+
+def masked_cotangent(view, counts_ref, both_ref, natural):
+    frames, _, patches, _ = both_ref.shape
+    rows = frames * SUB
+    live = live_rows(view, counts_ref, rows)
+    for group in range(patches // SUB):
+        wide = load_rows(both_ref, 1, group).astype(jnp.float32)
+        natural[pl.ds(group * rows, rows), :] = (wide * live).astype(jnp.bfloat16)
+    starts = [block * view.out_columns for block in view.block_order()]
+    return beside(natural, starts, view.out_columns)
+
+
+def grad_attended(view, weights, ordered, groups, target):
+    for parts in groups:
+        weight = stack_columns(view, weights, parts, view.in_columns, view.out_columns)
+        put_rows(view, target, parts, dot(ordered, weight, NT).astype(jnp.bfloat16))
+
+
+def early_depth(view):
+    return sum(part[2] for parts in view.early_rows for part in parts)
+
+
+def middle_kernel(view, counts_ref, both_ref, normed_ref, *rest):
+    weights = rest[:-4]
+    ordered_ref, ga_ref, partial_ref, natural = rest[-4:]
+    ordered_ref[...] = masked_cotangent(view, counts_ref, both_ref, natural)
+    grad_attended(view, weights, ordered_ref[...], view.early_rows, ga_ref)
+    depth = early_depth(view)
+    for block in range(view.early, view.blocks):
+        for start, size in chunks(view.in_columns):
+            weight = stack_rows(view, weights, block, (start, size), view.early_rows)
+            here = pl.ds((block - view.early) * view.in_columns + start, size)
+            partial_ref[:, here] = dot(normed_ref[:, :depth], weight, NN)
 
 
 def main_kernel(view, counts_ref, gain_ref, both_ref, normed_ref, stats_ref, front_ref, *rest):
-    weights = rest[:-11]
-    out_ref, grads, proj, ga, att, gproj, wide_sum, bias, scores, gprobs, low = rest[-11:]
+    weights = rest[:-10]
+    out_ref, proj, ga, att, gproj, wide_sum, bias, scores, gprobs, low = rest[-10:]
+    middle = weights[:3] if view.early_rows else None
+    weights = weights[3:] if view.early_rows else weights
     frames, _, patches, width = both_ref.shape
     groups = patches // SUB
     rows = frames * SUB
@@ -101,22 +154,10 @@
     def column(block, stride, start=0):
         return pl.multiple_of(block_order[block] * stride + start, 128)
 
-    def put_rows(target, parts, value):
-        done = 0
-        for index, first, depth in parts:
-            start = pl.multiple_of(row_starts[index] + first, 128)
-            target[:, pl.ds(start, depth)] = value[:, done : done + depth]
-            done += depth
-
     def real(index):
         return ((index // SUB) ^ device) < count
 
-    live = real(lax.broadcasted_iota(jnp.int32, (rows, 1), 0)).astype(jnp.float32)
-    for group in range(groups):
-        here = pl.ds(group * rows, rows)
-        grads[here, :] = (load_rows(both_ref, 1, group).astype(jnp.float32) * live).astype(
-            jnp.bfloat16
-        )
+    live = live_rows(view, counts_ref, rows)
     key = lax.broadcasted_iota(jnp.int32, (rows, 2 * rows), 0)
     query = lax.broadcasted_iota(jnp.int32, (rows, 2 * rows), 1)
     bias[...] = jnp.where((query % SUB == key % SUB) & real(key), 0.0, NEGATIVE)
@@ -124,18 +165,27 @@
     low_lanes = (lane < DH).astype(jnp.bfloat16)
     high_lanes = (lane >= DH).astype(jnp.bfloat16)
 
-    grads_ordered = beside(grads, [column(i, out_columns) for i in range(view.blocks)], out_columns)
-    for parts in view.rows:
-        weight = stack_columns(view, weights, parts, in_columns, out_columns)
-        put_rows(ga, parts, dot(grads_ordered, weight, NT).astype(jnp.bfloat16))
-
-    proj[:, pl.ds(column(0, in_columns), in_columns)] = front_ref[...]
-    for block in range(1, view.blocks):
+    depth = early_depth(view)
+    late_rows = view.rows[len(view.early_rows) :]
+    if middle:
+        ordered, ga_early, partial = middle
+        ga[...] = ga_early[...]
+        grad_attended(view, weights, ordered[...], late_rows, ga)
+    else:
+        ordered = masked_cotangent(view, counts_ref, both_ref, att)
+        grad_attended(view, weights, ordered, late_rows, ga)
+
+    for block in range(view.early):
+        held = front_ref[:, block * in_columns : (block + 1) * in_columns]
+        proj[:, pl.ds(column(block, in_columns), in_columns)] = held
+    for block in range(view.early, view.blocks):
         for start, size in chunks(in_columns):
-            weight = stack_rows(view, weights, block, (start, size))
-            proj[:, pl.ds(column(block, in_columns, start), size)] = dot(
-                normed_ref[...], weight, NN
-            ).astype(jnp.bfloat16)
+            weight = stack_rows(view, weights, block, (start, size), late_rows)
+            value = dot(normed_ref[:, depth:], weight, NN)
+            if middle:
+                here = pl.ds((block - view.early) * in_columns + start, size)
+                value = value + partial[:, here]
+            proj[:, pl.ds(column(block, in_columns, start), size)] = value.astype(jnp.bfloat16)
 
     def apart(block):
         return jnp.concatenate([block * low_lanes, block * high_lanes], axis=0)
@@ -216,7 +266,7 @@
     gproj_ordered = beside(gproj, [column(i, in_columns) for i in range(view.blocks)], in_columns)
     for parts in view.rows:
         weight = stack_columns(view, weights, parts, 0, in_columns)
-        put_rows(wide_sum, parts, dot(gproj_ordered, weight, NT))
+        put_rows(view, wide_sum, parts, dot(gproj_ordered, weight, NT))
 
     for group in range(groups):
         here = pl.ds(group * rows, rows)
@@ -242,7 +292,7 @@
             jax.ShapeDtypeStruct(shape, jnp.bfloat16),
             jax.ShapeDtypeStruct((total, width), jnp.bfloat16),
             jax.ShapeDtypeStruct((total, 128), jnp.float32),
-            jax.ShapeDtypeStruct((total, view.in_columns), jnp.bfloat16),
+            jax.ShapeDtypeStruct((total, view.early * view.in_columns), jnp.bfloat16),
         ),
         in_specs=[vmem] * (1 + len(sources)),
         out_specs=(vmem,) * 4,
@@ -251,6 +301,27 @@
         cost_estimate=pl.CostEstimate(flops=total, bytes_accessed=total, transcendentals=0),
         name="front",
     )(gain, *sources)
+
+
+def run_middle(counts, fronted, weights, view):
+    both, normed, _, _ = fronted
+    total, width = normed.shape
+    vmem = pl.BlockSpec(memory_space=pltpu.VMEM)
+    columns = (view.blocks - view.early) * view.in_columns
+    return pl.pallas_call(
+        functools.partial(middle_kernel, view),
+        out_shape=(
+            jax.ShapeDtypeStruct((total, width), jnp.bfloat16),
+            jax.ShapeDtypeStruct((total, width), jnp.bfloat16),
+            jax.ShapeDtypeStruct((total, columns), jnp.float32),
+        ),
+        in_specs=[pl.BlockSpec(memory_space=pltpu.SMEM)] + [vmem] * (2 + len(weights)),
+        out_specs=(vmem,) * 3,
+        scratch_shapes=[pltpu.VMEM((total, width), jnp.bfloat16)],
+        compiler_params=pltpu.CompilerParams(vmem_limit_bytes=VMEM_LIMIT),
+        cost_estimate=pl.CostEstimate(flops=total, bytes_accessed=total, transcendentals=0),
+        name="middle",
+    )(counts, both, normed, *weights)
 
 
 def run_main(counts, gain, fronted, weights, view):
@@ -266,7 +337,6 @@
         in_specs=[smem] + [vmem] * (5 + len(weights)),
         out_specs=vmem,
         scratch_shapes=[
-            pltpu.VMEM((total, width), jnp.bfloat16),
             pltpu.VMEM((total, 3 * width), jnp.bfloat16),
             pltpu.VMEM((total, width), jnp.bfloat16),
             pltpu.VMEM((total, width), jnp.bfloat16),
@@ -290,8 +360,9 @@
 
 
 class View:
-    def __init__(self, blocks, rows, in_columns, out_columns, piece, tokens, device, row_order, block_order):
-        self.blocks, self.rows = blocks, rows
+    def __init__(self, blocks, early, rows, early_rows, in_columns, out_columns, piece, tokens, device, row_order, block_order):
+        self.blocks, self.early = blocks, early
+        self.rows, self.early_rows = rows, early_rows
         self.in_columns, self.out_columns = in_columns, out_columns
         self.piece, self.tokens, self.device = piece, tokens, device
         self.row_order, self.block_order = row_order, block_order
@@ -373,7 +444,9 @@
     to_dy[half:, :] = pair_x[2 * half :, :]
 
 
-def gather_in_rounds(input_weights, output_weights, tokens, cotangent, gain, share, devices):
+def gather_in_rounds(
+    counts, input_weights, output_weights, tokens, cotangent, gain, share, devices
+):
     depth, in_columns = input_weights.shape
     out_columns = output_weights.shape[1]
     _, _, patches, width = tokens.shape
@@ -414,13 +487,13 @@
     second = [one, *across(one)]
     two, three, first[2], first[3] = lax.optimization_barrier((two, three, first[2], first[3]))
     third = [join(0, two, three)]
-    second[1], second[2], own, *first = lax.optimization_barrier(
-        (second[1], second[2], own, *first)
+    third += across(third[0])
+    second[1], second[2], own, third[0], *first = lax.optimization_barrier(
+        (second[1], second[2], own, third[0], *first)
     )
     first_other = other_core([own, *first])
     second_other = other_core(second)
     ready = [joined, *first, *first_other, *second, *second_other]
-    third += across(third[0])
 
     def tokens_in(sources, both_ref):
         core = lax.axis_index("frame") % 2
@@ -448,18 +521,21 @@
     ]
     others = [[(1, d, 0, depth, 0)] for d in (0, 2, 4)]
     pairs = [[(2, d, 0, depth, 0), (3, d, depth, depth, 0)] for d in (0, 2, 4)]
+    long = half + depth
     pairs += [
-        [(1, 6, 0, half, 0), (2, 6, half, depth, 0)],
-        [(1, 6, 0, half, half), (3, 6, half, depth, 0)],
+        [
+            (1, 6, 0, half, 0), (2, 6, half, depth, 0),
+            (1, 6, long, half, half), (3, 6, long + half, depth, 0),
+        ],
     ]
     arrays = []
     for group in (table, others, pairs):
         arrays += [(core, parts) for core in (0, 1) for parts in group]
 
-    def piece(base):
+    def piece(present):
         def value(refs, offset, distance, first, depth, lanes):
             found = [
-                (inside, refs[base + ref][start : start + size, lanes[0] : lanes[0] + lanes[1]])
+                (inside, refs[present.index(ref)][start : start + size, lanes[0] : lanes[0] + lanes[1]])
                 for ref, (core, parts) in enumerate(arrays)
                 for source, away, start, size, inside in parts
                 if (source, away ^ core) == (offset, distance)
@@ -468,20 +544,26 @@
 
         return value
 
-    def view(base):
+    row_groups = [[(d, 0, depth), (d + 1, 0, depth)] for d in range(0, devices, 2)]
+
+    def view(present):
         return View(
             4,
-            [[(d, 0, depth), (d + 1, 0, depth)] for d in range(0, devices, 2)],
+            1,
+            row_groups,
+            row_groups[:3],
             in_columns,
             out_columns,
-            piece(base),
+            piece(present),
             tokens_in,
             lambda: lax.axis_index("frame"),
             lambda: ([(lax.axis_index("frame") ^ d) * depth for d in range(devices)], depth),
             lambda: [lax.axis_index("clip") ^ offset for offset in range(4)],
         )
 
-    fronted = run_front(gain, (devices, 2, share, width), [mine, *ready[:10]], view(1))
+    fronted = run_front(
+        gain, (devices, 2, share, width), [mine, *ready[:10]], view([None, *range(10)])
+    )
     to_dx, to_dy = pl.pallas_call(
         functools.partial(turn_kernel, half),
         out_shape=(rows_of(depth + half), rows_of(depth + half)),
@@ -490,13 +572,20 @@
         compiler_params=SMALL,
         name="turn",
     )(second[1], second[2], third[1], third[2])
-    third += [swap(to_dx, 2, devices), swap(to_dy, 4, devices)]
-    third[3], *fronted = lax.optimization_barrier((third[3], *fronted))
-    third += other_core(third)
-    return fronted, [*ready, *third], view(0)
-
-
-def gather_plainly(input_weights, output_weights, tokens, cotangent, gain, share, devices):
+    last = [swap(to_dx, 2, devices), swap(to_dy, 4, devices)]
+    third_other = other_core(third)
+    middle = run_middle(
+        counts, fronted, [*ready, *third, *third_other], view([*range(16), 16, 17, 18, 20, 21, 22])
+    )
+    last[0], *middle = lax.optimization_barrier((last[0], *middle))
+    last = join(0, *last)
+    weights = [*middle, *ready, *third, last, *third_other, swap(last, 1, devices)]
+    return fronted, weights, view(list(range(24)))
+
+
+def gather_plainly(
+    counts, input_weights, output_weights, tokens, cotangent, gain, share, devices
+):
     _, slots, patches, width = tokens.shape
     whole = []
     for weights in (input_weights, output_weights):
@@ -524,7 +613,9 @@
     step = math.gcd(width, 256)
     view = View(
         1,
+        1,
         [[(0, first, step)] for first in range(0, width, step)],
+        [],
         in_columns,
         out_columns,
         piece,
@@ -546,7 +637,7 @@
     gather = gather_in_rounds if small else gather_plainly
     gain = norm_gain.reshape(1, width)
     fronted, weights, view = gather(
-        input_weights, output_weights, tokens, cotangent, gain, share, devices
+        counts, input_weights, output_weights, tokens, cotangent, gain, share, devices
     )
     back = run_main(counts, gain, fronted, weights, view)
     back = back.reshape(devices, slots, 2, share, width)

time: 91.5 us -> 93.9 us (1.026)
  waiting for transfers between devices: 37.8 us -> 39.4 us
    pallas_call x0 -> x1, Pallas kernels: none -> 1.67 us  [run_middle(): pl.pallas_call(functools.partial(middle_kernel, view), out_shape=(jax.Sha...]
    pallas_call x1, Pallas kernels: 9.91 us -> 8.33 us  [run_main(): pl.pallas_call(functools.partial(main_kernel, view), out_shape=jax.ShapeD...]
    ppermute x23 -> x22, waiting for transfers between devices: 29.6 us -> 31.2 us  [swap(): lax.ppermute(array, 'frame', [(f, f ^ distance) for f in range(devices)])]
    ppermute x23 -> x22, starting transfers between devices: 15 us -> 15.9 us  [swap(): lax.ppermute(array, 'frame', [(f, f ^ distance) for f in range(devices)])]
  transfers between devices with their start and end apart: 26 -> 25, of which waited for: 9 -> 9; matrix products, arithmetic and copies ran while one was open for 0% -> 0% of each run, Pallas kernels for 1% -> 3%
where the time goes in v11:
time: 93.9 us; the launch traced here: 93.7 us
  waiting for transfers between devices  39.4 us (42%)
  starting transfers between devices  20.1 us (21%)
  blocking collectives  17.8 us (19%)
  Pallas kernels  14 us (15%)
  between operations  1.47 us (2%)
  local copies, waits for them, and re-layouts  1.08 us (1%)
    ppermute x22, waiting for transfers between devices, swap(): lax.ppermute(array, 'frame', [(f, f ^ distance) for f in range(devices)])  31.2 us
    all_to_all x1, blocking collectives, per_device(): lax.all_to_all(back, 'frame', split_axis=0, concat_axis=0, tiled=True)  17.8 us
    ppermute x22, starting transfers between devices, swap(): lax.ppermute(array, 'frame', [(f, f ^ distance) for f in range(devices)])  15.9 us
    pallas_call x1, Pallas kernels, run_main(): pl.pallas_call(functools.partial(main_kernel, view), out_shape=jax.ShapeD...  8.33 us
    ppermute x3, waiting for transfers between devices, by_clip(): return lax.ppermute(array, 'clip', [(c, c ^ offset) for c in range(4)])  8.21 us
    ppermute x3, starting transfers between devices, by_clip(): return lax.ppermute(array, 'clip', [(c, c ^ offset) for c in range(4)])  4.17 us
    pallas_call x1, Pallas kernels, gather_in_rounds(): pl.pallas_call(functools.partial(pack_kernel, patches, share), out_shape=...  2.69 us
  transfers between devices with their start and end apart: 25, of which 9 were waited for; matrix products, arithmetic and copies ran while one was open for 0% of the time, Pallas kernels for 3%

profile of v11, /device:TPU:0, one launch (start us, length us, event | category | flops | bytes accessed | tf_op | source)
XLA Modules:
  0.0 93.7 jit_solution(4704477961056017654)
XLA Ops:
  0.6 0.0 copy-start.2
  0.6 2.7 %pack.1 = (bf16[128,1024]{1,0:T(8,128)(2,1)}, bf16[192,1024]{1,0:T(8,128)(2,1)}, bf16[64,1024]{1,0:T(8,128)(2,1)}, bf16[320,1024]{1,0:T(8,128)(2,1)}, bf16[320,1024]{1,0:T(8,128)(2,1)}) custom-call(bf16[128,768]{1,0:T(8,128)(2,1)} %refs_0_.1, bf16[128,256]{1,0:T(8,128)(2,1)} %refs_1_.1, bf16[1,1,196,1024]{3,2,1,0:T(8,128)(2,1)} %refs_2_.1, ...), custom_call_target="tpu_custom_call" | custom-call | tf_op jit(solution)/shard_map/pack/pallas_call | solution.py:459
  3.3 0.0 copy-start
  3.4 0.0 copy-start.1
  3.4 3.0 %collective-permute-start.1 = (bf16[320,1024]{1,0:T(8,128)(2,1)}, bf16[320,1024]{1,0:T(8,128)(2,1)S(1)}, u32[]{:S(2)}, u32[]{:S(2)}) collective-permute-start(bf16[320,1024]{1,0:T(8,128)(2,1)} %get-tuple-element.37), channel_id=1, source_target_pairs={{0,2},{1,3},{2,0},{3,1},{4,6},{5,7},{6,4},{7,5},{8,10},{9,11},{10,... | collective-permute-start | bytes 1966088 | tf_op jit(solution)/shard_map/ppermute | solution.py:372
  6.4 1.5 %collective-permute-start.2 = (bf16[320,1024]{1,0:T(8,128)(2,1)}, bf16[320,1024]{1,0:T(8,128)(2,1)S(1)}, u32[]{:S(2)}, u32[]{:S(2)}) collective-permute-start(bf16[320,1024]{1,0:T(8,128)(2,1)} %get-tuple-element.38), channel_id=1, source_target_pairs={{0,4},{1,5},{2,6},{3,7},{4,0},{5,1},{6,2},{7,3},{8,12},{9,13},{10,... | collective-permute-start | bytes 1966088 | tf_op jit(solution)/shard_map/ppermute | solution.py:372
  7.9 1.6 %collective-permute-start = (bf16[128,1024]{1,0:T(8,128)(2,1)}, bf16[128,1024]{1,0:T(8,128)(2,1)S(1)}, u32[]{:S(2)}, u32[]{:S(2)}) collective-permute-start(bf16[128,1024]{1,0:T(8,128)(2,1)} %get-tuple-element.36.refs_1_.rest_0_.rest_3_), channel_id=1, source_target_pairs={{0,8},{8,0},{16,24},{24,16},{1,9},{9,1},{17,25},{25,17},{2,10},{10... | collective-permute-start | bytes 786440 | tf_op jit(solution)/shard_map/ppermute | solution.py:474
  9.5 2.5 %collective-permute-start.6 = (bf16[128,1024]{1,0:T(8,128)(2,1)}, bf16[128,1024]{1,0:T(8,128)(2,1)S(1)}, u32[]{:S(2)}, u32[]{:S(2)}) collective-permute-start(bf16[128,1024]{1,0:T(8,128)(2,1)} %get-tuple-element.36.refs_1_.rest_0_.rest_3_), channel_id=1, source_target_pairs={{0,24},{8,16},{16,8},{24,0},{1,25},{9,17},{17,9},{25,1},{2,26},{10... | collective-permute-start | bytes 786440 | tf_op jit(solution)/shard_map/ppermute | solution.py:474
  11.9 0.1 collective-permute-start.5
  12.1 9.3 %collective-permute-done.1.refs_2_.rest_1_.rest_4_ = bf16[320,1024]{1,0:T(8,128)(2,1)S(1)} collective-permute-done((bf16[320,1024]{1,0:T(8,128)(2,1)}, bf16[320,1024]{1,0:T(8,128)(2,1)S(1)}, u32[]{:S(2)}, u32[]{:S(2)}) %collective-permute-start.1) | collective-permute-done | bytes 655392 | tf_op jit(solution)/shard_map/ppermute | solution.py:372
  21.3 1.8 %collective-permute-start.8 = (bf16[128,1024]{1,0:T(8,128)(2,1)S(1)}, bf16[128,1024]{1,0:T(8,128)(2,1)S(1)}, u32[]{:S(2)}, u32[]{:S(2)}) collective-permute-start(bf16[128,1024]{1,0:T(8,128)(2,1)S(1)} %slice.25), channel_id=1, source_target_pairs={{0,4},{1,5},{2,6},{3,7},{4,0},{5,1},{6,2},{7,3},{8,12},{9,13},{10,... | collective-permute-start | bytes 786440 | tf_op jit(solution)/shard_map/ppermute | solution.py:372
  23.2 0.0 collective-permute-done.2.refs_3_.rest_2_.rest_5_
  23.2 1.6 %collective-permute-start.7 = (bf16[128,1024]{1,0:T(8,128)(2,1)S(1)}, bf16[128,1024]{1,0:T(8,128)(2,1)S(1)}, u32[]{:S(2)}, u32[]{:S(2)}) collective-permute-start(bf16[128,1024]{1,0:T(8,128)(2,1)S(1)} %slice.24), channel_id=1, source_target_pairs={{0,2},{1,3},{2,0},{3,1},{4,6},{5,7},{6,4},{7,5},{8,10},{9,11},{10,... | collective-permute-start | bytes 786440 | tf_op jit(solution)/shard_map/ppermute | solution.py:372
  24.7 0.0 collective-permute-done.rest_10_.rest_13_
  24.7 0.5 collective-permute-start.4
  25.3 0.0 collective-permute-done.6.refs_1_
  25.3 1.1 %collective-permute-start.3 = (bf16[128,1024]{1,0:T(8,128)(2,1)S(1)}, bf16[128,1024]{1,0:T(8,128)(2,1)S(1)}, u32[]{:S(2)}, u32[]{:S(2)}) collective-permute-start(bf16[128,1024]{1,0:T(8,128)(2,1)S(1)} %collective-permute-done.rest_10_.rest_13_), channel_id=1, source_target_pairs={{0,2},{1,3},{2,0},{3,1},{4,6},{5,7},{6,4},{7,5},{8,10},{9,11},{10,... | collective-permute-start | bytes 786440 | tf_op jit(solution)/shard_map/ppermute | solution.py:372
  26.4 8.2 %collective-permute-done.5.refs_0_ = bf16[128,1024]{1,0:T(8,128)(2,1)S(1)} collective-permute-done((bf16[128,1024]{1,0:T(8,128)(2,1)}, bf16[128,1024]{1,0:T(8,128)(2,1)S(1)}, u32[]{:S(2)}, u32[]{:S(2)}) %collective-permute-start.5) | collective-permute-done | bytes 262176 | tf_op jit(solution)/shard_map/ppermute | solution.py:474
  34.6 0.0 collective-permute-start.17
  34.6 0.0 collective-permute-done.8.refs_5_.rest_4_.rest_7_
  34.6 0.0 collective-permute-done.7.refs_4_.rest_3_.rest_6_
  34.7 0.0 collective-permute-done.4.by_y.rest_12_.rest_15_
  34.7 1.1 %collective-permute-done.3.by_x.rest_11_.rest_14_ = bf16[128,1024]{1,0:T(8,128)(2,1)S(1)} collective-permute-done((bf16[128,1024]{1,0:T(8,128)(2,1)S(1)}, bf16[128,1024]{1,0:T(8,128)(2,1)S(1)}, u32[]{:S(2)}, u32[]{:S(2)}) %collective-permute-start.3) | collective-permute-done | bytes 262176 | tf_op jit(solution)/shard_map/ppermute | solution.py:372
  35.8 0.0 collective-permute-start.12
  35.8 0.5 collective-permute-start.13
  36.3 0.0 collective-permute-start.18
  36.3 0.5 collective-permute-start.19
  36.8 0.0 collective-permute-done.17.rest_13_.rest_16_
  36.8 1.1 %collective-permute-start.15 = (bf16[256,1024]{1,0:T(8,128)(2,1)S(1)}, bf16[256,1024]{1,0:T(8,128)(2,1)S(1)}, u32[]{:S(2)}, u32[]{:S(2)}) collective-permute-start(bf16[256,1024]{1,0:T(8,128)(2,1)S(1)} %join.2.rest_16_.rest_19_), channel_id=1, source_target_pairs={{0,4},{1,5},{2,6},{3,7},{4,0},{5,1},{6,2},{7,3},{8,12},{9,13},{10,... | collective-permute-start | bytes 1572872 | tf_op jit(solution)/shard_map/ppermute | solution.py:372
  37.9 0.0 collective-permute-done.12.refs_9_.rest_8_.rest_11_
  37.9 0.9 collective-permute-start.14
  38.8 0.0 collective-permute-done.13.refs_10_.rest_9_.rest_12_
  38.8 0.0 collective-permute-start.10
  38.8 0.0 collective-permute-done.18.rest_14_.rest_17_
  38.8 0.5 collective-permute-start.11
  39.3 0.0 collective-permute-done.19.rest_15_.rest_18_
  39.3 0.1 collective-permute-start.9
  39.4 2.8 %collective-permute-done.9.refs_6_.rest_5_.rest_8_ = bf16[192,1024]{1,0:T(8,128)(2,1)S(1)} collective-permute-done((bf16[192,1024]{1,0:T(8,128)(2,1)}, bf16[192,1024]{1,0:T(8,128)(2,1)S(1)}, u32[]{:S(2)}, u32[]{:S(2)}) %collective-permute-start.9) | collective-permute-done | bytes 393248 | tf_op jit(solution)/shard_map/ppermute | solution.py:372
  42.2 0.1 collective-permute-start.20
  42.4 8.3 %collective-permute-done.15.pair_y.rest_18_.rest_21_ = bf16[256,1024]{1,0:T(8,128)(2,1)S(1)} collective-permute-done((bf16[256,1024]{1,0:T(8,128)(2,1)S(1)}, bf16[256,1024]{1,0:T(8,128)(2,1)S(1)}, u32[]{:S(2)}, u32[]{:S(2)}) %collective-permute-start.15) | collective-permute-done | bytes 524320 | tf_op jit(solution)/shard_map/ppermute | solution.py:372
  50.6 0.0 collective-permute-start.22
  50.6 0.8 collective-permute-done.14.pair_x.rest_17_.rest_20_
  51.4 0.0 collective-permute-start.21
  51.4 0.1 turn.1
  51.5 0.0 collective-permute-done.10.refs_7_.rest_6_.rest_9_
  51.5 1.4 %collective-permute-start.16 = (bf16[192,1024]{1,0:T(8,128)(2,1)S(1)}, bf16[192,1024]{1,0:T(8,128)(2,1)S(1)}, u32[]{:S(2)}, u32[]{:S(2)}) collective-permute-start(bf16[192,1024]{1,0:T(8,128)(2,1)S(1)} %get-tuple-element.58), channel_id=1, source_target_pairs={{0,2},{1,3},{2,0},{3,1},{4,6},{5,7},{6,4},{7,5},{8,10},{9,11},{10,... | collective-permute-start | bytes 1179656 | tf_op jit(solution)/shard_map/ppermute | solution.py:372
  52.9 0.0 collective-permute-done.11.refs_8_.rest_7_.rest_10_
  52.9 1.1 %collective-permute-start.23 = (bf16[192,1024]{1,0:T(8,128)(2,1)S(1)}, bf16[192,1024]{1,0:T(8,128)(2,1)S(1)}, u32[]{:S(2)}, u32[]{:S(2)}) collective-permute-start(bf16[192,1024]{1,0:T(8,128)(2,1)S(1)} %get-tuple-element.67), channel_id=1, source_target_pairs={{0,4},{1,5},{2,6},{3,7},{4,0},{5,1},{6,2},{7,3},{8,12},{9,13},{10,... | collective-permute-start | bytes 1179656 | tf_op jit(solution)/shard_map/ppermute | solution.py:372
  54.7 0.0 copy-done.2
  54.7 0.0 copy-done
  54.7 1.1 %front.1 = (bf16[8,2,32,1024]{3,2,1,0:T(8,128)(2,1)S(1)}, bf16[256,1024]{1,0:T(8,128)(2,1)S(1)}, f32[256,128]{1,0:T(8,128)S(1)}, bf16[256,768]{1,0:T(8,128)(2,1)S(1)}) custom-call(f32[1,1024]{1,0:T(1,128)S(1)} %bitcast.11, bf16[64,1024]{1,0:T(8,128)(2,1)S(1)} %copy-done.1, bf16[128,1024]{1,0:T(8,128)(2,1)S(1)} %copy-done, ...), custom_call_target="tpu_custom_call" | custom-call | flops 256 | bytes 256 | tf_op jit(solution)/shard_map/front/pallas_call | solution.py:289
  55.8 0.0 collective-permute-done.20.rest_19_.rest_23_
  55.8 0.0 collective-permute-done.22.rest_21_.rest_25_
  55.8 0.0 collective-permute-done.21.rest_20_.rest_24_
  55.9 1.7 %middle.1 = (bf16[256,1024]{1,0:T(8,128)(2,1)S(1)}, bf16[256,1024]{1,0:T(8,128)(2,1)S(1)}, f32[256,2304]{1,0:T(8,128)S(1)}) custom-call(s32[1]{0:T(128)S(6)} %copy.9.counts_ref, bf16[8,2,32,1024]{3,2,1,0:T(8,128)(2,1)S(1)} %get-tuple-element.52.both_ref, bf16[256,1024]{1,0:T(8,128)(2,1)S(1)} %get-tuple-element.53.normed_ref, bf16[128,1024]{1,0:T(8,128)(2,1)S(1)} %copy-done, ...), custom_call_target="tpu_custom_call" | custom-call | flops 256 | bytes 256 | tf_op jit(solution)/shard_map/middle/pallas_call | solution.py:311
  57.5 5.6 %collective-permute-done.16.refs_0_ = bf16[192,1024]{1,0:T(8,128)(2,1)S(1)} collective-permute-done((bf16[192,1024]{1,0:T(8,128)(2,1)S(1)}, bf16[192,1024]{1,0:T(8,128)(2,1)S(1)}, u32[]{:S(2)}, u32[]{:S(2)}) %collective-permute-start.16) | collective-permute-done | bytes 393248 | tf_op jit(solution)/shard_map/ppermute | solution.py:372
  63.1 1.1 %collective-permute-done.23.refs_1_ = bf16[192,1024]{1,0:T(8,128)(2,1)S(1)} collective-permute-done((bf16[192,1024]{1,0:T(8,128)(2,1)S(1)}, bf16[192,1024]{1,0:T(8,128)(2,1)S(1)}, u32[]{:S(2)}, u32[]{:S(2)}) %collective-permute-start.23) | collective-permute-done | bytes 393248 | tf_op jit(solution)/shard_map/ppermute | solution.py:372
  64.1 0.1 join.3.rest_22_
  64.2 0.1 collective-permute-start.24
  64.3 2.3 %collective-permute-done.24.rest_26_ = bf16[384,1024]{1,0:T(8,128)(2,1)S(1)} collective-permute-done((bf16[384,1024]{1,0:T(8,128)(2,1)S(1)}, bf16[384,1024]{1,0:T(8,128)(2,1)S(1)}, u32[]{:S(2)}, u32[]{:S(2)}) %collective-permute-start.24) | collective-permute-done | bytes 786464 | tf_op jit(solution)/shard_map/ppermute | solution.py:372
  66.6 8.3 %main.1 = bf16[8,2,32,1024]{3,2,1,0:T(8,128)(2,1)S(1)} custom-call(s32[1]{0:T(128)S(6)} %copy.9.counts_ref, f32[1,1024]{1,0:T(1,128)S(1)} %bitcast.12, bf16[8,2,32,1024]{3,2,1,0:T(8,128)(2,1)S(1)} %get-tuple-element.52.both_ref, bf16[256,1024]{1,0:T(8,128)(2,1)S(1)} %get-tuple-element.53.normed_ref, f32[256,128]{1,0:T(8,128)S(1)} %get-tuple-element.54.stats_ref, ...), custom_call_target="tpu_custom_call" | custom-call | flops 3221225472 | bytes 10485760 | tf_op jit(solution)/shard_map/main/pallas_call | solution.py:334
  74.9 17.8 %all_to_all.5 = bf16[8,1,2,32,1024]{4,3,2,1,0:T(8,128)(2,1)S(1)} all-to-all(bf16[8,1,2,32,1024]{4,3,2,1,0:T(8,128)(2,1)S(1)} %bitcast.10), channel_id=1, replica_groups=mesh['clip'=4,'frame'=8] {'frame'}, dimensions={0} | all-to-all | bytes 2097152 | tf_op jit(solution)/shard_map/all_to_all | solution.py:644
  92.7 0.1 fusion
  92.8 0.9 %slice_bitcast_fusion = (bf16[1,1,196,1024]{3,2,1,0:T(8,128)(2,1)}, bf16[1,1,196,1024]{3,2,1,0:T(8,128)(2,1)}) fusion(bf16[1,256,1024]{2,1,0:T(8,128)(2,1)S(1)} %bitcast.13, bf16[1,256,1024]{2,1,0:T(8,128)(2,1)S(1)} %bitcast.14), kind=kLoop, calls=%fused_computation | loop fusion | bytes 1605632 | tf_op jit(solution)/shard_map/broadcast_in_dim | solution.py:648
  (4 shorter events, 0.1 us)
Async XLA Ops:
  0.6 54.0 %copy-start.2 = (f32[1024]{0:T(1024)S(1)}, f32[1024]{0:T(1024)}, u32[]{:S(2)}) copy-start(f32[1024]{0:T(1024)} %param.8) | copy-start | bytes 12292
  3.3 51.3 %copy-start = (bf16[128,1024]{1,0:T(8,128)(2,1)S(1)}, bf16[128,1024]{1,0:T(8,128)(2,1)}, u32[]{:S(2)}) copy-start(bf16[128,1024]{1,0:T(8,128)(2,1)} %get-tuple-element.36.refs_1_.rest_0_.rest_3_) | copy-start | bytes 786436
  3.4 51.3 %copy-start.1 = (bf16[64,1024]{1,0:T(8,128)(2,1)S(1)}, bf16[64,1024]{1,0:T(8,128)(2,1)}, u32[]{:S(2)}) copy-start(bf16[64,1024]{1,0:T(8,128)(2,1)} %get-tuple-element.35.refs_0_) | copy-start | bytes 393220
  3.4 17.9 %collective-permute-start.1 = (bf16[320,1024]{1,0:T(8,128)(2,1)}, bf16[320,1024]{1,0:T(8,128)(2,1)S(1)}, u32[]{:S(2)}, u32[]{:S(2)}) collective-permute-start(bf16[320,1024]{1,0:T(8,128)(2,1)} %get-tuple-element.37), channel_id=1, source_target_pairs={{0,2},{1,3},{2,0},{3,1},{4,6},{5,7},{6,4},{7,5},{8,10},{9,11},{10,... | collective-permute-start | bytes 1966088 | tf_op jit(solution)/shard_map/ppermute | solution.py:372
  6.4 16.8 %collective-permute-start.2 = (bf16[320,1024]{1,0:T(8,128)(2,1)}, bf16[320,1024]{1,0:T(8,128)(2,1)S(1)}, u32[]{:S(2)}, u32[]{:S(2)}) collective-permute-start(bf16[320,1024]{1,0:T(8,128)(2,1)} %get-tuple-element.38), channel_id=1, source_target_pairs={{0,4},{1,5},{2,6},{3,7},{4,0},{5,1},{6,2},{7,3},{8,12},{9,13},{10,... | collective-permute-start | bytes 1966088 | tf_op jit(solution)/shard_map/ppermute | solution.py:372
  7.9 16.9 %collective-permute-start = (bf16[128,1024]{1,0:T(8,128)(2,1)}, bf16[128,1024]{1,0:T(8,128)(2,1)S(1)}, u32[]{:S(2)}, u32[]{:S(2)}) collective-permute-start(bf16[128,1024]{1,0:T(8,128)(2,1)} %get-tuple-element.36.refs_1_.rest_0_.rest_3_), channel_id=1, source_target_pairs={{0,8},{8,0},{16,24},{24,16},{1,9},{9,1},{17,25},{25,17},{2,10},{10... | collective-permute-start | bytes 786440 | tf_op jit(solution)/shard_map/ppermute | solution.py:474
  9.5 15.8 %collective-permute-start.6 = (bf16[128,1024]{1,0:T(8,128)(2,1)}, bf16[128,1024]{1,0:T(8,128)(2,1)S(1)}, u32[]{:S(2)}, u32[]{:S(2)}) collective-permute-start(bf16[128,1024]{1,0:T(8,128)(2,1)} %get-tuple-element.36.refs_1_.rest_0_.rest_3_), channel_id=1, source_target_pairs={{0,24},{8,16},{16,8},{24,0},{1,25},{9,17},{17,9},{25,1},{2,26},{10... | collective-permute-start | bytes 786440 | tf_op jit(solution)/shard_map/ppermute | solution.py:474
  11.9 22.7 %collective-permute-start.5 = (bf16[128,1024]{1,0:T(8,128)(2,1)}, bf16[128,1024]{1,0:T(8,128)(2,1)S(1)}, u32[]{:S(2)}, u32[]{:S(2)}) collective-permute-start(bf16[128,1024]{1,0:T(8,128)(2,1)} %get-tuple-element.36.refs_1_.rest_0_.rest_3_), channel_id=1, source_target_pairs={{0,16},{8,24},{16,0},{24,8},{1,17},{9,25},{17,1},{25,9},{2,18},{10... | collective-permute-start | bytes 786440 | tf_op jit(solution)/shard_map/ppermute | solution.py:474
  21.3 13.3 %collective-permute-start.8 = (bf16[128,1024]{1,0:T(8,128)(2,1)S(1)}, bf16[128,1024]{1,0:T(8,128)(2,1)S(1)}, u32[]{:S(2)}, u32[]{:S(2)}) collective-permute-start(bf16[128,1024]{1,0:T(8,128)(2,1)S(1)} %slice.25), channel_id=1, source_target_pairs={{0,4},{1,5},{2,6},{3,7},{4,0},{5,1},{6,2},{7,3},{8,12},{9,13},{10,... | collective-permute-start | bytes 786440 | tf_op jit(solution)/shard_map/ppermute | solution.py:372
  23.2 11.4 %collective-permute-start.7 = (bf16[128,1024]{1,0:T(8,128)(2,1)S(1)}, bf16[128,1024]{1,0:T(8,128)(2,1)S(1)}, u32[]{:S(2)}, u32[]{:S(2)}) collective-permute-start(bf16[128,1024]{1,0:T(8,128)(2,1)S(1)} %slice.24), channel_id=1, source_target_pairs={{0,2},{1,3},{2,0},{3,1},{4,6},{5,7},{6,4},{7,5},{8,10},{9,11},{10,... | collective-permute-start | bytes 786440 | tf_op jit(solution)/shard_map/ppermute | solution.py:372
  24.7 9.9 %collective-permute-start.4 = (bf16[128,1024]{1,0:T(8,128)(2,1)S(1)}, bf16[128,1024]{1,0:T(8,128)(2,1)S(1)}, u32[]{:S(2)}, u32[]{:S(2)}) collective-permute-start(bf16[128,1024]{1,0:T(8,128)(2,1)S(1)} %collective-permute-done.rest_10_.rest_13_), channel_id=1, source_target_pairs={{0,4},{1,5},{2,6},{3,7},{4,0},{5,1},{6,2},{7,3},{8,12},{9,13},{10,... | collective-permute-start | bytes 786440 | tf_op jit(solution)/shard_map/ppermute | solution.py:372
  25.3 10.5 %collective-permute-start.3 = (bf16[128,1024]{1,0:T(8,128)(2,1)S(1)}, bf16[128,1024]{1,0:T(8,128)(2,1)S(1)}, u32[]{:S(2)}, u32[]{:S(2)}) collective-permute-start(bf16[128,1024]{1,0:T(8,128)(2,1)S(1)} %collective-permute-done.rest_10_.rest_13_), channel_id=1, source_target_pairs={{0,2},{1,3},{2,0},{3,1},{4,6},{5,7},{6,4},{7,5},{8,10},{9,11},{10,... | collective-permute-start | bytes 786440 | tf_op jit(solution)/shard_map/ppermute | solution.py:372
  34.6 2.2 %collective-permute-start.17 = (bf16[128,1024]{1,0:T(8,128)(2,1)S(1)}, bf16[128,1024]{1,0:T(8,128)(2,1)S(1)}, u32[]{:S(2)}, u32[]{:S(2)}) collective-permute-start(bf16[128,1024]{1,0:T(8,128)(2,1)S(1)} %collective-permute-done.rest_10_.rest_13_), channel_id=1, source_target_pairs={{0,1},{1,0},{2,3},{3,2},{4,5},{5,4},{6,7},{7,6},{8,9},{9,8},{10,11... | collective-permute-start | bytes 786440 | tf_op jit(solution)/shard_map/ppermute | solution.py:372
  35.8 2.1 %collective-permute-start.12 = (bf16[128,1024]{1,0:T(8,128)(2,1)S(1)}, bf16[128,1024]{1,0:T(8,128)(2,1)S(1)}, u32[]{:S(2)}, u32[]{:S(2)}) collective-permute-start(bf16[128,1024]{1,0:T(8,128)(2,1)S(1)} %collective-permute-done.7.refs_4_.rest_3_.rest_6_), channel_id=1, source_target_pairs={{0,1},{1,0},{2,3},{3,2},{4,5},{5,4},{6,7},{7,6},{8,9},{9,8},{10,11... | collective-permute-start | bytes 786440 | tf_op jit(solution)/shard_map/ppermute | solution.py:372
  35.8 3.0 %collective-permute-start.13 = (bf16[128,1024]{1,0:T(8,128)(2,1)S(1)}, bf16[128,1024]{1,0:T(8,128)(2,1)S(1)}, u32[]{:S(2)}, u32[]{:S(2)}) collective-permute-start(bf16[128,1024]{1,0:T(8,128)(2,1)S(1)} %collective-permute-done.8.refs_5_.rest_4_.rest_7_), channel_id=1, source_target_pairs={{0,1},{1,0},{2,3},{3,2},{4,5},{5,4},{6,7},{7,6},{8,9},{9,8},{10,11... | collective-permute-start | bytes 786440 | tf_op jit(solution)/shard_map/ppermute | solution.py:372
  36.3 2.5 %collective-permute-start.18 = (bf16[128,1024]{1,0:T(8,128)(2,1)S(1)}, bf16[128,1024]{1,0:T(8,128)(2,1)S(1)}, u32[]{:S(2)}, u32[]{:S(2)}) collective-permute-start(bf16[128,1024]{1,0:T(8,128)(2,1)S(1)} %collective-permute-done.3.by_x.rest_11_.rest_14_), channel_id=1, source_target_pairs={{0,1},{1,0},{2,3},{3,2},{4,5},{5,4},{6,7},{7,6},{8,9},{9,8},{10,11... | collective-permute-start | bytes 786440 | tf_op jit(solution)/shard_map/ppermute | solution.py:372
  36.3 3.0 %collective-permute-start.19 = (bf16[128,1024]{1,0:T(8,128)(2,1)S(1)}, bf16[128,1024]{1,0:T(8,128)(2,1)S(1)}, u32[]{:S(2)}, u32[]{:S(2)}) collective-permute-start(bf16[128,1024]{1,0:T(8,128)(2,1)S(1)} %collective-permute-done.4.by_y.rest_12_.rest_15_), channel_id=1, source_target_pairs={{0,1},{1,0},{2,3},{3,2},{4,5},{5,4},{6,7},{7,6},{8,9},{9,8},{10,11... | collective-permute-start | bytes 786440 | tf_op jit(solution)/shard_map/ppermute | solution.py:372
  36.8 13.8 %collective-permute-start.15 = (bf16[256,1024]{1,0:T(8,128)(2,1)S(1)}, bf16[256,1024]{1,0:T(8,128)(2,1)S(1)}, u32[]{:S(2)}, u32[]{:S(2)}) collective-permute-start(bf16[256,1024]{1,0:T(8,128)(2,1)S(1)} %join.2.rest_16_.rest_19_), channel_id=1, source_target_pairs={{0,4},{1,5},{2,6},{3,7},{4,0},{5,1},{6,2},{7,3},{8,12},{9,13},{10,... | collective-permute-start | bytes 1572872 | tf_op jit(solution)/shard_map/ppermute | solution.py:372
  37.9 13.6 %collective-permute-start.14 = (bf16[256,1024]{1,0:T(8,128)(2,1)S(1)}, bf16[256,1024]{1,0:T(8,128)(2,1)S(1)}, u32[]{:S(2)}, u32[]{:S(2)}) collective-permute-start(bf16[256,1024]{1,0:T(8,128)(2,1)S(1)} %join.2.rest_16_.rest_19_), channel_id=1, source_target_pairs={{0,2},{1,3},{2,0},{3,1},{4,6},{5,7},{6,4},{7,5},{8,10},{9,11},{10,... | collective-permute-start | bytes 1572872 | tf_op jit(solution)/shard_map/ppermute | solution.py:372
  38.8 12.7 %collective-permute-start.10 = (bf16[320,1024]{1,0:T(8,128)(2,1)S(1)}, bf16[320,1024]{1,0:T(8,128)(2,1)S(1)}, u32[]{:S(2)}, u32[]{:S(2)}) collective-permute-start(bf16[320,1024]{1,0:T(8,128)(2,1)S(1)} %collective-permute-done.1.refs_2_.rest_1_.rest_4_), channel_id=1, source_target_pairs={{0,1},{1,0},{2,3},{3,2},{4,5},{5,4},{6,7},{7,6},{8,9},{9,8},{10,11... | collective-permute-start | bytes 1966088 | tf_op jit(solution)/shard_map/ppermute | solution.py:372
  38.8 14.1 %collective-permute-start.11 = (bf16[320,1024]{1,0:T(8,128)(2,1)S(1)}, bf16[320,1024]{1,0:T(8,128)(2,1)S(1)}, u32[]{:S(2)}, u32[]{:S(2)}) collective-permute-start(bf16[320,1024]{1,0:T(8,128)(2,1)S(1)} %collective-permute-done.2.refs_3_.rest_2_.rest_5_), channel_id=1, source_target_pairs={{0,1},{1,0},{2,3},{3,2},{4,5},{5,4},{6,7},{7,6},{8,9},{9,8},{10,11... | collective-permute-start | bytes 1966088 | tf_op jit(solution)/shard_map/ppermute | solution.py:372
  39.3 2.9 %collective-permute-start.9 = (bf16[192,1024]{1,0:T(8,128)(2,1)}, bf16[192,1024]{1,0:T(8,128)(2,1)S(1)}, u32[]{:S(2)}, u32[]{:S(2)}) collective-permute-start(bf16[192,1024]{1,0:T(8,128)(2,1)} %get-tuple-element.51), channel_id=1, source_target_pairs={{0,1},{1,0},{2,3},{3,2},{4,5},{5,4},{6,7},{7,6},{8,9},{9,8},{10,11... | collective-permute-start | bytes 1179656 | tf_op jit(solution)/shard_map/ppermute | solution.py:372
  42.2 13.6 %collective-permute-start.20 = (bf16[256,1024]{1,0:T(8,128)(2,1)S(1)}, bf16[256,1024]{1,0:T(8,128)(2,1)S(1)}, u32[]{:S(2)}, u32[]{:S(2)}) collective-permute-start(bf16[256,1024]{1,0:T(8,128)(2,1)S(1)} %join.2.rest_16_.rest_19_), channel_id=1, source_target_pairs={{0,1},{1,0},{2,3},{3,2},{4,5},{5,4},{6,7},{7,6},{8,9},{9,8},{10,11... | collective-permute-start | bytes 1572872 | tf_op jit(solution)/shard_map/ppermute | solution.py:372
  50.6 5.2 %collective-permute-start.22 = (bf16[256,1024]{1,0:T(8,128)(2,1)S(1)}, bf16[256,1024]{1,0:T(8,128)(2,1)S(1)}, u32[]{:S(2)}, u32[]{:S(2)}) collective-permute-start(bf16[256,1024]{1,0:T(8,128)(2,1)S(1)} %collective-permute-done.15.pair_y.rest_18_.rest_21_), channel_id=1, source_target_pairs={{0,1},{1,0},{2,3},{3,2},{4,5},{5,4},{6,7},{7,6},{8,9},{9,8},{10,11... | collective-permute-start | bytes 1572872 | tf_op jit(solution)/shard_map/ppermute | solution.py:372
  51.4 4.4 %collective-permute-start.21 = (bf16[256,1024]{1,0:T(8,128)(2,1)S(1)}, bf16[256,1024]{1,0:T(8,128)(2,1)S(1)}, u32[]{:S(2)}, u32[]{:S(2)}) collective-permute-start(bf16[256,1024]{1,0:T(8,128)(2,1)S(1)} %collective-permute-done.14.pair_x.rest_17_.rest_20_), channel_id=1, source_target_pairs={{0,1},{1,0},{2,3},{3,2},{4,5},{5,4},{6,7},{7,6},{8,9},{9,8},{10,11... | collective-permute-start | bytes 1572872 | tf_op jit(solution)/shard_map/ppermute | solution.py:372
  51.5 11.6 %collective-permute-start.16 = (bf16[192,1024]{1,0:T(8,128)(2,1)S(1)}, bf16[192,1024]{1,0:T(8,128)(2,1)S(1)}, u32[]{:S(2)}, u32[]{:S(2)}) collective-permute-start(bf16[192,1024]{1,0:T(8,128)(2,1)S(1)} %get-tuple-element.58), channel_id=1, source_target_pairs={{0,2},{1,3},{2,0},{3,1},{4,6},{5,7},{6,4},{7,5},{8,10},{9,11},{10,... | collective-permute-start | bytes 1179656 | tf_op jit(solution)/shard_map/ppermute | solution.py:372
  52.9 11.2 %collective-permute-start.23 = (bf16[192,1024]{1,0:T(8,128)(2,1)S(1)}, bf16[192,1024]{1,0:T(8,128)(2,1)S(1)}, u32[]{:S(2)}, u32[]{:S(2)}) collective-permute-start(bf16[192,1024]{1,0:T(8,128)(2,1)S(1)} %get-tuple-element.67), channel_id=1, source_target_pairs={{0,4},{1,5},{2,6},{3,7},{4,0},{5,1},{6,2},{7,3},{8,12},{9,13},{10,... | collective-permute-start | bytes 1179656 | tf_op jit(solution)/shard_map/ppermute | solution.py:372
  64.2 2.4 %collective-permute-start.24 = (bf16[384,1024]{1,0:T(8,128)(2,1)S(1)}, bf16[384,1024]{1,0:T(8,128)(2,1)S(1)}, u32[]{:S(2)}, u32[]{:S(2)}) collective-permute-start(bf16[384,1024]{1,0:T(8,128)(2,1)S(1)} %join.3.rest_22_), channel_id=1, source_target_pairs={{0,1},{1,0},{2,3},{3,2},{4,5},{5,4},{6,7},{7,6},{8,9},{9,8},{10,11... | collective-permute-start | bytes 2359304 | tf_op jit(solution)/shard_map/ppermute | solution.py:372

commit v12 on v11

--- a/solution.py
+++ b/solution.py
@@ -437,6 +437,21 @@
         put(target, depth + 2 * block, (chip ^ 3) * 2 + core_by)
 
 
+def trim_kernel(half, block, x_ref, y_ref, dx_ref, dy_ref, x_out, y_out, d_out):
+    other = 1 - lax.axis_index("frame") % 2
+    tail = half + 2 * block
+    for source, target in ((x_ref, x_out), (y_ref, y_out)):
+        rows = pl.ds(pl.multiple_of(half + other * block, SUB), block)
+        target[:half, :] = source[:half, :]
+        target[half : half + block, :] = source[rows, :]
+        target[half + block :, :] = source[tail : tail + half, :]
+    d_out[:half, :] = dx_ref[:half, :]
+    d_out[half : 2 * half, :] = dy_ref[:half, :]
+    d_out[2 * half :, :] = jnp.where(
+        other == 0, dy_ref[half : half + block, :], dx_ref[half : half + block, :]
+    )
+
+
 def turn_kernel(half, by_x, by_y, pair_x, pair_y, to_dx, to_dy):
     to_dx[:half, :] = by_y[:half, :]
     to_dx[half:, :] = pair_y[: 2 * half, :]
@@ -487,27 +502,36 @@
     second = [one, *across(one)]
     two, three, first[2], first[3] = lax.optimization_barrier((two, three, first[2], first[3]))
     third = [join(0, two, three)]
-    third += across(third[0])
-    second[1], second[2], own, third[0], *first = lax.optimization_barrier(
-        (second[1], second[2], own, third[0], *first)
-    )
-    first_other = other_core([own, *first])
+    second[1], second[2], own, *first = lax.optimization_barrier(
+        (second[1], second[2], own, *first)
+    )
+    first_other = other_core(
+        [
+            own,
+            *pl.pallas_call(
+                functools.partial(trim_kernel, half, block),
+                out_shape=(rows_of(depth + block),) * 3,
+                in_specs=[vmem] * 4,
+                out_specs=(vmem,) * 3,
+                compiler_params=SMALL,
+                name="trim",
+            )(*first),
+        ]
+    )
     second_other = other_core(second)
     ready = [joined, *first, *first_other, *second, *second_other]
+    third += across(third[0])
 
     def tokens_in(sources, both_ref):
         core = lax.axis_index("frame") % 2
-        mine_ref, _, x_ref, y_ref, dx_ref, dy_ref, own2, x2, y2, dx2, dy2 = sources[:11]
-        rows = pl.ds(pl.multiple_of(half + core * block, block), block)
+        mine_ref, _, x_ref, y_ref, dx_ref, dy_ref, own2, x2, y2, d2 = sources[:10]
+        rows = pl.ds(pl.multiple_of(half + core * block, SUB), block)
         behind = slice(half, half + block)
-
-        def diagonal(by_x, by_y):
-            return jnp.where(core == 0, by_y[behind, :], by_x[behind, :])
-
         found = (
             mine_ref[...], own2[depth : depth + block, :],
-            x_ref[rows, :], x2[rows, :], y_ref[rows, :], y2[rows, :],
-            diagonal(dx_ref, dy_ref), diagonal(dx2, dy2),
+            x_ref[rows, :], x2[behind, :], y_ref[rows, :], y2[behind, :],
+            jnp.where(core == 0, dy_ref[behind, :], dx_ref[behind, :]),
+            d2[depth : depth + block, :],
         )
         for distance, value in enumerate(found):
             both_ref[distance] = value.reshape(2, share, width)
@@ -518,6 +542,12 @@
         [(0, 4, 0, half, half), (0, 4, tail, half, 0)],
         [(0, 6, 0, half, 0)],
         [(0, 6, 0, half, half)],
+    ]
+    trimmed = [
+        [(0, 0, 0, depth, 0)],
+        [(0, 2, 0, half, 0), (0, 2, half + block, half, half)],
+        [(0, 4, 0, half, half), (0, 4, half + block, half, 0)],
+        [(0, 6, 0, depth, 0)],
     ]
     others = [[(1, d, 0, depth, 0)] for d in (0, 2, 4)]
     pairs = [[(2, d, 0, depth, 0), (3, d, depth, depth, 0)] for d in (0, 2, 4)]
@@ -528,8 +558,8 @@
             (1, 6, long, half, half), (3, 6, long + half, depth, 0),
         ],
     ]
-    arrays = []
-    for group in (table, others, pairs):
+    arrays = [(core, parts) for core, group in enumerate((table, trimmed)) for parts in group]
+    for group in (others, pairs):
         arrays += [(core, parts) for core in (0, 1) for parts in group]
 
     def piece(present):
@@ -562,7 +592,7 @@
         )
 
     fronted = run_front(
-        gain, (devices, 2, share, width), [mine, *ready[:10]], view([None, *range(10)])
+        gain, (devices, 2, share, width), [mine, *ready[:9]], view([None, *range(9)])
     )
     to_dx, to_dy = pl.pallas_call(
         functools.partial(turn_kernel, half),
@@ -573,14 +603,17 @@
         name="turn",
     )(second[1], second[2], third[1], third[2])
     last = [swap(to_dx, 2, devices), swap(to_dy, 4, devices)]
+    last[0], *fronted = lax.optimization_barrier((last[0], *fronted))
     third_other = other_core(third)
+    last[0], third_other[1], third_other[2] = lax.optimization_barrier(
+        (last[0], third_other[1], third_other[2])
+    )
     middle = run_middle(
-        counts, fronted, [*ready, *third, *third_other], view([*range(16), 16, 17, 18, 20, 21, 22])
-    )
-    last[0], *middle = lax.optimization_barrier((last[0], *middle))
+        counts, fronted, [*ready, *third, *third_other], view([*range(15), 15, 16, 17, 19, 20, 21])
+    )
     last = join(0, *last)
     weights = [*middle, *ready, *third, last, *third_other, swap(last, 1, devices)]
-    return fronted, weights, view(list(range(24)))
+    return fronted, weights, view(list(range(23)))
 
 
 def gather_plainly(

time: 93.9 us -> 93.4 us (level)
    ppermute x22 -> x21, starting transfers between devices: 15.9 us -> 15.1 us  [swap(): lax.ppermute(array, 'frame', [(f, f ^ distance) for f in range(devices)])]
    ppermute x22 -> x21, waiting for transfers between devices: 31.2 us -> 31.3 us  [swap(): lax.ppermute(array, 'frame', [(f, f ^ distance) for f in range(devices)])]
  transfers between devices with their start and end apart: 25 -> 24, of which waited for: 9 -> 10; matrix products, arithmetic and copies ran while one was open for 0% -> 0% of each run, Pallas kernels for 3% -> 3%
where the time goes in v12:
time: 93.4 us; the launch traced here: 93.3 us
  waiting for transfers between devices  39.4 us (42%)
  starting transfers between devices  19.3 us (21%)
  blocking collectives  18 us (19%)
  Pallas kernels  14 us (15%)
  between operations  1.42 us (2%)
  local copies, waits for them, and re-layouts  1.08 us (1%)
    ppermute x21, waiting for transfers between devices, swap(): lax.ppermute(array, 'frame', [(f, f ^ distance) for f in range(devices)])  31.3 us
    all_to_all x1, blocking collectives, per_device(): lax.all_to_all(back, 'frame', split_axis=0, concat_axis=0, tiled=True)  18 us
    ppermute x21, starting transfers between devices, swap(): lax.ppermute(array, 'frame', [(f, f ^ distance) for f in range(devices)])  15.1 us
    pallas_call x1, Pallas kernels, run_main(): pl.pallas_call(functools.partial(main_kernel, view), out_shape=jax.ShapeD...  8.34 us
    ppermute x3, waiting for transfers between devices, by_clip(): return lax.ppermute(array, 'clip', [(c, c ^ offset) for c in range(4)])  8.17 us
    ppermute x3, starting transfers between devices, by_clip(): return lax.ppermute(array, 'clip', [(c, c ^ offset) for c in range(4)])  4.17 us
    pallas_call x1, Pallas kernels, gather_in_rounds(): pl.pallas_call(functools.partial(pack_kernel, patches, share), out_shape=...  2.69 us
  transfers between devices with their start and end apart: 24, of which 10 were waited for; matrix products, arithmetic and copies ran while one was open for 0% of the time, Pallas kernels for 3%

profile of v12, /device:TPU:0, one launch (start us, length us, event | category | flops | bytes accessed | tf_op | source)
XLA Modules:
  0.0 93.3 jit_solution(2807593349771858401)
XLA Ops:
  0.6 2.7 %pack.1 = (bf16[128,1024]{1,0:T(8,128)(2,1)}, bf16[192,1024]{1,0:T(8,128)(2,1)}, bf16[64,1024]{1,0:T(8,128)(2,1)}, bf16[320,1024]{1,0:T(8,128)(2,1)}, bf16[320,1024]{1,0:T(8,128)(2,1)}) custom-call(bf16[128,768]{1,0:T(8,128)(2,1)} %refs_0_.1, bf16[128,256]{1,0:T(8,128)(2,1)} %refs_1_.1, bf16[1,1,196,1024]{3,2,1,0:T(8,128)(2,1)} %refs_2_.1, ...), custom_call_target="tpu_custom_call" | custom-call | tf_op jit(solution)/shard_map/pack/pallas_call | solution.py:474
  3.3 3.0 %collective-permute-start.1 = (bf16[320,1024]{1,0:T(8,128)(2,1)}, bf16[320,1024]{1,0:T(8,128)(2,1)S(1)}, u32[]{:S(2)}, u32[]{:S(2)}) collective-permute-start(bf16[320,1024]{1,0:T(8,128)(2,1)} %get-tuple-element.42), channel_id=1, source_target_pairs={{0,2},{1,3},{2,0},{3,1},{4,6},{5,7},{6,4},{7,5},{8,10},{9,11},{10,... | collective-permute-start | bytes 1966088 | tf_op jit(solution)/shard_map/ppermute | solution.py:372
  6.3 1.5 %collective-permute-start.2 = (bf16[320,1024]{1,0:T(8,128)(2,1)}, bf16[320,1024]{1,0:T(8,128)(2,1)S(1)}, u32[]{:S(2)}, u32[]{:S(2)}) collective-permute-start(bf16[320,1024]{1,0:T(8,128)(2,1)} %get-tuple-element.43), channel_id=1, source_target_pairs={{0,4},{1,5},{2,6},{3,7},{4,0},{5,1},{6,2},{7,3},{8,12},{9,13},{10,... | collective-permute-start | bytes 1966088 | tf_op jit(solution)/shard_map/ppermute | solution.py:372
  7.8 1.6 %collective-permute-start = (bf16[128,1024]{1,0:T(8,128)(2,1)}, bf16[128,1024]{1,0:T(8,128)(2,1)S(1)}, u32[]{:S(2)}, u32[]{:S(2)}) collective-permute-start(bf16[128,1024]{1,0:T(8,128)(2,1)} %get-tuple-element.41.refs_1_.rest_0_.rest_3_), channel_id=1, source_target_pairs={{0,8},{8,0},{16,24},{24,16},{1,9},{9,1},{17,25},{25,17},{2,10},{10... | collective-permute-start | bytes 786440 | tf_op jit(solution)/shard_map/ppermute | solution.py:489
  9.4 2.5 %collective-permute-start.6 = (bf16[128,1024]{1,0:T(8,128)(2,1)}, bf16[128,1024]{1,0:T(8,128)(2,1)S(1)}, u32[]{:S(2)}, u32[]{:S(2)}) collective-permute-start(bf16[128,1024]{1,0:T(8,128)(2,1)} %get-tuple-element.41.refs_1_.rest_0_.rest_3_), channel_id=1, source_target_pairs={{0,24},{8,16},{16,8},{24,0},{1,25},{9,17},{17,9},{25,1},{2,26},{10... | collective-permute-start | bytes 786440 | tf_op jit(solution)/shard_map/ppermute | solution.py:489
  11.9 0.1 collective-permute-start.5
  12.0 9.3 %collective-permute-done.1.x_ref.refs_2_.rest_1_.rest_4_ = bf16[320,1024]{1,0:T(8,128)(2,1)S(1)} collective-permute-done((bf16[320,1024]{1,0:T(8,128)(2,1)}, bf16[320,1024]{1,0:T(8,128)(2,1)S(1)}, u32[]{:S(2)}, u32[]{:S(2)}) %collective-permute-start.1) | collective-permute-done | bytes 655392 | tf_op jit(solution)/shard_map/ppermute | solution.py:372
  21.3 1.8 %collective-permute-start.8 = (bf16[128,1024]{1,0:T(8,128)(2,1)S(1)}, bf16[128,1024]{1,0:T(8,128)(2,1)S(1)}, u32[]{:S(2)}, u32[]{:S(2)}) collective-permute-start(bf16[128,1024]{1,0:T(8,128)(2,1)S(1)} %slice.25), channel_id=1, source_target_pairs={{0,4},{1,5},{2,6},{3,7},{4,0},{5,1},{6,2},{7,3},{8,12},{9,13},{10,... | collective-permute-start | bytes 786440 | tf_op jit(solution)/shard_map/ppermute | solution.py:372
  23.1 0.0 collective-permute-done.2.y_ref.refs_3_.rest_2_.rest_5_
  23.2 0.0 copy-start
  23.2 0.0 copy-start.1
  23.2 0.0 copy-start.2
  23.2 1.6 %collective-permute-start.7 = (bf16[128,1024]{1,0:T(8,128)(2,1)S(1)}, bf16[128,1024]{1,0:T(8,128)(2,1)S(1)}, u32[]{:S(2)}, u32[]{:S(2)}) collective-permute-start(bf16[128,1024]{1,0:T(8,128)(2,1)S(1)} %slice.24), channel_id=1, source_target_pairs={{0,2},{1,3},{2,0},{3,1},{4,6},{5,7},{6,4},{7,5},{8,10},{9,11},{10,... | collective-permute-start | bytes 786440 | tf_op jit(solution)/shard_map/ppermute | solution.py:372
  24.7 0.0 collective-permute-done.rest_9_.rest_12_
  24.7 0.5 collective-permute-start.4
  25.3 0.0 collective-permute-done.6.refs_1_
  25.3 1.1 %collective-permute-start.3 = (bf16[128,1024]{1,0:T(8,128)(2,1)S(1)}, bf16[128,1024]{1,0:T(8,128)(2,1)S(1)}, u32[]{:S(2)}, u32[]{:S(2)}) collective-permute-start(bf16[128,1024]{1,0:T(8,128)(2,1)S(1)} %collective-permute-done.rest_9_.rest_12_), channel_id=1, source_target_pairs={{0,2},{1,3},{2,0},{3,1},{4,6},{5,7},{6,4},{7,5},{8,10},{9,11},{10,... | collective-permute-start | bytes 786440 | tf_op jit(solution)/shard_map/ppermute | solution.py:372
  26.4 8.2 %collective-permute-done.5.refs_0_ = bf16[128,1024]{1,0:T(8,128)(2,1)S(1)} collective-permute-done((bf16[128,1024]{1,0:T(8,128)(2,1)}, bf16[128,1024]{1,0:T(8,128)(2,1)S(1)}, u32[]{:S(2)}, u32[]{:S(2)}) %collective-permute-start.5) | collective-permute-done | bytes 262176 | tf_op jit(solution)/shard_map/ppermute | solution.py:489
  34.6 0.0 collective-permute-done.8.dy_ref.refs_5_.rest_4_.rest_7_
  34.6 0.0 collective-permute-done.7.dx_ref.refs_4_.rest_3_.rest_6_
  34.6 0.6 collective-permute-start.10
  35.2 0.5 collective-permute-start.9
  35.7 0.0 collective-permute-done.4.by_y.rest_11_.rest_14_
  35.7 0.0 collective-permute-done.3.by_x.rest_10_.rest_13_
  35.8 0.0 collective-permute-start.12
  35.8 0.1 trim.1
  35.9 0.6 collective-permute-start.13
  36.4 0.1 collective-permute-start.14
  36.5 10.4 %collective-permute-done.10.pair_y.rest_17_.rest_20_ = bf16[256,1024]{1,0:T(8,128)(2,1)S(1)} collective-permute-done((bf16[256,1024]{1,0:T(8,128)(2,1)S(1)}, bf16[256,1024]{1,0:T(8,128)(2,1)S(1)}, u32[]{:S(2)}, u32[]{:S(2)}) %collective-permute-start.10) | collective-permute-done | bytes 524320 | tf_op jit(solution)/shard_map/ppermute | solution.py:372
  46.9 0.0 collective-permute-start.21
  46.9 0.2 collective-permute-done.9.pair_x.rest_16_.rest_19_
  47.1 0.3 collective-permute-start.20
  47.4 0.0 collective-permute-done.12.refs_6_.rest_5_.rest_8_
  47.4 0.2 collective-permute-start.15
  47.6 0.1 turn.1
  47.7 0.0 collective-permute-done.13.refs_7_.rest_6_.rest_9_
  47.7 1.5 %collective-permute-start.11 = (bf16[192,1024]{1,0:T(8,128)(2,1)S(1)}, bf16[192,1024]{1,0:T(8,128)(2,1)S(1)}, u32[]{:S(2)}, u32[]{:S(2)}) collective-permute-start(bf16[192,1024]{1,0:T(8,128)(2,1)S(1)} %get-tuple-element.54), channel_id=1, source_target_pairs={{0,2},{1,3},{2,0},{3,1},{4,6},{5,7},{6,4},{7,5},{8,10},{9,11},{10,... | collective-permute-start | bytes 1179656 | tf_op jit(solution)/shard_map/ppermute | solution.py:372
  49.1 0.0 collective-permute-done.14.refs_8_.rest_7_.rest_10_
  49.1 0.7 collective-permute-start.22
  49.8 0.3 collective-permute-done.15.refs_9_.rest_8_.rest_11_
  50.1 0.0 copy-done
  50.1 0.0 copy-done.1
  50.1 0.0 copy-done.2
  50.1 1.1 %front.1 = (bf16[8,2,32,1024]{3,2,1,0:T(8,128)(2,1)S(1)}, bf16[256,1024]{1,0:T(8,128)(2,1)S(1)}, f32[256,128]{1,0:T(8,128)S(1)}, bf16[256,768]{1,0:T(8,128)(2,1)S(1)}) custom-call(f32[1,1024]{1,0:T(1,128)S(1)} %bitcast.11, bf16[64,1024]{1,0:T(8,128)(2,1)S(1)} %copy-done.1, bf16[128,1024]{1,0:T(8,128)(2,1)S(1)} %copy-done, ...), custom_call_target="tpu_custom_call" | custom-call | flops 256 | bytes 256 | tf_op jit(solution)/shard_map/front/pallas_call | solution.py:289
  51.2 7.8 %collective-permute-done.11.refs_0_ = bf16[192,1024]{1,0:T(8,128)(2,1)S(1)} collective-permute-done((bf16[192,1024]{1,0:T(8,128)(2,1)S(1)}, bf16[192,1024]{1,0:T(8,128)(2,1)S(1)}, u32[]{:S(2)}, u32[]{:S(2)}) %collective-permute-start.11) | collective-permute-done | bytes 393248 | tf_op jit(solution)/shard_map/ppermute | solution.py:372
  59.0 0.0 collective-permute-done.21.rest_20_.rest_24_
  59.0 0.0 collective-permute-done.20.rest_19_.rest_23_
  59.1 0.8 collective-permute-done.22.refs_1_
  59.9 0.1 join.3.rest_21_
  59.9 0.1 collective-permute-start.23
  60.0 0.5 collective-permute-start.19
  60.5 0.1 collective-permute-start.16
  60.6 0.4 collective-permute-start.17
  61.0 0.1 collective-permute-start.18
  61.8 1.7 %collective-permute-done.16.rest_12_.rest_15_ = bf16[128,1024]{1,0:T(8,128)(2,1)S(1)} collective-permute-done((bf16[128,1024]{1,0:T(8,128)(2,1)S(1)}, bf16[128,1024]{1,0:T(8,128)(2,1)S(1)}, u32[]{:S(2)}, u32[]{:S(2)}) %collective-permute-start.16) | collective-permute-done | bytes 262176 | tf_op jit(solution)/shard_map/ppermute | solution.py:372
  63.4 0.4 collective-permute-done.17.rest_13_.rest_16_
  63.8 0.4 collective-permute-done.18.rest_14_.rest_17_
  64.2 0.0 collective-permute-done.19.rest_18_.rest_22_
  64.2 1.7 %middle.1 = (bf16[256,1024]{1,0:T(8,128)(2,1)S(1)}, bf16[256,1024]{1,0:T(8,128)(2,1)S(1)}, f32[256,2304]{1,0:T(8,128)S(1)}) custom-call(s32[1]{0:T(128)S(6)} %copy.9.counts_ref, bf16[8,2,32,1024]{3,2,1,0:T(8,128)(2,1)S(1)} %get-tuple-element.68.both_ref, bf16[256,1024]{1,0:T(8,128)(2,1)S(1)} %get-tuple-element.69.normed_ref, bf16[128,1024]{1,0:T(8,128)(2,1)S(1)} %copy-done, ...), custom_call_target="tpu_custom_call" | custom-call | flops 256 | bytes 256 | tf_op jit(solution)/shard_map/middle/pallas_call | solution.py:311
  65.9 0.0 collective-permute-done.23.rest_25_
  65.9 8.3 %main.1 = bf16[8,2,32,1024]{3,2,1,0:T(8,128)(2,1)S(1)} custom-call(s32[1]{0:T(128)S(6)} %copy.9.counts_ref, f32[1,1024]{1,0:T(1,128)S(1)} %bitcast.12, bf16[8,2,32,1024]{3,2,1,0:T(8,128)(2,1)S(1)} %get-tuple-element.68.both_ref, bf16[256,1024]{1,0:T(8,128)(2,1)S(1)} %get-tuple-element.69.normed_ref, f32[256,128]{1,0:T(8,128)S(1)} %get-tuple-element.70.stats_ref, ...), custom_call_target="tpu_custom_call" | custom-call | flops 3221225472 | bytes 10485760 | tf_op jit(solution)/shard_map/main/pallas_call | solution.py:334
  74.2 18.0 %all_to_all.5 = bf16[8,1,2,32,1024]{4,3,2,1,0:T(8,128)(2,1)S(1)} all-to-all(bf16[8,1,2,32,1024]{4,3,2,1,0:T(8,128)(2,1)S(1)} %bitcast.10), channel_id=1, replica_groups=mesh['clip'=4,'frame'=8] {'frame'}, dimensions={0} | all-to-all | bytes 2097152 | tf_op jit(solution)/shard_map/all_to_all | solution.py:677
  92.2 0.1 fusion
  92.3 0.9 %slice_bitcast_fusion = (bf16[1,1,196,1024]{3,2,1,0:T(8,128)(2,1)}, bf16[1,1,196,1024]{3,2,1,0:T(8,128)(2,1)}) fusion(bf16[1,256,1024]{2,1,0:T(8,128)(2,1)S(1)} %bitcast.13, bf16[1,256,1024]{2,1,0:T(8,128)(2,1)S(1)} %bitcast.14), kind=kLoop, calls=%fused_computation | loop fusion | bytes 1605632 | tf_op jit(solution)/shard_map/broadcast_in_dim | solution.py:681
  (3 shorter events, 0.1 us)
Async XLA Ops:
  3.3 17.9 %collective-permute-start.1 = (bf16[320,1024]{1,0:T(8,128)(2,1)}, bf16[320,1024]{1,0:T(8,128)(2,1)S(1)}, u32[]{:S(2)}, u32[]{:S(2)}) collective-permute-start(bf16[320,1024]{1,0:T(8,128)(2,1)} %get-tuple-element.42), channel_id=1, source_target_pairs={{0,2},{1,3},{2,0},{3,1},{4,6},{5,7},{6,4},{7,5},{8,10},{9,11},{10,... | collective-permute-start | bytes 1966088 | tf_op jit(solution)/shard_map/ppermute | solution.py:372
  6.3 16.8 %collective-permute-start.2 = (bf16[320,1024]{1,0:T(8,128)(2,1)}, bf16[320,1024]{1,0:T(8,128)(2,1)S(1)}, u32[]{:S(2)}, u32[]{:S(2)}) collective-permute-start(bf16[320,1024]{1,0:T(8,128)(2,1)} %get-tuple-element.43), channel_id=1, source_target_pairs={{0,4},{1,5},{2,6},{3,7},{4,0},{5,1},{6,2},{7,3},{8,12},{9,13},{10,... | collective-permute-start | bytes 1966088 | tf_op jit(solution)/shard_map/ppermute | solution.py:372
  7.8 16.9 %collective-permute-start = (bf16[128,1024]{1,0:T(8,128)(2,1)}, bf16[128,1024]{1,0:T(8,128)(2,1)S(1)}, u32[]{:S(2)}, u32[]{:S(2)}) collective-permute-start(bf16[128,1024]{1,0:T(8,128)(2,1)} %get-tuple-element.41.refs_1_.rest_0_.rest_3_), channel_id=1, source_target_pairs={{0,8},{8,0},{16,24},{24,16},{1,9},{9,1},{17,25},{25,17},{2,10},{10... | collective-permute-start | bytes 786440 | tf_op jit(solution)/shard_map/ppermute | solution.py:489
  9.4 15.8 %collective-permute-start.6 = (bf16[128,1024]{1,0:T(8,128)(2,1)}, bf16[128,1024]{1,0:T(8,128)(2,1)S(1)}, u32[]{:S(2)}, u32[]{:S(2)}) collective-permute-start(bf16[128,1024]{1,0:T(8,128)(2,1)} %get-tuple-element.41.refs_1_.rest_0_.rest_3_), channel_id=1, source_target_pairs={{0,24},{8,16},{16,8},{24,0},{1,25},{9,17},{17,9},{25,1},{2,26},{10... | collective-permute-start | bytes 786440 | tf_op jit(solution)/shard_map/ppermute | solution.py:489
  11.9 22.7 %collective-permute-start.5 = (bf16[128,1024]{1,0:T(8,128)(2,1)}, bf16[128,1024]{1,0:T(8,128)(2,1)S(1)}, u32[]{:S(2)}, u32[]{:S(2)}) collective-permute-start(bf16[128,1024]{1,0:T(8,128)(2,1)} %get-tuple-element.41.refs_1_.rest_0_.rest_3_), channel_id=1, source_target_pairs={{0,16},{8,24},{16,0},{24,8},{1,17},{9,25},{17,1},{25,9},{2,18},{10... | collective-permute-start | bytes 786440 | tf_op jit(solution)/shard_map/ppermute | solution.py:489
  21.3 13.3 %collective-permute-start.8 = (bf16[128,1024]{1,0:T(8,128)(2,1)S(1)}, bf16[128,1024]{1,0:T(8,128)(2,1)S(1)}, u32[]{:S(2)}, u32[]{:S(2)}) collective-permute-start(bf16[128,1024]{1,0:T(8,128)(2,1)S(1)} %slice.25), channel_id=1, source_target_pairs={{0,4},{1,5},{2,6},{3,7},{4,0},{5,1},{6,2},{7,3},{8,12},{9,13},{10,... | collective-permute-start | bytes 786440 | tf_op jit(solution)/shard_map/ppermute | solution.py:372
  23.2 26.9 %copy-start = (bf16[128,1024]{1,0:T(8,128)(2,1)S(1)}, bf16[128,1024]{1,0:T(8,128)(2,1)}, u32[]{:S(2)}) copy-start(bf16[128,1024]{1,0:T(8,128)(2,1)} %get-tuple-element.41.refs_1_.rest_0_.rest_3_) | copy-start | bytes 786436
  23.2 26.9 %copy-start.1 = (bf16[64,1024]{1,0:T(8,128)(2,1)S(1)}, bf16[64,1024]{1,0:T(8,128)(2,1)}, u32[]{:S(2)}) copy-start(bf16[64,1024]{1,0:T(8,128)(2,1)} %get-tuple-element.55.refs_0_) | copy-start | bytes 393220
  23.2 26.9 %copy-start.2 = (f32[1024]{0:T(1024)S(1)}, f32[1024]{0:T(1024)}, u32[]{:S(2)}) copy-start(f32[1024]{0:T(1024)} %param.8) | copy-start | bytes 12292
  23.2 11.4 %collective-permute-start.7 = (bf16[128,1024]{1,0:T(8,128)(2,1)S(1)}, bf16[128,1024]{1,0:T(8,128)(2,1)S(1)}, u32[]{:S(2)}, u32[]{:S(2)}) collective-permute-start(bf16[128,1024]{1,0:T(8,128)(2,1)S(1)} %slice.24), channel_id=1, source_target_pairs={{0,2},{1,3},{2,0},{3,1},{4,6},{5,7},{6,4},{7,5},{8,10},{9,11},{10,... | collective-permute-start | bytes 786440 | tf_op jit(solution)/shard_map/ppermute | solution.py:372
  24.7 11.0 %collective-permute-start.4 = (bf16[128,1024]{1,0:T(8,128)(2,1)S(1)}, bf16[128,1024]{1,0:T(8,128)(2,1)S(1)}, u32[]{:S(2)}, u32[]{:S(2)}) collective-permute-start(bf16[128,1024]{1,0:T(8,128)(2,1)S(1)} %collective-permute-done.rest_9_.rest_12_), channel_id=1, source_target_pairs={{0,4},{1,5},{2,6},{3,7},{4,0},{5,1},{6,2},{7,3},{8,12},{9,13},{10,... | collective-permute-start | bytes 786440 | tf_op jit(solution)/shard_map/ppermute | solution.py:372
  25.3 10.5 %collective-permute-start.3 = (bf16[128,1024]{1,0:T(8,128)(2,1)S(1)}, bf16[128,1024]{1,0:T(8,128)(2,1)S(1)}, u32[]{:S(2)}, u32[]{:S(2)}) collective-permute-start(bf16[128,1024]{1,0:T(8,128)(2,1)S(1)} %collective-permute-done.rest_9_.rest_12_), channel_id=1, source_target_pairs={{0,2},{1,3},{2,0},{3,1},{4,6},{5,7},{6,4},{7,5},{8,10},{9,11},{10,... | collective-permute-start | bytes 786440 | tf_op jit(solution)/shard_map/ppermute | solution.py:372
  34.6 12.2 %collective-permute-start.10 = (bf16[256,1024]{1,0:T(8,128)(2,1)S(1)}, bf16[256,1024]{1,0:T(8,128)(2,1)S(1)}, u32[]{:S(2)}, u32[]{:S(2)}) collective-permute-start(bf16[256,1024]{1,0:T(8,128)(2,1)S(1)} %join.2.rest_15_.rest_18_), channel_id=1, source_target_pairs={{0,4},{1,5},{2,6},{3,7},{4,0},{5,1},{6,2},{7,3},{8,12},{9,13},{10,... | collective-permute-start | bytes 1572872 | tf_op jit(solution)/shard_map/ppermute | solution.py:372
  35.2 11.9 %collective-permute-start.9 = (bf16[256,1024]{1,0:T(8,128)(2,1)S(1)}, bf16[256,1024]{1,0:T(8,128)(2,1)S(1)}, u32[]{:S(2)}, u32[]{:S(2)}) collective-permute-start(bf16[256,1024]{1,0:T(8,128)(2,1)S(1)} %join.2.rest_15_.rest_18_), channel_id=1, source_target_pairs={{0,2},{1,3},{2,0},{3,1},{4,6},{5,7},{6,4},{7,5},{8,10},{9,11},{10,... | collective-permute-start | bytes 1572872 | tf_op jit(solution)/shard_map/ppermute | solution.py:372
  35.8 11.6 %collective-permute-start.12 = (bf16[192,1024]{1,0:T(8,128)(2,1)}, bf16[192,1024]{1,0:T(8,128)(2,1)S(1)}, u32[]{:S(2)}, u32[]{:S(2)}) collective-permute-start(bf16[192,1024]{1,0:T(8,128)(2,1)} %get-tuple-element.60), channel_id=1, source_target_pairs={{0,1},{1,0},{2,3},{3,2},{4,5},{5,4},{6,7},{7,6},{8,9},{9,8},{10,11... | collective-permute-start | bytes 1179656 | tf_op jit(solution)/shard_map/ppermute | solution.py:372
  35.9 11.8 %collective-permute-start.13 = (bf16[192,1024]{1,0:T(8,128)(2,1)S(1)}, bf16[192,1024]{1,0:T(8,128)(2,1)S(1)}, u32[]{:S(2)}, u32[]{:S(2)}) collective-permute-start(bf16[192,1024]{1,0:T(8,128)(2,1)S(1)} %get-tuple-element.61), channel_id=1, source_target_pairs={{0,1},{1,0},{2,3},{3,2},{4,5},{5,4},{6,7},{7,6},{8,9},{9,8},{10,11... | collective-permute-start | bytes 1179656 | tf_op jit(solution)/shard_map/ppermute | solution.py:372
  36.4 12.7 %collective-permute-start.14 = (bf16[192,1024]{1,0:T(8,128)(2,1)S(1)}, bf16[192,1024]{1,0:T(8,128)(2,1)S(1)}, u32[]{:S(2)}, u32[]{:S(2)}) collective-permute-start(bf16[192,1024]{1,0:T(8,128)(2,1)S(1)} %get-tuple-element.62), channel_id=1, source_target_pairs={{0,1},{1,0},{2,3},{3,2},{4,5},{5,4},{6,7},{7,6},{8,9},{9,8},{10,11... | collective-permute-start | bytes 1179656 | tf_op jit(solution)/shard_map/ppermute | solution.py:372
  46.9 12.2 %collective-permute-start.21 = (bf16[256,1024]{1,0:T(8,128)(2,1)S(1)}, bf16[256,1024]{1,0:T(8,128)(2,1)S(1)}, u32[]{:S(2)}, u32[]{:S(2)}) collective-permute-start(bf16[256,1024]{1,0:T(8,128)(2,1)S(1)} %collective-permute-done.10.pair_y.rest_17_.rest_20_), channel_id=1, source_target_pairs={{0,1},{1,0},{2,3},{3,2},{4,5},{5,4},{6,7},{7,6},{8,9},{9,8},{10,11... | collective-permute-start | bytes 1572872 | tf_op jit(solution)/shard_map/ppermute | solution.py:372
  47.1 12.0 %collective-permute-start.20 = (bf16[256,1024]{1,0:T(8,128)(2,1)S(1)}, bf16[256,1024]{1,0:T(8,128)(2,1)S(1)}, u32[]{:S(2)}, u32[]{:S(2)}) collective-permute-start(bf16[256,1024]{1,0:T(8,128)(2,1)S(1)} %collective-permute-done.9.pair_x.rest_16_.rest_19_), channel_id=1, source_target_pairs={{0,1},{1,0},{2,3},{3,2},{4,5},{5,4},{6,7},{7,6},{8,9},{9,8},{10,11... | collective-permute-start | bytes 1572872 | tf_op jit(solution)/shard_map/ppermute | solution.py:372
  47.4 2.7 %collective-permute-start.15 = (bf16[192,1024]{1,0:T(8,128)(2,1)S(1)}, bf16[192,1024]{1,0:T(8,128)(2,1)S(1)}, u32[]{:S(2)}, u32[]{:S(2)}) collective-permute-start(bf16[192,1024]{1,0:T(8,128)(2,1)S(1)} %get-tuple-element.63), channel_id=1, source_target_pairs={{0,1},{1,0},{2,3},{3,2},{4,5},{5,4},{6,7},{7,6},{8,9},{9,8},{10,11... | collective-permute-start | bytes 1179656 | tf_op jit(solution)/shard_map/ppermute | solution.py:372
  47.7 11.4 %collective-permute-start.11 = (bf16[192,1024]{1,0:T(8,128)(2,1)S(1)}, bf16[192,1024]{1,0:T(8,128)(2,1)S(1)}, u32[]{:S(2)}, u32[]{:S(2)}) collective-permute-start(bf16[192,1024]{1,0:T(8,128)(2,1)S(1)} %get-tuple-element.54), channel_id=1, source_target_pairs={{0,2},{1,3},{2,0},{3,1},{4,6},{5,7},{6,4},{7,5},{8,10},{9,11},{10,... | collective-permute-start | bytes 1179656 | tf_op jit(solution)/shard_map/ppermute | solution.py:372
  49.1 10.7 %collective-permute-start.22 = (bf16[192,1024]{1,0:T(8,128)(2,1)S(1)}, bf16[192,1024]{1,0:T(8,128)(2,1)S(1)}, u32[]{:S(2)}, u32[]{:S(2)}) collective-permute-start(bf16[192,1024]{1,0:T(8,128)(2,1)S(1)} %get-tuple-element.79), channel_id=1, source_target_pairs={{0,4},{1,5},{2,6},{3,7},{4,0},{5,1},{6,2},{7,3},{8,12},{9,13},{10,... | collective-permute-start | bytes 1179656 | tf_op jit(solution)/shard_map/ppermute | solution.py:372
  59.9 5.9 %collective-permute-start.23 = (bf16[384,1024]{1,0:T(8,128)(2,1)S(1)}, bf16[384,1024]{1,0:T(8,128)(2,1)S(1)}, u32[]{:S(2)}, u32[]{:S(2)}) collective-permute-start(bf16[384,1024]{1,0:T(8,128)(2,1)S(1)} %join.3.rest_21_), channel_id=1, source_target_pairs={{0,1},{1,0},{2,3},{3,2},{4,5},{5,4},{6,7},{7,6},{8,9},{9,8},{10,11... | collective-permute-start | bytes 2359304 | tf_op jit(solution)/shard_map/ppermute | solution.py:372
  60.0 4.1 %collective-permute-start.19 = (bf16[256,1024]{1,0:T(8,128)(2,1)S(1)}, bf16[256,1024]{1,0:T(8,128)(2,1)S(1)}, u32[]{:S(2)}, u32[]{:S(2)}) collective-permute-start(bf16[256,1024]{1,0:T(8,128)(2,1)S(1)} %join.2.rest_15_.rest_18_), channel_id=1, source_target_pairs={{0,1},{1,0},{2,3},{3,2},{4,5},{5,4},{6,7},{7,6},{8,9},{9,8},{10,11... | collective-permute-start | bytes 1572872 | tf_op jit(solution)/shard_map/ppermute | solution.py:372
  60.5 2.9 %collective-permute-start.16 = (bf16[128,1024]{1,0:T(8,128)(2,1)S(1)}, bf16[128,1024]{1,0:T(8,128)(2,1)S(1)}, u32[]{:S(2)}, u32[]{:S(2)}) collective-permute-start(bf16[128,1024]{1,0:T(8,128)(2,1)S(1)} %collective-permute-done.rest_9_.rest_12_), channel_id=1, source_target_pairs={{0,1},{1,0},{2,3},{3,2},{4,5},{5,4},{6,7},{7,6},{8,9},{9,8},{10,11... | collective-permute-start | bytes 786440 | tf_op jit(solution)/shard_map/ppermute | solution.py:372
  60.6 3.2 %collective-permute-start.17 = (bf16[128,1024]{1,0:T(8,128)(2,1)S(1)}, bf16[128,1024]{1,0:T(8,128)(2,1)S(1)}, u32[]{:S(2)}, u32[]{:S(2)}) collective-permute-start(bf16[128,1024]{1,0:T(8,128)(2,1)S(1)} %collective-permute-done.3.by_x.rest_10_.rest_13_), channel_id=1, source_target_pairs={{0,1},{1,0},{2,3},{3,2},{4,5},{5,4},{6,7},{7,6},{8,9},{9,8},{10,11... | collective-permute-start | bytes 786440 | tf_op jit(solution)/shard_map/ppermute | solution.py:372
  61.0 3.1 %collective-permute-start.18 = (bf16[128,1024]{1,0:T(8,128)(2,1)S(1)}, bf16[128,1024]{1,0:T(8,128)(2,1)S(1)}, u32[]{:S(2)}, u32[]{:S(2)}) collective-permute-start(bf16[128,1024]{1,0:T(8,128)(2,1)S(1)} %collective-permute-done.4.by_y.rest_11_.rest_14_), channel_id=1, source_target_pairs={{0,1},{1,0},{2,3},{3,2},{4,5},{5,4},{6,7},{7,6},{8,9},{9,8},{10,11... | collective-permute-start | bytes 786440 | tf_op jit(solution)/shard_map/ppermute | solution.py:372

commit v13 on v11

--- a/solution.py
+++ b/solution.py
@@ -487,13 +487,13 @@
     second = [one, *across(one)]
     two, three, first[2], first[3] = lax.optimization_barrier((two, three, first[2], first[3]))
     third = [join(0, two, three)]
-    third += across(third[0])
-    second[1], second[2], own, third[0], *first = lax.optimization_barrier(
-        (second[1], second[2], own, third[0], *first)
+    second[1], second[2], own, *first = lax.optimization_barrier(
+        (second[1], second[2], own, *first)
     )
     first_other = other_core([own, *first])
     second_other = other_core(second)
     ready = [joined, *first, *first_other, *second, *second_other]
+    third += across(third[0])
 
     def tokens_in(sources, both_ref):
         core = lax.axis_index("frame") % 2
@@ -521,12 +521,9 @@
     ]
     others = [[(1, d, 0, depth, 0)] for d in (0, 2, 4)]
     pairs = [[(2, d, 0, depth, 0), (3, d, depth, depth, 0)] for d in (0, 2, 4)]
-    long = half + depth
     pairs += [
-        [
-            (1, 6, 0, half, 0), (2, 6, half, depth, 0),
-            (1, 6, long, half, half), (3, 6, long + half, depth, 0),
-        ],
+        [(1, 6, 0, half, 0), (2, 6, half, depth, 0)],
+        [(1, 6, 0, half, half), (3, 6, half, depth, 0)],
     ]
     arrays = []
     for group in (table, others, pairs):
@@ -572,15 +569,17 @@
         compiler_params=SMALL,
         name="turn",
     )(second[1], second[2], third[1], third[2])
-    last = [swap(to_dx, 2, devices), swap(to_dy, 4, devices)]
-    third_other = other_core(third)
+    third += [swap(to_dx, 2, devices), swap(to_dy, 4, devices)]
+    held, *fronted = lax.optimization_barrier((third[0], *fronted))
+    third_other = other_core([held, *third[1:]])
     middle = run_middle(
-        counts, fronted, [*ready, *third, *third_other], view([*range(16), 16, 17, 18, 20, 21, 22])
-    )
-    last[0], *middle = lax.optimization_barrier((last[0], *middle))
-    last = join(0, *last)
-    weights = [*middle, *ready, *third, last, *third_other, swap(last, 1, devices)]
-    return fronted, weights, view(list(range(24)))
+        counts,
+        fronted,
+        [*ready, *third[:3], *third_other[:3]],
+        view([*range(16), 16, 17, 18, 21, 22, 23]),
+    )
+    weights = [*middle, *ready, *third, *third_other]
+    return fronted, weights, view(list(range(26)))
 
 
 def gather_plainly(

time: 93.9 us -> 91.8 us (0.978)
  waiting for transfers between devices: 39.4 us -> 37.6 us
  starting transfers between devices: 20.1 us -> 19.1 us
    ppermute x22 -> x23, waiting for transfers between devices: 31.2 us -> 29.4 us  [swap(): lax.ppermute(array, 'frame', [(f, f ^ distance) for f in range(devices)])]
    ppermute x22 -> x23, starting transfers between devices: 15.9 us -> 14.9 us  [swap(): lax.ppermute(array, 'frame', [(f, f ^ distance) for f in range(devices)])]
  transfers between devices with their start and end apart: 25 -> 26, of which waited for: 9 -> 8; matrix products, arithmetic and copies ran while one was open for 0% -> 0% of each run, Pallas kernels for 3% -> 3%
where the time goes in v13:
time: 91.8 us; the launch traced here: 91.6 us
  waiting for transfers between devices  37.6 us (41%)
  starting transfers between devices  19.1 us (21%)
  blocking collectives  18.4 us (20%)
  Pallas kernels  14 us (15%)
  between operations  1.45 us (2%)
  local copies, waits for them, and re-layouts  1.08 us (1%)
    ppermute x23, waiting for transfers between devices, swap(): lax.ppermute(array, 'frame', [(f, f ^ distance) for f in range(devices)])  29.4 us
    all_to_all x1, blocking collectives, per_device(): lax.all_to_all(back, 'frame', split_axis=0, concat_axis=0, tiled=True)  18.4 us
    ppermute x23, starting transfers between devices, swap(): lax.ppermute(array, 'frame', [(f, f ^ distance) for f in range(devices)])  14.9 us
    pallas_call x1, Pallas kernels, run_main(): pl.pallas_call(functools.partial(main_kernel, view), out_shape=jax.ShapeD...  8.37 us
    ppermute x3, waiting for transfers between devices, by_clip(): return lax.ppermute(array, 'clip', [(c, c ^ offset) for c in range(4)])  8.21 us
    ppermute x3, starting transfers between devices, by_clip(): return lax.ppermute(array, 'clip', [(c, c ^ offset) for c in range(4)])  4.17 us
    pallas_call x1, Pallas kernels, gather_in_rounds(): pl.pallas_call(functools.partial(pack_kernel, patches, share), out_shape=...  2.69 us
  transfers between devices with their start and end apart: 26, of which 8 were waited for; matrix products, arithmetic and copies ran while one was open for 0% of the time, Pallas kernels for 3%

profile of v13, /device:TPU:0, one launch (start us, length us, event | category | flops | bytes accessed | tf_op | source)
XLA Modules:
  0.0 91.6 jit_solution(17312866528931895801)
XLA Ops:
  0.6 0.0 copy-start.2
  0.6 2.7 %pack.1 = (bf16[128,1024]{1,0:T(8,128)(2,1)}, bf16[192,1024]{1,0:T(8,128)(2,1)}, bf16[64,1024]{1,0:T(8,128)(2,1)}, bf16[320,1024]{1,0:T(8,128)(2,1)}, bf16[320,1024]{1,0:T(8,128)(2,1)}) custom-call(bf16[128,768]{1,0:T(8,128)(2,1)} %refs_0_.1, bf16[128,256]{1,0:T(8,128)(2,1)} %refs_1_.1, bf16[1,1,196,1024]{3,2,1,0:T(8,128)(2,1)} %refs_2_.1, ...), custom_call_target="tpu_custom_call" | custom-call | tf_op jit(solution)/shard_map/pack/pallas_call | solution.py:459
  3.3 0.0 copy-start
  3.3 0.0 copy-start.1
  3.4 3.0 %collective-permute-start.2 = (bf16[320,1024]{1,0:T(8,128)(2,1)}, bf16[320,1024]{1,0:T(8,128)(2,1)S(1)}, u32[]{:S(2)}, u32[]{:S(2)}) collective-permute-start(bf16[320,1024]{1,0:T(8,128)(2,1)} %get-tuple-element.36), channel_id=1, source_target_pairs={{0,4},{1,5},{2,6},{3,7},{4,0},{5,1},{6,2},{7,3},{8,12},{9,13},{10,... | collective-permute-start | bytes 1966088 | tf_op jit(solution)/shard_map/ppermute | solution.py:372
  6.4 1.5 %collective-permute-start.4 = (bf16[320,1024]{1,0:T(8,128)(2,1)}, bf16[320,1024]{1,0:T(8,128)(2,1)S(1)}, u32[]{:S(2)}, u32[]{:S(2)}) collective-permute-start(bf16[320,1024]{1,0:T(8,128)(2,1)} %get-tuple-element.37), channel_id=1, source_target_pairs={{0,2},{1,3},{2,0},{3,1},{4,6},{5,7},{6,4},{7,5},{8,10},{9,11},{10,... | collective-permute-start | bytes 1966088 | tf_op jit(solution)/shard_map/ppermute | solution.py:372
  7.9 1.6 %collective-permute-start.6 = (bf16[128,1024]{1,0:T(8,128)(2,1)}, bf16[128,1024]{1,0:T(8,128)(2,1)S(1)}, u32[]{:S(2)}, u32[]{:S(2)}) collective-permute-start(bf16[128,1024]{1,0:T(8,128)(2,1)} %get-tuple-element.35.refs_1_.rest_0_.rest_3_), channel_id=1, source_target_pairs={{0,8},{8,0},{16,24},{24,16},{1,9},{9,1},{17,25},{25,17},{2,10},{10... | collective-permute-start | bytes 786440 | tf_op jit(solution)/shard_map/ppermute | solution.py:474
  9.5 2.5 %collective-permute-start.1 = (bf16[128,1024]{1,0:T(8,128)(2,1)}, bf16[128,1024]{1,0:T(8,128)(2,1)S(1)}, u32[]{:S(2)}, u32[]{:S(2)}) collective-permute-start(bf16[128,1024]{1,0:T(8,128)(2,1)} %get-tuple-element.35.refs_1_.rest_0_.rest_3_), channel_id=1, source_target_pairs={{0,24},{8,16},{16,8},{24,0},{1,25},{9,17},{17,9},{25,1},{2,26},{10... | collective-permute-start | bytes 786440 | tf_op jit(solution)/shard_map/ppermute | solution.py:474
  11.9 0.1 collective-permute-start
  12.1 9.3 %collective-permute-done.2.refs_3_.rest_2_.rest_5_ = bf16[320,1024]{1,0:T(8,128)(2,1)S(1)} collective-permute-done((bf16[320,1024]{1,0:T(8,128)(2,1)}, bf16[320,1024]{1,0:T(8,128)(2,1)S(1)}, u32[]{:S(2)}, u32[]{:S(2)}) %collective-permute-start.2) | collective-permute-done | bytes 655392 | tf_op jit(solution)/shard_map/ppermute | solution.py:372
  21.4 1.8 %collective-permute-start.3 = (bf16[128,1024]{1,0:T(8,128)(2,1)S(1)}, bf16[128,1024]{1,0:T(8,128)(2,1)S(1)}, u32[]{:S(2)}, u32[]{:S(2)}) collective-permute-start(bf16[128,1024]{1,0:T(8,128)(2,1)S(1)} %slice.24), channel_id=1, source_target_pairs={{0,2},{1,3},{2,0},{3,1},{4,6},{5,7},{6,4},{7,5},{8,10},{9,11},{10,... | collective-permute-start | bytes 786440 | tf_op jit(solution)/shard_map/ppermute | solution.py:372
  23.1 0.0 collective-permute-done.4.refs_2_.rest_1_.rest_4_
  23.2 1.6 %collective-permute-start.5 = (bf16[128,1024]{1,0:T(8,128)(2,1)S(1)}, bf16[128,1024]{1,0:T(8,128)(2,1)S(1)}, u32[]{:S(2)}, u32[]{:S(2)}) collective-permute-start(bf16[128,1024]{1,0:T(8,128)(2,1)S(1)} %slice.25), channel_id=1, source_target_pairs={{0,4},{1,5},{2,6},{3,7},{4,0},{5,1},{6,2},{7,3},{8,12},{9,13},{10,... | collective-permute-start | bytes 786440 | tf_op jit(solution)/shard_map/ppermute | solution.py:372
  24.7 0.0 collective-permute-done.6.rest_10_.rest_13_
  24.7 0.5 collective-permute-start.8
  25.3 0.0 collective-permute-done.1.refs_1_
  25.3 1.1 %collective-permute-start.7 = (bf16[128,1024]{1,0:T(8,128)(2,1)S(1)}, bf16[128,1024]{1,0:T(8,128)(2,1)S(1)}, u32[]{:S(2)}, u32[]{:S(2)}) collective-permute-start(bf16[128,1024]{1,0:T(8,128)(2,1)S(1)} %collective-permute-done.6.rest_10_.rest_13_), channel_id=1, source_target_pairs={{0,2},{1,3},{2,0},{3,1},{4,6},{5,7},{6,4},{7,5},{8,10},{9,11},{10,... | collective-permute-start | bytes 786440 | tf_op jit(solution)/shard_map/ppermute | solution.py:372
  26.4 8.2 %collective-permute-done.refs_0_ = bf16[128,1024]{1,0:T(8,128)(2,1)S(1)} collective-permute-done((bf16[128,1024]{1,0:T(8,128)(2,1)}, bf16[128,1024]{1,0:T(8,128)(2,1)S(1)}, u32[]{:S(2)}, u32[]{:S(2)}) %collective-permute-start) | collective-permute-done | bytes 262176 | tf_op jit(solution)/shard_map/ppermute | solution.py:474
  34.6 0.0 collective-permute-done.3.refs_4_.rest_3_.rest_6_
  34.6 0.0 collective-permute-done.5.refs_5_.rest_4_.rest_7_
  34.7 0.6 collective-permute-start.18
  35.2 0.5 collective-permute-start.17
  35.8 0.0 collective-permute-done.8.rest_12_.by_y.rest_15_
  35.8 0.0 collective-permute-done.7.rest_11_.by_x.rest_14_
  35.8 0.0 collective-permute-start.10
  35.8 0.5 collective-permute-start.11
  36.3 0.0 collective-permute-start.9
  36.4 10.6 %collective-permute-done.18.rest_18_.pair_y.rest_21_ = bf16[256,1024]{1,0:T(8,128)(2,1)S(1)} collective-permute-done((bf16[256,1024]{1,0:T(8,128)(2,1)S(1)}, bf16[256,1024]{1,0:T(8,128)(2,1)S(1)}, u32[]{:S(2)}, u32[]{:S(2)}) %collective-permute-start.18) | collective-permute-done | bytes 524320 | tf_op jit(solution)/shard_map/ppermute | solution.py:372
  47.0 0.0 collective-permute-start.12
  47.0 0.1 collective-permute-done.17.rest_17_.pair_x.rest_20_
  47.1 0.4 collective-permute-start.13
  47.5 0.1 turn.1
  47.5 1.0 %collective-permute-done.12.refs_9_.rest_8_.rest_11_ = bf16[128,1024]{1,0:T(8,128)(2,1)S(1)} collective-permute-done((bf16[128,1024]{1,0:T(8,128)(2,1)S(1)}, bf16[128,1024]{1,0:T(8,128)(2,1)S(1)}, u32[]{:S(2)}, u32[]{:S(2)}) %collective-permute-start.12) | collective-permute-done | bytes 262176 | tf_op jit(solution)/shard_map/ppermute | solution.py:372
  48.5 0.1 collective-permute-start.14
  48.6 0.2 collective-permute-done.13.refs_10_.rest_9_.rest_12_
  48.9 0.1 collective-permute-start.15
  49.0 0.0 collective-permute-done.9.refs_6_.rest_5_.rest_8_
  49.0 0.4 collective-permute-start.16
  49.4 0.0 collective-permute-done.10.refs_7_.rest_6_.rest_9_
  49.4 1.1 %collective-permute-start.22 = (bf16[192,1024]{1,0:T(8,128)(2,1)S(1)}, bf16[192,1024]{1,0:T(8,128)(2,1)S(1)}, u32[]{:S(2)}, u32[]{:S(2)}) collective-permute-start(bf16[192,1024]{1,0:T(8,128)(2,1)S(1)} %get-tuple-element.66), channel_id=1, source_target_pairs={{0,2},{1,3},{2,0},{3,1},{4,6},{5,7},{6,4},{7,5},{8,10},{9,11},{10,... | collective-permute-start | bytes 1179656 | tf_op jit(solution)/shard_map/ppermute | solution.py:372
  50.5 0.0 collective-permute-done.11.refs_8_.rest_7_.rest_10_
  50.5 0.9 %collective-permute-start.23 = (bf16[192,1024]{1,0:T(8,128)(2,1)S(1)}, bf16[192,1024]{1,0:T(8,128)(2,1)S(1)}, u32[]{:S(2)}, u32[]{:S(2)}) collective-permute-start(bf16[192,1024]{1,0:T(8,128)(2,1)S(1)} %get-tuple-element.67), channel_id=1, source_target_pairs={{0,4},{1,5},{2,6},{3,7},{4,0},{5,1},{6,2},{7,3},{8,12},{9,13},{10,... | collective-permute-start | bytes 1179656 | tf_op jit(solution)/shard_map/ppermute | solution.py:372
  51.5 0.0 copy-done.1
  51.5 1.1 %front.1 = (bf16[8,2,32,1024]{3,2,1,0:T(8,128)(2,1)S(1)}, bf16[256,1024]{1,0:T(8,128)(2,1)S(1)}, f32[256,128]{1,0:T(8,128)S(1)}, bf16[256,768]{1,0:T(8,128)(2,1)S(1)}) custom-call(f32[1,1024]{1,0:T(1,128)S(1)} %bitcast.11, bf16[64,1024]{1,0:T(8,128)(2,1)S(1)} %copy-done.1, bf16[128,1024]{1,0:T(8,128)(2,1)S(1)} %copy-done, ...), custom_call_target="tpu_custom_call" | custom-call | flops 256 | bytes 256 | tf_op jit(solution)/shard_map/front/pallas_call | solution.py:289
  52.6 0.0 collective-permute-done.14.rest_13_.rest_16_
  52.6 0.1 collective-permute-start.21
  52.7 0.0 collective-permute-done.15.rest_14_.rest_17_
  52.7 0.5 collective-permute-start.20
  53.2 0.0 collective-permute-done.16.rest_15_.rest_18_
  53.2 0.1 collective-permute-start.19
  53.3 7.3 %collective-permute-done.22.rest_22_ = bf16[192,1024]{1,0:T(8,128)(2,1)S(1)} collective-permute-done((bf16[192,1024]{1,0:T(8,128)(2,1)S(1)}, bf16[192,1024]{1,0:T(8,128)(2,1)S(1)}, u32[]{:S(2)}, u32[]{:S(2)}) %collective-permute-start.22) | collective-permute-done | bytes 393248 | tf_op jit(solution)/shard_map/ppermute | solution.py:372
  60.6 0.0 collective-permute-start.24
  60.6 0.8 collective-permute-done.23.rest_23_
  61.4 0.0 collective-permute-start.25
  62.1 0.0 collective-permute-done.21.rest_21_.rest_26_
  62.1 0.0 collective-permute-done.20.rest_20_.rest_25_
  62.1 0.0 collective-permute-done.19.rest_19_.rest_24_
  62.1 1.7 %middle.1 = (bf16[256,1024]{1,0:T(8,128)(2,1)S(1)}, bf16[256,1024]{1,0:T(8,128)(2,1)S(1)}, f32[256,2304]{1,0:T(8,128)S(1)}) custom-call(s32[1]{0:T(128)S(6)} %copy.9.counts_ref, bf16[8,2,32,1024]{3,2,1,0:T(8,128)(2,1)S(1)} %get-tuple-element.56.both_ref, bf16[256,1024]{1,0:T(8,128)(2,1)S(1)} %get-tuple-element.57.normed_ref, bf16[128,1024]{1,0:T(8,128)(2,1)S(1)} %copy-done, ...), custom_call_target="tpu_custom_call" | custom-call | flops 256 | bytes 256 | tf_op jit(solution)/shard_map/middle/pallas_call | solution.py:311
  63.8 0.0 collective-permute-done.24.rest_27_
  63.8 0.0 collective-permute-done.25.rest_28_
  63.8 8.4 %main.1 = bf16[8,2,32,1024]{3,2,1,0:T(8,128)(2,1)S(1)} custom-call(s32[1]{0:T(128)S(6)} %copy.9.counts_ref, f32[1,1024]{1,0:T(1,128)S(1)} %bitcast.12, bf16[8,2,32,1024]{3,2,1,0:T(8,128)(2,1)S(1)} %get-tuple-element.56.both_ref, bf16[256,1024]{1,0:T(8,128)(2,1)S(1)} %get-tuple-element.57.normed_ref, f32[256,128]{1,0:T(8,128)S(1)} %get-tuple-element.58.stats_ref, ...), custom_call_target="tpu_custom_call" | custom-call | flops 3221225472 | bytes 10485760 | tf_op jit(solution)/shard_map/main/pallas_call | solution.py:334
  72.2 18.4 %all_to_all.5 = bf16[8,1,2,32,1024]{4,3,2,1,0:T(8,128)(2,1)S(1)} all-to-all(bf16[8,1,2,32,1024]{4,3,2,1,0:T(8,128)(2,1)S(1)} %bitcast.10), channel_id=1, replica_groups=mesh['clip'=4,'frame'=8] {'frame'}, dimensions={0} | all-to-all | bytes 2097152 | tf_op jit(solution)/shard_map/all_to_all | solution.py:643
  90.6 0.1 fusion
  90.7 0.9 %slice_bitcast_fusion = (bf16[1,1,196,1024]{3,2,1,0:T(8,128)(2,1)}, bf16[1,1,196,1024]{3,2,1,0:T(8,128)(2,1)}) fusion(bf16[1,256,1024]{2,1,0:T(8,128)(2,1)S(1)} %bitcast.13, bf16[1,256,1024]{2,1,0:T(8,128)(2,1)S(1)} %bitcast.14), kind=kLoop, calls=%fused_computation | loop fusion | bytes 1605632 | tf_op jit(solution)/shard_map/broadcast_in_dim | solution.py:647
  (5 shorter events, 0.1 us)
Async XLA Ops:
  0.6 50.8 %copy-start.2 = (f32[1024]{0:T(1024)S(1)}, f32[1024]{0:T(1024)}, u32[]{:S(2)}) copy-start(f32[1024]{0:T(1024)} %param.8) | copy-start | bytes 12292
  3.3 48.1 %copy-start = (bf16[128,1024]{1,0:T(8,128)(2,1)S(1)}, bf16[128,1024]{1,0:T(8,128)(2,1)}, u32[]{:S(2)}) copy-start(bf16[128,1024]{1,0:T(8,128)(2,1)} %get-tuple-element.35.refs_1_.rest_0_.rest_3_) | copy-start | bytes 786436
  3.3 48.1 %copy-start.1 = (bf16[64,1024]{1,0:T(8,128)(2,1)S(1)}, bf16[64,1024]{1,0:T(8,128)(2,1)}, u32[]{:S(2)}) copy-start(bf16[64,1024]{1,0:T(8,128)(2,1)} %get-tuple-element.40.refs_0_) | copy-start | bytes 393220
  3.4 18.0 %collective-permute-start.2 = (bf16[320,1024]{1,0:T(8,128)(2,1)}, bf16[320,1024]{1,0:T(8,128)(2,1)S(1)}, u32[]{:S(2)}, u32[]{:S(2)}) collective-permute-start(bf16[320,1024]{1,0:T(8,128)(2,1)} %get-tuple-element.36), channel_id=1, source_target_pairs={{0,4},{1,5},{2,6},{3,7},{4,0},{5,1},{6,2},{7,3},{8,12},{9,13},{10,... | collective-permute-start | bytes 1966088 | tf_op jit(solution)/shard_map/ppermute | solution.py:372
  6.4 16.7 %collective-permute-start.4 = (bf16[320,1024]{1,0:T(8,128)(2,1)}, bf16[320,1024]{1,0:T(8,128)(2,1)S(1)}, u32[]{:S(2)}, u32[]{:S(2)}) collective-permute-start(bf16[320,1024]{1,0:T(8,128)(2,1)} %get-tuple-element.37), channel_id=1, source_target_pairs={{0,2},{1,3},{2,0},{3,1},{4,6},{5,7},{6,4},{7,5},{8,10},{9,11},{10,... | collective-permute-start | bytes 1966088 | tf_op jit(solution)/shard_map/ppermute | solution.py:372
  7.9 16.9 %collective-permute-start.6 = (bf16[128,1024]{1,0:T(8,128)(2,1)}, bf16[128,1024]{1,0:T(8,128)(2,1)S(1)}, u32[]{:S(2)}, u32[]{:S(2)}) collective-permute-start(bf16[128,1024]{1,0:T(8,128)(2,1)} %get-tuple-element.35.refs_1_.rest_0_.rest_3_), channel_id=1, source_target_pairs={{0,8},{8,0},{16,24},{24,16},{1,9},{9,1},{17,25},{25,17},{2,10},{10... | collective-permute-start | bytes 786440 | tf_op jit(solution)/shard_map/ppermute | solution.py:474
  9.5 15.8 %collective-permute-start.1 = (bf16[128,1024]{1,0:T(8,128)(2,1)}, bf16[128,1024]{1,0:T(8,128)(2,1)S(1)}, u32[]{:S(2)}, u32[]{:S(2)}) collective-permute-start(bf16[128,1024]{1,0:T(8,128)(2,1)} %get-tuple-element.35.refs_1_.rest_0_.rest_3_), channel_id=1, source_target_pairs={{0,24},{8,16},{16,8},{24,0},{1,25},{9,17},{17,9},{25,1},{2,26},{10... | collective-permute-start | bytes 786440 | tf_op jit(solution)/shard_map/ppermute | solution.py:474
  11.9 22.7 %collective-permute-start = (bf16[128,1024]{1,0:T(8,128)(2,1)}, bf16[128,1024]{1,0:T(8,128)(2,1)S(1)}, u32[]{:S(2)}, u32[]{:S(2)}) collective-permute-start(bf16[128,1024]{1,0:T(8,128)(2,1)} %get-tuple-element.35.refs_1_.rest_0_.rest_3_), channel_id=1, source_target_pairs={{0,16},{8,24},{16,0},{24,8},{1,17},{9,25},{17,1},{25,9},{2,18},{10... | collective-permute-start | bytes 786440 | tf_op jit(solution)/shard_map/ppermute | solution.py:474
  21.4 13.3 %collective-permute-start.3 = (bf16[128,1024]{1,0:T(8,128)(2,1)S(1)}, bf16[128,1024]{1,0:T(8,128)(2,1)S(1)}, u32[]{:S(2)}, u32[]{:S(2)}) collective-permute-start(bf16[128,1024]{1,0:T(8,128)(2,1)S(1)} %slice.24), channel_id=1, source_target_pairs={{0,2},{1,3},{2,0},{3,1},{4,6},{5,7},{6,4},{7,5},{8,10},{9,11},{10,... | collective-permute-start | bytes 786440 | tf_op jit(solution)/shard_map/ppermute | solution.py:372
  23.2 11.5 %collective-permute-start.5 = (bf16[128,1024]{1,0:T(8,128)(2,1)S(1)}, bf16[128,1024]{1,0:T(8,128)(2,1)S(1)}, u32[]{:S(2)}, u32[]{:S(2)}) collective-permute-start(bf16[128,1024]{1,0:T(8,128)(2,1)S(1)} %slice.25), channel_id=1, source_target_pairs={{0,4},{1,5},{2,6},{3,7},{4,0},{5,1},{6,2},{7,3},{8,12},{9,13},{10,... | collective-permute-start | bytes 786440 | tf_op jit(solution)/shard_map/ppermute | solution.py:372
  24.7 11.0 %collective-permute-start.8 = (bf16[128,1024]{1,0:T(8,128)(2,1)S(1)}, bf16[128,1024]{1,0:T(8,128)(2,1)S(1)}, u32[]{:S(2)}, u32[]{:S(2)}) collective-permute-start(bf16[128,1024]{1,0:T(8,128)(2,1)S(1)} %collective-permute-done.6.rest_10_.rest_13_), channel_id=1, source_target_pairs={{0,4},{1,5},{2,6},{3,7},{4,0},{5,1},{6,2},{7,3},{8,12},{9,13},{10,... | collective-permute-start | bytes 786440 | tf_op jit(solution)/shard_map/ppermute | solution.py:372
  25.3 10.5 %collective-permute-start.7 = (bf16[128,1024]{1,0:T(8,128)(2,1)S(1)}, bf16[128,1024]{1,0:T(8,128)(2,1)S(1)}, u32[]{:S(2)}, u32[]{:S(2)}) collective-permute-start(bf16[128,1024]{1,0:T(8,128)(2,1)S(1)} %collective-permute-done.6.rest_10_.rest_13_), channel_id=1, source_target_pairs={{0,2},{1,3},{2,0},{3,1},{4,6},{5,7},{6,4},{7,5},{8,10},{9,11},{10,... | collective-permute-start | bytes 786440 | tf_op jit(solution)/shard_map/ppermute | solution.py:372
  34.7 12.3 %collective-permute-start.18 = (bf16[256,1024]{1,0:T(8,128)(2,1)S(1)}, bf16[256,1024]{1,0:T(8,128)(2,1)S(1)}, u32[]{:S(2)}, u32[]{:S(2)}) collective-permute-start(bf16[256,1024]{1,0:T(8,128)(2,1)S(1)} %join.1.rest_16_.rest_19_), channel_id=1, source_target_pairs={{0,4},{1,5},{2,6},{3,7},{4,0},{5,1},{6,2},{7,3},{8,12},{9,13},{10,... | collective-permute-start | bytes 1572872 | tf_op jit(solution)/shard_map/ppermute | solution.py:372
  35.2 11.9 %collective-permute-start.17 = (bf16[256,1024]{1,0:T(8,128)(2,1)S(1)}, bf16[256,1024]{1,0:T(8,128)(2,1)S(1)}, u32[]{:S(2)}, u32[]{:S(2)}) collective-permute-start(bf16[256,1024]{1,0:T(8,128)(2,1)S(1)} %join.1.rest_16_.rest_19_), channel_id=1, source_target_pairs={{0,2},{1,3},{2,0},{3,1},{4,6},{5,7},{6,4},{7,5},{8,10},{9,11},{10,... | collective-permute-start | bytes 1572872 | tf_op jit(solution)/shard_map/ppermute | solution.py:372
  35.8 13.6 %collective-permute-start.10 = (bf16[320,1024]{1,0:T(8,128)(2,1)S(1)}, bf16[320,1024]{1,0:T(8,128)(2,1)S(1)}, u32[]{:S(2)}, u32[]{:S(2)}) collective-permute-start(bf16[320,1024]{1,0:T(8,128)(2,1)S(1)} %collective-permute-done.4.refs_2_.rest_1_.rest_4_), channel_id=1, source_target_pairs={{0,1},{1,0},{2,3},{3,2},{4,5},{5,4},{6,7},{7,6},{8,9},{9,8},{10,11... | collective-permute-start | bytes 1966088 | tf_op jit(solution)/shard_map/ppermute | solution.py:372
  35.8 14.7 %collective-permute-start.11 = (bf16[320,1024]{1,0:T(8,128)(2,1)S(1)}, bf16[320,1024]{1,0:T(8,128)(2,1)S(1)}, u32[]{:S(2)}, u32[]{:S(2)}) collective-permute-start(bf16[320,1024]{1,0:T(8,128)(2,1)S(1)} %collective-permute-done.2.refs_3_.rest_2_.rest_5_), channel_id=1, source_target_pairs={{0,1},{1,0},{2,3},{3,2},{4,5},{5,4},{6,7},{7,6},{8,9},{9,8},{10,11... | collective-permute-start | bytes 1966088 | tf_op jit(solution)/shard_map/ppermute | solution.py:372
  36.3 12.7 %collective-permute-start.9 = (bf16[192,1024]{1,0:T(8,128)(2,1)}, bf16[192,1024]{1,0:T(8,128)(2,1)S(1)}, u32[]{:S(2)}, u32[]{:S(2)}) collective-permute-start(bf16[192,1024]{1,0:T(8,128)(2,1)} %get-tuple-element.51), channel_id=1, source_target_pairs={{0,1},{1,0},{2,3},{3,2},{4,5},{5,4},{6,7},{7,6},{8,9},{9,8},{10,11... | collective-permute-start | bytes 1179656 | tf_op jit(solution)/shard_map/ppermute | solution.py:372
  47.0 1.5 %collective-permute-start.12 = (bf16[128,1024]{1,0:T(8,128)(2,1)S(1)}, bf16[128,1024]{1,0:T(8,128)(2,1)S(1)}, u32[]{:S(2)}, u32[]{:S(2)}) collective-permute-start(bf16[128,1024]{1,0:T(8,128)(2,1)S(1)} %collective-permute-done.3.refs_4_.rest_3_.rest_6_), channel_id=1, source_target_pairs={{0,1},{1,0},{2,3},{3,2},{4,5},{5,4},{6,7},{7,6},{8,9},{9,8},{10,11... | collective-permute-start | bytes 786440 | tf_op jit(solution)/shard_map/ppermute | solution.py:372
  47.1 1.8 %collective-permute-start.13 = (bf16[128,1024]{1,0:T(8,128)(2,1)S(1)}, bf16[128,1024]{1,0:T(8,128)(2,1)S(1)}, u32[]{:S(2)}, u32[]{:S(2)}) collective-permute-start(bf16[128,1024]{1,0:T(8,128)(2,1)S(1)} %collective-permute-done.5.refs_5_.rest_4_.rest_7_), channel_id=1, source_target_pairs={{0,1},{1,0},{2,3},{3,2},{4,5},{5,4},{6,7},{7,6},{8,9},{9,8},{10,11... | collective-permute-start | bytes 786440 | tf_op jit(solution)/shard_map/ppermute | solution.py:372
  48.5 4.1 %collective-permute-start.14 = (bf16[128,1024]{1,0:T(8,128)(2,1)S(1)}, bf16[128,1024]{1,0:T(8,128)(2,1)S(1)}, u32[]{:S(2)}, u32[]{:S(2)}) collective-permute-start(bf16[128,1024]{1,0:T(8,128)(2,1)S(1)} %collective-permute-done.6.rest_10_.rest_13_), channel_id=1, source_target_pairs={{0,1},{1,0},{2,3},{3,2},{4,5},{5,4},{6,7},{7,6},{8,9},{9,8},{10,11... | collective-permute-start | bytes 786440 | tf_op jit(solution)/shard_map/ppermute | solution.py:372
  48.9 3.8 %collective-permute-start.15 = (bf16[128,1024]{1,0:T(8,128)(2,1)S(1)}, bf16[128,1024]{1,0:T(8,128)(2,1)S(1)}, u32[]{:S(2)}, u32[]{:S(2)}) collective-permute-start(bf16[128,1024]{1,0:T(8,128)(2,1)S(1)} %collective-permute-done.7.rest_11_.by_x.rest_14_), channel_id=1, source_target_pairs={{0,1},{1,0},{2,3},{3,2},{4,5},{5,4},{6,7},{7,6},{8,9},{9,8},{10,11... | collective-permute-start | bytes 786440 | tf_op jit(solution)/shard_map/ppermute | solution.py:372
  49.0 4.2 %collective-permute-start.16 = (bf16[128,1024]{1,0:T(8,128)(2,1)S(1)}, bf16[128,1024]{1,0:T(8,128)(2,1)S(1)}, u32[]{:S(2)}, u32[]{:S(2)}) collective-permute-start(bf16[128,1024]{1,0:T(8,128)(2,1)S(1)} %collective-permute-done.8.rest_12_.by_y.rest_15_), channel_id=1, source_target_pairs={{0,1},{1,0},{2,3},{3,2},{4,5},{5,4},{6,7},{7,6},{8,9},{9,8},{10,11... | collective-permute-start | bytes 786440 | tf_op jit(solution)/shard_map/ppermute | solution.py:372
  49.4 11.2 %collective-permute-start.22 = (bf16[192,1024]{1,0:T(8,128)(2,1)S(1)}, bf16[192,1024]{1,0:T(8,128)(2,1)S(1)}, u32[]{:S(2)}, u32[]{:S(2)}) collective-permute-start(bf16[192,1024]{1,0:T(8,128)(2,1)S(1)} %get-tuple-element.66), channel_id=1, source_target_pairs={{0,2},{1,3},{2,0},{3,1},{4,6},{5,7},{6,4},{7,5},{8,10},{9,11},{10,... | collective-permute-start | bytes 1179656 | tf_op jit(solution)/shard_map/ppermute | solution.py:372
  50.5 10.9 %collective-permute-start.23 = (bf16[192,1024]{1,0:T(8,128)(2,1)S(1)}, bf16[192,1024]{1,0:T(8,128)(2,1)S(1)}, u32[]{:S(2)}, u32[]{:S(2)}) collective-permute-start(bf16[192,1024]{1,0:T(8,128)(2,1)S(1)} %get-tuple-element.67), channel_id=1, source_target_pairs={{0,4},{1,5},{2,6},{3,7},{4,0},{5,1},{6,2},{7,3},{8,12},{9,13},{10,... | collective-permute-start | bytes 1179656 | tf_op jit(solution)/shard_map/ppermute | solution.py:372
  52.6 9.4 %collective-permute-start.21 = (bf16[256,1024]{1,0:T(8,128)(2,1)S(1)}, bf16[256,1024]{1,0:T(8,128)(2,1)S(1)}, u32[]{:S(2)}, u32[]{:S(2)}) collective-permute-start(bf16[256,1024]{1,0:T(8,128)(2,1)S(1)} %collective-permute-done.18.rest_18_.pair_y.rest_21_), channel_id=1, source_target_pairs={{0,1},{1,0},{2,3},{3,2},{4,5},{5,4},{6,7},{7,6},{8,9},{9,8},{10,11... | collective-permute-start | bytes 1572872 | tf_op jit(solution)/shard_map/ppermute | solution.py:372
  52.7 9.4 %collective-permute-start.20 = (bf16[256,1024]{1,0:T(8,128)(2,1)S(1)}, bf16[256,1024]{1,0:T(8,128)(2,1)S(1)}, u32[]{:S(2)}, u32[]{:S(2)}) collective-permute-start(bf16[256,1024]{1,0:T(8,128)(2,1)S(1)} %collective-permute-done.17.rest_17_.pair_x.rest_20_), channel_id=1, source_target_pairs={{0,1},{1,0},{2,3},{3,2},{4,5},{5,4},{6,7},{7,6},{8,9},{9,8},{10,11... | collective-permute-start | bytes 1572872 | tf_op jit(solution)/shard_map/ppermute | solution.py:372
  53.2 8.9 %collective-permute-start.19 = (bf16[256,1024]{1,0:T(8,128)(2,1)S(1)}, bf16[256,1024]{1,0:T(8,128)(2,1)S(1)}, u32[]{:S(2)}, u32[]{:S(2)}) collective-permute-start(bf16[256,1024]{1,0:T(8,128)(2,1)S(1)} %join.1.rest_16_.rest_19_), channel_id=1, source_target_pairs={{0,1},{1,0},{2,3},{3,2},{4,5},{5,4},{6,7},{7,6},{8,9},{9,8},{10,11... | collective-permute-start | bytes 1572872 | tf_op jit(solution)/shard_map/ppermute | solution.py:372
  60.6 3.2 %collective-permute-start.24 = (bf16[192,1024]{1,0:T(8,128)(2,1)S(1)}, bf16[192,1024]{1,0:T(8,128)(2,1)S(1)}, u32[]{:S(2)}, u32[]{:S(2)}) collective-permute-start(bf16[192,1024]{1,0:T(8,128)(2,1)S(1)} %collective-permute-done.22.rest_22_), channel_id=1, source_target_pairs={{0,1},{1,0},{2,3},{3,2},{4,5},{5,4},{6,7},{7,6},{8,9},{9,8},{10,11... | collective-permute-start | bytes 1179656 | tf_op jit(solution)/shard_map/ppermute | solution.py:372
  61.4 2.4 %collective-permute-start.25 = (bf16[192,1024]{1,0:T(8,128)(2,1)S(1)}, bf16[192,1024]{1,0:T(8,128)(2,1)S(1)}, u32[]{:S(2)}, u32[]{:S(2)}) collective-permute-start(bf16[192,1024]{1,0:T(8,128)(2,1)S(1)} %collective-permute-done.23.rest_23_), channel_id=1, source_target_pairs={{0,1},{1,0},{2,3},{3,2},{4,5},{5,4},{6,7},{7,6},{8,9},{9,8},{10,11... | collective-permute-start | bytes 1179656 | tf_op jit(solution)/shard_map/ppermute | solution.py:372

commit v14 on v13

--- a/solution.py
+++ b/solution.py
@@ -491,8 +491,7 @@
         (second[1], second[2], own, *first)
     )
     first_other = other_core([own, *first])
-    second_other = other_core(second)
-    ready = [joined, *first, *first_other, *second, *second_other]
+    ready = [joined, *first, *first_other]
     third += across(third[0])
 
     def tokens_in(sources, both_ref):
@@ -525,9 +524,10 @@
         [(1, 6, 0, half, 0), (2, 6, half, depth, 0)],
         [(1, 6, 0, half, half), (3, 6, half, depth, 0)],
     ]
+    beyond = [[(1, d, d // 2 * depth, depth, 0) for d in (0, 2, 4)]]
     arrays = []
-    for group in (table, others, pairs):
-        arrays += [(core, parts) for core in (0, 1) for parts in group]
+    for groups in ((table, table), (others, beyond), (pairs, pairs)):
+        arrays += [(core, parts) for core in (0, 1) for parts in groups[core]]
 
     def piece(present):
         def value(refs, offset, distance, first, depth, lanes):
@@ -570,16 +570,17 @@
         name="turn",
     )(second[1], second[2], third[1], third[2])
     third += [swap(to_dx, 2, devices), swap(to_dy, 4, devices)]
-    held, *fronted = lax.optimization_barrier((third[0], *fronted))
-    third_other = other_core([held, *third[1:]])
+    late, fronted = lax.optimization_barrier((second, list(fronted)))
+    third_other = other_core(third)
+    ready += [*second, swap(join(0, *late), 1, devices)]
     middle = run_middle(
         counts,
         fronted,
         [*ready, *third[:3], *third_other[:3]],
-        view([*range(16), 16, 17, 18, 21, 22, 23]),
+        view([*range(14), 14, 15, 16, 19, 20, 21]),
     )
     weights = [*middle, *ready, *third, *third_other]
-    return fronted, weights, view(list(range(26)))
+    return fronted, weights, view(list(range(24)))
 
 
 def gather_plainly(

time: 91.8 us -> 91.5 us (level)
    ppermute x23 -> x21, waiting for transfers between devices: 29.4 us -> 30.2 us  [swap(): lax.ppermute(array, 'frame', [(f, f ^ distance) for f in range(devices)])]
    ppermute x23 -> x21, starting transfers between devices: 14.9 us -> 14.5 us  [swap(): lax.ppermute(array, 'frame', [(f, f ^ distance) for f in range(devices)])]
  transfers between devices with their start and end apart: 26 -> 24, of which waited for: 8 -> 8; matrix products, arithmetic and copies ran while one was open for 0% -> 0% of each run, Pallas kernels for 3% -> 3%
where the time goes in v14:
time: 91.5 us; the launch traced here: 91.4 us
  waiting for transfers between devices  38.4 us (42%)
  starting transfers between devices  18.6 us (20%)
  blocking collectives  17.8 us (19%)
  Pallas kernels  14 us (15%)
  between operations  1.47 us (2%)
  local copies, waits for them, and re-layouts  1.08 us (1%)
    ppermute x21, waiting for transfers between devices, swap(): lax.ppermute(array, 'frame', [(f, f ^ distance) for f in range(devices)])  30.2 us
    all_to_all x1, blocking collectives, per_device(): lax.all_to_all(back, 'frame', split_axis=0, concat_axis=0, tiled=True)  17.8 us
    ppermute x21, starting transfers between devices, swap(): lax.ppermute(array, 'frame', [(f, f ^ distance) for f in range(devices)])  14.5 us
    pallas_call x1, Pallas kernels, run_main(): pl.pallas_call(functools.partial(main_kernel, view), out_shape=jax.ShapeD...  8.35 us
    ppermute x3, waiting for transfers between devices, by_clip(): return lax.ppermute(array, 'clip', [(c, c ^ offset) for c in range(4)])  8.21 us
    ppermute x3, starting transfers between devices, by_clip(): return lax.ppermute(array, 'clip', [(c, c ^ offset) for c in range(4)])  4.17 us
    pallas_call x1, Pallas kernels, gather_in_rounds(): pl.pallas_call(functools.partial(pack_kernel, patches, share), out_shape=...  2.7 us
  transfers between devices with their start and end apart: 24, of which 8 were waited for; matrix products, arithmetic and copies ran while one was open for 0% of the time, Pallas kernels for 3%

profile of v14, /device:TPU:0, one launch (start us, length us, event | category | flops | bytes accessed | tf_op | source)
XLA Modules:
  0.0 91.4 jit_solution(1805273981694924030)
XLA Ops:
  0.6 0.0 copy-start.2
  0.6 2.7 %pack.1 = (bf16[128,1024]{1,0:T(8,128)(2,1)}, bf16[192,1024]{1,0:T(8,128)(2,1)}, bf16[64,1024]{1,0:T(8,128)(2,1)}, bf16[320,1024]{1,0:T(8,128)(2,1)}, bf16[320,1024]{1,0:T(8,128)(2,1)}) custom-call(bf16[128,768]{1,0:T(8,128)(2,1)} %refs_0_.1, bf16[128,256]{1,0:T(8,128)(2,1)} %refs_1_.1, bf16[1,1,196,1024]{3,2,1,0:T(8,128)(2,1)} %refs_2_.1, ...), custom_call_target="tpu_custom_call" | custom-call | tf_op jit(solution)/shard_map/pack/pallas_call | solution.py:459
  3.3 0.0 copy-start
  3.4 0.0 copy-start.1
  3.4 3.0 %collective-permute-start.1 = (bf16[320,1024]{1,0:T(8,128)(2,1)}, bf16[320,1024]{1,0:T(8,128)(2,1)S(1)}, u32[]{:S(2)}, u32[]{:S(2)}) collective-permute-start(bf16[320,1024]{1,0:T(8,128)(2,1)} %get-tuple-element.38), channel_id=1, source_target_pairs={{0,2},{1,3},{2,0},{3,1},{4,6},{5,7},{6,4},{7,5},{8,10},{9,11},{10,... | collective-permute-start | bytes 1966088 | tf_op jit(solution)/shard_map/ppermute | solution.py:372
  6.4 1.5 %collective-permute-start.2 = (bf16[320,1024]{1,0:T(8,128)(2,1)}, bf16[320,1024]{1,0:T(8,128)(2,1)S(1)}, u32[]{:S(2)}, u32[]{:S(2)}) collective-permute-start(bf16[320,1024]{1,0:T(8,128)(2,1)} %get-tuple-element.39), channel_id=1, source_target_pairs={{0,4},{1,5},{2,6},{3,7},{4,0},{5,1},{6,2},{7,3},{8,12},{9,13},{10,... | collective-permute-start | bytes 1966088 | tf_op jit(solution)/shard_map/ppermute | solution.py:372
  7.9 1.6 %collective-permute-start = (bf16[128,1024]{1,0:T(8,128)(2,1)}, bf16[128,1024]{1,0:T(8,128)(2,1)S(1)}, u32[]{:S(2)}, u32[]{:S(2)}) collective-permute-start(bf16[128,1024]{1,0:T(8,128)(2,1)} %get-tuple-element.37.refs_1_.rest_0_.rest_3_), channel_id=1, source_target_pairs={{0,8},{8,0},{16,24},{24,16},{1,9},{9,1},{17,25},{25,17},{2,10},{10... | collective-permute-start | bytes 786440 | tf_op jit(solution)/shard_map/ppermute | solution.py:474
  9.5 2.5 %collective-permute-start.6 = (bf16[128,1024]{1,0:T(8,128)(2,1)}, bf16[128,1024]{1,0:T(8,128)(2,1)S(1)}, u32[]{:S(2)}, u32[]{:S(2)}) collective-permute-start(bf16[128,1024]{1,0:T(8,128)(2,1)} %get-tuple-element.37.refs_1_.rest_0_.rest_3_), channel_id=1, source_target_pairs={{0,24},{8,16},{16,8},{24,0},{1,25},{9,17},{17,9},{25,1},{2,26},{10... | collective-permute-start | bytes 786440 | tf_op jit(solution)/shard_map/ppermute | solution.py:474
  11.9 0.1 collective-permute-start.5
  12.1 9.3 %collective-permute-done.1.refs_2_.rest_1_.rest_4_ = bf16[320,1024]{1,0:T(8,128)(2,1)S(1)} collective-permute-done((bf16[320,1024]{1,0:T(8,128)(2,1)}, bf16[320,1024]{1,0:T(8,128)(2,1)S(1)}, u32[]{:S(2)}, u32[]{:S(2)}) %collective-permute-start.1) | collective-permute-done | bytes 655392 | tf_op jit(solution)/shard_map/ppermute | solution.py:372
  21.3 1.8 %collective-permute-start.8 = (bf16[128,1024]{1,0:T(8,128)(2,1)S(1)}, bf16[128,1024]{1,0:T(8,128)(2,1)S(1)}, u32[]{:S(2)}, u32[]{:S(2)}) collective-permute-start(bf16[128,1024]{1,0:T(8,128)(2,1)S(1)} %slice.25), channel_id=1, source_target_pairs={{0,4},{1,5},{2,6},{3,7},{4,0},{5,1},{6,2},{7,3},{8,12},{9,13},{10,... | collective-permute-start | bytes 786440 | tf_op jit(solution)/shard_map/ppermute | solution.py:372
  23.2 0.0 collective-permute-done.2.refs_3_.rest_2_.rest_5_
  23.2 1.6 %collective-permute-start.7 = (bf16[128,1024]{1,0:T(8,128)(2,1)S(1)}, bf16[128,1024]{1,0:T(8,128)(2,1)S(1)}, u32[]{:S(2)}, u32[]{:S(2)}) collective-permute-start(bf16[128,1024]{1,0:T(8,128)(2,1)S(1)} %slice.24), channel_id=1, source_target_pairs={{0,2},{1,3},{2,0},{3,1},{4,6},{5,7},{6,4},{7,5},{8,10},{9,11},{10,... | collective-permute-start | bytes 786440 | tf_op jit(solution)/shard_map/ppermute | solution.py:372
  24.8 0.0 collective-permute-done.refs_0_.rest_10_.rest_13_
  24.8 0.5 collective-permute-start.4
  25.3 0.0 collective-permute-done.6.refs_1_
  25.3 1.1 %collective-permute-start.3 = (bf16[128,1024]{1,0:T(8,128)(2,1)S(1)}, bf16[128,1024]{1,0:T(8,128)(2,1)S(1)}, u32[]{:S(2)}, u32[]{:S(2)}) collective-permute-start(bf16[128,1024]{1,0:T(8,128)(2,1)S(1)} %collective-permute-done.refs_0_.rest_10_.rest_13_), channel_id=1, source_target_pairs={{0,2},{1,3},{2,0},{3,1},{4,6},{5,7},{6,4},{7,5},{8,10},{9,11},{10,... | collective-permute-start | bytes 786440 | tf_op jit(solution)/shard_map/ppermute | solution.py:372
  26.4 8.2 %collective-permute-done.5.refs_0_ = bf16[128,1024]{1,0:T(8,128)(2,1)S(1)} collective-permute-done((bf16[128,1024]{1,0:T(8,128)(2,1)}, bf16[128,1024]{1,0:T(8,128)(2,1)S(1)}, u32[]{:S(2)}, u32[]{:S(2)}) %collective-permute-start.5) | collective-permute-done | bytes 262176 | tf_op jit(solution)/shard_map/ppermute | solution.py:474
  34.6 0.0 collective-permute-done.8.refs_5_.rest_4_.rest_7_
  34.6 0.0 collective-permute-done.7.refs_4_.rest_3_.rest_6_
  34.7 0.6 collective-permute-start.16
  35.2 0.5 collective-permute-start.15
  35.8 0.0 collective-permute-done.4.refs_2_.rest_12_.by_y.rest_15_
  35.8 0.0 collective-permute-done.3.refs_1_.rest_11_.by_x.rest_14_
  35.8 0.0 collective-permute-start.12
  35.8 0.5 collective-permute-start.10
  36.3 0.1 collective-permute-start.11
  36.4 1.0 %collective-permute-done.12.refs_9_.rest_8_.rest_11_ = bf16[128,1024]{1,0:T(8,128)(2,1)S(1)} collective-permute-done((bf16[128,1024]{1,0:T(8,128)(2,1)S(1)}, bf16[128,1024]{1,0:T(8,128)(2,1)S(1)}, u32[]{:S(2)}, u32[]{:S(2)}) %collective-permute-start.12) | collective-permute-done | bytes 262176 | tf_op jit(solution)/shard_map/ppermute | solution.py:372
  37.3 0.1 collective-permute-start.9
  37.5 9.5 %collective-permute-done.16.rest_16_.pair_y.rest_19_ = bf16[256,1024]{1,0:T(8,128)(2,1)S(1)} collective-permute-done((bf16[256,1024]{1,0:T(8,128)(2,1)S(1)}, bf16[256,1024]{1,0:T(8,128)(2,1)S(1)}, u32[]{:S(2)}, u32[]{:S(2)}) %collective-permute-start.16) | collective-permute-done | bytes 524320 | tf_op jit(solution)/shard_map/ppermute | solution.py:372
  46.9 0.0 collective-permute-start.13
  46.9 0.2 collective-permute-done.15.rest_15_.pair_x.rest_18_
  47.1 0.3 collective-permute-start.17
  47.4 0.1 turn.1
  47.5 1.0 %collective-permute-done.13.refs_10_.rest_9_.rest_12_ = bf16[128,1024]{1,0:T(8,128)(2,1)S(1)} collective-permute-done((bf16[128,1024]{1,0:T(8,128)(2,1)S(1)}, bf16[128,1024]{1,0:T(8,128)(2,1)S(1)}, u32[]{:S(2)}, u32[]{:S(2)}) %collective-permute-start.13) | collective-permute-done | bytes 262176 | tf_op jit(solution)/shard_map/ppermute | solution.py:372
  48.4 0.0 collective-permute-done.9.refs_6_.rest_5_.rest_8_
  48.4 0.0 collective-permute-done.10.refs_7_.rest_6_.rest_9_
  48.4 0.0 collective-permute-done.11.refs_8_.rest_7_.rest_10_
  48.5 0.0 copy-done.2
  48.5 0.0 copy-done
  48.5 0.0 copy-done.1
  48.5 1.1 %front.1 = (bf16[8,2,32,1024]{3,2,1,0:T(8,128)(2,1)S(1)}, bf16[256,1024]{1,0:T(8,128)(2,1)S(1)}, f32[256,128]{1,0:T(8,128)S(1)}, bf16[256,768]{1,0:T(8,128)(2,1)S(1)}) custom-call(f32[1,1024]{1,0:T(1,128)S(1)} %bitcast.11, bf16[64,1024]{1,0:T(8,128)(2,1)S(1)} %copy-done.1, bf16[128,1024]{1,0:T(8,128)(2,1)S(1)} %copy-done, ...), custom_call_target="tpu_custom_call" | custom-call | flops 256 | bytes 256 | tf_op jit(solution)/shard_map/front/pallas_call | solution.py:289
  49.6 0.1 join.2
  49.7 0.2 collective-permute-start.14
  49.9 0.5 collective-permute-start.20
  50.4 1.2 %collective-permute-start.21 = (bf16[192,1024]{1,0:T(8,128)(2,1)S(1)}, bf16[192,1024]{1,0:T(8,128)(2,1)S(1)}, u32[]{:S(2)}, u32[]{:S(2)}) collective-permute-start(bf16[192,1024]{1,0:T(8,128)(2,1)S(1)} %get-tuple-element.71), channel_id=1, source_target_pairs={{0,4},{1,5},{2,6},{3,7},{4,0},{5,1},{6,2},{7,3},{8,12},{9,13},{10,... | collective-permute-start | bytes 1179656 | tf_op jit(solution)/shard_map/ppermute | solution.py:372
  51.7 0.0 collective-permute-start.19
  51.7 0.0 collective-permute-done.17.rest_17_.rest_22_
  51.7 0.5 collective-permute-start.18
  52.2 9.1 %collective-permute-done.20.rest_20_ = bf16[192,1024]{1,0:T(8,128)(2,1)S(1)} collective-permute-done((bf16[192,1024]{1,0:T(8,128)(2,1)S(1)}, bf16[192,1024]{1,0:T(8,128)(2,1)S(1)}, u32[]{:S(2)}, u32[]{:S(2)}) %collective-permute-start.20) | collective-permute-done | bytes 393248 | tf_op jit(solution)/shard_map/ppermute | solution.py:372
  61.3 0.0 collective-permute-start.22
  61.3 0.2 collective-permute-done.21.rest_21_
  61.5 0.3 collective-permute-start.23
  62.4 0.0 collective-permute-done.19.rest_19_.rest_24_
  62.4 0.0 collective-permute-done.18.rest_18_.rest_23_
  62.5 0.0 collective-permute-done.14.rest_13_.rest_16_
  62.5 1.7 %middle.1 = (bf16[256,1024]{1,0:T(8,128)(2,1)S(1)}, bf16[256,1024]{1,0:T(8,128)(2,1)S(1)}, f32[256,2304]{1,0:T(8,128)S(1)}) custom-call(s32[1]{0:T(128)S(6)} %copy.9.counts_ref, bf16[8,2,32,1024]{3,2,1,0:T(8,128)(2,1)S(1)} %get-tuple-element.58.both_ref, bf16[256,1024]{1,0:T(8,128)(2,1)S(1)} %get-tuple-element.59.normed_ref, bf16[128,1024]{1,0:T(8,128)(2,1)S(1)} %copy-done, ...), custom_call_target="tpu_custom_call" | custom-call | flops 256 | bytes 256 | tf_op jit(solution)/shard_map/middle/pallas_call | solution.py:311
  64.2 0.0 collective-permute-done.22.rest_25_
  64.2 0.0 collective-permute-done.23.rest_26_
  64.2 8.4 %main.1 = bf16[8,2,32,1024]{3,2,1,0:T(8,128)(2,1)S(1)} custom-call(s32[1]{0:T(128)S(6)} %copy.9.counts_ref, f32[1,1024]{1,0:T(1,128)S(1)} %bitcast.12, bf16[8,2,32,1024]{3,2,1,0:T(8,128)(2,1)S(1)} %get-tuple-element.58.both_ref, bf16[256,1024]{1,0:T(8,128)(2,1)S(1)} %get-tuple-element.59.normed_ref, f32[256,128]{1,0:T(8,128)S(1)} %get-tuple-element.60.stats_ref, ...), custom_call_target="tpu_custom_call" | custom-call | flops 3221225472 | bytes 10485760 | tf_op jit(solution)/shard_map/main/pallas_call | solution.py:334
  72.5 17.8 %all_to_all.5 = bf16[8,1,2,32,1024]{4,3,2,1,0:T(8,128)(2,1)S(1)} all-to-all(bf16[8,1,2,32,1024]{4,3,2,1,0:T(8,128)(2,1)S(1)} %bitcast.10), channel_id=1, replica_groups=mesh['clip'=4,'frame'=8] {'frame'}, dimensions={0} | all-to-all | bytes 2097152 | tf_op jit(solution)/shard_map/all_to_all | solution.py:644
  90.3 0.1 fusion
  90.4 0.9 %slice_bitcast_fusion = (bf16[1,1,196,1024]{3,2,1,0:T(8,128)(2,1)}, bf16[1,1,196,1024]{3,2,1,0:T(8,128)(2,1)}) fusion(bf16[1,256,1024]{2,1,0:T(8,128)(2,1)S(1)} %bitcast.13, bf16[1,256,1024]{2,1,0:T(8,128)(2,1)S(1)} %bitcast.14), kind=kLoop, calls=%fused_computation | loop fusion | bytes 1605632 | tf_op jit(solution)/shard_map/broadcast_in_dim | solution.py:648
  (3 shorter events, 0.1 us)
Async XLA Ops:
  0.6 47.8 %copy-start.2 = (f32[1024]{0:T(1024)S(1)}, f32[1024]{0:T(1024)}, u32[]{:S(2)}) copy-start(f32[1024]{0:T(1024)} %param.8) | copy-start | bytes 12292
  3.3 45.1 %copy-start = (bf16[128,1024]{1,0:T(8,128)(2,1)S(1)}, bf16[128,1024]{1,0:T(8,128)(2,1)}, u32[]{:S(2)}) copy-start(bf16[128,1024]{1,0:T(8,128)(2,1)} %get-tuple-element.37.refs_1_.rest_0_.rest_3_) | copy-start | bytes 786436
  3.4 45.1 %copy-start.1 = (bf16[64,1024]{1,0:T(8,128)(2,1)S(1)}, bf16[64,1024]{1,0:T(8,128)(2,1)}, u32[]{:S(2)}) copy-start(bf16[64,1024]{1,0:T(8,128)(2,1)} %get-tuple-element.48.refs_0_) | copy-start | bytes 393220
  3.4 17.9 %collective-permute-start.1 = (bf16[320,1024]{1,0:T(8,128)(2,1)}, bf16[320,1024]{1,0:T(8,128)(2,1)S(1)}, u32[]{:S(2)}, u32[]{:S(2)}) collective-permute-start(bf16[320,1024]{1,0:T(8,128)(2,1)} %get-tuple-element.38), channel_id=1, source_target_pairs={{0,2},{1,3},{2,0},{3,1},{4,6},{5,7},{6,4},{7,5},{8,10},{9,11},{10,... | collective-permute-start | bytes 1966088 | tf_op jit(solution)/shard_map/ppermute | solution.py:372
  6.4 16.8 %collective-permute-start.2 = (bf16[320,1024]{1,0:T(8,128)(2,1)}, bf16[320,1024]{1,0:T(8,128)(2,1)S(1)}, u32[]{:S(2)}, u32[]{:S(2)}) collective-permute-start(bf16[320,1024]{1,0:T(8,128)(2,1)} %get-tuple-element.39), channel_id=1, source_target_pairs={{0,4},{1,5},{2,6},{3,7},{4,0},{5,1},{6,2},{7,3},{8,12},{9,13},{10,... | collective-permute-start | bytes 1966088 | tf_op jit(solution)/shard_map/ppermute | solution.py:372
  7.9 16.9 %collective-permute-start = (bf16[128,1024]{1,0:T(8,128)(2,1)}, bf16[128,1024]{1,0:T(8,128)(2,1)S(1)}, u32[]{:S(2)}, u32[]{:S(2)}) collective-permute-start(bf16[128,1024]{1,0:T(8,128)(2,1)} %get-tuple-element.37.refs_1_.rest_0_.rest_3_), channel_id=1, source_target_pairs={{0,8},{8,0},{16,24},{24,16},{1,9},{9,1},{17,25},{25,17},{2,10},{10... | collective-permute-start | bytes 786440 | tf_op jit(solution)/shard_map/ppermute | solution.py:474
  9.5 15.8 %collective-permute-start.6 = (bf16[128,1024]{1,0:T(8,128)(2,1)}, bf16[128,1024]{1,0:T(8,128)(2,1)S(1)}, u32[]{:S(2)}, u32[]{:S(2)}) collective-permute-start(bf16[128,1024]{1,0:T(8,128)(2,1)} %get-tuple-element.37.refs_1_.rest_0_.rest_3_), channel_id=1, source_target_pairs={{0,24},{8,16},{16,8},{24,0},{1,25},{9,17},{17,9},{25,1},{2,26},{10... | collective-permute-start | bytes 786440 | tf_op jit(solution)/shard_map/ppermute | solution.py:474
  11.9 22.7 %collective-permute-start.5 = (bf16[128,1024]{1,0:T(8,128)(2,1)}, bf16[128,1024]{1,0:T(8,128)(2,1)S(1)}, u32[]{:S(2)}, u32[]{:S(2)}) collective-permute-start(bf16[128,1024]{1,0:T(8,128)(2,1)} %get-tuple-element.37.refs_1_.rest_0_.rest_3_), channel_id=1, source_target_pairs={{0,16},{8,24},{16,0},{24,8},{1,17},{9,25},{17,1},{25,9},{2,18},{10... | collective-permute-start | bytes 786440 | tf_op jit(solution)/shard_map/ppermute | solution.py:474
  21.3 13.3 %collective-permute-start.8 = (bf16[128,1024]{1,0:T(8,128)(2,1)S(1)}, bf16[128,1024]{1,0:T(8,128)(2,1)S(1)}, u32[]{:S(2)}, u32[]{:S(2)}) collective-permute-start(bf16[128,1024]{1,0:T(8,128)(2,1)S(1)} %slice.25), channel_id=1, source_target_pairs={{0,4},{1,5},{2,6},{3,7},{4,0},{5,1},{6,2},{7,3},{8,12},{9,13},{10,... | collective-permute-start | bytes 786440 | tf_op jit(solution)/shard_map/ppermute | solution.py:372
  23.2 11.4 %collective-permute-start.7 = (bf16[128,1024]{1,0:T(8,128)(2,1)S(1)}, bf16[128,1024]{1,0:T(8,128)(2,1)S(1)}, u32[]{:S(2)}, u32[]{:S(2)}) collective-permute-start(bf16[128,1024]{1,0:T(8,128)(2,1)S(1)} %slice.24), channel_id=1, source_target_pairs={{0,2},{1,3},{2,0},{3,1},{4,6},{5,7},{6,4},{7,5},{8,10},{9,11},{10,... | collective-permute-start | bytes 786440 | tf_op jit(solution)/shard_map/ppermute | solution.py:372
  24.8 11.0 %collective-permute-start.4 = (bf16[128,1024]{1,0:T(8,128)(2,1)S(1)}, bf16[128,1024]{1,0:T(8,128)(2,1)S(1)}, u32[]{:S(2)}, u32[]{:S(2)}) collective-permute-start(bf16[128,1024]{1,0:T(8,128)(2,1)S(1)} %collective-permute-done.refs_0_.rest_10_.rest_13_), channel_id=1, source_target_pairs={{0,4},{1,5},{2,6},{3,7},{4,0},{5,1},{6,2},{7,3},{8,12},{9,13},{10,... | collective-permute-start | bytes 786440 | tf_op jit(solution)/shard_map/ppermute | solution.py:372
  25.3 10.5 %collective-permute-start.3 = (bf16[128,1024]{1,0:T(8,128)(2,1)S(1)}, bf16[128,1024]{1,0:T(8,128)(2,1)S(1)}, u32[]{:S(2)}, u32[]{:S(2)}) collective-permute-start(bf16[128,1024]{1,0:T(8,128)(2,1)S(1)} %collective-permute-done.refs_0_.rest_10_.rest_13_), channel_id=1, source_target_pairs={{0,2},{1,3},{2,0},{3,1},{4,6},{5,7},{6,4},{7,5},{8,10},{9,11},{10,... | collective-permute-start | bytes 786440 | tf_op jit(solution)/shard_map/ppermute | solution.py:372
  34.7 12.2 %collective-permute-start.16 = (bf16[256,1024]{1,0:T(8,128)(2,1)S(1)}, bf16[256,1024]{1,0:T(8,128)(2,1)S(1)}, u32[]{:S(2)}, u32[]{:S(2)}) collective-permute-start(bf16[256,1024]{1,0:T(8,128)(2,1)S(1)} %join.3.rest_14_.rest_17_), channel_id=1, source_target_pairs={{0,4},{1,5},{2,6},{3,7},{4,0},{5,1},{6,2},{7,3},{8,12},{9,13},{10,... | collective-permute-start | bytes 1572872 | tf_op jit(solution)/shard_map/ppermute | solution.py:372
  35.2 11.9 %collective-permute-start.15 = (bf16[256,1024]{1,0:T(8,128)(2,1)S(1)}, bf16[256,1024]{1,0:T(8,128)(2,1)S(1)}, u32[]{:S(2)}, u32[]{:S(2)}) collective-permute-start(bf16[256,1024]{1,0:T(8,128)(2,1)S(1)} %join.3.rest_14_.rest_17_), channel_id=1, source_target_pairs={{0,2},{1,3},{2,0},{3,1},{4,6},{5,7},{6,4},{7,5},{8,10},{9,11},{10,... | collective-permute-start | bytes 1572872 | tf_op jit(solution)/shard_map/ppermute | solution.py:372
  35.8 1.5 %collective-permute-start.12 = (bf16[128,1024]{1,0:T(8,128)(2,1)S(1)}, bf16[128,1024]{1,0:T(8,128)(2,1)S(1)}, u32[]{:S(2)}, u32[]{:S(2)}) collective-permute-start(bf16[128,1024]{1,0:T(8,128)(2,1)S(1)} %collective-permute-done.7.refs_4_.rest_3_.rest_6_), channel_id=1, source_target_pairs={{0,1},{1,0},{2,3},{3,2},{4,5},{5,4},{6,7},{7,6},{8,9},{9,8},{10,11... | collective-permute-start | bytes 786440 | tf_op jit(solution)/shard_map/ppermute | solution.py:372
  35.8 12.7 %collective-permute-start.10 = (bf16[320,1024]{1,0:T(8,128)(2,1)S(1)}, bf16[320,1024]{1,0:T(8,128)(2,1)S(1)}, u32[]{:S(2)}, u32[]{:S(2)}) collective-permute-start(bf16[320,1024]{1,0:T(8,128)(2,1)S(1)} %collective-permute-done.1.refs_2_.rest_1_.rest_4_), channel_id=1, source_target_pairs={{0,1},{1,0},{2,3},{3,2},{4,5},{5,4},{6,7},{7,6},{8,9},{9,8},{10,11... | collective-permute-start | bytes 1966088 | tf_op jit(solution)/shard_map/ppermute | solution.py:372
  36.3 12.2 %collective-permute-start.11 = (bf16[320,1024]{1,0:T(8,128)(2,1)S(1)}, bf16[320,1024]{1,0:T(8,128)(2,1)S(1)}, u32[]{:S(2)}, u32[]{:S(2)}) collective-permute-start(bf16[320,1024]{1,0:T(8,128)(2,1)S(1)} %collective-permute-done.2.refs_3_.rest_2_.rest_5_), channel_id=1, source_target_pairs={{0,1},{1,0},{2,3},{3,2},{4,5},{5,4},{6,7},{7,6},{8,9},{9,8},{10,11... | collective-permute-start | bytes 1966088 | tf_op jit(solution)/shard_map/ppermute | solution.py:372
  37.3 11.1 %collective-permute-start.9 = (bf16[192,1024]{1,0:T(8,128)(2,1)}, bf16[192,1024]{1,0:T(8,128)(2,1)S(1)}, u32[]{:S(2)}, u32[]{:S(2)}) collective-permute-start(bf16[192,1024]{1,0:T(8,128)(2,1)} %get-tuple-element.53), channel_id=1, source_target_pairs={{0,1},{1,0},{2,3},{3,2},{4,5},{5,4},{6,7},{7,6},{8,9},{9,8},{10,11... | collective-permute-start | bytes 1179656 | tf_op jit(solution)/shard_map/ppermute | solution.py:372
  46.9 1.5 %collective-permute-start.13 = (bf16[128,1024]{1,0:T(8,128)(2,1)S(1)}, bf16[128,1024]{1,0:T(8,128)(2,1)S(1)}, u32[]{:S(2)}, u32[]{:S(2)}) collective-permute-start(bf16[128,1024]{1,0:T(8,128)(2,1)S(1)} %collective-permute-done.8.refs_5_.rest_4_.rest_7_), channel_id=1, source_target_pairs={{0,1},{1,0},{2,3},{3,2},{4,5},{5,4},{6,7},{7,6},{8,9},{9,8},{10,11... | collective-permute-start | bytes 786440 | tf_op jit(solution)/shard_map/ppermute | solution.py:372
  47.1 4.5 %collective-permute-start.17 = (bf16[256,1024]{1,0:T(8,128)(2,1)S(1)}, bf16[256,1024]{1,0:T(8,128)(2,1)S(1)}, u32[]{:S(2)}, u32[]{:S(2)}) collective-permute-start(bf16[256,1024]{1,0:T(8,128)(2,1)S(1)} %join.3.rest_14_.rest_17_), channel_id=1, source_target_pairs={{0,1},{1,0},{2,3},{3,2},{4,5},{5,4},{6,7},{7,6},{8,9},{9,8},{10,11... | collective-permute-start | bytes 1572872 | tf_op jit(solution)/shard_map/ppermute | solution.py:372
  49.7 12.8 %collective-permute-start.14 = (bf16[384,1024]{1,0:T(8,128)(2,1)S(1)}, bf16[384,1024]{1,0:T(8,128)(2,1)S(1)}, u32[]{:S(2)}, u32[]{:S(2)}) collective-permute-start(bf16[384,1024]{1,0:T(8,128)(2,1)S(1)} %join.2), channel_id=1, source_target_pairs={{0,1},{1,0},{2,3},{3,2},{4,5},{5,4},{6,7},{7,6},{8,9},{9,8},{10,11... | collective-permute-start | bytes 2359304 | tf_op jit(solution)/shard_map/ppermute | solution.py:372
  49.9 11.4 %collective-permute-start.20 = (bf16[192,1024]{1,0:T(8,128)(2,1)S(1)}, bf16[192,1024]{1,0:T(8,128)(2,1)S(1)}, u32[]{:S(2)}, u32[]{:S(2)}) collective-permute-start(bf16[192,1024]{1,0:T(8,128)(2,1)S(1)} %get-tuple-element.70), channel_id=1, source_target_pairs={{0,2},{1,3},{2,0},{3,1},{4,6},{5,7},{6,4},{7,5},{8,10},{9,11},{10,... | collective-permute-start | bytes 1179656 | tf_op jit(solution)/shard_map/ppermute | solution.py:372
  50.4 11.1 %collective-permute-start.21 = (bf16[192,1024]{1,0:T(8,128)(2,1)S(1)}, bf16[192,1024]{1,0:T(8,128)(2,1)S(1)}, u32[]{:S(2)}, u32[]{:S(2)}) collective-permute-start(bf16[192,1024]{1,0:T(8,128)(2,1)S(1)} %get-tuple-element.71), channel_id=1, source_target_pairs={{0,4},{1,5},{2,6},{3,7},{4,0},{5,1},{6,2},{7,3},{8,12},{9,13},{10,... | collective-permute-start | bytes 1179656 | tf_op jit(solution)/shard_map/ppermute | solution.py:372
  51.7 10.8 %collective-permute-start.19 = (bf16[256,1024]{1,0:T(8,128)(2,1)S(1)}, bf16[256,1024]{1,0:T(8,128)(2,1)S(1)}, u32[]{:S(2)}, u32[]{:S(2)}) collective-permute-start(bf16[256,1024]{1,0:T(8,128)(2,1)S(1)} %collective-permute-done.16.rest_16_.pair_y.rest_19_), channel_id=1, source_target_pairs={{0,1},{1,0},{2,3},{3,2},{4,5},{5,4},{6,7},{7,6},{8,9},{9,8},{10,11... | collective-permute-start | bytes 1572872 | tf_op jit(solution)/shard_map/ppermute | solution.py:372
  51.7 10.8 %collective-permute-start.18 = (bf16[256,1024]{1,0:T(8,128)(2,1)S(1)}, bf16[256,1024]{1,0:T(8,128)(2,1)S(1)}, u32[]{:S(2)}, u32[]{:S(2)}) collective-permute-start(bf16[256,1024]{1,0:T(8,128)(2,1)S(1)} %collective-permute-done.15.rest_15_.pair_x.rest_18_), channel_id=1, source_target_pairs={{0,1},{1,0},{2,3},{3,2},{4,5},{5,4},{6,7},{7,6},{8,9},{9,8},{10,11... | collective-permute-start | bytes 1572872 | tf_op jit(solution)/shard_map/ppermute | solution.py:372
  61.3 2.9 %collective-permute-start.22 = (bf16[192,1024]{1,0:T(8,128)(2,1)S(1)}, bf16[192,1024]{1,0:T(8,128)(2,1)S(1)}, u32[]{:S(2)}, u32[]{:S(2)}) collective-permute-start(bf16[192,1024]{1,0:T(8,128)(2,1)S(1)} %collective-permute-done.20.rest_20_), channel_id=1, source_target_pairs={{0,1},{1,0},{2,3},{3,2},{4,5},{5,4},{6,7},{7,6},{8,9},{9,8},{10,11... | collective-permute-start | bytes 1179656 | tf_op jit(solution)/shard_map/ppermute | solution.py:372
  61.5 2.6 %collective-permute-start.23 = (bf16[192,1024]{1,0:T(8,128)(2,1)S(1)}, bf16[192,1024]{1,0:T(8,128)(2,1)S(1)}, u32[]{:S(2)}, u32[]{:S(2)}) collective-permute-start(bf16[192,1024]{1,0:T(8,128)(2,1)S(1)} %collective-permute-done.21.rest_21_), channel_id=1, source_target_pairs={{0,1},{1,0},{2,3},{3,2},{4,5},{5,4},{6,7},{7,6},{8,9},{9,8},{10,11... | collective-permute-start | bytes 1179656 | tf_op jit(solution)/shard_map/ppermute | solution.py:372

commit v15 on v9

--- a/solution.py
+++ b/solution.py
@@ -147,7 +147,7 @@
         return pl.ds(pl.multiple_of(part * width + pair * PAIR, PAIR), PAIR)
 
     chunk = scores.shape[0]
-    unroll = min(chunk, 4)
+    unroll = min(chunk, 8)
 
     def each(body):
         @pl.loop(0, chunk // unroll)

time: 91.5 us -> 89.6 us (0.979)
  Pallas kernels: 13.8 us -> 11.9 us
    pallas_call x1, Pallas kernels: 9.91 us -> 8.01 us  [run_main(): pl.pallas_call(functools.partial(main_kernel, view), out_shape=jax.ShapeD...]
where the time goes in v15:
time: 89.6 us; the launch traced here: 89.4 us
  waiting for transfers between devices  37.8 us (42%)
  starting transfers between devices  19.2 us (21%)
  blocking collectives  18 us (20%)
  Pallas kernels  11.9 us (13%)
  between operations  1.44 us (2%)
  local copies, waits for them, and re-layouts  1.08 us (1%)
    ppermute x23, waiting for transfers between devices, swap(): lax.ppermute(array, 'frame', [(f, f ^ distance) for f in range(devices)])  29.6 us
    all_to_all x1, blocking collectives, per_device(): lax.all_to_all(back, 'frame', split_axis=0, concat_axis=0, tiled=True)  18 us
    ppermute x23, starting transfers between devices, swap(): lax.ppermute(array, 'frame', [(f, f ^ distance) for f in range(devices)])  15 us
    ppermute x3, waiting for transfers between devices, by_clip(): return lax.ppermute(array, 'clip', [(c, c ^ offset) for c in range(4)])  8.19 us
    pallas_call x1, Pallas kernels, run_main(): pl.pallas_call(functools.partial(main_kernel, view), out_shape=jax.ShapeD...  8.01 us
    ppermute x3, starting transfers between devices, by_clip(): return lax.ppermute(array, 'clip', [(c, c ^ offset) for c in range(4)])  4.17 us
    pallas_call x1, Pallas kernels, gather_in_rounds(): pl.pallas_call(functools.partial(pack_kernel, patches, share), out_shape=...  2.68 us
  transfers between devices with their start and end apart: 26, of which 9 were waited for; matrix products, arithmetic and copies ran while one was open for 0% of the time, Pallas kernels for 1%

profile of v15, /device:TPU:0, one launch (start us, length us, event | category | flops | bytes accessed | tf_op | source)
XLA Modules:
  0.0 89.4 jit_solution(12068056296660569908)
XLA Ops:
  0.6 2.7 %pack.1 = (bf16[128,1024]{1,0:T(8,128)(2,1)}, bf16[192,1024]{1,0:T(8,128)(2,1)}, bf16[64,1024]{1,0:T(8,128)(2,1)}, bf16[320,1024]{1,0:T(8,128)(2,1)}, bf16[320,1024]{1,0:T(8,128)(2,1)}) custom-call(bf16[128,768]{1,0:T(8,128)(2,1)} %refs_0_.1, bf16[128,256]{1,0:T(8,128)(2,1)} %refs_1_.1, bf16[1,1,196,1024]{3,2,1,0:T(8,128)(2,1)} %refs_2_.1, ...), custom_call_target="tpu_custom_call" | custom-call | tf_op jit(solution)/shard_map/pack/pallas_call | solution.py:386
  3.3 3.0 %collective-permute-start.1 = (bf16[320,1024]{1,0:T(8,128)(2,1)}, bf16[320,1024]{1,0:T(8,128)(2,1)S(1)}, u32[]{:S(2)}, u32[]{:S(2)}) collective-permute-start(bf16[320,1024]{1,0:T(8,128)(2,1)} %get-tuple-element.33), channel_id=1, source_target_pairs={{0,2},{1,3},{2,0},{3,1},{4,6},{5,7},{6,4},{7,5},{8,10},{9,11},{10,... | collective-permute-start | bytes 1966088 | tf_op jit(solution)/shard_map/ppermute | solution.py:301
  6.3 1.5 %collective-permute-start.2 = (bf16[320,1024]{1,0:T(8,128)(2,1)}, bf16[320,1024]{1,0:T(8,128)(2,1)S(1)}, u32[]{:S(2)}, u32[]{:S(2)}) collective-permute-start(bf16[320,1024]{1,0:T(8,128)(2,1)} %get-tuple-element.34), channel_id=1, source_target_pairs={{0,4},{1,5},{2,6},{3,7},{4,0},{5,1},{6,2},{7,3},{8,12},{9,13},{10,... | collective-permute-start | bytes 1966088 | tf_op jit(solution)/shard_map/ppermute | solution.py:301
  7.8 1.6 %collective-permute-start = (bf16[128,1024]{1,0:T(8,128)(2,1)}, bf16[128,1024]{1,0:T(8,128)(2,1)S(1)}, u32[]{:S(2)}, u32[]{:S(2)}) collective-permute-start(bf16[128,1024]{1,0:T(8,128)(2,1)} %get-tuple-element.32.refs_1_.rest_0_), channel_id=1, source_target_pairs={{0,8},{8,0},{16,24},{24,16},{1,9},{9,1},{17,25},{25,17},{2,10},{10... | collective-permute-start | bytes 786440 | tf_op jit(solution)/shard_map/ppermute | solution.py:401
  9.4 2.5 %collective-permute-start.6 = (bf16[128,1024]{1,0:T(8,128)(2,1)}, bf16[128,1024]{1,0:T(8,128)(2,1)S(1)}, u32[]{:S(2)}, u32[]{:S(2)}) collective-permute-start(bf16[128,1024]{1,0:T(8,128)(2,1)} %get-tuple-element.32.refs_1_.rest_0_), channel_id=1, source_target_pairs={{0,24},{8,16},{16,8},{24,0},{1,25},{9,17},{17,9},{25,1},{2,26},{10... | collective-permute-start | bytes 786440 | tf_op jit(solution)/shard_map/ppermute | solution.py:401
  11.9 0.1 collective-permute-start.5
  12.0 9.3 %collective-permute-done.1.refs_2_.rest_1_ = bf16[320,1024]{1,0:T(8,128)(2,1)S(1)} collective-permute-done((bf16[320,1024]{1,0:T(8,128)(2,1)}, bf16[320,1024]{1,0:T(8,128)(2,1)S(1)}, u32[]{:S(2)}, u32[]{:S(2)}) %collective-permute-start.1) | collective-permute-done | bytes 655392 | tf_op jit(solution)/shard_map/ppermute | solution.py:301
  21.3 1.8 %collective-permute-start.8 = (bf16[128,1024]{1,0:T(8,128)(2,1)S(1)}, bf16[128,1024]{1,0:T(8,128)(2,1)S(1)}, u32[]{:S(2)}, u32[]{:S(2)}) collective-permute-start(bf16[128,1024]{1,0:T(8,128)(2,1)S(1)} %slice.25), channel_id=1, source_target_pairs={{0,4},{1,5},{2,6},{3,7},{4,0},{5,1},{6,2},{7,3},{8,12},{9,13},{10,... | collective-permute-start | bytes 786440 | tf_op jit(solution)/shard_map/ppermute | solution.py:301
  23.1 0.0 collective-permute-done.2.refs_3_.rest_2_
  23.2 0.0 copy-start.3
  23.2 1.6 %collective-permute-start.7 = (bf16[128,1024]{1,0:T(8,128)(2,1)S(1)}, bf16[128,1024]{1,0:T(8,128)(2,1)S(1)}, u32[]{:S(2)}, u32[]{:S(2)}) collective-permute-start(bf16[128,1024]{1,0:T(8,128)(2,1)S(1)} %slice.24), channel_id=1, source_target_pairs={{0,2},{1,3},{2,0},{3,1},{4,6},{5,7},{6,4},{7,5},{8,10},{9,11},{10,... | collective-permute-start | bytes 786440 | tf_op jit(solution)/shard_map/ppermute | solution.py:301
  24.7 0.0 collective-permute-done.rest_10_
  24.7 0.5 collective-permute-start.4
  25.2 0.0 collective-permute-done.6.refs_1_
  25.2 1.1 %collective-permute-start.3 = (bf16[128,1024]{1,0:T(8,128)(2,1)S(1)}, bf16[128,1024]{1,0:T(8,128)(2,1)S(1)}, u32[]{:S(2)}, u32[]{:S(2)}) collective-permute-start(bf16[128,1024]{1,0:T(8,128)(2,1)S(1)} %collective-permute-done.rest_10_), channel_id=1, source_target_pairs={{0,2},{1,3},{2,0},{3,1},{4,6},{5,7},{6,4},{7,5},{8,10},{9,11},{10,... | collective-permute-start | bytes 786440 | tf_op jit(solution)/shard_map/ppermute | solution.py:301
  26.4 8.2 %collective-permute-done.5.refs_0_ = bf16[128,1024]{1,0:T(8,128)(2,1)S(1)} collective-permute-done((bf16[128,1024]{1,0:T(8,128)(2,1)}, bf16[128,1024]{1,0:T(8,128)(2,1)S(1)}, u32[]{:S(2)}, u32[]{:S(2)}) %collective-permute-start.5) | collective-permute-done | bytes 262176 | tf_op jit(solution)/shard_map/ppermute | solution.py:401
  34.6 0.0 collective-permute-done.8.refs_5_.rest_4_
  34.6 0.0 collective-permute-done.7.refs_4_.rest_3_
  34.6 0.6 collective-permute-start.10
  35.2 0.5 collective-permute-start.9
  35.7 0.0 collective-permute-start.17
  35.7 0.0 collective-permute-done.4.by_y.rest_12_
  35.7 0.0 collective-permute-done.3.by_x.rest_11_
  35.8 0.0 copy-start.1
  35.8 0.6 collective-permute-start.18
  36.3 0.1 collective-permute-start.13
  36.4 0.9 collective-permute-done.17.rest_13_
  37.3 0.1 collective-permute-start.14
  37.4 0.2 collective-permute-done.18.rest_14_
  37.6 0.2 collective-permute-start.15
  37.9 9.0 %collective-permute-done.10.pair_y.rest_18_ = bf16[256,1024]{1,0:T(8,128)(2,1)S(1)} collective-permute-done((bf16[256,1024]{1,0:T(8,128)(2,1)S(1)}, bf16[256,1024]{1,0:T(8,128)(2,1)S(1)}, u32[]{:S(2)}, u32[]{:S(2)}) %collective-permute-start.10) | collective-permute-done | bytes 524320 | tf_op jit(solution)/shard_map/ppermute | solution.py:301
  46.9 0.0 collective-permute-start.16
  46.9 0.2 collective-permute-done.9.pair_x.rest_17_
  47.1 0.0 copy-done.3
  47.1 0.3 collective-permute-start.12
  47.4 0.1 turn.1
  47.4 0.0 copy-start.2
  47.4 0.0 collective-permute-done.15.refs_9_.rest_8_
  47.5 1.2 %collective-permute-start.11 = (bf16[192,1024]{1,0:T(8,128)(2,1)S(1)}, bf16[192,1024]{1,0:T(8,128)(2,1)S(1)}, u32[]{:S(2)}, u32[]{:S(2)}) collective-permute-start(bf16[192,1024]{1,0:T(8,128)(2,1)S(1)} %get-tuple-element.45), channel_id=1, source_target_pairs={{0,2},{1,3},{2,0},{3,1},{4,6},{5,7},{6,4},{7,5},{8,10},{9,11},{10,... | collective-permute-start | bytes 1179656 | tf_op jit(solution)/shard_map/ppermute | solution.py:301
  48.6 0.0 collective-permute-done.16.refs_10_.rest_9_
  48.6 0.7 collective-permute-start.20
  49.3 0.0 collective-permute-done.12.refs_6_.rest_5_
  49.3 0.0 collective-permute-start.19
  49.3 0.0 collective-permute-done.13.refs_7_.rest_6_
  49.3 0.5 collective-permute-start.21
  49.8 0.0 collective-permute-done.14.refs_8_.rest_7_
  49.8 0.1 collective-permute-start.23
  49.9 8.9 %collective-permute-done.11.rest_19_ = bf16[192,1024]{1,0:T(8,128)(2,1)S(1)} collective-permute-done((bf16[192,1024]{1,0:T(8,128)(2,1)S(1)}, bf16[192,1024]{1,0:T(8,128)(2,1)S(1)}, u32[]{:S(2)}, u32[]{:S(2)}) %collective-permute-start.11) | collective-permute-done | bytes 393248 | tf_op jit(solution)/shard_map/ppermute | solution.py:301
  58.8 0.0 collective-permute-start.22
  58.8 0.0 copy-done
  58.8 1.1 %front.1 = (bf16[8,2,32,1024]{3,2,1,0:T(8,128)(2,1)S(1)}, bf16[256,1024]{1,0:T(8,128)(2,1)S(1)}, f32[256,128]{1,0:T(8,128)S(1)}, bf16[256,768]{1,0:T(8,128)(2,1)S(1)}) custom-call(f32[1,1024]{1,0:T(1,128)S(1)} %bitcast.11, bf16[64,1024]{1,0:T(8,128)(2,1)S(1)} %copy-done.1, bf16[128,1024]{1,0:T(8,128)(2,1)S(1)} %copy-done, ...), custom_call_target="tpu_custom_call" | custom-call | flops 256 | bytes 256 | tf_op jit(solution)/shard_map/front/pallas_call | solution.py:239
  59.9 0.0 collective-permute-done.20.rest_20_
  59.9 0.6 collective-permute-start.25
  60.5 0.0 collective-permute-done.19.rest_15_
  60.5 0.1 collective-permute-start.24
  61.2 0.0 collective-permute-done.21.rest_21_
  61.2 0.0 collective-permute-done.23.rest_23_
  61.2 0.0 collective-permute-done.22.rest_22_
  61.3 0.6 collective-permute-done.25.rest_25_
  61.8 0.6 collective-permute-done.24.rest_24_
  62.4 8.0 %main.1 = bf16[8,2,32,1024]{3,2,1,0:T(8,128)(2,1)S(1)} custom-call(s32[1]{0:T(128)S(6)} %copy.9.counts_ref, f32[1,1024]{1,0:T(1,128)S(1)} %bitcast.12, bf16[8,2,32,1024]{3,2,1,0:T(8,128)(2,1)S(1)} %get-tuple-element.56.both_ref, bf16[256,1024]{1,0:T(8,128)(2,1)S(1)} %get-tuple-element.57.normed_ref, f32[256,128]{1,0:T(8,128)S(1)} %get-tuple-element.58.stats_ref, ...), custom_call_target="tpu_custom_call" | custom-call | flops 3221225472 | bytes 10485760 | tf_op jit(solution)/shard_map/main/pallas_call | solution.py:263
  70.4 18.0 %all_to_all.5 = bf16[8,1,2,32,1024]{4,3,2,1,0:T(8,128)(2,1)S(1)} all-to-all(bf16[8,1,2,32,1024]{4,3,2,1,0:T(8,128)(2,1)S(1)} %bitcast.10), channel_id=1, replica_groups=mesh['clip'=4,'frame'=8] {'frame'}, dimensions={0} | all-to-all | bytes 2097152 | tf_op jit(solution)/shard_map/all_to_all | solution.py:553
  88.4 0.1 fusion
  88.5 0.9 %slice_bitcast_fusion = (bf16[1,1,196,1024]{3,2,1,0:T(8,128)(2,1)}, bf16[1,1,196,1024]{3,2,1,0:T(8,128)(2,1)}) fusion(bf16[1,256,1024]{2,1,0:T(8,128)(2,1)S(1)} %bitcast.13, bf16[1,256,1024]{2,1,0:T(8,128)(2,1)S(1)} %bitcast.14), kind=kLoop, calls=%fused_computation | loop fusion | bytes 1605632 | tf_op jit(solution)/shard_map/broadcast_in_dim | solution.py:557
  (6 shorter events, 0.1 us)
Async XLA Ops:
  3.3 17.9 %collective-permute-start.1 = (bf16[320,1024]{1,0:T(8,128)(2,1)}, bf16[320,1024]{1,0:T(8,128)(2,1)S(1)}, u32[]{:S(2)}, u32[]{:S(2)}) collective-permute-start(bf16[320,1024]{1,0:T(8,128)(2,1)} %get-tuple-element.33), channel_id=1, source_target_pairs={{0,2},{1,3},{2,0},{3,1},{4,6},{5,7},{6,4},{7,5},{8,10},{9,11},{10,... | collective-permute-start | bytes 1966088 | tf_op jit(solution)/shard_map/ppermute | solution.py:301
  6.3 16.8 %collective-permute-start.2 = (bf16[320,1024]{1,0:T(8,128)(2,1)}, bf16[320,1024]{1,0:T(8,128)(2,1)S(1)}, u32[]{:S(2)}, u32[]{:S(2)}) collective-permute-start(bf16[320,1024]{1,0:T(8,128)(2,1)} %get-tuple-element.34), channel_id=1, source_target_pairs={{0,4},{1,5},{2,6},{3,7},{4,0},{5,1},{6,2},{7,3},{8,12},{9,13},{10,... | collective-permute-start | bytes 1966088 | tf_op jit(solution)/shard_map/ppermute | solution.py:301
  7.8 16.9 %collective-permute-start = (bf16[128,1024]{1,0:T(8,128)(2,1)}, bf16[128,1024]{1,0:T(8,128)(2,1)S(1)}, u32[]{:S(2)}, u32[]{:S(2)}) collective-permute-start(bf16[128,1024]{1,0:T(8,128)(2,1)} %get-tuple-element.32.refs_1_.rest_0_), channel_id=1, source_target_pairs={{0,8},{8,0},{16,24},{24,16},{1,9},{9,1},{17,25},{25,17},{2,10},{10... | collective-permute-start | bytes 786440 | tf_op jit(solution)/shard_map/ppermute | solution.py:401
  9.4 15.8 %collective-permute-start.6 = (bf16[128,1024]{1,0:T(8,128)(2,1)}, bf16[128,1024]{1,0:T(8,128)(2,1)S(1)}, u32[]{:S(2)}, u32[]{:S(2)}) collective-permute-start(bf16[128,1024]{1,0:T(8,128)(2,1)} %get-tuple-element.32.refs_1_.rest_0_), channel_id=1, source_target_pairs={{0,24},{8,16},{16,8},{24,0},{1,25},{9,17},{17,9},{25,1},{2,26},{10... | collective-permute-start | bytes 786440 | tf_op jit(solution)/shard_map/ppermute | solution.py:401
  11.9 22.7 %collective-permute-start.5 = (bf16[128,1024]{1,0:T(8,128)(2,1)}, bf16[128,1024]{1,0:T(8,128)(2,1)S(1)}, u32[]{:S(2)}, u32[]{:S(2)}) collective-permute-start(bf16[128,1024]{1,0:T(8,128)(2,1)} %get-tuple-element.32.refs_1_.rest_0_), channel_id=1, source_target_pairs={{0,16},{8,24},{16,0},{24,8},{1,17},{9,25},{17,1},{25,9},{2,18},{10... | collective-permute-start | bytes 786440 | tf_op jit(solution)/shard_map/ppermute | solution.py:401
  21.3 13.3 %collective-permute-start.8 = (bf16[128,1024]{1,0:T(8,128)(2,1)S(1)}, bf16[128,1024]{1,0:T(8,128)(2,1)S(1)}, u32[]{:S(2)}, u32[]{:S(2)}) collective-permute-start(bf16[128,1024]{1,0:T(8,128)(2,1)S(1)} %slice.25), channel_id=1, source_target_pairs={{0,4},{1,5},{2,6},{3,7},{4,0},{5,1},{6,2},{7,3},{8,12},{9,13},{10,... | collective-permute-start | bytes 786440 | tf_op jit(solution)/shard_map/ppermute | solution.py:301
  23.2 23.9 %copy-start.3 = (bf16[192,1024]{1,0:T(8,128)(2,1)S(1)}, bf16[192,1024]{1,0:T(8,128)(2,1)}, u32[]{:S(2)}) copy-start(bf16[192,1024]{1,0:T(8,128)(2,1)} %get-tuple-element.51) | copy-start | bytes 1179652
  23.2 11.4 %collective-permute-start.7 = (bf16[128,1024]{1,0:T(8,128)(2,1)S(1)}, bf16[128,1024]{1,0:T(8,128)(2,1)S(1)}, u32[]{:S(2)}, u32[]{:S(2)}) collective-permute-start(bf16[128,1024]{1,0:T(8,128)(2,1)S(1)} %slice.24), channel_id=1, source_target_pairs={{0,2},{1,3},{2,0},{3,1},{4,6},{5,7},{6,4},{7,5},{8,10},{9,11},{10,... | collective-permute-start | bytes 786440 | tf_op jit(solution)/shard_map/ppermute | solution.py:301
  24.7 11.0 %collective-permute-start.4 = (bf16[128,1024]{1,0:T(8,128)(2,1)S(1)}, bf16[128,1024]{1,0:T(8,128)(2,1)S(1)}, u32[]{:S(2)}, u32[]{:S(2)}) collective-permute-start(bf16[128,1024]{1,0:T(8,128)(2,1)S(1)} %collective-permute-done.rest_10_), channel_id=1, source_target_pairs={{0,4},{1,5},{2,6},{3,7},{4,0},{5,1},{6,2},{7,3},{8,12},{9,13},{10,... | collective-permute-start | bytes 786440 | tf_op jit(solution)/shard_map/ppermute | solution.py:301
  25.2 10.5 %collective-permute-start.3 = (bf16[128,1024]{1,0:T(8,128)(2,1)S(1)}, bf16[128,1024]{1,0:T(8,128)(2,1)S(1)}, u32[]{:S(2)}, u32[]{:S(2)}) collective-permute-start(bf16[128,1024]{1,0:T(8,128)(2,1)S(1)} %collective-permute-done.rest_10_), channel_id=1, source_target_pairs={{0,2},{1,3},{2,0},{3,1},{4,6},{5,7},{6,4},{7,5},{8,10},{9,11},{10,... | collective-permute-start | bytes 786440 | tf_op jit(solution)/shard_map/ppermute | solution.py:301
  34.6 12.2 %collective-permute-start.10 = (bf16[256,1024]{1,0:T(8,128)(2,1)S(1)}, bf16[256,1024]{1,0:T(8,128)(2,1)S(1)}, u32[]{:S(2)}, u32[]{:S(2)}) collective-permute-start(bf16[256,1024]{1,0:T(8,128)(2,1)S(1)} %join.1.rest_16_), channel_id=1, source_target_pairs={{0,4},{1,5},{2,6},{3,7},{4,0},{5,1},{6,2},{7,3},{8,12},{9,13},{10,... | collective-permute-start | bytes 1572872 | tf_op jit(solution)/shard_map/ppermute | solution.py:301
  35.2 11.9 %collective-permute-start.9 = (bf16[256,1024]{1,0:T(8,128)(2,1)S(1)}, bf16[256,1024]{1,0:T(8,128)(2,1)S(1)}, u32[]{:S(2)}, u32[]{:S(2)}) collective-permute-start(bf16[256,1024]{1,0:T(8,128)(2,1)S(1)} %join.1.rest_16_), channel_id=1, source_target_pairs={{0,2},{1,3},{2,0},{3,1},{4,6},{5,7},{6,4},{7,5},{8,10},{9,11},{10,... | collective-permute-start | bytes 1572872 | tf_op jit(solution)/shard_map/ppermute | solution.py:301
  35.7 1.5 %collective-permute-start.17 = (bf16[128,1024]{1,0:T(8,128)(2,1)S(1)}, bf16[128,1024]{1,0:T(8,128)(2,1)S(1)}, u32[]{:S(2)}, u32[]{:S(2)}) collective-permute-start(bf16[128,1024]{1,0:T(8,128)(2,1)S(1)} %collective-permute-done.rest_10_), channel_id=1, source_target_pairs={{0,1},{1,0},{2,3},{3,2},{4,5},{5,4},{6,7},{7,6},{8,9},{9,8},{10,11... | collective-permute-start | bytes 786440 | tf_op jit(solution)/shard_map/ppermute | solution.py:301
  35.7 23.0 %copy-start = (bf16[128,1024]{1,0:T(8,128)(2,1)S(1)}, bf16[128,1024]{1,0:T(8,128)(2,1)}, u32[]{:S(2)}) copy-start(bf16[128,1024]{1,0:T(8,128)(2,1)} %get-tuple-element.32.refs_1_.rest_0_) | copy-start | bytes 786436
  35.8 23.0 %copy-start.1 = (bf16[64,1024]{1,0:T(8,128)(2,1)S(1)}, bf16[64,1024]{1,0:T(8,128)(2,1)}, u32[]{:S(2)}) copy-start(bf16[64,1024]{1,0:T(8,128)(2,1)} %get-tuple-element.46.refs_0_) | copy-start | bytes 393220
  35.8 1.9 %collective-permute-start.18 = (bf16[128,1024]{1,0:T(8,128)(2,1)S(1)}, bf16[128,1024]{1,0:T(8,128)(2,1)S(1)}, u32[]{:S(2)}, u32[]{:S(2)}) collective-permute-start(bf16[128,1024]{1,0:T(8,128)(2,1)S(1)} %collective-permute-done.3.by_x.rest_11_), channel_id=1, source_target_pairs={{0,1},{1,0},{2,3},{3,2},{4,5},{5,4},{6,7},{7,6},{8,9},{9,8},{10,11... | collective-permute-start | bytes 786440 | tf_op jit(solution)/shard_map/ppermute | solution.py:301
  36.3 13.0 %collective-permute-start.13 = (bf16[320,1024]{1,0:T(8,128)(2,1)S(1)}, bf16[320,1024]{1,0:T(8,128)(2,1)S(1)}, u32[]{:S(2)}, u32[]{:S(2)}) collective-permute-start(bf16[320,1024]{1,0:T(8,128)(2,1)S(1)} %collective-permute-done.1.refs_2_.rest_1_), channel_id=1, source_target_pairs={{0,1},{1,0},{2,3},{3,2},{4,5},{5,4},{6,7},{7,6},{8,9},{9,8},{10,11... | collective-permute-start | bytes 1966088 | tf_op jit(solution)/shard_map/ppermute | solution.py:301
  37.3 12.6 %collective-permute-start.14 = (bf16[320,1024]{1,0:T(8,128)(2,1)S(1)}, bf16[320,1024]{1,0:T(8,128)(2,1)S(1)}, u32[]{:S(2)}, u32[]{:S(2)}) collective-permute-start(bf16[320,1024]{1,0:T(8,128)(2,1)S(1)} %collective-permute-done.2.refs_3_.rest_2_), channel_id=1, source_target_pairs={{0,1},{1,0},{2,3},{3,2},{4,5},{5,4},{6,7},{7,6},{8,9},{9,8},{10,11... | collective-permute-start | bytes 1966088 | tf_op jit(solution)/shard_map/ppermute | solution.py:301
  37.6 9.8 %collective-permute-start.15 = (bf16[128,1024]{1,0:T(8,128)(2,1)S(1)}, bf16[128,1024]{1,0:T(8,128)(2,1)S(1)}, u32[]{:S(2)}, u32[]{:S(2)}) collective-permute-start(bf16[128,1024]{1,0:T(8,128)(2,1)S(1)} %collective-permute-done.7.refs_4_.rest_3_), channel_id=1, source_target_pairs={{0,1},{1,0},{2,3},{3,2},{4,5},{5,4},{6,7},{7,6},{8,9},{9,8},{10,11... | collective-permute-start | bytes 786440 | tf_op jit(solution)/shard_map/ppermute | solution.py:301
  46.9 1.8 %collective-permute-start.16 = (bf16[128,1024]{1,0:T(8,128)(2,1)S(1)}, bf16[128,1024]{1,0:T(8,128)(2,1)S(1)}, u32[]{:S(2)}, u32[]{:S(2)}) collective-permute-start(bf16[128,1024]{1,0:T(8,128)(2,1)S(1)} %collective-permute-done.8.refs_5_.rest_4_), channel_id=1, source_target_pairs={{0,1},{1,0},{2,3},{3,2},{4,5},{5,4},{6,7},{7,6},{8,9},{9,8},{10,11... | collective-permute-start | bytes 786440 | tf_op jit(solution)/shard_map/ppermute | solution.py:301
  47.1 2.2 %collective-permute-start.12 = (bf16[192,1024]{1,0:T(8,128)(2,1)S(1)}, bf16[192,1024]{1,0:T(8,128)(2,1)S(1)}, u32[]{:S(2)}, u32[]{:S(2)}) collective-permute-start(bf16[192,1024]{1,0:T(8,128)(2,1)S(1)} %copy-done.3), channel_id=1, source_target_pairs={{0,1},{1,0},{2,3},{3,2},{4,5},{5,4},{6,7},{7,6},{8,9},{9,8},{10,11... | collective-permute-start | bytes 1179656 | tf_op jit(solution)/shard_map/ppermute | solution.py:301
  47.4 11.3 %copy-start.2 = (f32[1024]{0:T(1024)S(1)}, f32[1024]{0:T(1024)}, u32[]{:S(2)}) copy-start(f32[1024]{0:T(1024)} %param.8) | copy-start | bytes 12292
  47.5 11.3 %collective-permute-start.11 = (bf16[192,1024]{1,0:T(8,128)(2,1)S(1)}, bf16[192,1024]{1,0:T(8,128)(2,1)S(1)}, u32[]{:S(2)}, u32[]{:S(2)}) collective-permute-start(bf16[192,1024]{1,0:T(8,128)(2,1)S(1)} %get-tuple-element.45), channel_id=1, source_target_pairs={{0,2},{1,3},{2,0},{3,1},{4,6},{5,7},{6,4},{7,5},{8,10},{9,11},{10,... | collective-permute-start | bytes 1179656 | tf_op jit(solution)/shard_map/ppermute | solution.py:301
  48.6 11.3 %collective-permute-start.20 = (bf16[192,1024]{1,0:T(8,128)(2,1)S(1)}, bf16[192,1024]{1,0:T(8,128)(2,1)S(1)}, u32[]{:S(2)}, u32[]{:S(2)}) collective-permute-start(bf16[192,1024]{1,0:T(8,128)(2,1)S(1)} %get-tuple-element.61), channel_id=1, source_target_pairs={{0,4},{1,5},{2,6},{3,7},{4,0},{5,1},{6,2},{7,3},{8,12},{9,13},{10,... | collective-permute-start | bytes 1179656 | tf_op jit(solution)/shard_map/ppermute | solution.py:301
  49.3 11.2 %collective-permute-start.19 = (bf16[128,1024]{1,0:T(8,128)(2,1)S(1)}, bf16[128,1024]{1,0:T(8,128)(2,1)S(1)}, u32[]{:S(2)}, u32[]{:S(2)}) collective-permute-start(bf16[128,1024]{1,0:T(8,128)(2,1)S(1)} %collective-permute-done.4.by_y.rest_12_), channel_id=1, source_target_pairs={{0,1},{1,0},{2,3},{3,2},{4,5},{5,4},{6,7},{7,6},{8,9},{9,8},{10,11... | collective-permute-start | bytes 786440 | tf_op jit(solution)/shard_map/ppermute | solution.py:301
  49.3 11.9 %collective-permute-start.21 = (bf16[256,1024]{1,0:T(8,128)(2,1)S(1)}, bf16[256,1024]{1,0:T(8,128)(2,1)S(1)}, u32[]{:S(2)}, u32[]{:S(2)}) collective-permute-start(bf16[256,1024]{1,0:T(8,128)(2,1)S(1)} %join.1.rest_16_), channel_id=1, source_target_pairs={{0,1},{1,0},{2,3},{3,2},{4,5},{5,4},{6,7},{7,6},{8,9},{9,8},{10,11... | collective-permute-start | bytes 1572872 | tf_op jit(solution)/shard_map/ppermute | solution.py:301
  49.8 11.4 %collective-permute-start.23 = (bf16[256,1024]{1,0:T(8,128)(2,1)S(1)}, bf16[256,1024]{1,0:T(8,128)(2,1)S(1)}, u32[]{:S(2)}, u32[]{:S(2)}) collective-permute-start(bf16[256,1024]{1,0:T(8,128)(2,1)S(1)} %collective-permute-done.10.pair_y.rest_18_), channel_id=1, source_target_pairs={{0,1},{1,0},{2,3},{3,2},{4,5},{5,4},{6,7},{7,6},{8,9},{9,8},{10,11... | collective-permute-start | bytes 1572872 | tf_op jit(solution)/shard_map/ppermute | solution.py:301
  58.8 2.5 %collective-permute-start.22 = (bf16[256,1024]{1,0:T(8,128)(2,1)S(1)}, bf16[256,1024]{1,0:T(8,128)(2,1)S(1)}, u32[]{:S(2)}, u32[]{:S(2)}) collective-permute-start(bf16[256,1024]{1,0:T(8,128)(2,1)S(1)} %collective-permute-done.9.pair_x.rest_17_), channel_id=1, source_target_pairs={{0,1},{1,0},{2,3},{3,2},{4,5},{5,4},{6,7},{7,6},{8,9},{9,8},{10,11... | collective-permute-start | bytes 1572872 | tf_op jit(solution)/shard_map/ppermute | solution.py:301
  59.9 1.9 %collective-permute-start.25 = (bf16[192,1024]{1,0:T(8,128)(2,1)S(1)}, bf16[192,1024]{1,0:T(8,128)(2,1)S(1)}, u32[]{:S(2)}, u32[]{:S(2)}) collective-permute-start(bf16[192,1024]{1,0:T(8,128)(2,1)S(1)} %collective-permute-done.20.rest_20_), channel_id=1, source_target_pairs={{0,1},{1,0},{2,3},{3,2},{4,5},{5,4},{6,7},{7,6},{8,9},{9,8},{10,11... | collective-permute-start | bytes 1179656 | tf_op jit(solution)/shard_map/ppermute | solution.py:301
  60.5 1.9 %collective-permute-start.24 = (bf16[192,1024]{1,0:T(8,128)(2,1)S(1)}, bf16[192,1024]{1,0:T(8,128)(2,1)S(1)}, u32[]{:S(2)}, u32[]{:S(2)}) collective-permute-start(bf16[192,1024]{1,0:T(8,128)(2,1)S(1)} %collective-permute-done.11.rest_19_), channel_id=1, source_target_pairs={{0,1},{1,0},{2,3},{3,2},{4,5},{5,4},{6,7},{7,6},{8,9},{9,8},{10,11... | collective-permute-start | bytes 1179656 | tf_op jit(solution)/shard_map/ppermute | solution.py:301
